TPU v7x, 256 devices: a whole 4x4x8 slice. The times are simulated.
256 devices in a mesh: dp: 4 (over y_lo, core), fsdp: 64 (over y_hi, x, z).
Axes of the slice: x: 4, y: 4 (y_hi: 2, y_lo: 2; y = y_hi * 2 + y_lo), z: 8, core: 2. Of those that a mesh axis runs over, the one named last changes fastest.
Arguments:
- acts: bfloat16 [4, 32768, 4096], P('dp', 'fsdp')
- token_ids: int32 [4, 32768], P('dp', 'fsdp'), may hold values from 127232 to 128255
- turn_ids: int32 [4, 32768], P('dp', 'fsdp'), may hold values from 0 to 255, never falling along the last dimension, each value on 1 to 512 neighbouring positions
- value_weight: bfloat16 [4096, 512], P('fsdp'), may hold values from -0.09375 to 0.09375
- norm_gain: float32 [512], replicated, may hold values from 0.5 to 1.5
- query_grad: float32 [4096, 512], P('fsdp'), may hold values from -6 to 6
Outputs:
- estimate: float32 [4096, 512], P('fsdp')
All inputs are finite; a program needn't handle non-finite values.
Results may differ from a plain program's by a relative error of at most 0.0032.
Values may be sent and summed in bfloat16 or wider, within the bound.
No kernel may reach another device: no remote copies, remote signals or barrier semaphores. Data moves between devices by JAX's collectives and lax.ppermute only.
A program may use at most 64 MiB of HBM per device.

v0:
```python
import jax
import jax.numpy as jnp
from jax import lax
from jax.sharding import Mesh, PartitionSpec as P

TURN_DEV = 4
ITERS = 2

damping = 1.0
lissa_scale = 12.0
first_special = 128000

FINE = ("ylo", "core", "yhi", "x", "z")
GROUP = ("ylo", "core")
SHARD = ("yhi", "x", "z")
PLANE = ("ylo", "yhi", "x")


def core_swap(value):
    return lax.ppermute(value, "core", [(0, 1), (1, 0)])


def exchange(blocks, axes):
    return lax.all_to_all(blocks, axes, split_axis=0, concat_axis=0, tiled=True)


def spread(block, axes):
    n = lax.axis_size(axes)
    return exchange(jnp.broadcast_to(block[None], (n,) + block.shape), axes)


def gather_plane(block):
    plane = spread(block, PLANE)
    n = lax.axis_size("ylo")
    plane = plane.reshape(n, plane.shape[0] // n * plane.shape[1], plane.shape[2])
    mine = jnp.concatenate([plane[i] for i in range(n)], axis=1)
    return mine, core_swap(mine)


def gather_line(block):
    line = spread(block, "z")
    return line.reshape(line.shape[0] * line.shape[1], line.shape[2])


def reduce_blocks(inputs, adjoint):
    half = adjoint.shape[1] // 2

    def outer(part):
        return lax.dot_general(
            inputs, part, (((0,), (0,)), ((), ())), preferred_element_type=jnp.float32
        )

    other = core_swap(outer(adjoint[:, half:]).astype(jnp.bfloat16))
    chip = outer(adjoint[:, :half]) + other.astype(jnp.float32)
    n_low, n_plane, n_line = lax.axis_size("ylo"), lax.axis_size(PLANE), lax.axis_size("z")
    cols = half // n_low
    columns = jnp.stack([chip[:, i * cols : (i + 1) * cols] for i in range(n_low)])
    columns = columns.astype(jnp.bfloat16).reshape(n_plane, -1, cols)
    line = jnp.sum(exchange(columns, PLANE).astype(jnp.float32), axis=0)
    line = line.astype(jnp.bfloat16).reshape(n_line, -1, cols)
    return jnp.sum(exchange(line, "z").astype(jnp.float32), axis=0)


def norm_jacobian(vector, unit_values, root_mean):
    inner = jnp.mean(unit_values * vector, axis=-1, keepdims=True)
    return (vector - unit_values * inner) / root_mean


def turn_counts(text_mask, turn_ids):
    n = lax.axis_size(SHARD)
    first, last = turn_ids[0], turn_ids[-1]

    def edge(turn):
        count = jnp.sum(jnp.where(turn_ids == turn, text_mask, 0.0))
        row = jnp.stack([turn.astype(jnp.float32), count])
        return jnp.broadcast_to(row[:, None, None], (2, 8, 128))

    left = lax.ppermute(edge(last), SHARD, [(i, i + 1) for i in range(n - 1)])
    right = lax.ppermute(edge(first), SHARD, [(i + 1, i) for i in range(n - 1)])
    same = turn_ids[:, None] == turn_ids[None, :]
    counts = jnp.sum(jnp.where(same, text_mask[None, :], 0.0), axis=1)
    as_float = turn_ids.astype(jnp.float32)
    for other in (left, right):
        counts = counts + jnp.where(as_float == other[0, 0, 0], other[1, 0, 0], 0.0)
    return counts


def local(acts, token_ids, turn_ids, value_weight, norm_gain, query_grad):
    inputs = acts.reshape(acts.shape[1], acts.shape[2])
    ids = turn_ids.reshape(-1)
    features = value_weight.shape[1]
    n_group = lax.axis_size(GROUP)
    turn_total = TURN_DEV * lax.axis_size(SHARD) * n_group
    cols = features // n_group
    me = lax.axis_index(GROUP)
    core = lax.axis_index("core")
    text_mask = (token_ids.reshape(-1) < first_special).astype(jnp.float32)

    def own(array):
        return lax.dynamic_slice(array, (0, me * cols), (array.shape[0], cols))

    def project(halves):
        return jnp.concatenate(
            [jnp.dot(inputs, half, preferred_element_type=jnp.float32) for half in halves], axis=1
        )

    gain = norm_gain.reshape(2, 2, cols)
    gain = jnp.concatenate(
        [jnp.where(core == 0, gain[:, 0], gain[:, 1]), jnp.where(core == 0, gain[:, 1], gain[:, 0])]
    ).reshape(-1)
    gain_square = gain * gain
    query = own(query_grad)

    both = gather_line(jnp.concatenate([own(value_weight), query.astype(jnp.bfloat16)], axis=1))
    values = project(gather_plane(both[:, :cols]))
    tangent = project(gather_plane(both[:, cols:]))
    own_count = turn_counts(text_mask, ids)
    turn_weight = text_mask / (jnp.maximum(own_count, 1.0) * jnp.float32(turn_total))
    root_mean = jnp.sqrt(jnp.mean(values * values, axis=-1, keepdims=True) + 1e-06)
    unit_values = values / root_mean
    estimate = query
    for step in range(ITERS):
        if step:
            tangent = project(gather_plane(gather_line(estimate.astype(jnp.bfloat16))))
        inner = gain_square * norm_jacobian(tangent, unit_values, root_mean)
        adjoint = (turn_weight[:, None] * norm_jacobian(inner, unit_values, root_mean)).astype(
            jnp.bfloat16
        )
        curvature = reduce_blocks(inputs, adjoint)
        estimate = query + estimate - (curvature + damping * estimate) / lissa_scale
    whole = spread(estimate, GROUP)
    return jnp.concatenate([whole[i] for i in range(n_group)], axis=1)


def solution(mesh):
    fine = Mesh(mesh.devices.reshape(2, 2, 2, 4, 8), FINE)
    placed = (
        P(GROUP, SHARD, None),
        P(GROUP, SHARD),
        P(GROUP, SHARD),
        P(SHARD, None),
        P(),
        P(SHARD, None),
    )
    return jax.shard_map(
        local, mesh=fine, in_specs=placed, out_specs=P(SHARD, None), check_vma=False
    )
```

profile of v0, /device:TPU:1, one launch (start us, length us, event | category | flops | bytes accessed | tf_op | source)
XLA Modules:
  0.0 266.5 jit_solution(8248687541646253392)
XLA Ops:
  0.0 0.8 dynamic-slice_convert_fusion
  0.8 19.2 %all_to_all.50 = bf16[8,64,256]{2,1,0:T(8,128)(2,1)S(1)} all-to-all(bf16[8,64,256]{2,1,0:T(8,128)(2,1)S(1)} %broadcast_in_dim.53), channel_id=1, replica_groups=mesh['ylo'=2,'core'=2,'yhi'=2,'x'=4,'z'=8] {'z'}, dimensions={0} | all-to-all | bytes 524288 | tf_op jit(solution)/shard_map/all_to_all | solution.py:24
  20.0 0.4 broadcast_in_dim.96
  20.4 32.2 %all_to_all.51 = bf16[16,512,128]{2,1,0:T(8,128)(2,1)} all-to-all(bf16[16,512,128]{2,1,0:T(8,128)(2,1)S(1)} %broadcast_in_dim.96), channel_id=1, replica_groups=mesh['ylo'=2,'core'=2,'yhi'=2,'x'=4,'z'=8] {'ylo','yhi','x'}, dimensions={0} | all-to-all | bytes 4194304 | tf_op jit(solution)/shard_map/all_to_all | solution.py:24
  52.6 1.8 broadcast_in_dim.54
  54.4 3.8 %all-to-all-start.1 = ((bf16[16,512,128]{2,1,0:T(8,128)(2,1)}), bf16[16,512,128]{2,1,0:T(8,128)(2,1)S(1)}, u32[]{:S(2)}, u32[]{:S(2)}) async-start(bf16[16,512,128]{2,1,0:T(8,128)(2,1)} %broadcast_in_dim.54), calls=%async_computation.1 | async-start | bytes 4194304 | tf_op jit(solution)/shard_map/all_to_all | solution.py:24
  58.3 0.6 fusion.57
  59.5 1.9 select_reduce_fusion.2
  61.5 0.8 pad_maximum_fusion.11
  62.3 1.3 collective-permute-start.1
  64.2 0.7 pad_maximum_fusion.10
  65.0 4.0 %collective-permute-start = (f32[2,8,128]{2,1,0:T(8,128)S(1)}, f32[2,8,128]{2,1,0:T(8,128)S(1)}, u32[]{:S(2)}, u32[]{:S(2)}) collective-permute-start(f32[2,8,128]{2,1,0:T(8,128)S(1)} %broadcast_in_dim.49), channel_id=1, source_target_pairs={{0,1},{1,2},{2,3},{3,4},{4,5},{5,6},{6,7},{7,8},{8,9},{9,10},{10,1... | collective-permute-start | bytes 24584 | tf_op jit(solution)/shard_map/ppermute | solution.py:78
  69.0 0.2 select_reduce_fusion
  69.2 1.7 fusion.52
  70.9 1.6 pad_maximum_fusion.1
  72.6 4.5 %collective-permute-start.3 = (bf16[4096,256]{1,0:T(8,128)(2,1)}, bf16[4096,256]{1,0:T(8,128)(2,1)}, u32[]{:S(2)}, u32[]{:S(2)}) collective-permute-start(bf16[4096,256]{1,0:T(8,128)(2,1)} %pad_maximum_fusion.1), channel_id=1, source_target_pairs={{0,64},{64,0},{1,65},{65,1},{2,66},{66,2},{3,67},{67,3},{4,68},{68... | collective-permute-start | bytes 6291464 | tf_op jit(solution)/shard_map/ppermute | solution.py:20
  77.1 6.4 %all-to-all-done.1 = bf16[16,512,128]{2,1,0:T(8,128)(2,1)S(1)} async-done(((bf16[16,512,128]{2,1,0:T(8,128)(2,1)}), bf16[16,512,128]{2,1,0:T(8,128)(2,1)S(1)}, u32[]{:S(2)}, u32[]{:S(2)}) %all-to-all-start.1) | async-done | bytes 2097184 | tf_op jit(solution)/shard_map/all_to_all | solution.py:24
  83.5 0.2 fusion.53
  83.7 0.2 pad_maximum_fusion
  84.0 6.4 %collective-permute-start.2 = (bf16[4096,256]{1,0:T(8,128)(2,1)S(1)}, bf16[4096,256]{1,0:T(8,128)(2,1)S(1)}, u32[]{:S(2)}, u32[]{:S(2)}) collective-permute-start(bf16[4096,256]{1,0:T(8,128)(2,1)S(1)} %pad_maximum_fusion), channel_id=1, source_target_pairs={{0,64},{64,0},{1,65},{65,1},{2,66},{66,2},{3,67},{67,3},{4,68},{68... | collective-permute-start | bytes 6291464 | tf_op jit(solution)/shard_map/ppermute | solution.py:20
  90.4 0.6 fusion.56
  91.0 0.5 fusion.55
  91.6 2.5 multiply_divide_fusion
  94.1 1.3 fusion.24
  95.4 1.3 fusion.18
  96.7 2.9 %fusion.27 = f32[512,256]{0,1:T(8,128)S(1)} fusion(bf16[4096,256]{1,0:T(8,128)(2,1)} %collective-permute-done.3, bf16[1,512,4096]{2,1,0:T(8,128)(2,1)S(1)} %copy-done.6), kind=kOutput, calls=%fused_computation.32 | convolution fusion | flops 1073741824 | bytes 6815744 | tf_op jit(solution)/shard_map/dot_general | solution.py:104
  99.8 1.3 fusion.21
  101.1 0.3 multiply_reduce_fusion.3
  101.4 0.3 multiply_reduce_fusion.2
  101.6 0.4 multiply_convert_fusion.1
  102.0 1.3 fusion
  103.3 0.3 collective-permute-start.4
  103.6 4.1 %collective-permute-done.4 = bf16[4096,256]{0,1:T(8,128)(2,1)S(1)} collective-permute-done((bf16[4096,256]{0,1:T(8,128)(2,1)S(1)}, bf16[4096,256]{0,1:T(8,128)(2,1)S(1)}, u32[]{:S(2)}, u32[]{:S(2)}) %collective-permute-start.4) | collective-permute-done | bytes 2097184 | tf_op jit(solution)/shard_map/ppermute | solution.py:20
  107.7 1.3 add_convert_fusion.1
  109.0 0.2 slice_bitcast_fusion.3
  109.2 0.2 pad_maximum_fusion.2
  109.4 2.5 copy.20
  111.9 31.9 %all_to_all.52 = bf16[16,512,128]{2,1,0:T(8,128)(2,1)S(1)} all-to-all(bf16[16,512,128]{2,1,0:T(8,128)(2,1)} %bitcast.114), channel_id=1, replica_groups=mesh['ylo'=2,'core'=2,'yhi'=2,'x'=4,'z'=8] {'ylo','yhi','x'}, dimensions={0} | all-to-all | bytes 4194304 | tf_op jit(solution)/shard_map/all_to_all | solution.py:24
  143.8 0.3 reduce_sum.120
  144.1 11.7 %all_to_all.53 = bf16[8,64,128]{2,1,0:T(8,128)(2,1)S(1)} all-to-all(bf16[8,64,128]{2,1,0:T(8,128)(2,1)S(1)} %bitcast.130), channel_id=1, replica_groups=mesh['ylo'=2,'core'=2,'yhi'=2,'x'=4,'z'=8] {'z'}, dimensions={0} | all-to-all | bytes 262144 | tf_op jit(solution)/shard_map/all_to_all | solution.py:24
  155.9 10.3 %all_to_all.54 = bf16[8,64,128]{2,1,0:T(8,128)(2,1)S(1)} all-to-all(bf16[8,64,128]{2,1,0:T(8,128)(2,1)S(1)} %broadcast_in_dim.97), channel_id=1, replica_groups=mesh['ylo'=2,'core'=2,'yhi'=2,'x'=4,'z'=8] {'z'}, dimensions={0} | all-to-all | bytes 262144 | tf_op jit(solution)/shard_map/all_to_all | solution.py:24
  166.2 0.4 broadcast_in_dim.99
  166.6 27.5 %all_to_all.55 = bf16[16,512,128]{2,1,0:T(8,128)(2,1)S(1)} all-to-all(bf16[16,512,128]{2,1,0:T(8,128)(2,1)S(1)} %broadcast_in_dim.99), channel_id=1, replica_groups=mesh['ylo'=2,'core'=2,'yhi'=2,'x'=4,'z'=8] {'ylo','yhi','x'}, dimensions={0} | all-to-all | bytes 4194304 | tf_op jit(solution)/shard_map/all_to_all | solution.py:24
  194.1 0.1 fusion.51
  194.2 0.2 pad_maximum_fusion.3
  194.5 4.7 %collective-permute-start.5 = (bf16[4096,256]{1,0:T(8,128)(2,1)S(1)}, bf16[4096,256]{1,0:T(8,128)(2,1)S(1)}, u32[]{:S(2)}, u32[]{:S(2)}) collective-permute-start(bf16[4096,256]{1,0:T(8,128)(2,1)S(1)} %pad_maximum_fusion.3), channel_id=1, source_target_pairs={{0,64},{64,0},{1,65},{65,1},{2,66},{66,2},{3,67},{67,3},{4,68},{68... | collective-permute-start | bytes 6291464 | tf_op jit(solution)/shard_map/ppermute | solution.py:20
  199.1 1.3 fusion.30
  200.4 2.5 collective-permute-done.5
  202.9 1.3 fusion.33
  204.2 0.3 multiply_reduce_fusion.1
  204.5 0.3 multiply_reduce_fusion
  204.8 0.4 multiply_convert_fusion
  205.2 1.3 fusion.1
  206.4 0.5 collective-permute-start.6
  206.9 3.8 %collective-permute-done.6 = bf16[4096,256]{0,1:T(8,128)(2,1)S(1)} collective-permute-done((bf16[4096,256]{0,1:T(8,128)(2,1)S(1)}, bf16[4096,256]{0,1:T(8,128)(2,1)S(1)}, u32[]{:S(2)}, u32[]{:S(2)}) %collective-permute-start.6) | collective-permute-done | bytes 2097184 | tf_op jit(solution)/shard_map/ppermute | solution.py:20
  210.7 1.3 add_convert_fusion
  212.0 0.2 slice_bitcast_fusion.1
  212.2 0.2 pad_maximum_fusion.4
  212.4 2.5 copy.21
  214.9 31.6 %all_to_all.56 = bf16[16,512,128]{2,1,0:T(8,128)(2,1)S(1)} all-to-all(bf16[16,512,128]{2,1,0:T(8,128)(2,1)} %bitcast.115), channel_id=1, replica_groups=mesh['ylo'=2,'core'=2,'yhi'=2,'x'=4,'z'=8] {'ylo','yhi','x'}, dimensions={0} | all-to-all | bytes 4194304 | tf_op jit(solution)/shard_map/all_to_all | solution.py:24
  246.5 0.3 reduce_sum.124
  246.8 10.3 %all_to_all.57 = bf16[8,64,128]{2,1,0:T(8,128)(2,1)S(1)} all-to-all(bf16[8,64,128]{2,1,0:T(8,128)(2,1)S(1)} %bitcast.129), channel_id=1, replica_groups=mesh['ylo'=2,'core'=2,'yhi'=2,'x'=4,'z'=8] {'z'}, dimensions={0} | all-to-all | bytes 262144 | tf_op jit(solution)/shard_map/all_to_all | solution.py:24
  257.2 8.6 %all_to_all.58 = f32[4,64,128]{2,1,0:T(8,128)S(1)} all-to-all(f32[4,64,128]{2,1,0:T(8,128)S(1)} %broadcast_in_dim.100), channel_id=1, replica_groups=mesh['ylo'=2,'core'=2,'yhi'=2,'x'=4,'z'=8] {'ylo','core'}, dimensions={0} | all-to-all | bytes 262144 | tf_op jit(solution)/shard_map/all_to_all | solution.py:24
  265.8 0.7 pad_maximum_fusion.8
  (42 shorter events, 0.5 us)
Async XLA Ops:
  54.4 3.9 %copy-start.3 = (s32[1,512]{1,0:T(1,128)S(1)}, s32[1,512]{1,0:T(1,128)}, u32[]{:S(2)}) copy-start(s32[1,512]{1,0:T(1,128)} %param.8) | copy-start | bytes 6148
  54.4 5.1 %copy-start.4 = (s32[1,512]{1,0:T(1,128)S(1)}, s32[1,512]{1,0:T(1,128)}, u32[]{:S(2)}) copy-start(s32[1,512]{1,0:T(1,128)} %param.7) | copy-start | bytes 6148
  54.4 14.8 %copy-start.5 = (f32[512]{0:T(512)S(1)}, f32[512]{0:T(512)}, u32[]{:S(2)}) copy-start(f32[512]{0:T(512)} %param.10) | copy-start | bytes 6148
  54.4 29.1 %all-to-all-start.1 = ((bf16[16,512,128]{2,1,0:T(8,128)(2,1)}), bf16[16,512,128]{2,1,0:T(8,128)(2,1)S(1)}, u32[]{:S(2)}, u32[]{:S(2)}) async-start(bf16[16,512,128]{2,1,0:T(8,128)(2,1)} %broadcast_in_dim.54), calls=%async_computation.1 | async-start | bytes 4194304 | tf_op jit(solution)/shard_map/all_to_all | solution.py:24
  62.3 28.1 %collective-permute-start.1 = (f32[2,8,128]{2,1,0:T(8,128)S(1)}, f32[2,8,128]{2,1,0:T(8,128)S(1)}, u32[]{:S(2)}, u32[]{:S(2)}) collective-permute-start(f32[2,8,128]{2,1,0:T(8,128)S(1)} %broadcast_in_dim.51), channel_id=1, source_target_pairs={{1,0},{2,1},{3,2},{4,3},{5,4},{6,5},{7,6},{8,7},{9,8},{10,9},{11,1... | collective-permute-start | bytes 24584 | tf_op jit(solution)/shard_map/ppermute | solution.py:79
  65.0 26.0 %collective-permute-start = (f32[2,8,128]{2,1,0:T(8,128)S(1)}, f32[2,8,128]{2,1,0:T(8,128)S(1)}, u32[]{:S(2)}, u32[]{:S(2)}) collective-permute-start(f32[2,8,128]{2,1,0:T(8,128)S(1)} %broadcast_in_dim.49), channel_id=1, source_target_pairs={{0,1},{1,2},{2,3},{3,4},{4,5},{5,6},{6,7},{7,8},{8,9},{9,10},{10,1... | collective-permute-start | bytes 24584 | tf_op jit(solution)/shard_map/ppermute | solution.py:78
  70.9 1.6 copy-start
  72.6 24.2 %collective-permute-start.3 = (bf16[4096,256]{1,0:T(8,128)(2,1)}, bf16[4096,256]{1,0:T(8,128)(2,1)}, u32[]{:S(2)}, u32[]{:S(2)}) collective-permute-start(bf16[4096,256]{1,0:T(8,128)(2,1)} %pad_maximum_fusion.1), channel_id=1, source_target_pairs={{0,64},{64,0},{1,65},{65,1},{2,66},{66,2},{3,67},{67,3},{4,68},{68... | collective-permute-start | bytes 6291464 | tf_op jit(solution)/shard_map/ppermute | solution.py:20
  83.5 10.6 %copy-start.6 = (bf16[1,512,4096]{2,1,0:T(8,128)(2,1)S(1)}, bf16[1,512,4096]{2,1,0:T(8,128)(2,1)}, u32[]{:S(2)}) copy-start(bf16[1,512,4096]{2,1,0:T(8,128)(2,1)} %param.6) | copy-start | bytes 12582916
  83.7 10.4 %copy-start.1 = (bf16[8,512,128]{2,1,0:T(8,128)(2,1)S(1)}, bf16[8,512,128]{2,1,0:T(8,128)(2,1)}, u32[]{:S(2)}) copy-start(bf16[8,512,128]{2,1,0:T(8,128)(2,1)} %copy-done) | copy-start | bytes 3145732
  84.0 15.8 %collective-permute-start.2 = (bf16[4096,256]{1,0:T(8,128)(2,1)S(1)}, bf16[4096,256]{1,0:T(8,128)(2,1)S(1)}, u32[]{:S(2)}, u32[]{:S(2)}) collective-permute-start(bf16[4096,256]{1,0:T(8,128)(2,1)S(1)} %pad_maximum_fusion), channel_id=1, source_target_pairs={{0,64},{64,0},{1,65},{65,1},{2,66},{66,2},{3,67},{67,3},{4,68},{68... | collective-permute-start | bytes 6291464 | tf_op jit(solution)/shard_map/ppermute | solution.py:20
  103.3 4.4 %collective-permute-start.4 = (bf16[4096,256]{0,1:T(8,128)(2,1)S(1)}, bf16[4096,256]{0,1:T(8,128)(2,1)S(1)}, u32[]{:S(2)}, u32[]{:S(2)}) collective-permute-start(bf16[4096,256]{0,1:T(8,128)(2,1)S(1)} %fusion), channel_id=1, source_target_pairs={{0,64},{64,0},{1,65},{65,1},{2,66},{66,2},{3,67},{67,3},{4,68},{68... | collective-permute-start | bytes 6291464 | tf_op jit(solution)/shard_map/ppermute | solution.py:20
  143.8 12.0 %copy-start.2 = (f32[64,512]{1,0:T(8,128)S(1)}, f32[64,512]{1,0:T(8,128)}, u32[]{:S(2)}) copy-start(f32[64,512]{1,0:T(8,128)} %param.11) | copy-start | bytes 393220
  194.2 4.9 %copy-start.7 = (bf16[1,512,4096]{2,1,0:T(8,128)(2,1)S(1)}, bf16[1,512,4096]{2,1,0:T(8,128)(2,1)}, u32[]{:S(2)}) copy-start(bf16[1,512,4096]{2,1,0:T(8,128)(2,1)} %param.6) | copy-start | bytes 12582916
  194.5 8.5 %collective-permute-start.5 = (bf16[4096,256]{1,0:T(8,128)(2,1)S(1)}, bf16[4096,256]{1,0:T(8,128)(2,1)S(1)}, u32[]{:S(2)}, u32[]{:S(2)}) collective-permute-start(bf16[4096,256]{1,0:T(8,128)(2,1)S(1)} %pad_maximum_fusion.3), channel_id=1, source_target_pairs={{0,64},{64,0},{1,65},{65,1},{2,66},{66,2},{3,67},{67,3},{4,68},{68... | collective-permute-start | bytes 6291464 | tf_op jit(solution)/shard_map/ppermute | solution.py:20
  206.4 4.2 %collective-permute-start.6 = (bf16[4096,256]{0,1:T(8,128)(2,1)S(1)}, bf16[4096,256]{0,1:T(8,128)(2,1)S(1)}, u32[]{:S(2)}, u32[]{:S(2)}) collective-permute-start(bf16[4096,256]{0,1:T(8,128)(2,1)S(1)} %fusion.1), channel_id=1, source_target_pairs={{0,64},{64,0},{1,65},{65,1},{2,66},{66,2},{3,67},{67,3},{4,68},{68... | collective-permute-start | bytes 6291464 | tf_op jit(solution)/shard_map/ppermute | solution.py:20
where the time goes:
time: 267 us
  blocking collectives  183 us (69%)
  starting transfers between devices  25.5 us (10%)
  waiting for transfers between devices  16.9 us (6%)
  matrix products  14.4 us (5%)
  local copies, waits for them, and re-layouts  12.7 us (5%)
  other arithmetic  12 us (4%)
    all_to_all x9, blocking collectives, exchange(): return lax.all_to_all(blocks, axes, split_axis=0, concat_axis=0, tiled=True)  183 us
    ppermute x5, starting transfers between devices, core_swap(): return lax.ppermute(value, 'core', [(0, 1), (1, 0)])  16.4 us
    ppermute x5, waiting for transfers between devices, core_swap(): return lax.ppermute(value, 'core', [(0, 1), (1, 0)])  10.4 us
    dot_general x6, matrix products, project(): jnp.dot(inputs, half, preferred_element_type=jnp.float32)  9.35 us
    all_to_all x1, waiting for transfers between devices, exchange(): return lax.all_to_all(blocks, axes, split_axis=0, concat_axis=0, tiled=True)  6.45 us
    another operation x4, local copies, waits for them, and re-layouts, reduce_blocks(): jnp.stack([chip[:, i * cols:(i + 1) * cols] for i in range(n_low)])  5.39 us
  transfers between devices with their start and end apart: 8, of which 4 were waited for; matrix products, arithmetic and copies ran while one was open for 7% of the time, Pallas kernels for 0%

commit v1 on v0

--- a/solution.py
+++ b/solution.py
@@ -13,7 +13,7 @@
 FINE = ("ylo", "core", "yhi", "x", "z")
 GROUP = ("ylo", "core")
 SHARD = ("yhi", "x", "z")
-PLANE = ("ylo", "yhi", "x")
+LINE = ("ylo", "yhi", "z")
 
 
 def core_swap(value):
@@ -29,17 +29,17 @@
     return exchange(jnp.broadcast_to(block[None], (n,) + block.shape), axes)
 
 
-def gather_plane(block):
-    plane = spread(block, PLANE)
+def gather_line(block):
     n = lax.axis_size("ylo")
-    plane = plane.reshape(n, plane.shape[0] // n * plane.shape[1], plane.shape[2])
-    mine = jnp.concatenate([plane[i] for i in range(n)], axis=1)
-    return mine, core_swap(mine)
+    line = spread(block, LINE)
+    line = line.reshape(n, line.shape[0] // n * line.shape[1], line.shape[2])
+    return [line[i] for i in range(n)]
 
 
-def gather_line(block):
-    line = spread(block, "z")
-    return line.reshape(line.shape[0] * line.shape[1], line.shape[2])
+def gather_rows(pieces):
+    rows = spread(jnp.concatenate(pieces, axis=1), "x")
+    mine = rows.reshape(rows.shape[0] * rows.shape[1], rows.shape[2])
+    return mine, core_swap(mine)
 
 
 def reduce_blocks(inputs, adjoint):
@@ -52,13 +52,13 @@
 
     other = core_swap(outer(adjoint[:, half:]).astype(jnp.bfloat16))
     chip = outer(adjoint[:, :half]) + other.astype(jnp.float32)
-    n_low, n_plane, n_line = lax.axis_size("ylo"), lax.axis_size(PLANE), lax.axis_size("z")
+    n_low, n_line, n_x = lax.axis_size("ylo"), lax.axis_size(LINE), lax.axis_size("x")
     cols = half // n_low
-    columns = jnp.stack([chip[:, i * cols : (i + 1) * cols] for i in range(n_low)])
-    columns = columns.astype(jnp.bfloat16).reshape(n_plane, -1, cols)
-    line = jnp.sum(exchange(columns, PLANE).astype(jnp.float32), axis=0)
-    line = line.astype(jnp.bfloat16).reshape(n_line, -1, cols)
-    return jnp.sum(exchange(line, "z").astype(jnp.float32), axis=0)
+    rows = chip.astype(jnp.bfloat16).reshape(n_x, -1, half)
+    line = jnp.sum(exchange(rows, "x").astype(jnp.float32), axis=0).astype(jnp.bfloat16)
+    line = jnp.concatenate([line[:, i * cols : (i + 1) * cols] for i in range(n_low)], axis=0)
+    parts = exchange(line.reshape(n_line, -1, cols), LINE)
+    return jnp.sum(parts.astype(jnp.float32), axis=0)
 
 
 def norm_jacobian(vector, unit_values, root_mean):
@@ -86,7 +86,9 @@
 
 
 def local(acts, token_ids, turn_ids, value_weight, norm_gain, query_grad):
-    inputs = acts.reshape(acts.shape[1], acts.shape[2])
+    n_yhi, n_x = lax.axis_size("yhi"), lax.axis_size("x")
+    inputs = acts.reshape(acts.shape[1], n_yhi, n_x, -1).transpose(0, 2, 1, 3)
+    inputs = inputs.reshape(acts.shape[1], acts.shape[2])
     ids = turn_ids.reshape(-1)
     features = value_weight.shape[1]
     n_group = lax.axis_size(GROUP)
@@ -112,8 +114,8 @@
     query = own(query_grad)
 
     both = gather_line(jnp.concatenate([own(value_weight), query.astype(jnp.bfloat16)], axis=1))
-    values = project(gather_plane(both[:, :cols]))
-    tangent = project(gather_plane(both[:, cols:]))
+    values = project(gather_rows([piece[:, :cols] for piece in both]))
+    tangent = project(gather_rows([piece[:, cols:] for piece in both]))
     own_count = turn_counts(text_mask, ids)
     turn_weight = text_mask / (jnp.maximum(own_count, 1.0) * jnp.float32(turn_total))
     root_mean = jnp.sqrt(jnp.mean(values * values, axis=-1, keepdims=True) + 1e-06)
@@ -121,7 +123,7 @@
     estimate = query
     for step in range(ITERS):
         if step:
-            tangent = project(gather_plane(gather_line(estimate.astype(jnp.bfloat16))))
+            tangent = project(gather_rows(gather_line(estimate.astype(jnp.bfloat16))))
         inner = gain_square * norm_jacobian(tangent, unit_values, root_mean)
         adjoint = (turn_weight[:, None] * norm_jacobian(inner, unit_values, root_mean)).astype(
             jnp.bfloat16

time: 267 us -> 304 us (1.14)
  waiting for transfers between devices: 16.9 us -> 30.9 us
  blocking collectives: 183 us -> 191 us
  local copies, waits for them, and re-layouts: 12.7 us -> 19.2 us
  starting transfers between devices: 25.5 us -> 31.5 us
    all_to_all x1 -> x2, waiting for transfers between devices: 6.45 us -> 20.8 us  [exchange(): return lax.all_to_all(blocks, axes, split_axis=0, concat_axis=0, tiled=True)]
    all_to_all x9 -> x8, blocking collectives: 183 us -> 191 us  [exchange(): return lax.all_to_all(blocks, axes, split_axis=0, concat_axis=0, tiled=True)]
    ppermute x1, starting transfers between devices: 3.98 us -> 11.1 us  [turn_counts(): left = lax.ppermute(edge(last), SHARD, [(i, i + 1) for i in range(n - 1)])]
    unnamed x16 -> x13, local copies, waits for them, and re-layouts: 0.03 us -> 6.58 us
    ppermute x5, starting transfers between devices: 16.4 us -> 10.5 us  [core_swap(): return lax.ppermute(value, 'core', [(0, 1), (1, 0)])]
    another operation x4 -> x0, local copies, waits for them, and re-layouts: 5.39 us -> none  [reduce_blocks(): jnp.stack([chip[:, i * cols:(i + 1) * cols] for i in range(n_low)])]
    all_to_all x1 -> x2, starting transfers between devices: 3.85 us -> 8.64 us  [exchange(): return lax.all_to_all(blocks, axes, split_axis=0, concat_axis=0, tiled=True)]
    transpose x0 -> x1, local copies, waits for them, and re-layouts: none -> 4.38 us  [local(): inputs = acts.reshape(acts.shape[1], n_yhi, n_x, -1).transpose(0, 2, 1, 3)]
  transfers between devices with their start and end apart: 8 -> 9, of which waited for: 4 -> 4; matrix products, arithmetic and copies ran while one was open for 7% -> 10% of each run, Pallas kernels for 0% -> 0%
where the time goes in v1:
time: 304 us; the launch traced here: 303 us
  blocking collectives  191 us (63%)
  starting transfers between devices  31.5 us (10%)
  waiting for transfers between devices  30.9 us (10%)
  local copies, waits for them, and re-layouts  19.2 us (6%)
  matrix products  17.3 us (6%)
  other arithmetic  11 us (4%)
    all_to_all x8, blocking collectives, exchange(): return lax.all_to_all(blocks, axes, split_axis=0, concat_axis=0, tiled=True)  191 us
    all_to_all x2, waiting for transfers between devices, exchange(): return lax.all_to_all(blocks, axes, split_axis=0, concat_axis=0, tiled=True)  20.8 us
    dot_general x6, matrix products, project(): jnp.dot(inputs, half, preferred_element_type=jnp.float32)  12.1 us
    ppermute x1, starting transfers between devices, turn_counts(): left = lax.ppermute(edge(last), SHARD, [(i, i + 1) for i in range(n - 1)])  11.1 us
    ppermute x5, starting transfers between devices, core_swap(): return lax.ppermute(value, 'core', [(0, 1), (1, 0)])  10.5 us
    ppermute x5, waiting for transfers between devices, core_swap(): return lax.ppermute(value, 'core', [(0, 1), (1, 0)])  10.1 us
    all_to_all x2, starting transfers between devices, exchange(): return lax.all_to_all(blocks, axes, split_axis=0, concat_axis=0, tiled=True)  8.64 us
    unnamed x13, local copies, waits for them, and re-layouts  6.58 us
  transfers between devices with their start and end apart: 9, of which 4 were waited for; matrix products, arithmetic and copies ran while one was open for 10% of the time, Pallas kernels for 0%

profile of v1, /device:TPU:1, one launch (start us, length us, event | category | flops | bytes accessed | tf_op | source)
XLA Modules:
  0.0 302.6 jit_solution(16860639774117948008)
XLA Ops:
  0.0 0.8 dynamic-slice_convert_fusion
  0.8 0.1 broadcast_in_dim.51
  0.9 36.5 %all_to_all.50 = bf16[32,64,256]{2,1,0:T(8,128)(2,1)S(1)} all-to-all(bf16[32,64,256]{2,1,0:T(8,128)(2,1)S(1)} %broadcast_in_dim.51), channel_id=1, replica_groups=mesh['ylo'=2,'core'=2,'yhi'=2,'x'=4,'z'=8] {'ylo','yhi','z'}, dimensions={0} | all-to-all | bytes 2097152 | tf_op jit(solution)/shard_map/all_to_all | solution.py:24
  37.4 0.1 fusion.13
  37.6 1.5 broadcast_in_dim.53
  39.1 4.0 %all-to-all-start.2 = ((bf16[4,1024,256]{2,1,0:T(8,128)(2,1)}), bf16[4,1024,256]{2,1,0:T(8,128)(2,1)S(1)}, u32[]{:S(2)}, u32[]{:S(2)}) async-start(bf16[4,1024,256]{2,1,0:T(8,128)(2,1)} %broadcast_in_dim.53), calls=%async_computation.2 | async-start | bytes 4194304 | tf_op jit(solution)/shard_map/all_to_all | solution.py:24
  43.2 20.8 %all-to-all-done.2 = bf16[4,1024,256]{2,1,0:T(8,128)(2,1)S(1)} async-done(((bf16[4,1024,256]{2,1,0:T(8,128)(2,1)}), bf16[4,1024,256]{2,1,0:T(8,128)(2,1)S(1)}, u32[]{:S(2)}, u32[]{:S(2)}) %all-to-all-start.2) | async-done | bytes 2097184 | tf_op jit(solution)/shard_map/all_to_all | solution.py:24
  63.9 1.4 broadcast_in_dim.52
  65.4 4.6 %all-to-all-start.1 = ((bf16[4,1024,256]{2,1,0:T(8,128)(2,1)}), bf16[4,1024,256]{2,1,0:T(8,128)(2,1)}, u32[]{:S(2)}, u32[]{:S(2)}) async-start(bf16[4,1024,256]{2,1,0:T(8,128)(2,1)} %broadcast_in_dim.52), calls=%async_computation.1 | async-start | bytes 4194304 | tf_op jit(solution)/shard_map/all_to_all | solution.py:24
  70.0 0.7 fusion.21
  71.4 2.0 select_reduce_fusion.2
  73.3 0.7 pad_maximum_fusion.11
  74.1 1.3 collective-permute-start.1
  76.1 0.6 pad_maximum_fusion.10
  76.8 11.1 %collective-permute-start = (f32[2,8,128]{2,1,0:T(8,128)S(1)}, f32[2,8,128]{2,1,0:T(8,128)S(1)}, u32[]{:S(2)}, u32[]{:S(2)}) collective-permute-start(f32[2,8,128]{2,1,0:T(8,128)S(1)} %broadcast_in_dim.47), channel_id=1, source_target_pairs={{0,1},{1,2},{2,3},{3,4},{4,5},{5,6},{6,7},{7,8},{8,9},{9,10},{10,1... | collective-permute-start | bytes 24584 | tf_op jit(solution)/shard_map/ppermute | solution.py:78
  87.9 3.3 %collective-permute-start.3 = (bf16[4096,256]{1,0:T(8,128)(2,1)S(1)}, bf16[4096,256]{1,0:T(8,128)(2,1)}, u32[]{:S(2)}, u32[]{:S(2)}) collective-permute-start(bf16[4096,256]{1,0:T(8,128)(2,1)S(1)} %bitcast.106), channel_id=1, source_target_pairs={{0,64},{64,0},{1,65},{65,1},{2,66},{66,2},{3,67},{67,3},{4,68},{68... | collective-permute-start | bytes 6291464 | tf_op jit(solution)/shard_map/ppermute | solution.py:20
  91.2 0.2 select_reduce_fusion
  91.5 6.6 %copy.46 = bf16[1,512,4096]{1,2,0:T(8,128)(2,1)} copy(bf16[1,512,4096]{2,1,0:T(8,128)(2,1)} %param.6) | data formatting | bytes 8388608 | tf_op args[0]
  98.0 4.4 %copy.47 = bf16[512,4,2,512]{0,3,2,1:T(8,128)(2,1)} copy(bf16[512,4,2,512]{0,3,1,2:T(8,128)(2,1)} %bitcast.101) | data formatting | bytes 8388608 | tf_op jit(solution)/shard_map/transpose | solution.py:90
  102.4 0.6 fusion.20
  103.0 0.6 fusion.19
  103.6 2.5 multiply_divide_fusion
  106.2 4.2 %convolution_bitcast_fusion.7 = f32[512,256]{0,1:T(8,128)S(1)} fusion(bf16[4096,256]{1,0:T(8,128)(2,1)} %bitcast.20, bf16[512,4096]{0,1:T(8,128)(2,1)} %bitcast.91), kind=kOutput, calls=%fused_computation.15 | convolution fusion | flops 1073741824 | bytes 6815744 | tf_op jit(solution)/shard_map/dot_general | solution.py:106
  110.4 1.3 convolution_bitcast_fusion.5
  111.7 2.8 convolution_bitcast_fusion.4
  114.5 0.1 multiply_reduce_fusion.4
  114.7 1.3 convolution_bitcast_fusion.6
  115.9 0.3 multiply_reduce_fusion.3
  116.2 0.3 multiply_reduce_fusion.2
  116.5 0.4 multiply_convert_fusion.1
  116.9 1.3 fusion
  118.2 0.6 collective-permute-start.4
  118.8 3.8 %collective-permute-done.4 = bf16[4096,256]{0,1:T(8,128)(2,1)S(1)} collective-permute-done((bf16[4096,256]{0,1:T(8,128)(2,1)S(1)}, bf16[4096,256]{0,1:T(8,128)(2,1)S(1)}, u32[]{:S(2)}, u32[]{:S(2)}) %collective-permute-start.4) | collective-permute-done | bytes 2097184 | tf_op jit(solution)/shard_map/ppermute | solution.py:20
  122.6 1.3 add_convert_fusion.1
  123.9 0.2 copy.66
  124.1 29.7 %all_to_all.51 = bf16[4,1024,256]{1,2,0:T(8,128)(2,1)S(1)} all-to-all(bf16[4,1024,256]{1,2,0:T(8,128)(2,1)S(1)} %bitcast.102), channel_id=1, replica_groups=mesh['ylo'=2,'core'=2,'yhi'=2,'x'=4,'z'=8] {'x'}, dimensions={0} | all-to-all | bytes 4194304 | tf_op jit(solution)/shard_map/all_to_all | solution.py:24
  153.8 1.3 reduce_sum.120
  155.1 1.1 fusion.16
  156.2 0.3 copy.50
  156.5 20.3 %all_to_all.52 = bf16[32,64,128]{2,1,0:T(8,128)(2,1)S(1)} all-to-all(bf16[32,64,128]{2,1,0:T(8,128)(2,1)S(1)} %bitcast.110), channel_id=1, replica_groups=mesh['ylo'=2,'core'=2,'yhi'=2,'x'=4,'z'=8] {'ylo','yhi','z'}, dimensions={0} | all-to-all | bytes 1048576 | tf_op jit(solution)/shard_map/all_to_all | solution.py:24
  176.8 0.1 convert_reduce_fusion.1
  176.9 0.1 broadcast_in_dim.54
  177.0 20.6 %all_to_all.53 = bf16[32,64,128]{2,1,0:T(8,128)(2,1)S(1)} all-to-all(bf16[32,64,128]{2,1,0:T(8,128)(2,1)S(1)} %broadcast_in_dim.54), channel_id=1, replica_groups=mesh['ylo'=2,'core'=2,'yhi'=2,'x'=4,'z'=8] {'ylo','yhi','z'}, dimensions={0} | all-to-all | bytes 1048576 | tf_op jit(solution)/shard_map/all_to_all | solution.py:24
  197.7 0.1 broadcast_in_dim.55
  197.9 23.9 %all_to_all.54 = bf16[4,1024,256]{2,1,0:T(8,128)(2,1)S(1)} all-to-all(bf16[4,1024,256]{2,1,0:T(8,128)(2,1)S(1)} %broadcast_in_dim.55), channel_id=1, replica_groups=mesh['ylo'=2,'core'=2,'yhi'=2,'x'=4,'z'=8] {'x'}, dimensions={0} | all-to-all | bytes 4194304 | tf_op jit(solution)/shard_map/all_to_all | solution.py:24
  221.7 6.1 %collective-permute-start.5 = (bf16[4096,256]{1,0:T(8,128)(2,1)S(1)}, bf16[4096,256]{1,0:T(8,128)(2,1)S(1)}, u32[]{:S(2)}, u32[]{:S(2)}) collective-permute-start(bf16[4096,256]{1,0:T(8,128)(2,1)S(1)} %bitcast.108), channel_id=1, source_target_pairs={{0,64},{64,0},{1,65},{65,1},{2,66},{66,2},{3,67},{67,3},{4,68},{68... | collective-permute-start | bytes 6291464 | tf_op jit(solution)/shard_map/ppermute | solution.py:20
  227.9 1.3 convolution_bitcast_fusion.3
  229.2 2.5 collective-permute-done.5
  231.7 1.3 convolution_bitcast_fusion.2
  232.9 0.3 multiply_reduce_fusion.1
  233.2 0.3 multiply_reduce_fusion
  233.5 0.4 multiply_convert_fusion
  233.9 1.3 fusion.1
  235.2 0.5 collective-permute-start.6
  235.7 3.8 %collective-permute-done.6 = bf16[4096,256]{0,1:T(8,128)(2,1)S(1)} collective-permute-done((bf16[4096,256]{0,1:T(8,128)(2,1)S(1)}, bf16[4096,256]{0,1:T(8,128)(2,1)S(1)}, u32[]{:S(2)}, u32[]{:S(2)}) %collective-permute-start.6) | collective-permute-done | bytes 2097184 | tf_op jit(solution)/shard_map/ppermute | solution.py:20
  239.5 1.3 add_convert_fusion
  240.8 0.2 copy.65
  241.0 28.6 %all_to_all.55 = bf16[4,1024,256]{1,2,0:T(8,128)(2,1)S(1)} all-to-all(bf16[4,1024,256]{1,2,0:T(8,128)(2,1)S(1)} %bitcast.103), channel_id=1, replica_groups=mesh['ylo'=2,'core'=2,'yhi'=2,'x'=4,'z'=8] {'x'}, dimensions={0} | all-to-all | bytes 4194304 | tf_op jit(solution)/shard_map/all_to_all | solution.py:24
  269.5 0.4 reduce_sum.124
  270.0 0.3 copy.53
  270.3 20.9 %all_to_all.56 = bf16[32,64,128]{2,1,0:T(8,128)(2,1)S(1)} all-to-all(bf16[32,64,128]{2,1,0:T(8,128)(2,1)S(1)} %bitcast.111), channel_id=1, replica_groups=mesh['ylo'=2,'core'=2,'yhi'=2,'x'=4,'z'=8] {'ylo','yhi','z'}, dimensions={0} | all-to-all | bytes 1048576 | tf_op jit(solution)/shard_map/all_to_all | solution.py:24
  291.2 0.1 convert_reduce_fusion
  291.4 10.5 %all_to_all.57 = f32[4,64,128]{2,1,0:T(8,128)S(1)} all-to-all(f32[4,64,128]{2,1,0:T(8,128)S(1)} %broadcast_in_dim.98), channel_id=1, replica_groups=mesh['ylo'=2,'core'=2,'yhi'=2,'x'=4,'z'=8] {'ylo','core'}, dimensions={0} | all-to-all | bytes 262144 | tf_op jit(solution)/shard_map/all_to_all | solution.py:24
  301.9 0.7 pad_maximum_fusion.8
  (43 shorter events, 0.7 us)
Async XLA Ops:
  39.1 24.8 %all-to-all-start.2 = ((bf16[4,1024,256]{2,1,0:T(8,128)(2,1)}), bf16[4,1024,256]{2,1,0:T(8,128)(2,1)S(1)}, u32[]{:S(2)}, u32[]{:S(2)}) async-start(bf16[4,1024,256]{2,1,0:T(8,128)(2,1)} %broadcast_in_dim.53), calls=%async_computation.2 | async-start | bytes 4194304 | tf_op jit(solution)/shard_map/all_to_all | solution.py:24
  65.4 4.6 %copy-start.3 = (s32[1,512]{1,0:T(1,128)S(1)}, s32[1,512]{1,0:T(1,128)}, u32[]{:S(2)}) copy-start(s32[1,512]{1,0:T(1,128)} %param.8) | copy-start | bytes 6148
  65.4 6.0 %copy-start.4 = (s32[1,512]{1,0:T(1,128)S(1)}, s32[1,512]{1,0:T(1,128)}, u32[]{:S(2)}) copy-start(s32[1,512]{1,0:T(1,128)} %param.7) | copy-start | bytes 6148
  65.4 26.1 %copy-start.5 = (f32[512]{0:T(512)S(1)}, f32[512]{0:T(512)}, u32[]{:S(2)}) copy-start(f32[512]{0:T(512)} %param.10) | copy-start | bytes 6148
  65.4 37.0 %all-to-all-start.1 = ((bf16[4,1024,256]{2,1,0:T(8,128)(2,1)}), bf16[4,1024,256]{2,1,0:T(8,128)(2,1)}, u32[]{:S(2)}, u32[]{:S(2)}) async-start(bf16[4,1024,256]{2,1,0:T(8,128)(2,1)} %broadcast_in_dim.52), calls=%async_computation.1 | async-start | bytes 4194304 | tf_op jit(solution)/shard_map/all_to_all | solution.py:24
  74.1 28.3 %collective-permute-start.1 = (f32[2,8,128]{2,1,0:T(8,128)S(1)}, f32[2,8,128]{2,1,0:T(8,128)S(1)}, u32[]{:S(2)}, u32[]{:S(2)}) collective-permute-start(f32[2,8,128]{2,1,0:T(8,128)S(1)} %broadcast_in_dim.49), channel_id=1, source_target_pairs={{1,0},{2,1},{3,2},{4,3},{5,4},{6,5},{7,6},{8,7},{9,8},{10,9},{11,1... | collective-permute-start | bytes 24584 | tf_op jit(solution)/shard_map/ppermute | solution.py:79
  76.8 26.2 %collective-permute-start = (f32[2,8,128]{2,1,0:T(8,128)S(1)}, f32[2,8,128]{2,1,0:T(8,128)S(1)}, u32[]{:S(2)}, u32[]{:S(2)}) collective-permute-start(f32[2,8,128]{2,1,0:T(8,128)S(1)} %broadcast_in_dim.47), channel_id=1, source_target_pairs={{0,1},{1,2},{2,3},{3,4},{4,5},{5,6},{6,7},{7,8},{8,9},{9,10},{10,1... | collective-permute-start | bytes 24584 | tf_op jit(solution)/shard_map/ppermute | solution.py:78
  87.9 23.7 %collective-permute-start.3 = (bf16[4096,256]{1,0:T(8,128)(2,1)S(1)}, bf16[4096,256]{1,0:T(8,128)(2,1)}, u32[]{:S(2)}, u32[]{:S(2)}) collective-permute-start(bf16[4096,256]{1,0:T(8,128)(2,1)S(1)} %bitcast.106), channel_id=1, source_target_pairs={{0,64},{64,0},{1,65},{65,1},{2,66},{66,2},{3,67},{67,3},{4,68},{68... | collective-permute-start | bytes 6291464 | tf_op jit(solution)/shard_map/ppermute | solution.py:20
  102.4 12.2 %collective-permute-start.2 = (bf16[4096,256]{1,0:T(8,128)(2,1)}, bf16[4096,256]{1,0:T(8,128)(2,1)S(1)}, u32[]{:S(2)}, u32[]{:S(2)}) collective-permute-start(bf16[4096,256]{1,0:T(8,128)(2,1)} %bitcast.20), channel_id=1, source_target_pairs={{0,64},{64,0},{1,65},{65,1},{2,66},{66,2},{3,67},{67,3},{4,68},{68... | collective-permute-start | bytes 6291464 | tf_op jit(solution)/shard_map/ppermute | solution.py:20
  106.1 4.2 %copy-start = (bf16[512,4,2,512]{0,3,2,1:T(8,128)(2,1)S(1)}, bf16[512,4,2,512]{0,3,2,1:T(8,128)(2,1)}, u32[]{:S(2)}) copy-start(bf16[512,4,2,512]{0,3,2,1:T(8,128)(2,1)} %copy.47) | copy-start | bytes 12582916
  118.2 4.4 %collective-permute-start.4 = (bf16[4096,256]{0,1:T(8,128)(2,1)S(1)}, bf16[4096,256]{0,1:T(8,128)(2,1)S(1)}, u32[]{:S(2)}, u32[]{:S(2)}) collective-permute-start(bf16[4096,256]{0,1:T(8,128)(2,1)S(1)} %fusion), channel_id=1, source_target_pairs={{0,64},{64,0},{1,65},{65,1},{2,66},{66,2},{3,67},{67,3},{4,68},{68... | collective-permute-start | bytes 6291464 | tf_op jit(solution)/shard_map/ppermute | solution.py:20
  156.2 20.7 %copy-start.2 = (f32[64,512]{1,0:T(8,128)S(1)}, f32[64,512]{1,0:T(8,128)}, u32[]{:S(2)}) copy-start(f32[64,512]{1,0:T(8,128)} %param.11) | copy-start | bytes 393220
  197.9 30.0 %copy-start.1 = (bf16[512,4,2,512]{0,3,2,1:T(8,128)(2,1)S(1)}, bf16[512,4,2,512]{0,3,2,1:T(8,128)(2,1)}, u32[]{:S(2)}) copy-start(bf16[512,4,2,512]{0,3,2,1:T(8,128)(2,1)} %copy.47) | copy-start | bytes 12582916
  221.7 9.9 %collective-permute-start.5 = (bf16[4096,256]{1,0:T(8,128)(2,1)S(1)}, bf16[4096,256]{1,0:T(8,128)(2,1)S(1)}, u32[]{:S(2)}, u32[]{:S(2)}) collective-permute-start(bf16[4096,256]{1,0:T(8,128)(2,1)S(1)} %bitcast.108), channel_id=1, source_target_pairs={{0,64},{64,0},{1,65},{65,1},{2,66},{66,2},{3,67},{67,3},{4,68},{68... | collective-permute-start | bytes 6291464 | tf_op jit(solution)/shard_map/ppermute | solution.py:20
  235.2 4.2 %collective-permute-start.6 = (bf16[4096,256]{0,1:T(8,128)(2,1)S(1)}, bf16[4096,256]{0,1:T(8,128)(2,1)S(1)}, u32[]{:S(2)}, u32[]{:S(2)}) collective-permute-start(bf16[4096,256]{0,1:T(8,128)(2,1)S(1)} %fusion.1), channel_id=1, source_target_pairs={{0,64},{64,0},{1,65},{65,1},{2,66},{66,2},{3,67},{67,3},{4,68},{68... | collective-permute-start | bytes 6291464 | tf_op jit(solution)/shard_map/ppermute | solution.py:20

commit v2 on v0

v2 whole, which is shorter than its diff:
```python
import jax
import jax.numpy as jnp
from jax import lax
from jax.experimental import pallas as pl
from jax.experimental.pallas import tpu as pltpu
from jax.sharding import Mesh, PartitionSpec as P

TURN_DEV = 4
ITERS = 2

damping = 1.0
lissa_scale = 12.0
first_special = 128000

FINE = ("ylo", "core", "yhi", "x", "z")
GROUP = ("ylo", "core")
SHARD = ("yhi", "x", "z")
PLANE = ("ylo", "yhi", "x")


def core_swap(value):
    return lax.ppermute(value, "core", [(0, 1), (1, 0)])


def exchange(blocks, axes):
    return lax.all_to_all(blocks, axes, split_axis=0, concat_axis=0, tiled=True)


def spread(block, axes):
    n = lax.axis_size(axes)
    return exchange(jnp.broadcast_to(block[None], (n,) + block.shape), axes)


def gather_plane(block):
    plane = spread(block, PLANE)
    n = lax.axis_size("ylo")
    mine = plane.reshape((n, plane.shape[0] // n) + block.shape)
    return mine, core_swap(mine)


def gather_line(block):
    line = spread(block, "z")
    return line.reshape(line.shape[0] * line.shape[1], line.shape[2])


def kernel_params():
    return pltpu.CompilerParams(
        dimension_semantics=("arbitrary",), vmem_limit_bytes=32 * 1024 * 1024
    )


def times_rows(acts_ref, rows_ref):
    rows = jnp.concatenate([rows_ref[0, 0], rows_ref[1, 0]], axis=1)
    return jnp.dot(acts_ref[...], rows, preferred_element_type=jnp.float32)


def project_kernel(acts_ref, rows_ref, out_ref):
    part = times_rows(acts_ref, rows_ref)

    @pl.when(pl.program_id(0) == 0)
    def _():
        out_ref[...] = part

    @pl.when(pl.program_id(0) > 0)
    def _():
        out_ref[...] += part


def project(inputs, rows):
    n_low, n_chunk, chunk, cols = rows.shape
    tokens = inputs.shape[0]
    return pl.pallas_call(
        project_kernel,
        grid=(n_chunk,),
        in_specs=[
            pl.BlockSpec((tokens, chunk), lambda i: (0, i)),
            pl.BlockSpec((n_low, 1, chunk, cols), lambda i: (0, i, 0, 0)),
        ],
        out_specs=pl.BlockSpec((tokens, n_low * cols), lambda i: (0, 0)),
        out_shape=jax.ShapeDtypeStruct((tokens, n_low * cols), jnp.float32),
        compiler_params=kernel_params(),
        cost_estimate=pl.CostEstimate(
            flops=2 * inputs.size * n_low * cols,
            bytes_accessed=2 * (inputs.size + rows.size) + 4 * tokens * n_low * cols,
            transcendentals=0,
        ),
    )(inputs, rows)


def adjoint_kernel(
    n_chunk,
    acts_ref,
    rows_ref,
    tangent_ref,
    values_ref,
    other_values_ref,
    gain_ref,
    weight_ref,
    own_ref,
    sent_ref,
    total_ref,
    other_ref,
):
    step = pl.program_id(0)
    tokens, half = tangent_ref.shape
    features = 2 * half

    @pl.when(step == 0)
    def _():
        total_ref[...] = times_rows(acts_ref, rows_ref)

    @pl.when((step > 0) & (step < n_chunk))
    def _():
        total_ref[...] += times_rows(acts_ref, rows_ref)

    @pl.when(step == n_chunk - 1)
    def _():
        size = min(128, tokens)

        def mean(first, second):
            whole = jnp.sum(first, axis=-1, keepdims=True) + jnp.sum(second, axis=-1, keepdims=True)
            return whole * (1.0 / features)

        for start in range(0, tokens, size):
            at = slice(start, start + size)
            value = (values_ref[at, :], other_values_ref[at, :])
            tangent = (tangent_ref[at, :], total_ref[at, :])
            inverse = 1.0 / jnp.sqrt(mean(value[0] * value[0], value[1] * value[1]) + 1e-06)
            unit = [v * inverse for v in value]

            def jacobian(vector):
                inner = mean(unit[0] * vector[0], unit[1] * vector[1])
                return [(v - u * inner) * inverse for v, u in zip(vector, unit)]

            scaled = [gain_ref[i : i + 1, :] * v for i, v in enumerate(jacobian(tangent))]
            weight = weight_ref[at, :]
            own, other = [weight * v for v in jacobian(scaled)]
            own_ref[:, at] = own.T.astype(jnp.bfloat16)
            other_ref[:, at] = other.T.astype(jnp.bfloat16)

    @pl.when(step >= n_chunk)
    def _():
        block = jnp.dot(other_ref[...], acts_ref[...], preferred_element_type=jnp.float32)
        block = block.astype(jnp.bfloat16)
        sent_ref[0, 0] = block[: half // 2]
        sent_ref[1, 0] = block[half // 2 :]


def adjoint_products(inputs, rows, tangent, values, gain_square, weight):
    n_low, n_chunk, chunk, cols = rows.shape
    tokens, half = tangent.shape

    def whole(*shape):
        return pl.BlockSpec(shape, lambda i: (0,) * len(shape))

    return pl.pallas_call(
        lambda *refs: adjoint_kernel(n_chunk, *refs),
        grid=(2 * n_chunk,),
        in_specs=[
            pl.BlockSpec((tokens, chunk), lambda i: (0, i % n_chunk)),
            pl.BlockSpec(
                (n_low, 1, chunk, cols), lambda i: (0, jnp.minimum(i, n_chunk - 1), 0, 0)
            ),
            whole(tokens, half),
            whole(tokens, half),
            whole(tokens, half),
            whole(2, half),
            whole(tokens, 1),
        ],
        out_specs=[
            whole(half, tokens),
            pl.BlockSpec(
                (n_low, 1, cols, chunk), lambda i: (0, jnp.maximum(i - n_chunk, 0), 0, 0)
            ),
        ],
        out_shape=[
            jax.ShapeDtypeStruct((half, tokens), jnp.bfloat16),
            jax.ShapeDtypeStruct((n_low, n_chunk, cols, chunk), jnp.bfloat16),
        ],
        scratch_shapes=[
            pltpu.VMEM((tokens, half), jnp.float32),
            pltpu.VMEM((half, tokens), jnp.bfloat16),
        ],
        compiler_params=kernel_params(),
    )(inputs, rows, tangent, values[0], values[1], gain_square, weight)


def curvature_kernel(acts_ref, adjoint_ref, other_ref, out_ref):
    block = jnp.dot(adjoint_ref[...], acts_ref[...], preferred_element_type=jnp.float32)
    half = block.shape[0] // 2
    for i in range(2):
        total = block[i * half : (i + 1) * half] + other_ref[i, 0].astype(jnp.float32)
        out_ref[i, 0] = total.astype(jnp.bfloat16)


def curvature_blocks(inputs, adjoint, other):
    n_low, n_chunk, cols, chunk = other.shape
    tokens = inputs.shape[0]
    piece = pl.BlockSpec((n_low, 1, cols, chunk), lambda i: (0, i, 0, 0))
    return pl.pallas_call(
        curvature_kernel,
        grid=(n_chunk,),
        in_specs=[
            pl.BlockSpec((tokens, chunk), lambda i: (0, i)),
            pl.BlockSpec(adjoint.shape, lambda i: (0, 0)),
            piece,
        ],
        out_specs=piece,
        out_shape=jax.ShapeDtypeStruct(other.shape, jnp.bfloat16),
        compiler_params=kernel_params(),
    )(inputs, adjoint, other)


def reduce_blocks(blocks):
    n_low, n_chunk, cols, chunk = blocks.shape
    n_line = lax.axis_size("z")
    parts = exchange(blocks.reshape(n_low * n_chunk, cols, chunk), PLANE)
    line = jnp.sum(parts.astype(jnp.float32), axis=0).astype(jnp.bfloat16)
    line = line.reshape(cols, n_line, chunk // n_line).transpose(1, 2, 0)
    return jnp.sum(exchange(line, "z").astype(jnp.float32), axis=0)


def turn_counts(text_mask, turn_ids):
    n = lax.axis_size(SHARD)
    first, last = turn_ids[0], turn_ids[-1]

    def edge(turn):
        count = jnp.sum(jnp.where(turn_ids == turn, text_mask, 0.0))
        row = jnp.stack([turn.astype(jnp.float32), count])
        return jnp.broadcast_to(row[:, None, None], (2, 8, 128))

    left = lax.ppermute(edge(last), SHARD, [(i, i + 1) for i in range(n - 1)])
    right = lax.ppermute(edge(first), SHARD, [(i + 1, i) for i in range(n - 1)])
    same = turn_ids[:, None] == turn_ids[None, :]
    counts = jnp.sum(jnp.where(same, text_mask[None, :], 0.0), axis=1)
    as_float = turn_ids.astype(jnp.float32)
    for other in (left, right):
        counts = counts + jnp.where(as_float == other[0, 0, 0], other[1, 0, 0], 0.0)
    return counts


def local(acts, token_ids, turn_ids, value_weight, norm_gain, query_grad):
    inputs = acts.reshape(acts.shape[1], acts.shape[2])
    ids = turn_ids.reshape(-1)
    features = value_weight.shape[1]
    n_group = lax.axis_size(GROUP)
    turn_total = TURN_DEV * lax.axis_size(SHARD) * n_group
    cols = features // n_group
    me = lax.axis_index(GROUP)
    core = lax.axis_index("core")
    text_mask = (token_ids.reshape(-1) < first_special).astype(jnp.float32)

    def own(array):
        return lax.dynamic_slice(array, (0, me * cols), (array.shape[0], cols))

    gain = norm_gain.reshape(2, 2, cols)
    gain = jnp.stack(
        [jnp.where(core == 0, gain[:, 0], gain[:, 1]), jnp.where(core == 0, gain[:, 1], gain[:, 0])]
    ).reshape(2, -1)
    gain_square = gain * gain
    query = own(query_grad)

    both = gather_line(jnp.concatenate([own(value_weight), query.astype(jnp.bfloat16)], axis=1))
    values = [project(inputs, half) for half in gather_plane(both[:, :cols])]
    mine, other = gather_plane(both[:, cols:])
    own_count = turn_counts(text_mask, ids)
    turn_weight = text_mask / (jnp.maximum(own_count, 1.0) * jnp.float32(turn_total))
    weight = turn_weight[:, None]
    estimate = query
    for step in range(ITERS):
        if step:
            mine, other = gather_plane(gather_line(estimate.astype(jnp.bfloat16)))
        tangent = project(inputs, mine)
        adjoint, sent = adjoint_products(inputs, other, tangent, values, gain_square, weight)
        curvature = reduce_blocks(curvature_blocks(inputs, adjoint, core_swap(sent)))
        estimate = query + estimate - (curvature + damping * estimate) / lissa_scale
    whole = spread(estimate, GROUP)
    return jnp.concatenate([whole[i] for i in range(n_group)], axis=1)


def solution(mesh):
    fine = Mesh(mesh.devices.reshape(2, 2, 2, 4, 8), FINE)
    placed = (
        P(GROUP, SHARD, None),
        P(GROUP, SHARD),
        P(GROUP, SHARD),
        P(SHARD, None),
        P(),
        P(SHARD, None),
    )
    return jax.shard_map(
        local, mesh=fine, in_specs=placed, out_specs=P(SHARD, None), check_vma=False
    )
```

time: 267 us -> 302 us (1.13)
  Pallas kernels: 0 us -> 40 us
  matrix products: 14.4 us -> 0 us
  waiting for transfers between devices: 16.9 us -> 29.8 us
  blocking collectives: 183 us -> 188 us
  other arithmetic: 12 us -> 8.94 us
    pallas_call x0 -> x8, Pallas kernels: none -> 40 us  [the longest x2 18.3 us: adjoint_products(): pl.pallas_call(lambda *refs: adjoint_kernel(n_chunk, *refs), grid=(2 * n_...]
    all_to_all x1, waiting for transfers between devices: 6.45 us -> 21 us  [exchange(): return lax.all_to_all(blocks, axes, split_axis=0, concat_axis=0, tiled=True)]
    dot_general x10 -> x0, matrix products: 14.4 us -> none  [the longest x6 9.35 us: project(): jnp.dot(inputs, half, preferred_element_type=jnp.float32)]
    another operation x4 -> x0, local copies, waits for them, and re-layouts: 5.39 us -> none  [reduce_blocks(): jnp.stack([chip[:, i * cols:(i + 1) * cols] for i in range(n_low)])]
    all_to_all x9, blocking collectives: 183 us -> 188 us  [exchange(): return lax.all_to_all(blocks, axes, split_axis=0, concat_axis=0, tiled=True)]
    unnamed x16 -> x12, local copies, waits for them, and re-layouts: 0.03 us -> 3.79 us
  transfers between devices with their start and end apart: 8 -> 8, of which waited for: 4 -> 5; matrix products, arithmetic and copies ran while one was open for 7% -> 3% of each run, Pallas kernels for 0% -> 5%
where the time goes in v2:
time: 302 us; the launch traced here: 301 us
  blocking collectives  188 us (62%)
  Pallas kernels  40 us (13%)
  waiting for transfers between devices  29.8 us (10%)
  starting transfers between devices  23.6 us (8%)
  local copies, waits for them, and re-layouts  9.7 us (3%)
  other arithmetic  8.94 us (3%)
    all_to_all x9, blocking collectives, exchange(): return lax.all_to_all(blocks, axes, split_axis=0, concat_axis=0, tiled=True)  188 us
    all_to_all x1, waiting for transfers between devices, exchange(): return lax.all_to_all(blocks, axes, split_axis=0, concat_axis=0, tiled=True)  21 us
    pallas_call x2, Pallas kernels, adjoint_products(): pl.pallas_call(lambda *refs: adjoint_kernel(n_chunk, *refs), grid=(2 * n_...  18.3 us
    ppermute x5, starting transfers between devices, core_swap(): return lax.ppermute(value, 'core', [(0, 1), (1, 0)])  17.2 us
    pallas_call x4, Pallas kernels, project(): pl.pallas_call(project_kernel, grid=(n_chunk,), in_specs=[pl.BlockSpec((t...  15.6 us
    ppermute x5, waiting for transfers between devices, core_swap(): return lax.ppermute(value, 'core', [(0, 1), (1, 0)])  8.12 us
    pallas_call x2, Pallas kernels, curvature_blocks(): pl.pallas_call(curvature_kernel, grid=(n_chunk,), in_specs=[pl.BlockSpec(...  6.11 us
  transfers between devices with their start and end apart: 8, of which 5 were waited for; matrix products, arithmetic and copies ran while one was open for 3% of the time, Pallas kernels for 5%

profile of v2, /device:TPU:1, one launch (start us, length us, event | category | flops | bytes accessed | tf_op | source)
XLA Modules:
  0.0 301.3 jit_solution(4909187546660194272)
XLA Ops:
  0.0 0.8 dynamic-slice_convert_fusion
  0.8 19.2 %all_to_all.50 = bf16[8,64,256]{2,1,0:T(8,128)(2,1)S(1)} all-to-all(bf16[8,64,256]{2,1,0:T(8,128)(2,1)S(1)} %broadcast_in_dim.85), channel_id=1, replica_groups=mesh['ylo'=2,'core'=2,'yhi'=2,'x'=4,'z'=8] {'z'}, dimensions={0} | all-to-all | bytes 524288 | tf_op jit(solution)/shard_map/all_to_all | solution.py:26
  20.0 0.4 broadcast_in_dim.87
  20.4 32.2 %all_to_all.51 = bf16[16,512,128]{2,1,0:T(8,128)(2,1)} all-to-all(bf16[16,512,128]{2,1,0:T(8,128)(2,1)S(1)} %broadcast_in_dim.87), channel_id=1, replica_groups=mesh['ylo'=2,'core'=2,'yhi'=2,'x'=4,'z'=8] {'ylo','yhi','x'}, dimensions={0} | all-to-all | bytes 4194304 | tf_op jit(solution)/shard_map/all_to_all | solution.py:26
  52.6 1.7 broadcast_in_dim.86
  54.4 3.8 %all-to-all-start.1 = ((bf16[16,512,128]{2,1,0:T(8,128)(2,1)}), bf16[16,512,128]{2,1,0:T(8,128)(2,1)S(1)}, u32[]{:S(2)}, u32[]{:S(2)}) async-start(bf16[16,512,128]{2,1,0:T(8,128)(2,1)} %broadcast_in_dim.86), calls=%async_computation.1 | async-start | bytes 4194304 | tf_op jit(solution)/shard_map/all_to_all | solution.py:26
  58.2 4.0 %collective-permute-start.1 = (bf16[2,8,512,128]{3,2,1,0:T(8,128)(2,1)}, bf16[2,8,512,128]{3,2,1,0:T(8,128)(2,1)}, u32[]{:S(2)}, u32[]{:S(2)}) collective-permute-start(bf16[2,8,512,128]{3,2,1,0:T(8,128)(2,1)} %bitcast.58), channel_id=1, source_target_pairs={{0,64},{64,0},{1,65},{65,1},{2,66},{66,2},{3,67},{67,3},{4,68},{68... | collective-permute-start | bytes 6291464 | tf_op jit(solution)/shard_map/ppermute | solution.py:22
  62.3 21.0 %all-to-all-done.1 = bf16[16,512,128]{2,1,0:T(8,128)(2,1)S(1)} async-done(((bf16[16,512,128]{2,1,0:T(8,128)(2,1)}), bf16[16,512,128]{2,1,0:T(8,128)(2,1)S(1)}, u32[]{:S(2)}, u32[]{:S(2)}) %all-to-all-start.1) | async-done | bytes 2097184 | tf_op jit(solution)/shard_map/all_to_all | solution.py:26
  83.3 6.4 %collective-permute-start = (bf16[2,8,512,128]{3,2,1,0:T(8,128)(2,1)S(1)}, bf16[2,8,512,128]{3,2,1,0:T(8,128)(2,1)}, u32[]{:S(2)}, u32[]{:S(2)}) collective-permute-start(bf16[2,8,512,128]{3,2,1,0:T(8,128)(2,1)S(1)} %bitcast.56), channel_id=1, source_target_pairs={{0,64},{64,0},{1,65},{65,1},{2,66},{66,2},{3,67},{67,3},{4,68},{68... | collective-permute-start | bytes 6291464 | tf_op jit(solution)/shard_map/ppermute | solution.py:22
  89.7 0.6 fusion.10
  91.0 1.9 select_reduce_fusion.1
  92.9 0.6 pad_maximum_fusion.2
  93.5 0.1 broadcast_in_dim.93
  93.6 1.3 collective-permute-start.2
  95.5 0.7 pad_maximum_fusion.3
  96.2 0.1 broadcast_in_dim.96
  96.3 1.3 collective-permute-start.3
  97.5 0.2 select_reduce_fusion
  97.8 0.0 copy-done.5
  97.8 0.1 copy.25
  98.0 0.0 collective-permute-done.2
  98.0 0.6 fusion.9
  98.6 1.3 fusion.2
  99.9 0.1 copy.23
  100.0 0.6 collective-permute-done.3
  100.6 0.6 fusion.8
  101.2 1.3 fusion.3
  102.5 0.1 copy.24
  102.6 0.1 multiply_divide_fusion.refs_6_
  102.7 0.0 copy-start
  102.7 2.2 copy-done
  104.9 1.6 copy-done.2
  106.5 3.2 %shard_map.65.refs_3_ = f32[512,256]{1,0:T(8,128)S(1)} custom-call(bf16[512,4096]{1,0:T(8,128)(2,1)S(1)} %bitcast.48, bf16[2,8,512,128]{3,2,1,0:T(8,128)(2,1)S(1)} %bitcast.59), custom_call_target="tpu_custom_call" | custom-call | flops 1073741824 | bytes 6815744 | tf_op jit(solution)/shard_map/pallas_call | solution.py:72
  109.7 3.2 %shard_map.64.refs_2_ = f32[512,256]{1,0:T(8,128)S(1)} custom-call(bf16[512,4096]{1,0:T(8,128)(2,1)S(1)} %bitcast.49, bf16[2,8,512,128]{3,2,1,0:T(8,128)(2,1)S(1)} %bitcast.57), custom_call_target="tpu_custom_call" | custom-call | flops 1073741824 | bytes 6815744 | tf_op jit(solution)/shard_map/pallas_call | solution.py:72
  113.0 0.0 collective-permute-done.1.rows_ref
  113.0 5.8 %shard_map.66.refs_4_ = f32[512,256]{1,0:T(8,128)S(1)} custom-call(bf16[512,4096]{1,0:T(8,128)(2,1)S(1)} %bitcast.50, bf16[2,8,512,128]{3,2,1,0:T(8,128)(2,1)} %collective-permute-done.1.rows_ref), custom_call_target="tpu_custom_call" | custom-call | flops 1073741824 | bytes 6815744 | tf_op jit(solution)/shard_map/pallas_call | solution.py:72
  118.8 0.0 collective-permute-done.refs_1_
  118.8 10.4 %shard_map.67 = (bf16[256,512]{1,0:T(8,128)(2,1)S(1)}, bf16[2,8,128,512]{3,2,1,0:T(8,128)(2,1)S(1)}) custom-call(bf16[512,4096]{1,0:T(8,128)(2,1)S(1)} %bitcast.51, bf16[2,8,512,128]{3,2,1,0:T(8,128)(2,1)} %collective-permute-done.refs_1_, f32[512,256]{1,0:T(8,128)S(1)} %shard_map.64.refs_2_, f32[512,256]{1,0:T(8,128)S(1)} %shard_map.65.refs_3_, ...), custom_call_target="tpu_custom_call" | custom-call | tf_op jit(solution)/shard_map/pallas_call | solution.py:156
  129.3 1.3 collective-permute-start.4
  130.6 3.8 %collective-permute-done.4.other_ref = bf16[2,8,128,512]{3,2,1,0:T(8,128)(2,1)S(1)} collective-permute-done((bf16[2,8,128,512]{3,2,1,0:T(8,128)(2,1)S(1)}, bf16[2,8,128,512]{3,2,1,0:T(8,128)(2,1)S(1)}, u32[]{:S(2)}, u32[]{:S(2)}) %collective-permute-start.4) | collective-permute-done | bytes 2097184 | tf_op jit(solution)/shard_map/ppermute | solution.py:22
  134.4 3.1 %shard_map.68 = bf16[2,8,128,512]{3,2,1,0:T(8,128)(2,1)S(1)} custom-call(bf16[512,4096]{1,0:T(8,128)(2,1)S(1)} %bitcast.52, bf16[256,512]{1,0:T(8,128)(2,1)S(1)} %get-tuple-element.9.adjoint_ref, bf16[2,8,128,512]{3,2,1,0:T(8,128)(2,1)S(1)} %collective-permute-done.4.other_ref), custom_call_target="tpu_custom_call" | custom-call | tf_op jit(solution)/shard_map/pallas_call | solution.py:200
  137.4 35.7 %all_to_all.52 = bf16[16,128,512]{2,1,0:T(8,128)(2,1)S(1)} all-to-all(bf16[16,128,512]{2,1,0:T(8,128)(2,1)S(1)} %bitcast.62), channel_id=1, replica_groups=mesh['ylo'=2,'core'=2,'yhi'=2,'x'=4,'z'=8] {'ylo','yhi','x'}, dimensions={0} | all-to-all | bytes 4194304 | tf_op jit(solution)/shard_map/all_to_all | solution.py:26
  173.1 0.3 reduce_sum.75
  173.4 0.1 copy.26
  173.5 13.5 %all_to_all.53 = bf16[8,64,128]{2,1,0:T(8,128)(2,1)S(1)} all-to-all(bf16[8,64,128]{2,1,0:T(8,128)(2,1)S(1)} %bitcast.66), channel_id=1, replica_groups=mesh['ylo'=2,'core'=2,'yhi'=2,'x'=4,'z'=8] {'z'}, dimensions={0} | all-to-all | bytes 262144 | tf_op jit(solution)/shard_map/all_to_all | solution.py:26
  187.1 0.8 fusion
  187.9 10.3 %all_to_all.54 = bf16[8,64,128]{2,1,0:T(8,128)(2,1)S(1)} all-to-all(bf16[8,64,128]{2,1,0:T(8,128)(2,1)S(1)} %broadcast_in_dim.98), channel_id=1, replica_groups=mesh['ylo'=2,'core'=2,'yhi'=2,'x'=4,'z'=8] {'z'}, dimensions={0} | all-to-all | bytes 262144 | tf_op jit(solution)/shard_map/all_to_all | solution.py:26
  198.2 0.4 broadcast_in_dim.100
  198.6 0.0 copy-start.1
  198.6 27.3 %all_to_all.55 = bf16[16,512,128]{2,1,0:T(8,128)(2,1)S(1)} all-to-all(bf16[16,512,128]{2,1,0:T(8,128)(2,1)S(1)} %broadcast_in_dim.100), channel_id=1, replica_groups=mesh['ylo'=2,'core'=2,'yhi'=2,'x'=4,'z'=8] {'ylo','yhi','x'}, dimensions={0} | all-to-all | bytes 4194304 | tf_op jit(solution)/shard_map/all_to_all | solution.py:26
  225.9 5.0 %collective-permute-start.5 = (bf16[2,8,512,128]{3,2,1,0:T(8,128)(2,1)S(1)}, bf16[2,8,512,128]{3,2,1,0:T(8,128)(2,1)S(1)}, u32[]{:S(2)}, u32[]{:S(2)}) collective-permute-start(bf16[2,8,512,128]{3,2,1,0:T(8,128)(2,1)S(1)} %bitcast.60), channel_id=1, source_target_pairs={{0,64},{64,0},{1,65},{65,1},{2,66},{66,2},{3,67},{67,3},{4,68},{68... | collective-permute-start | bytes 6291464 | tf_op jit(solution)/shard_map/ppermute | solution.py:22
  230.9 3.2 %shard_map.69.refs_2_ = f32[512,256]{1,0:T(8,128)S(1)} custom-call(bf16[512,4096]{1,0:T(8,128)(2,1)S(1)} %bitcast.53, bf16[2,8,512,128]{3,2,1,0:T(8,128)(2,1)S(1)} %bitcast.61), custom_call_target="tpu_custom_call" | custom-call | flops 1073741824 | bytes 6815744 | tf_op jit(solution)/shard_map/pallas_call | solution.py:72
  234.2 0.5 collective-permute-done.5.refs_1_
  234.7 7.8 %shard_map.70 = (bf16[256,512]{1,0:T(8,128)(2,1)S(1)}, bf16[2,8,128,512]{3,2,1,0:T(8,128)(2,1)S(1)}) custom-call(bf16[512,4096]{1,0:T(8,128)(2,1)S(1)} %bitcast.54, bf16[2,8,512,128]{3,2,1,0:T(8,128)(2,1)S(1)} %collective-permute-done.5.refs_1_, f32[512,256]{1,0:T(8,128)S(1)} %shard_map.69.refs_2_, f32[512,256]{1,0:T(8,128)S(1)} %shard_map.65.refs_3_, ...), custom_call_target="tpu_custom_call" | custom-call | tf_op jit(solution)/shard_map/pallas_call | solution.py:156
  242.5 0.5 collective-permute-start.6
  243.0 3.8 %collective-permute-done.6.other_ref = bf16[2,8,128,512]{3,2,1,0:T(8,128)(2,1)S(1)} collective-permute-done((bf16[2,8,128,512]{3,2,1,0:T(8,128)(2,1)S(1)}, bf16[2,8,128,512]{3,2,1,0:T(8,128)(2,1)S(1)}, u32[]{:S(2)}, u32[]{:S(2)}) %collective-permute-start.6) | collective-permute-done | bytes 2097184 | tf_op jit(solution)/shard_map/ppermute | solution.py:22
  246.8 3.1 %shard_map.71 = bf16[2,8,128,512]{3,2,1,0:T(8,128)(2,1)S(1)} custom-call(bf16[512,4096]{1,0:T(8,128)(2,1)S(1)} %bitcast.55, bf16[256,512]{1,0:T(8,128)(2,1)S(1)} %get-tuple-element.11.adjoint_ref, bf16[2,8,128,512]{3,2,1,0:T(8,128)(2,1)S(1)} %collective-permute-done.6.other_ref), custom_call_target="tpu_custom_call" | custom-call | tf_op jit(solution)/shard_map/pallas_call | solution.py:200
  249.9 30.6 %all_to_all.56 = bf16[16,128,512]{2,1,0:T(8,128)(2,1)S(1)} all-to-all(bf16[16,128,512]{2,1,0:T(8,128)(2,1)S(1)} %bitcast.63), channel_id=1, replica_groups=mesh['ylo'=2,'core'=2,'yhi'=2,'x'=4,'z'=8] {'ylo','yhi','x'}, dimensions={0} | all-to-all | bytes 4194304 | tf_op jit(solution)/shard_map/all_to_all | solution.py:26
  280.5 0.3 reduce_sum.77
  280.8 0.1 copy.27
  280.9 10.3 %all_to_all.57 = bf16[8,64,128]{2,1,0:T(8,128)(2,1)S(1)} all-to-all(bf16[8,64,128]{2,1,0:T(8,128)(2,1)S(1)} %bitcast.67), channel_id=1, replica_groups=mesh['ylo'=2,'core'=2,'yhi'=2,'x'=4,'z'=8] {'z'}, dimensions={0} | all-to-all | bytes 262144 | tf_op jit(solution)/shard_map/all_to_all | solution.py:26
  291.3 0.8 multiply_subtract_fusion
  292.1 8.6 %all_to_all.58 = f32[4,64,128]{2,1,0:T(8,128)S(1)} all-to-all(f32[4,64,128]{2,1,0:T(8,128)S(1)} %broadcast_in_dim.101), channel_id=1, replica_groups=mesh['ylo'=2,'core'=2,'yhi'=2,'x'=4,'z'=8] {'ylo','core'}, dimensions={0} | all-to-all | bytes 262144 | tf_op jit(solution)/shard_map/all_to_all | solution.py:26
  300.7 0.7 pad_maximum_fusion
  (18 shorter events, 0.2 us)
Async XLA Ops:
  54.4 7.9 %copy-start.4 = (s32[1,512]{1,0:T(1,128)S(1)}, s32[1,512]{1,0:T(1,128)}, u32[]{:S(2)}) copy-start(s32[1,512]{1,0:T(1,128)} %param.7) | copy-start | bytes 6148
  54.4 35.4 %copy-start.3 = (s32[1,512]{1,0:T(1,128)S(1)}, s32[1,512]{1,0:T(1,128)}, u32[]{:S(2)}) copy-start(s32[1,512]{1,0:T(1,128)} %param.8) | copy-start | bytes 6148
  54.4 43.4 %copy-start.5 = (f32[512]{0:T(512)S(1)}, f32[512]{0:T(512)}, u32[]{:S(2)}) copy-start(f32[512]{0:T(512)} %param.10) | copy-start | bytes 6148
  54.4 29.0 %all-to-all-start.1 = ((bf16[16,512,128]{2,1,0:T(8,128)(2,1)}), bf16[16,512,128]{2,1,0:T(8,128)(2,1)S(1)}, u32[]{:S(2)}, u32[]{:S(2)}) async-start(bf16[16,512,128]{2,1,0:T(8,128)(2,1)} %broadcast_in_dim.86), calls=%async_computation.1 | async-start | bytes 4194304 | tf_op jit(solution)/shard_map/all_to_all | solution.py:26
  58.2 54.8 %collective-permute-start.1 = (bf16[2,8,512,128]{3,2,1,0:T(8,128)(2,1)}, bf16[2,8,512,128]{3,2,1,0:T(8,128)(2,1)}, u32[]{:S(2)}, u32[]{:S(2)}) collective-permute-start(bf16[2,8,512,128]{3,2,1,0:T(8,128)(2,1)} %bitcast.58), channel_id=1, source_target_pairs={{0,64},{64,0},{1,65},{65,1},{2,66},{66,2},{3,67},{67,3},{4,68},{68... | collective-permute-start | bytes 6291464 | tf_op jit(solution)/shard_map/ppermute | solution.py:22
  83.3 35.5 %collective-permute-start = (bf16[2,8,512,128]{3,2,1,0:T(8,128)(2,1)S(1)}, bf16[2,8,512,128]{3,2,1,0:T(8,128)(2,1)}, u32[]{:S(2)}, u32[]{:S(2)}) collective-permute-start(bf16[2,8,512,128]{3,2,1,0:T(8,128)(2,1)S(1)} %bitcast.56), channel_id=1, source_target_pairs={{0,64},{64,0},{1,65},{65,1},{2,66},{66,2},{3,67},{67,3},{4,68},{68... | collective-permute-start | bytes 6291464 | tf_op jit(solution)/shard_map/ppermute | solution.py:22
  93.6 4.4 %collective-permute-start.2 = (f32[2,8,128]{2,1,0:T(8,128)S(1)}, f32[2,8,128]{2,1,0:T(8,128)S(1)}, u32[]{:S(2)}, u32[]{:S(2)}) collective-permute-start(f32[2,8,128]{2,1,0:T(8,128)S(1)} %broadcast_in_dim.93), channel_id=1, source_target_pairs={{0,1},{1,2},{2,3},{3,4},{4,5},{5,6},{6,7},{7,8},{8,9},{9,10},{10,1... | collective-permute-start | bytes 24584 | tf_op jit(solution)/shard_map/ppermute | solution.py:232
  96.3 4.4 %collective-permute-start.3 = (f32[2,8,128]{2,1,0:T(8,128)S(1)}, f32[2,8,128]{2,1,0:T(8,128)S(1)}, u32[]{:S(2)}, u32[]{:S(2)}) collective-permute-start(f32[2,8,128]{2,1,0:T(8,128)S(1)} %broadcast_in_dim.96), channel_id=1, source_target_pairs={{1,0},{2,1},{3,2},{4,3},{5,4},{6,5},{7,6},{8,7},{9,8},{10,9},{11,1... | collective-permute-start | bytes 24584 | tf_op jit(solution)/shard_map/ppermute | solution.py:233
  102.7 2.2 copy-start
  104.9 1.6 copy-start.2
  129.3 5.1 %collective-permute-start.4 = (bf16[2,8,128,512]{3,2,1,0:T(8,128)(2,1)S(1)}, bf16[2,8,128,512]{3,2,1,0:T(8,128)(2,1)S(1)}, u32[]{:S(2)}, u32[]{:S(2)}) collective-permute-start(bf16[2,8,128,512]{3,2,1,0:T(8,128)(2,1)S(1)} %get-tuple-element.10), channel_id=1, source_target_pairs={{0,64},{64,0},{1,65},{65,1},{2,66},{66,2},{3,67},{67,3},{4,68},{68... | collective-permute-start | bytes 6291464 | tf_op jit(solution)/shard_map/ppermute | solution.py:22
  198.6 32.3 %copy-start.1 = (bf16[1,512,4096]{2,1,0:T(8,128)(2,1)S(1)}, bf16[1,512,4096]{2,1,0:T(8,128)(2,1)}, u32[]{:S(2)}) copy-start(bf16[1,512,4096]{2,1,0:T(8,128)(2,1)} %param.6) | copy-start | bytes 12582916
  225.9 8.8 %collective-permute-start.5 = (bf16[2,8,512,128]{3,2,1,0:T(8,128)(2,1)S(1)}, bf16[2,8,512,128]{3,2,1,0:T(8,128)(2,1)S(1)}, u32[]{:S(2)}, u32[]{:S(2)}) collective-permute-start(bf16[2,8,512,128]{3,2,1,0:T(8,128)(2,1)S(1)} %bitcast.60), channel_id=1, source_target_pairs={{0,64},{64,0},{1,65},{65,1},{2,66},{66,2},{3,67},{67,3},{4,68},{68... | collective-permute-start | bytes 6291464 | tf_op jit(solution)/shard_map/ppermute | solution.py:22
  242.5 4.2 %collective-permute-start.6 = (bf16[2,8,128,512]{3,2,1,0:T(8,128)(2,1)S(1)}, bf16[2,8,128,512]{3,2,1,0:T(8,128)(2,1)S(1)}, u32[]{:S(2)}, u32[]{:S(2)}) collective-permute-start(bf16[2,8,128,512]{3,2,1,0:T(8,128)(2,1)S(1)} %get-tuple-element.12), channel_id=1, source_target_pairs={{0,64},{64,0},{1,65},{65,1},{2,66},{66,2},{3,67},{67,3},{4,68},{68... | collective-permute-start | bytes 6291464 | tf_op jit(solution)/shard_map/ppermute | solution.py:22

commit v3 on v0

--- a/solution.py
+++ b/solution.py
@@ -33,8 +33,7 @@
     plane = spread(block, PLANE)
     n = lax.axis_size("ylo")
     plane = plane.reshape(n, plane.shape[0] // n * plane.shape[1], plane.shape[2])
-    mine = jnp.concatenate([plane[i] for i in range(n)], axis=1)
-    return mine, core_swap(mine)
+    return [plane[i] for i in range(n)]
 
 
 def gather_line(block):
@@ -47,17 +46,17 @@
 
     def outer(part):
         return lax.dot_general(
-            inputs, part, (((0,), (0,)), ((), ())), preferred_element_type=jnp.float32
+            part, inputs, (((0,), (0,)), ((), ())), preferred_element_type=jnp.float32
         )
 
     other = core_swap(outer(adjoint[:, half:]).astype(jnp.bfloat16))
-    chip = outer(adjoint[:, :half]) + other.astype(jnp.float32)
+    chip = (outer(adjoint[:, :half]) + other.astype(jnp.float32)).astype(jnp.bfloat16)
     n_low, n_plane, n_line = lax.axis_size("ylo"), lax.axis_size(PLANE), lax.axis_size("z")
     cols = half // n_low
-    columns = jnp.stack([chip[:, i * cols : (i + 1) * cols] for i in range(n_low)])
-    columns = columns.astype(jnp.bfloat16).reshape(n_plane, -1, cols)
-    line = jnp.sum(exchange(columns, PLANE).astype(jnp.float32), axis=0)
-    line = line.astype(jnp.bfloat16).reshape(n_line, -1, cols)
+    blocks = chip.reshape(n_low, cols, n_plane // n_low, -1).transpose(0, 2, 1, 3)
+    parts = exchange(blocks.reshape(n_plane, cols, -1), PLANE)
+    line = jnp.sum(parts.astype(jnp.float32), axis=0).astype(jnp.bfloat16)
+    line = line.reshape(cols, n_line, -1).transpose(1, 2, 0)
     return jnp.sum(exchange(line, "z").astype(jnp.float32), axis=0)
 
 
@@ -77,12 +76,10 @@
 
     left = lax.ppermute(edge(last), SHARD, [(i, i + 1) for i in range(n - 1)])
     right = lax.ppermute(edge(first), SHARD, [(i + 1, i) for i in range(n - 1)])
-    same = turn_ids[:, None] == turn_ids[None, :]
-    counts = jnp.sum(jnp.where(same, text_mask[None, :], 0.0), axis=1)
-    as_float = turn_ids.astype(jnp.float32)
-    for other in (left, right):
-        counts = counts + jnp.where(as_float == other[0, 0, 0], other[1, 0, 0], 0.0)
-    return counts
+    ids = jnp.concatenate([turn_ids.astype(jnp.float32), left[0, 0, :1], right[0, 0, :1]])
+    texts = jnp.concatenate([text_mask, left[1, 0, :1], right[1, 0, :1]])
+    same = turn_ids.astype(jnp.float32)[:, None] == ids[None, :]
+    return jnp.sum(jnp.where(same, texts[None, :], 0.0), axis=1)
 
 
 def local(acts, token_ids, turn_ids, value_weight, norm_gain, query_grad):
@@ -99,10 +96,8 @@
     def own(array):
         return lax.dynamic_slice(array, (0, me * cols), (array.shape[0], cols))
 
-    def project(halves):
-        return jnp.concatenate(
-            [jnp.dot(inputs, half, preferred_element_type=jnp.float32) for half in halves], axis=1
-        )
+    def times(rows):
+        return jnp.dot(inputs, rows, preferred_element_type=jnp.float32)
 
     gain = norm_gain.reshape(2, 2, cols)
     gain = jnp.concatenate(
@@ -111,17 +106,22 @@
     gain_square = gain * gain
     query = own(query_grad)
 
-    both = gather_line(jnp.concatenate([own(value_weight), query.astype(jnp.bfloat16)], axis=1))
-    values = project(gather_plane(both[:, :cols]))
-    tangent = project(gather_plane(both[:, cols:]))
     own_count = turn_counts(text_mask, ids)
     turn_weight = text_mask / (jnp.maximum(own_count, 1.0) * jnp.float32(turn_total))
+    both = gather_line(jnp.concatenate([own(value_weight), query.astype(jnp.bfloat16)], axis=1))
+    both, turn_weight = lax.optimization_barrier((both, turn_weight))
+    mine = gather_plane(both)
+    products = [times(rows) for rows in mine + [core_swap(rows) for rows in mine]]
+    values = jnp.concatenate([product[:, :cols] for product in products], axis=1)
+    tangent = jnp.concatenate([product[:, cols:] for product in products], axis=1)
     root_mean = jnp.sqrt(jnp.mean(values * values, axis=-1, keepdims=True) + 1e-06)
     unit_values = values / root_mean
     estimate = query
     for step in range(ITERS):
         if step:
-            tangent = project(gather_plane(gather_line(estimate.astype(jnp.bfloat16))))
+            mine = jnp.stack(gather_plane(gather_line(estimate.astype(jnp.bfloat16))))
+            halves = [jnp.concatenate([pair[0], pair[1]], axis=1) for pair in (mine, core_swap(mine))]
+            tangent = jnp.concatenate([times(half) for half in halves], axis=1)
         inner = gain_square * norm_jacobian(tangent, unit_values, root_mean)
         adjoint = (turn_weight[:, None] * norm_jacobian(inner, unit_values, root_mean)).astype(
             jnp.bfloat16

time: 267 us -> 268 us (level)
  matrix products: 14.4 us -> 17.6 us
    another operation x4 -> x0, local copies, waits for them, and re-layouts: 5.39 us -> none  [reduce_blocks(): jnp.stack([chip[:, i * cols:(i + 1) * cols] for i in range(n_low)])]
    ppermute x5, starting transfers between devices: 16.4 us -> 11 us  [core_swap(): return lax.ppermute(value, 'core', [(0, 1), (1, 0)])]
    all_to_all x1, starting transfers between devices: 3.85 us -> 8.78 us  [exchange(): return lax.all_to_all(blocks, axes, split_axis=0, concat_axis=0, tiled=True)]
    dot_general x10, matrix products: 14.4 us -> 17.6 us  [the longest x6 12.4 us: times(): return jnp.dot(inputs, rows, preferred_element_type=jnp.float32)]
    all_to_all x9 -> x8, blocking collectives: 183 us -> 184 us  [exchange(): return lax.all_to_all(blocks, axes, split_axis=0, concat_axis=0, tiled=True)]
  transfers between devices with their start and end apart: 8 -> 8, of which waited for: 4 -> 4; matrix products, arithmetic and copies ran while one was open for 7% -> 6% of each run, Pallas kernels for 0% -> 0%
where the time goes in v3:
time: 268 us; the launch traced here: 267 us
  blocking collectives  184 us (69%)
  starting transfers between devices  26 us (10%)
  matrix products  17.6 us (7%)
  waiting for transfers between devices  15.6 us (6%)
  other arithmetic  11.7 us (4%)
  local copies, waits for them, and re-layouts  10.4 us (4%)
    all_to_all x8, blocking collectives, exchange(): return lax.all_to_all(blocks, axes, split_axis=0, concat_axis=0, tiled=True)  184 us
    dot_general x6, matrix products, times(): return jnp.dot(inputs, rows, preferred_element_type=jnp.float32)  12.4 us
    ppermute x5, starting transfers between devices, core_swap(): return lax.ppermute(value, 'core', [(0, 1), (1, 0)])  11 us
    ppermute x5, waiting for transfers between devices, core_swap(): return lax.ppermute(value, 'core', [(0, 1), (1, 0)])  10.1 us
    all_to_all x1, starting transfers between devices, exchange(): return lax.all_to_all(blocks, axes, split_axis=0, concat_axis=0, tiled=True)  8.78 us
    all_to_all x1, waiting for transfers between devices, exchange(): return lax.all_to_all(blocks, axes, split_axis=0, concat_axis=0, tiled=True)  5.58 us
  transfers between devices with their start and end apart: 8, of which 4 were waited for; matrix products, arithmetic and copies ran while one was open for 6% of the time, Pallas kernels for 0%

profile of v3, /device:TPU:1, one launch (start us, length us, event | category | flops | bytes accessed | tf_op | source)
XLA Modules:
  0.0 267.4 jit_solution(16380726091000514185)
XLA Ops:
  0.0 1.3 fusion.72
  2.0 2.0 compare_reduce_fusion.1
  4.0 0.7 compare_convert_fusion
  4.7 0.6 select_reduce_fusion.2
  5.3 0.6 pad_maximum_fusion.9
  6.0 1.3 collective-permute-start.1
  8.0 0.7 pad_maximum_fusion.8
  8.8 5.0 %collective-permute-start = (f32[2,8,128]{2,1,0:T(8,128)S(1)}, f32[2,8,128]{2,1,0:T(8,128)S(1)}, u32[]{:S(2)}, u32[]{:S(2)}) collective-permute-start(f32[2,8,128]{2,1,0:T(8,128)S(1)} %broadcast_in_dim.35), channel_id=1, source_target_pairs={{0,1},{1,2},{2,3},{3,4},{4,5},{5,6},{6,7},{7,8},{8,9},{9,10},{10,1... | collective-permute-start | bytes 24584 | tf_op jit(solution)/shard_map/ppermute | solution.py:77
  13.8 0.8 dynamic-slice_convert_fusion
  14.6 0.7 broadcast_in_dim.33
  15.3 8.8 %all-to-all-start = ((bf16[8,64,256]{2,1,0:T(8,128)(2,1)}), bf16[8,64,256]{2,1,0:T(8,128)(2,1)S(1)}, u32[]{:S(2)}, u32[]{:S(2)}) async-start(bf16[8,64,256]{2,1,0:T(8,128)(2,1)} %broadcast_in_dim.33), calls=%async_computation | async-start | bytes 524288 | tf_op jit(solution)/shard_map/all_to_all | solution.py:24
  24.1 0.7 convert_element_type.66
  24.8 0.6 fusion.70
  25.3 0.5 fusion.69
  25.9 2.5 pad_maximum_fusion.6
  28.4 0.2 select_reduce_fusion
  28.6 5.6 %all-to-all-done = bf16[8,64,256]{2,1,0:T(8,128)(2,1)S(1)} async-done(((bf16[8,64,256]{2,1,0:T(8,128)(2,1)}), bf16[8,64,256]{2,1,0:T(8,128)(2,1)S(1)}, u32[]{:S(2)}, u32[]{:S(2)}) %all-to-all-start) | async-done | bytes 262176 | tf_op jit(solution)/shard_map/all_to_all | solution.py:24
  34.2 0.4 broadcast_in_dim.39
  34.6 56.3 %all_to_all.45 = bf16[16,512,256]{2,1,0:T(8,128)(2,1)S(1)} all-to-all(bf16[16,512,256]{2,1,0:T(8,128)(2,1)S(1)} %broadcast_in_dim.39), channel_id=1, replica_groups=mesh['ylo'=2,'core'=2,'yhi'=2,'x'=4,'z'=8] {'ylo','yhi','x'}, dimensions={0} | all-to-all | bytes 8388608 | tf_op jit(solution)/shard_map/all_to_all | solution.py:24
  90.9 1.6 fusion.63
  92.5 4.2 %collective-permute-start.2 = (bf16[4096,256]{1,0:T(8,128)(2,1)}, bf16[4096,256]{1,0:T(8,128)(2,1)}, u32[]{:S(2)}, u32[]{:S(2)}) collective-permute-start(bf16[4096,256]{1,0:T(8,128)(2,1)} %bitcast.19), channel_id=1, source_target_pairs={{0,64},{64,0},{1,65},{65,1},{2,66},{66,2},{3,67},{67,3},{4,68},{68... | collective-permute-start | bytes 6291464 | tf_op jit(solution)/shard_map/ppermute | solution.py:20
  96.8 4.3 %fusion.24 = f32[512,256]{0,1:T(8,128)S(1)} fusion(bf16[4096,256]{1,0:T(8,128)(2,1)} %bitcast.19, bf16[1,512,4096]{2,1,0:T(8,128)(2,1)} %param.6), kind=kOutput, calls=%fused_computation.29 | convolution fusion | flops 1073741824 | bytes 6815744 | tf_op jit(solution)/shard_map/dot_general | solution.py:100
  101.2 1.3 fusion.27
  102.6 2.9 %fusion.30 = f32[512,256]{0,1:T(8,128)S(1)} fusion(bf16[4096,256]{1,0:T(8,128)(2,1)} %collective-permute-done.2, bf16[1,512,4096]{2,1,0:T(8,128)(2,1)S(1)} %copy-done.2), kind=kOutput, calls=%fused_computation.31 | convolution fusion | flops 1073741824 | bytes 6815744 | tf_op jit(solution)/shard_map/dot_general | solution.py:100
  105.5 1.3 fusion.33
  106.9 0.1 multiply_reduce_fusion.4
  107.0 0.3 multiply_reduce_fusion.3
  107.3 0.3 multiply_reduce_fusion.2
  107.6 0.4 multiply_convert_fusion.1
  108.0 1.3 convolution_convert_fusion.1
  109.3 0.9 collective-permute-start.4
  110.2 3.8 %collective-permute-done.4 = bf16[256,4096]{1,0:T(8,128)(2,1)S(1)} collective-permute-done((bf16[256,4096]{1,0:T(8,128)(2,1)S(1)}, bf16[256,4096]{1,0:T(8,128)(2,1)S(1)}, u32[]{:S(2)}, u32[]{:S(2)}) %collective-permute-start.4) | collective-permute-done | bytes 2097184 | tf_op jit(solution)/shard_map/ppermute | solution.py:20
  114.0 1.3 add_convert_fusion.1
  115.2 0.9 copy.33
  116.2 0.7 copy.28
  116.8 30.6 %all_to_all.46 = bf16[16,128,512]{2,1,0:T(8,128)(2,1)S(1)} all-to-all(bf16[16,128,512]{2,1,0:T(8,128)(2,1)S(1)} %bitcast.114), channel_id=1, replica_groups=mesh['ylo'=2,'core'=2,'yhi'=2,'x'=4,'z'=8] {'ylo','yhi','x'}, dimensions={0} | all-to-all | bytes 4194304 | tf_op jit(solution)/shard_map/all_to_all | solution.py:24
  147.4 0.3 reduce_sum.120
  147.7 0.1 copy.29
  147.9 10.5 %all_to_all.47 = bf16[8,64,128]{2,1,0:T(8,128)(2,1)S(1)} all-to-all(bf16[8,64,128]{2,1,0:T(8,128)(2,1)S(1)} %bitcast.127), channel_id=1, replica_groups=mesh['ylo'=2,'core'=2,'yhi'=2,'x'=4,'z'=8] {'z'}, dimensions={0} | all-to-all | bytes 262144 | tf_op jit(solution)/shard_map/all_to_all | solution.py:24
  158.5 10.3 %all_to_all.48 = bf16[8,64,128]{2,1,0:T(8,128)(2,1)S(1)} all-to-all(bf16[8,64,128]{2,1,0:T(8,128)(2,1)S(1)} %broadcast_in_dim.40), channel_id=1, replica_groups=mesh['ylo'=2,'core'=2,'yhi'=2,'x'=4,'z'=8] {'z'}, dimensions={0} | all-to-all | bytes 262144 | tf_op jit(solution)/shard_map/all_to_all | solution.py:24
  168.8 0.4 broadcast_in_dim.42
  169.2 27.0 %all_to_all.49 = bf16[16,512,128]{2,1,0:T(8,128)(2,1)S(1)} all-to-all(bf16[16,512,128]{2,1,0:T(8,128)(2,1)S(1)} %broadcast_in_dim.42), channel_id=1, replica_groups=mesh['ylo'=2,'core'=2,'yhi'=2,'x'=4,'z'=8] {'ylo','yhi','x'}, dimensions={0} | all-to-all | bytes 4194304 | tf_op jit(solution)/shard_map/all_to_all | solution.py:24
  196.2 0.1 fusion.64
  196.4 0.2 pad_maximum_fusion
  196.6 5.1 %collective-permute-start.5 = (bf16[2,4096,128]{2,1,0:T(8,128)(2,1)S(1)}, bf16[2,4096,128]{2,1,0:T(8,128)(2,1)S(1)}, u32[]{:S(2)}, u32[]{:S(2)}) collective-permute-start(bf16[2,4096,128]{2,1,0:T(8,128)(2,1)S(1)} %pad_maximum_fusion), channel_id=1, source_target_pairs={{0,64},{64,0},{1,65},{65,1},{2,66},{66,2},{3,67},{67,3},{4,68},{68... | collective-permute-start | bytes 6291464 | tf_op jit(solution)/shard_map/ppermute | solution.py:20
  201.7 1.3 fusion.36
  203.0 2.5 collective-permute-done.5
  205.5 0.1 slice_bitcast_fusion.1
  205.6 1.3 fusion.41
  206.9 0.3 multiply_reduce_fusion.1
  207.2 0.3 multiply_reduce_fusion
  207.5 0.4 multiply_convert_fusion
  207.9 1.3 convolution_convert_fusion
  209.2 0.7 collective-permute-start.6
  209.9 3.8 %collective-permute-done.6 = bf16[256,4096]{1,0:T(8,128)(2,1)S(1)} collective-permute-done((bf16[256,4096]{1,0:T(8,128)(2,1)S(1)}, bf16[256,4096]{1,0:T(8,128)(2,1)S(1)}, u32[]{:S(2)}, u32[]{:S(2)}) %collective-permute-start.6) | collective-permute-done | bytes 2097184 | tf_op jit(solution)/shard_map/ppermute | solution.py:20
  213.7 1.4 add_convert_fusion
  215.0 0.9 copy.34
  216.0 0.7 copy.30
  216.6 30.6 %all_to_all.50 = bf16[16,128,512]{2,1,0:T(8,128)(2,1)S(1)} all-to-all(bf16[16,128,512]{2,1,0:T(8,128)(2,1)S(1)} %bitcast.116), channel_id=1, replica_groups=mesh['ylo'=2,'core'=2,'yhi'=2,'x'=4,'z'=8] {'ylo','yhi','x'}, dimensions={0} | all-to-all | bytes 4194304 | tf_op jit(solution)/shard_map/all_to_all | solution.py:24
  247.3 0.3 reduce_sum.124
  247.5 0.1 copy.31
  247.7 10.3 %all_to_all.51 = bf16[8,64,128]{2,1,0:T(8,128)(2,1)S(1)} all-to-all(bf16[8,64,128]{2,1,0:T(8,128)(2,1)S(1)} %bitcast.128), channel_id=1, replica_groups=mesh['ylo'=2,'core'=2,'yhi'=2,'x'=4,'z'=8] {'z'}, dimensions={0} | all-to-all | bytes 262144 | tf_op jit(solution)/shard_map/all_to_all | solution.py:24
  258.1 8.6 %all_to_all.52 = f32[4,64,128]{2,1,0:T(8,128)S(1)} all-to-all(f32[4,64,128]{2,1,0:T(8,128)S(1)} %broadcast_in_dim.43), channel_id=1, replica_groups=mesh['ylo'=2,'core'=2,'yhi'=2,'x'=4,'z'=8] {'ylo','core'}, dimensions={0} | all-to-all | bytes 262144 | tf_op jit(solution)/shard_map/all_to_all | solution.py:24
  266.7 0.7 pad_maximum_fusion.4
  (36 shorter events, 0.6 us)
Async XLA Ops:
  6.0 18.7 %collective-permute-start.1 = (f32[2,8,128]{2,1,0:T(8,128)S(1)}, f32[2,8,128]{2,1,0:T(8,128)S(1)}, u32[]{:S(2)}, u32[]{:S(2)}) collective-permute-start(f32[2,8,128]{2,1,0:T(8,128)S(1)} %broadcast_in_dim.36), channel_id=1, source_target_pairs={{1,0},{2,1},{3,2},{4,3},{5,4},{6,5},{7,6},{8,7},{9,8},{10,9},{11,1... | collective-permute-start | bytes 24584 | tf_op jit(solution)/shard_map/ppermute | solution.py:78
  8.8 16.5 %collective-permute-start = (f32[2,8,128]{2,1,0:T(8,128)S(1)}, f32[2,8,128]{2,1,0:T(8,128)S(1)}, u32[]{:S(2)}, u32[]{:S(2)}) collective-permute-start(f32[2,8,128]{2,1,0:T(8,128)S(1)} %broadcast_in_dim.35), channel_id=1, source_target_pairs={{0,1},{1,2},{2,3},{3,4},{4,5},{5,6},{6,7},{7,8},{8,9},{9,10},{10,1... | collective-permute-start | bytes 24584 | tf_op jit(solution)/shard_map/ppermute | solution.py:77
  15.3 18.9 %all-to-all-start = ((bf16[8,64,256]{2,1,0:T(8,128)(2,1)}), bf16[8,64,256]{2,1,0:T(8,128)(2,1)S(1)}, u32[]{:S(2)}, u32[]{:S(2)}) async-start(bf16[8,64,256]{2,1,0:T(8,128)(2,1)} %broadcast_in_dim.33), calls=%async_computation | async-start | bytes 524288 | tf_op jit(solution)/shard_map/all_to_all | solution.py:24
  90.9 5.8 %copy-start.1 = (f32[512]{0:T(512)S(1)}, f32[512]{0:T(512)}, u32[]{:S(2)}) copy-start(f32[512]{0:T(512)} %param.10) | copy-start | bytes 6148
  92.5 10.0 %collective-permute-start.2 = (bf16[4096,256]{1,0:T(8,128)(2,1)}, bf16[4096,256]{1,0:T(8,128)(2,1)}, u32[]{:S(2)}, u32[]{:S(2)}) collective-permute-start(bf16[4096,256]{1,0:T(8,128)(2,1)} %bitcast.19), channel_id=1, source_target_pairs={{0,64},{64,0},{1,65},{65,1},{2,66},{66,2},{3,67},{67,3},{4,68},{68... | collective-permute-start | bytes 6291464 | tf_op jit(solution)/shard_map/ppermute | solution.py:20
  96.7 4.4 %copy-start.2 = (bf16[1,512,4096]{2,1,0:T(8,128)(2,1)S(1)}, bf16[1,512,4096]{2,1,0:T(8,128)(2,1)}, u32[]{:S(2)}) copy-start(bf16[1,512,4096]{2,1,0:T(8,128)(2,1)} %param.6) | copy-start | bytes 12582916
  96.7 8.8 %collective-permute-start.3 = (bf16[4096,256]{1,0:T(8,128)(2,1)S(1)}, bf16[4096,256]{1,0:T(8,128)(2,1)S(1)}, u32[]{:S(2)}, u32[]{:S(2)}) collective-permute-start(bf16[4096,256]{1,0:T(8,128)(2,1)S(1)} %bitcast.123), channel_id=1, source_target_pairs={{0,64},{64,0},{1,65},{65,1},{2,66},{66,2},{3,67},{67,3},{4,68},{68... | collective-permute-start | bytes 6291464 | tf_op jit(solution)/shard_map/ppermute | solution.py:20
  109.3 4.7 %collective-permute-start.4 = (bf16[256,4096]{1,0:T(8,128)(2,1)S(1)}, bf16[256,4096]{1,0:T(8,128)(2,1)S(1)}, u32[]{:S(2)}, u32[]{:S(2)}) collective-permute-start(bf16[256,4096]{1,0:T(8,128)(2,1)S(1)} %convolution_convert_fusion.1), channel_id=1, source_target_pairs={{0,64},{64,0},{1,65},{65,1},{2,66},{66,2},{3,67},{67,3},{4,68},{68... | collective-permute-start | bytes 6291464 | tf_op jit(solution)/shard_map/ppermute | solution.py:20
  147.4 10.9 %copy-start = (f32[64,512]{1,0:T(8,128)S(1)}, f32[64,512]{1,0:T(8,128)}, u32[]{:S(2)}) copy-start(f32[64,512]{1,0:T(8,128)} %param.11) | copy-start | bytes 393220
  196.3 5.3 %copy-start.3 = (bf16[1,512,4096]{2,1,0:T(8,128)(2,1)S(1)}, bf16[1,512,4096]{2,1,0:T(8,128)(2,1)}, u32[]{:S(2)}) copy-start(bf16[1,512,4096]{2,1,0:T(8,128)(2,1)} %param.6) | copy-start | bytes 12582916
  196.6 8.9 %collective-permute-start.5 = (bf16[2,4096,128]{2,1,0:T(8,128)(2,1)S(1)}, bf16[2,4096,128]{2,1,0:T(8,128)(2,1)S(1)}, u32[]{:S(2)}, u32[]{:S(2)}) collective-permute-start(bf16[2,4096,128]{2,1,0:T(8,128)(2,1)S(1)} %pad_maximum_fusion), channel_id=1, source_target_pairs={{0,64},{64,0},{1,65},{65,1},{2,66},{66,2},{3,67},{67,3},{4,68},{68... | collective-permute-start | bytes 6291464 | tf_op jit(solution)/shard_map/ppermute | solution.py:20
  209.2 4.5 %collective-permute-start.6 = (bf16[256,4096]{1,0:T(8,128)(2,1)S(1)}, bf16[256,4096]{1,0:T(8,128)(2,1)S(1)}, u32[]{:S(2)}, u32[]{:S(2)}) collective-permute-start(bf16[256,4096]{1,0:T(8,128)(2,1)S(1)} %convolution_convert_fusion), channel_id=1, source_target_pairs={{0,64},{64,0},{1,65},{65,1},{2,66},{66,2},{3,67},{67,3},{4,68},{68... | collective-permute-start | bytes 6291464 | tf_op jit(solution)/shard_map/ppermute | solution.py:20

commit v4 on v3

--- a/solution.py
+++ b/solution.py
@@ -29,11 +29,35 @@
     return exchange(jnp.broadcast_to(block[None], (n,) + block.shape), axes)
 
 
+def ring_gather(block):
+    n = lax.axis_size("z")
+    me = lax.axis_index("z")
+    whole = jnp.zeros((block.shape[0], n) + block.shape[1:], block.dtype)
+
+    def shift(value, step):
+        return lax.ppermute(value, "z", [(i, (i + step) % n) for i in range(n)])
+
+    def put(whole, piece, owner, start=0):
+        return lax.dynamic_update_slice(whole, piece[:, None], (start, owner % n, 0, 0))
+
+    whole = put(whole, block, me)
+    before = after = block
+    for step in range(1, n // 2):
+        before, after = shift(before, 1), shift(after, -1)
+        whole = put(whole, before, me + n - step)
+        whole = put(whole, after, me + step)
+    half = block.shape[0] // 2
+    whole = put(whole, shift(before[:half], 1), me + n // 2)
+    return put(whole, shift(after[half:], -1), me + n // 2, half)
+
+
+def gather_ring(block):
+    n = lax.axis_size("ylo")
+    return ring_gather(spread(block, PLANE)).reshape(n, -1, block.shape[1])
+
+
 def gather_plane(block):
-    plane = spread(block, PLANE)
-    n = lax.axis_size("ylo")
-    plane = plane.reshape(n, plane.shape[0] // n * plane.shape[1], plane.shape[2])
-    return [plane[i] for i in range(n)]
+    return spread(block, PLANE).reshape(lax.axis_size("ylo"), -1, block.shape[1])
 
 
 def gather_line(block):
@@ -96,8 +120,11 @@
     def own(array):
         return lax.dynamic_slice(array, (0, me * cols), (array.shape[0], cols))
 
-    def times(rows):
-        return jnp.dot(inputs, rows, preferred_element_type=jnp.float32)
+    def project(mine):
+        halves = [jnp.concatenate([pair[0], pair[1]], axis=1) for pair in (mine, core_swap(mine))]
+        return jnp.concatenate(
+            [jnp.dot(inputs, half, preferred_element_type=jnp.float32) for half in halves], axis=1
+        )
 
     gain = norm_gain.reshape(2, 2, cols)
     gain = jnp.concatenate(
@@ -108,20 +135,14 @@
 
     own_count = turn_counts(text_mask, ids)
     turn_weight = text_mask / (jnp.maximum(own_count, 1.0) * jnp.float32(turn_total))
-    both = gather_line(jnp.concatenate([own(value_weight), query.astype(jnp.bfloat16)], axis=1))
-    both, turn_weight = lax.optimization_barrier((both, turn_weight))
-    mine = gather_plane(both)
-    products = [times(rows) for rows in mine + [core_swap(rows) for rows in mine]]
-    values = jnp.concatenate([product[:, :cols] for product in products], axis=1)
-    tangent = jnp.concatenate([product[:, cols:] for product in products], axis=1)
+    tangent = project(gather_ring(query.astype(jnp.bfloat16)))
+    values = project(gather_plane(gather_line(own(value_weight))))
     root_mean = jnp.sqrt(jnp.mean(values * values, axis=-1, keepdims=True) + 1e-06)
     unit_values = values / root_mean
     estimate = query
     for step in range(ITERS):
         if step:
-            mine = jnp.stack(gather_plane(gather_line(estimate.astype(jnp.bfloat16))))
-            halves = [jnp.concatenate([pair[0], pair[1]], axis=1) for pair in (mine, core_swap(mine))]
-            tangent = jnp.concatenate([times(half) for half in halves], axis=1)
+            tangent = project(gather_plane(gather_line(estimate.astype(jnp.bfloat16))))
         inner = gain_square * norm_jacobian(tangent, unit_values, root_mean)
         adjoint = (turn_weight[:, None] * norm_jacobian(inner, unit_values, root_mean)).astype(
             jnp.bfloat16

time: 268 us -> 264 us (0.985)
  blocking collectives: 184 us -> 134 us
  starting transfers between devices: 26 us -> 52.3 us
  local copies, waits for them, and re-layouts: 10.4 us -> 25.9 us
  waiting for transfers between devices: 15.6 us -> 22.2 us
  matrix products: 17.6 us -> 12.8 us
    all_to_all x8 -> x7, blocking collectives: 184 us -> 134 us  [exchange(): return lax.all_to_all(blocks, axes, split_axis=0, concat_axis=0, tiled=True)]
    all_to_all x1 -> x3, starting transfers between devices: 8.78 us -> 24.1 us  [exchange(): return lax.all_to_all(blocks, axes, split_axis=0, concat_axis=0, tiled=True)]
    ppermute x0 -> x8, starting transfers between devices: none -> 11 us  [shift(): return lax.ppermute(value, 'z', [(i, (i + step) % n) for i in range(n)])]
    ppermute x0 -> x8, waiting for transfers between devices: none -> 7.92 us  [shift(): return lax.ppermute(value, 'z', [(i, (i + step) % n) for i in range(n)])]
    dynamic_update_slice x0 -> x9, local copies, waits for them, and re-layouts: none -> 6.78 us  [put(): lax.dynamic_update_slice(whole, piece[:, None], (start, owner % n, 0, 0))]
    dot_general x6, matrix products: 12.4 us -> 7.75 us  [project(): jnp.dot(inputs, half, preferred_element_type=jnp.float32)]
    all_to_all x1 -> x3, waiting for transfers between devices: 5.58 us -> 4.05 us  [exchange(): return lax.all_to_all(blocks, axes, split_axis=0, concat_axis=0, tiled=True)]
  transfers between devices with their start and end apart: 8 -> 18, of which waited for: 4 -> 7; matrix products, arithmetic and copies ran while one was open for 6% -> 12% of each run, Pallas kernels for 0% -> 0%
where the time goes in v4:
time: 264 us; the launch traced here: 263 us
  blocking collectives  134 us (51%)
  starting transfers between devices  52.3 us (20%)
  local copies, waits for them, and re-layouts  25.9 us (10%)
  waiting for transfers between devices  22.2 us (8%)
  other arithmetic  13.9 us (5%)
  matrix products  12.8 us (5%)
    all_to_all x7, blocking collectives, exchange(): return lax.all_to_all(blocks, axes, split_axis=0, concat_axis=0, tiled=True)  134 us
    all_to_all x3, starting transfers between devices, exchange(): return lax.all_to_all(blocks, axes, split_axis=0, concat_axis=0, tiled=True)  24.1 us
    ppermute x5, starting transfers between devices, core_swap(): return lax.ppermute(value, 'core', [(0, 1), (1, 0)])  12.4 us
    ppermute x8, starting transfers between devices, shift(): return lax.ppermute(value, 'z', [(i, (i + step) % n) for i in range(n)])  11 us
    ppermute x5, waiting for transfers between devices, core_swap(): return lax.ppermute(value, 'core', [(0, 1), (1, 0)])  10.2 us
    ppermute x8, waiting for transfers between devices, shift(): return lax.ppermute(value, 'z', [(i, (i + step) % n) for i in range(n)])  7.92 us
    dot_general x6, matrix products, project(): jnp.dot(inputs, half, preferred_element_type=jnp.float32)  7.75 us
    dynamic_update_slice x9, local copies, waits for them, and re-layouts, put(): lax.dynamic_update_slice(whole, piece[:, None], (start, owner % n, 0, 0))  6.78 us
  transfers between devices with their start and end apart: 18, of which 7 were waited for; matrix products, arithmetic and copies ran while one was open for 12% of the time, Pallas kernels for 0%

profile of v4, /device:TPU:1, one launch (start us, length us, event | category | flops | bytes accessed | tf_op | source)
XLA Modules:
  0.0 262.7 jit_solution(3837554894292362290)
XLA Ops:
  0.0 0.8 dynamic-slice_convert_fusion
  0.8 0.7 broadcast_in_dim.115
  1.5 7.6 %all-to-all-start = ((bf16[16,64,128]{2,1,0:T(8,128)(2,1)}), bf16[16,64,128]{2,1,0:T(8,128)(2,1)S(1)}, u32[]{:S(2)}, u32[]{:S(2)}) async-start(bf16[16,64,128]{2,1,0:T(8,128)(2,1)} %broadcast_in_dim.115), calls=%async_computation | async-start | bytes 524288 | tf_op jit(solution)/shard_map/all_to_all | solution.py:24
  9.1 1.3 fusion.92
  11.1 2.0 compare_reduce_fusion.1
  13.0 0.7 compare_convert_fusion
  15.1 3.5 %collective-permute-start = (f32[2,8,128]{2,1,0:T(8,128)S(1)}, f32[2,8,128]{2,1,0:T(8,128)S(1)}, u32[]{:S(2)}, u32[]{:S(2)}) collective-permute-start(f32[2,8,128]{2,1,0:T(8,128)S(1)} %broadcast_in_dim.58), channel_id=1, source_target_pairs={{0,1},{1,2},{2,3},{3,4},{4,5},{5,6},{6,7},{7,8},{8,9},{9,10},{10,1... | collective-permute-start | bytes 24584 | tf_op jit(solution)/shard_map/ppermute | solution.py:101
  19.3 0.7 pad_maximum_fusion.7
  20.0 1.3 collective-permute-start.1
  21.3 0.8 fusion.93
  22.8 9.8 %all-to-all-start.1 = ((bf16[8,64,128]{2,1,0:T(8,128)(2,1)}), bf16[8,64,128]{2,1,0:T(8,128)(2,1)S(1)}, u32[]{:S(2)}, u32[]{:S(2)}) async-start(bf16[8,64,128]{2,1,0:T(8,128)(2,1)} %broadcast_in_dim.125), calls=%async_computation.1 | async-start | bytes 262144 | tf_op jit(solution)/shard_map/all_to_all | solution.py:24
  32.8 0.7 convert_element_type.69
  33.5 1.5 collective-permute-start.2
  34.9 1.2 collective-permute-start.3
  36.7 4.0 %all-to-all-done.1 = bf16[8,64,128]{2,1,0:T(8,128)(2,1)S(1)} async-done(((bf16[8,64,128]{2,1,0:T(8,128)(2,1)}), bf16[8,64,128]{2,1,0:T(8,128)(2,1)S(1)}, u32[]{:S(2)}, u32[]{:S(2)}) %all-to-all-start.1) | async-done | bytes 131104 | tf_op jit(solution)/shard_map/all_to_all | solution.py:24
  40.7 1.8 broadcast_in_dim.127
  42.5 6.7 %all-to-all-start.2 = ((bf16[16,512,128]{2,1,0:T(8,128)(2,1)}), bf16[16,512,128]{2,1,0:T(8,128)(2,1)S(1)}, u32[]{:S(2)}, u32[]{:S(2)}) async-start(bf16[16,512,128]{2,1,0:T(8,128)(2,1)} %broadcast_in_dim.127), calls=%async_computation.2 | async-start | bytes 4194304 | tf_op jit(solution)/shard_map/all_to_all | solution.py:24
  49.1 1.9 broadcast_in_dim.114
  51.0 0.8 bitcast_dynamic-update-slice_fusion.6
  52.0 2.5 collective-permute-start.5
  54.5 0.8 bitcast_dynamic-update-slice_fusion.5
  55.2 0.8 bitcast_dynamic-update-slice_fusion.4
  56.0 2.5 collective-permute-done.4
  58.5 2.7 %collective-permute-start.7 = (bf16[16,64,128]{2,1,0:T(8,128)(2,1)S(1)}, bf16[16,64,128]{2,1,0:T(8,128)(2,1)S(1)}, u32[]{:S(2)}, u32[]{:S(2)}) collective-permute-start(bf16[16,64,128]{2,1,0:T(8,128)(2,1)S(1)} %collective-permute-done.5), channel_id=1, source_target_pairs={{0,7},{1,0},{2,1},{3,2},{4,3},{5,4},{6,5},{7,6},{8,15},{9,8},{10,9... | collective-permute-start | bytes 786440 | tf_op jit(solution)/shard_map/ppermute | solution.py:38
  61.2 0.8 bitcast_dynamic-update-slice_fusion.3
  62.0 0.8 bitcast_dynamic-update-slice_fusion.2
  62.7 3.2 %collective-permute-done.6 = bf16[16,64,128]{2,1,0:T(8,128)(2,1)S(1)} collective-permute-done((bf16[16,64,128]{2,1,0:T(8,128)(2,1)S(1)}, bf16[16,64,128]{2,1,0:T(8,128)(2,1)S(1)}, u32[]{:S(2)}, u32[]{:S(2)}) %collective-permute-start.6) | collective-permute-done | bytes 262176 | tf_op jit(solution)/shard_map/ppermute | solution.py:38
  66.1 2.9 %collective-permute-start.9 = (bf16[8,64,128]{2,1,0:T(8,128)(2,1)S(1)}, bf16[8,64,128]{2,1,0:T(8,128)(2,1)S(1)}, u32[]{:S(2)}, u32[]{:S(2)}) collective-permute-start(bf16[8,64,128]{2,1,0:T(8,128)(2,1)S(1)} %slice.137), channel_id=1, source_target_pairs={{0,7},{1,0},{2,1},{3,2},{4,3},{5,4},{6,5},{7,6},{8,15},{9,8},{10,9... | collective-permute-start | bytes 393224 | tf_op jit(solution)/shard_map/ppermute | solution.py:38
  69.0 0.8 bitcast_dynamic-update-slice_fusion.1
  69.7 0.8 bitcast_dynamic-update-slice_fusion
  70.5 2.2 collective-permute-done.8
  72.7 0.7 bitcast_dynamic-update-slice_fusion.7
  73.4 0.7 bitcast_dynamic-update-slice_fusion.8
  74.1 6.6 %collective-permute-start.10 = (bf16[2,4096,128]{2,1,0:T(8,128)(2,1)}, bf16[2,4096,128]{2,1,0:T(8,128)(2,1)}, u32[]{:S(2)}, u32[]{:S(2)}) collective-permute-start(bf16[2,4096,128]{2,1,0:T(8,128)(2,1)} %bitcast.39), channel_id=1, source_target_pairs={{0,64},{64,0},{1,65},{65,1},{2,66},{66,2},{3,67},{67,3},{4,68},{68... | collective-permute-start | bytes 6291464 | tf_op jit(solution)/shard_map/ppermute | solution.py:20
  81.3 2.6 pad_maximum_fusion.4
  84.1 2.0 fusion.89
  86.0 0.9 copy-done.3
  86.9 1.3 fusion.36
  88.7 1.7 copy-done.4
  90.4 1.3 fusion.46
  91.7 1.7 slice_bitcast_fusion.5
  93.4 1.3 fusion.41
  94.8 1.3 fusion.51
  97.2 1.3 convolution_convert_fusion.1
  98.6 4.1 %collective-permute-done.12 = bf16[256,4096]{1,0:T(8,128)(2,1)S(1)} collective-permute-done((bf16[256,4096]{1,0:T(8,128)(2,1)S(1)}, bf16[256,4096]{1,0:T(8,128)(2,1)S(1)}, u32[]{:S(2)}, u32[]{:S(2)}) %collective-permute-start.12) | collective-permute-done | bytes 2097184 | tf_op jit(solution)/shard_map/ppermute | solution.py:20
  102.7 1.3 add_convert_fusion.1
  104.0 0.9 copy.65
  104.9 0.7 copy.60
  105.6 35.3 %all_to_all.50 = bf16[16,128,512]{2,1,0:T(8,128)(2,1)} all-to-all(bf16[16,128,512]{2,1,0:T(8,128)(2,1)S(1)} %bitcast.157), channel_id=1, replica_groups=mesh['ylo'=2,'core'=2,'yhi'=2,'x'=4,'z'=8] {'ylo','yhi','x'}, dimensions={0} | all-to-all | bytes 4194304 | tf_op jit(solution)/shard_map/all_to_all | solution.py:24
  140.9 1.9 reduce_sum.120
  142.9 11.4 %all_to_all.51 = bf16[8,64,128]{2,1,0:T(8,128)(2,1)S(1)} all-to-all(bf16[8,64,128]{2,1,0:T(8,128)(2,1)S(1)} %bitcast.170), channel_id=1, replica_groups=mesh['ylo'=2,'core'=2,'yhi'=2,'x'=4,'z'=8] {'z'}, dimensions={0} | all-to-all | bytes 262144 | tf_op jit(solution)/shard_map/all_to_all | solution.py:24
  154.4 10.4 %all_to_all.52 = bf16[8,64,128]{2,1,0:T(8,128)(2,1)S(1)} all-to-all(bf16[8,64,128]{2,1,0:T(8,128)(2,1)S(1)} %broadcast_in_dim.128), channel_id=1, replica_groups=mesh['ylo'=2,'core'=2,'yhi'=2,'x'=4,'z'=8] {'z'}, dimensions={0} | all-to-all | bytes 262144 | tf_op jit(solution)/shard_map/all_to_all | solution.py:24
  165.2 27.0 %all_to_all.53 = bf16[16,512,128]{2,1,0:T(8,128)(2,1)S(1)} all-to-all(bf16[16,512,128]{2,1,0:T(8,128)(2,1)S(1)} %broadcast_in_dim.130), channel_id=1, replica_groups=mesh['ylo'=2,'core'=2,'yhi'=2,'x'=4,'z'=8] {'ylo','yhi','x'}, dimensions={0} | all-to-all | bytes 4194304 | tf_op jit(solution)/shard_map/all_to_all | solution.py:24
  192.2 5.0 %collective-permute-start.13 = (bf16[2,4096,128]{2,1,0:T(8,128)(2,1)S(1)}, bf16[2,4096,128]{2,1,0:T(8,128)(2,1)S(1)}, u32[]{:S(2)}, u32[]{:S(2)}) collective-permute-start(bf16[2,4096,128]{2,1,0:T(8,128)(2,1)S(1)} %bitcast.155), channel_id=1, source_target_pairs={{0,64},{64,0},{1,65},{65,1},{2,66},{66,2},{3,67},{67,3},{4,68},{68... | collective-permute-start | bytes 6291464 | tf_op jit(solution)/shard_map/ppermute | solution.py:20
  197.5 1.3 fusion.56
  198.8 2.3 collective-permute-done.13
  201.2 1.3 fusion.61
  203.4 1.3 convolution_convert_fusion
  205.2 3.8 %collective-permute-done.14 = bf16[256,4096]{1,0:T(8,128)(2,1)S(1)} collective-permute-done((bf16[256,4096]{1,0:T(8,128)(2,1)S(1)}, bf16[256,4096]{1,0:T(8,128)(2,1)S(1)}, u32[]{:S(2)}, u32[]{:S(2)}) %collective-permute-start.14) | collective-permute-done | bytes 2097184 | tf_op jit(solution)/shard_map/ppermute | solution.py:20
  208.9 1.3 add_convert_fusion
  210.2 0.9 copy.66
  211.8 30.7 %all_to_all.54 = bf16[16,128,512]{2,1,0:T(8,128)(2,1)S(1)} all-to-all(bf16[16,128,512]{2,1,0:T(8,128)(2,1)S(1)} %bitcast.159), channel_id=1, replica_groups=mesh['ylo'=2,'core'=2,'yhi'=2,'x'=4,'z'=8] {'ylo','yhi','x'}, dimensions={0} | all-to-all | bytes 4194304 | tf_op jit(solution)/shard_map/all_to_all | solution.py:24
  243.0 10.3 %all_to_all.55 = bf16[8,64,128]{2,1,0:T(8,128)(2,1)S(1)} all-to-all(bf16[8,64,128]{2,1,0:T(8,128)(2,1)S(1)} %bitcast.171), channel_id=1, replica_groups=mesh['ylo'=2,'core'=2,'yhi'=2,'x'=4,'z'=8] {'z'}, dimensions={0} | all-to-all | bytes 262144 | tf_op jit(solution)/shard_map/all_to_all | solution.py:24
  253.4 8.6 %all_to_all.56 = f32[4,64,128]{2,1,0:T(8,128)S(1)} all-to-all(f32[4,64,128]{2,1,0:T(8,128)S(1)} %broadcast_in_dim.131), channel_id=1, replica_groups=mesh['ylo'=2,'core'=2,'yhi'=2,'x'=4,'z'=8] {'ylo','core'}, dimensions={0} | all-to-all | bytes 262144 | tf_op jit(solution)/shard_map/all_to_all | solution.py:24
  (70 shorter events, 9.7 us)
Async XLA Ops:
  0.0 22.1 %copy-start = (bf16[64,512]{1,0:T(8,128)(2,1)S(1)}, bf16[64,512]{1,0:T(8,128)(2,1)}, u32[]{:S(2)}) copy-start(bf16[64,512]{1,0:T(8,128)(2,1)} %param.9) | copy-start | bytes 196612
  1.5 20.6 %all-to-all-start = ((bf16[16,64,128]{2,1,0:T(8,128)(2,1)}), bf16[16,64,128]{2,1,0:T(8,128)(2,1)S(1)}, u32[]{:S(2)}, u32[]{:S(2)}) async-start(bf16[16,64,128]{2,1,0:T(8,128)(2,1)} %broadcast_in_dim.115), calls=%async_computation | async-start | bytes 524288 | tf_op jit(solution)/shard_map/all_to_all | solution.py:24
  15.1 21.0 %collective-permute-start = (f32[2,8,128]{2,1,0:T(8,128)S(1)}, f32[2,8,128]{2,1,0:T(8,128)S(1)}, u32[]{:S(2)}, u32[]{:S(2)}) collective-permute-start(f32[2,8,128]{2,1,0:T(8,128)S(1)} %broadcast_in_dim.58), channel_id=1, source_target_pairs={{0,1},{1,2},{2,3},{3,4},{4,5},{5,6},{6,7},{7,8},{8,9},{9,10},{10,1... | collective-permute-start | bytes 24584 | tf_op jit(solution)/shard_map/ppermute | solution.py:101
  20.0 60.6 %collective-permute-start.1 = (f32[2,8,128]{2,1,0:T(8,128)S(1)}, f32[2,8,128]{2,1,0:T(8,128)S(1)}, u32[]{:S(2)}, u32[]{:S(2)}) collective-permute-start(f32[2,8,128]{2,1,0:T(8,128)S(1)} %broadcast_in_dim.59), channel_id=1, source_target_pairs={{1,0},{2,1},{3,2},{4,3},{5,4},{6,5},{7,6},{8,7},{9,8},{10,9},{11,1... | collective-permute-start | bytes 24584 | tf_op jit(solution)/shard_map/ppermute | solution.py:102
  22.8 17.9 %all-to-all-start.1 = ((bf16[8,64,128]{2,1,0:T(8,128)(2,1)}), bf16[8,64,128]{2,1,0:T(8,128)(2,1)S(1)}, u32[]{:S(2)}, u32[]{:S(2)}) async-start(bf16[8,64,128]{2,1,0:T(8,128)(2,1)} %broadcast_in_dim.125), calls=%async_computation.1 | async-start | bytes 262144 | tf_op jit(solution)/shard_map/all_to_all | solution.py:24
  33.5 18.3 %collective-permute-start.2 = (bf16[16,64,128]{2,1,0:T(8,128)(2,1)S(1)}, bf16[16,64,128]{2,1,0:T(8,128)(2,1)S(1)}, u32[]{:S(2)}, u32[]{:S(2)}) collective-permute-start(bf16[16,64,128]{2,1,0:T(8,128)(2,1)S(1)} %all-to-all-done), channel_id=1, source_target_pairs={{0,1},{1,2},{2,3},{3,4},{4,5},{5,6},{6,7},{7,0},{8,9},{9,10},{10,1... | collective-permute-start | bytes 786440 | tf_op jit(solution)/shard_map/ppermute | solution.py:38
  34.9 17.1 %collective-permute-start.3 = (bf16[16,64,128]{2,1,0:T(8,128)(2,1)S(1)}, bf16[16,64,128]{2,1,0:T(8,128)(2,1)S(1)}, u32[]{:S(2)}, u32[]{:S(2)}) collective-permute-start(bf16[16,64,128]{2,1,0:T(8,128)(2,1)S(1)} %all-to-all-done), channel_id=1, source_target_pairs={{0,7},{1,0},{2,1},{3,2},{4,3},{5,4},{6,5},{7,6},{8,15},{9,8},{10,9... | collective-permute-start | bytes 786440 | tf_op jit(solution)/shard_map/ppermute | solution.py:38
  42.5 45.7 %all-to-all-start.2 = ((bf16[16,512,128]{2,1,0:T(8,128)(2,1)}), bf16[16,512,128]{2,1,0:T(8,128)(2,1)S(1)}, u32[]{:S(2)}, u32[]{:S(2)}) async-start(bf16[16,512,128]{2,1,0:T(8,128)(2,1)} %broadcast_in_dim.127), calls=%async_computation.2 | async-start | bytes 4194304 | tf_op jit(solution)/shard_map/all_to_all | solution.py:24
  51.8 6.7 %collective-permute-start.4 = (bf16[16,64,128]{2,1,0:T(8,128)(2,1)S(1)}, bf16[16,64,128]{2,1,0:T(8,128)(2,1)S(1)}, u32[]{:S(2)}, u32[]{:S(2)}) collective-permute-start(bf16[16,64,128]{2,1,0:T(8,128)(2,1)S(1)} %collective-permute-done.2), channel_id=1, source_target_pairs={{0,1},{1,2},{2,3},{3,4},{4,5},{5,6},{6,7},{7,0},{8,9},{9,10},{10,1... | collective-permute-start | bytes 786440 | tf_op jit(solution)/shard_map/ppermute | solution.py:38
  52.0 6.5 %collective-permute-start.5 = (bf16[16,64,128]{2,1,0:T(8,128)(2,1)S(1)}, bf16[16,64,128]{2,1,0:T(8,128)(2,1)S(1)}, u32[]{:S(2)}, u32[]{:S(2)}) collective-permute-start(bf16[16,64,128]{2,1,0:T(8,128)(2,1)S(1)} %collective-permute-done.3), channel_id=1, source_target_pairs={{0,7},{1,0},{2,1},{3,2},{4,3},{5,4},{6,5},{7,6},{8,15},{9,8},{10,9... | collective-permute-start | bytes 786440 | tf_op jit(solution)/shard_map/ppermute | solution.py:38
  58.5 7.4 %collective-permute-start.6 = (bf16[16,64,128]{2,1,0:T(8,128)(2,1)S(1)}, bf16[16,64,128]{2,1,0:T(8,128)(2,1)S(1)}, u32[]{:S(2)}, u32[]{:S(2)}) collective-permute-start(bf16[16,64,128]{2,1,0:T(8,128)(2,1)S(1)} %collective-permute-done.4), channel_id=1, source_target_pairs={{0,1},{1,2},{2,3},{3,4},{4,5},{5,6},{6,7},{7,0},{8,9},{9,10},{10,1... | collective-permute-start | bytes 786440 | tf_op jit(solution)/shard_map/ppermute | solution.py:38
  58.5 7.5 %collective-permute-start.7 = (bf16[16,64,128]{2,1,0:T(8,128)(2,1)S(1)}, bf16[16,64,128]{2,1,0:T(8,128)(2,1)S(1)}, u32[]{:S(2)}, u32[]{:S(2)}) collective-permute-start(bf16[16,64,128]{2,1,0:T(8,128)(2,1)S(1)} %collective-permute-done.5), channel_id=1, source_target_pairs={{0,7},{1,0},{2,1},{3,2},{4,3},{5,4},{6,5},{7,6},{8,15},{9,8},{10,9... | collective-permute-start | bytes 786440 | tf_op jit(solution)/shard_map/ppermute | solution.py:38
  65.9 6.8 %collective-permute-start.8 = (bf16[8,64,128]{2,1,0:T(8,128)(2,1)S(1)}, bf16[8,64,128]{2,1,0:T(8,128)(2,1)S(1)}, u32[]{:S(2)}, u32[]{:S(2)}) collective-permute-start(bf16[8,64,128]{2,1,0:T(8,128)(2,1)S(1)} %slice.136), channel_id=1, source_target_pairs={{0,1},{1,2},{2,3},{3,4},{4,5},{5,6},{6,7},{7,0},{8,9},{9,10},{10,1... | collective-permute-start | bytes 393224 | tf_op jit(solution)/shard_map/ppermute | solution.py:38
  66.1 7.3 %collective-permute-start.9 = (bf16[8,64,128]{2,1,0:T(8,128)(2,1)S(1)}, bf16[8,64,128]{2,1,0:T(8,128)(2,1)S(1)}, u32[]{:S(2)}, u32[]{:S(2)}) collective-permute-start(bf16[8,64,128]{2,1,0:T(8,128)(2,1)S(1)} %slice.137), channel_id=1, source_target_pairs={{0,7},{1,0},{2,1},{3,2},{4,3},{5,4},{6,5},{7,6},{8,15},{9,8},{10,9... | collective-permute-start | bytes 393224 | tf_op jit(solution)/shard_map/ppermute | solution.py:38
  74.1 17.6 %collective-permute-start.10 = (bf16[2,4096,128]{2,1,0:T(8,128)(2,1)}, bf16[2,4096,128]{2,1,0:T(8,128)(2,1)}, u32[]{:S(2)}, u32[]{:S(2)}) collective-permute-start(bf16[2,4096,128]{2,1,0:T(8,128)(2,1)} %bitcast.39), channel_id=1, source_target_pairs={{0,64},{64,0},{1,65},{65,1},{2,66},{66,2},{3,67},{67,3},{4,68},{68... | collective-permute-start | bytes 6291464 | tf_op jit(solution)/shard_map/ppermute | solution.py:20
  84.1 2.8 %copy-start.3 = (bf16[1,512,4096]{2,1,0:T(8,128)(2,1)S(1)}, bf16[1,512,4096]{2,1,0:T(8,128)(2,1)}, u32[]{:S(2)}) copy-start(bf16[1,512,4096]{2,1,0:T(8,128)(2,1)} %param.6) | copy-start | bytes 12582916
  88.2 2.2 copy-start.4
  88.2 6.5 %collective-permute-start.11 = (bf16[2,4096,128]{2,1,0:T(8,128)(2,1)S(1)}, bf16[2,4096,128]{2,1,0:T(8,128)(2,1)S(1)}, u32[]{:S(2)}, u32[]{:S(2)}) collective-permute-start(bf16[2,4096,128]{2,1,0:T(8,128)(2,1)S(1)} %bitcast.154), channel_id=1, source_target_pairs={{0,64},{64,0},{1,65},{65,1},{2,66},{66,2},{3,67},{67,3},{4,68},{68... | collective-permute-start | bytes 6291464 | tf_op jit(solution)/shard_map/ppermute | solution.py:20
  98.5 4.2 %collective-permute-start.12 = (bf16[256,4096]{1,0:T(8,128)(2,1)S(1)}, bf16[256,4096]{1,0:T(8,128)(2,1)S(1)}, u32[]{:S(2)}, u32[]{:S(2)}) collective-permute-start(bf16[256,4096]{1,0:T(8,128)(2,1)S(1)} %convolution_convert_fusion.1), channel_id=1, source_target_pairs={{0,64},{64,0},{1,65},{65,1},{2,66},{66,2},{3,67},{67,3},{4,68},{68... | collective-permute-start | bytes 6291464 | tf_op jit(solution)/shard_map/ppermute | solution.py:20
  140.9 13.5 %copy-start.2 = (f32[64,512]{1,0:T(8,128)S(1)}, f32[64,512]{1,0:T(8,128)}, u32[]{:S(2)}) copy-start(f32[64,512]{1,0:T(8,128)} %param.11) | copy-start | bytes 393220
  192.2 5.2 %copy-start.5 = (bf16[1,512,4096]{2,1,0:T(8,128)(2,1)S(1)}, bf16[1,512,4096]{2,1,0:T(8,128)(2,1)}, u32[]{:S(2)}) copy-start(bf16[1,512,4096]{2,1,0:T(8,128)(2,1)} %param.6) | copy-start | bytes 12582916
  192.2 8.8 %collective-permute-start.13 = (bf16[2,4096,128]{2,1,0:T(8,128)(2,1)S(1)}, bf16[2,4096,128]{2,1,0:T(8,128)(2,1)S(1)}, u32[]{:S(2)}, u32[]{:S(2)}) collective-permute-start(bf16[2,4096,128]{2,1,0:T(8,128)(2,1)S(1)} %bitcast.155), channel_id=1, source_target_pairs={{0,64},{64,0},{1,65},{65,1},{2,66},{66,2},{3,67},{67,3},{4,68},{68... | collective-permute-start | bytes 6291464 | tf_op jit(solution)/shard_map/ppermute | solution.py:20
  204.7 4.2 %collective-permute-start.14 = (bf16[256,4096]{1,0:T(8,128)(2,1)S(1)}, bf16[256,4096]{1,0:T(8,128)(2,1)S(1)}, u32[]{:S(2)}, u32[]{:S(2)}) collective-permute-start(bf16[256,4096]{1,0:T(8,128)(2,1)S(1)} %convolution_convert_fusion), channel_id=1, source_target_pairs={{0,64},{64,0},{1,65},{65,1},{2,66},{66,2},{3,67},{67,3},{4,68},{68... | collective-permute-start | bytes 6291464 | tf_op jit(solution)/shard_map/ppermute | solution.py:20
  211.8 50.9 %copy-start.1 = (bf16[64,512]{1,0:T(8,128)(2,1)S(1)}, bf16[64,512]{1,0:T(8,128)(2,1)}, u32[]{:S(2)}) copy-start(bf16[64,512]{1,0:T(8,128)(2,1)} %param.9) | copy-start | bytes 196612

commit v5 on v4

--- a/solution.py
+++ b/solution.py
@@ -51,11 +51,6 @@
     return put(whole, shift(after[half:], -1), me + n // 2, half)
 
 
-def gather_ring(block):
-    n = lax.axis_size("ylo")
-    return ring_gather(spread(block, PLANE)).reshape(n, -1, block.shape[1])
-
-
 def gather_plane(block):
     return spread(block, PLANE).reshape(lax.axis_size("ylo"), -1, block.shape[1])
 
@@ -91,19 +86,14 @@
 
 def turn_counts(text_mask, turn_ids):
     n = lax.axis_size(SHARD)
-    first, last = turn_ids[0], turn_ids[-1]
-
-    def edge(turn):
-        count = jnp.sum(jnp.where(turn_ids == turn, text_mask, 0.0))
-        row = jnp.stack([turn.astype(jnp.float32), count])
-        return jnp.broadcast_to(row[:, None, None], (2, 8, 128))
-
-    left = lax.ppermute(edge(last), SHARD, [(i, i + 1) for i in range(n - 1)])
-    right = lax.ppermute(edge(first), SHARD, [(i + 1, i) for i in range(n - 1)])
-    ids = jnp.concatenate([turn_ids.astype(jnp.float32), left[0, 0, :1], right[0, 0, :1]])
-    texts = jnp.concatenate([text_mask, left[1, 0, :1], right[1, 0, :1]])
-    same = turn_ids.astype(jnp.float32)[:, None] == ids[None, :]
-    return jnp.sum(jnp.where(same, texts[None, :], 0.0), axis=1)
+    turns = turn_ids.astype(jnp.float32)
+    here = jnp.stack([turns, text_mask])
+    left = lax.ppermute(here, SHARD, [(i, i + 1) for i in range(n - 1)])
+    right = lax.ppermute(here, SHARD, [(i + 1, i) for i in range(n - 1)])
+    return sum(
+        jnp.sum(jnp.where(turns[:, None] == other[0][None, :], other[1][None, :], 0.0), axis=1)
+        for other in (here, left, right)
+    )
 
 
 def local(acts, token_ids, turn_ids, value_weight, norm_gain, query_grad):
@@ -133,10 +123,14 @@
     gain_square = gain * gain
     query = own(query_grad)
 
+    line = gather_line(own(value_weight))
+    block, line = lax.optimization_barrier((query.astype(jnp.bfloat16), line))
+    plane = spread(block, PLANE)
+    plane, line = lax.optimization_barrier((plane, line))
+    tangent = project(ring_gather(plane).reshape(lax.axis_size("ylo"), -1, cols))
+    values = project(gather_plane(line))
     own_count = turn_counts(text_mask, ids)
     turn_weight = text_mask / (jnp.maximum(own_count, 1.0) * jnp.float32(turn_total))
-    tangent = project(gather_ring(query.astype(jnp.bfloat16)))
-    values = project(gather_plane(gather_line(own(value_weight))))
     root_mean = jnp.sqrt(jnp.mean(values * values, axis=-1, keepdims=True) + 1e-06)
     unit_values = values / root_mean
     estimate = query

time: 264 us -> 256 us (0.970)
  other arithmetic: 13.9 us -> 7.6 us
    all_to_all x3, waiting for transfers between devices: 4.05 us -> 7.84 us  [exchange(): return lax.all_to_all(blocks, axes, split_axis=0, concat_axis=0, tiled=True)]
  transfers between devices with their start and end apart: 18 -> 18, of which waited for: 7 -> 8; matrix products, arithmetic and copies ran while one was open for 12% -> 9% of each run, Pallas kernels for 0% -> 0%
where the time goes in v5:
time: 256 us; the launch traced here: 255 us
  blocking collectives  136 us (53%)
  starting transfers between devices  49.8 us (19%)
  waiting for transfers between devices  24.7 us (10%)
  local copies, waits for them, and re-layouts  24 us (9%)
  matrix products  12.8 us (5%)
  other arithmetic  7.6 us (3%)
    all_to_all x7, blocking collectives, exchange(): return lax.all_to_all(blocks, axes, split_axis=0, concat_axis=0, tiled=True)  136 us
    all_to_all x3, starting transfers between devices, exchange(): return lax.all_to_all(blocks, axes, split_axis=0, concat_axis=0, tiled=True)  22.4 us
    ppermute x5, starting transfers between devices, core_swap(): return lax.ppermute(value, 'core', [(0, 1), (1, 0)])  11.7 us
    ppermute x8, starting transfers between devices, shift(): return lax.ppermute(value, 'z', [(i, (i + step) % n) for i in range(n)])  10.9 us
    ppermute x5, waiting for transfers between devices, core_swap(): return lax.ppermute(value, 'core', [(0, 1), (1, 0)])  10.2 us
    all_to_all x3, waiting for transfers between devices, exchange(): return lax.all_to_all(blocks, axes, split_axis=0, concat_axis=0, tiled=True)  7.84 us
    dot_general x6, matrix products, project(): jnp.dot(inputs, half, preferred_element_type=jnp.float32)  7.75 us
    dynamic_update_slice x9, local copies, waits for them, and re-layouts, put(): lax.dynamic_update_slice(whole, piece[:, None], (start, owner % n, 0, 0))  6.7 us
  transfers between devices with their start and end apart: 18, of which 8 were waited for; matrix products, arithmetic and copies ran while one was open for 9% of the time, Pallas kernels for 0%

profile of v5, /device:TPU:1, one launch (start us, length us, event | category | flops | bytes accessed | tf_op | source)
XLA Modules:
  0.0 255.3 jit_solution(2263268452889430101)
XLA Ops:
  0.0 0.8 copy-done
  0.8 0.7 broadcast_in_dim.117
  1.5 9.0 %all-to-all-start = ((bf16[8,64,128]{2,1,0:T(8,128)(2,1)}), bf16[8,64,128]{2,1,0:T(8,128)(2,1)S(1)}, u32[]{:S(2)}, u32[]{:S(2)}) async-start(bf16[8,64,128]{2,1,0:T(8,128)(2,1)} %broadcast_in_dim.117), calls=%async_computation | async-start | bytes 262144 | tf_op jit(solution)/shard_map/all_to_all | solution.py:24
  10.5 0.7 compare_convert_fusion
  11.2 0.7 convert_element_type.66
  11.9 3.4 %collective-permute-start = (f32[2,512]{1,0:T(2,128)S(1)}, f32[2,512]{1,0:T(2,128)S(1)}, u32[]{:S(2)}, u32[]{:S(2)}) collective-permute-start(f32[2,512]{1,0:T(2,128)S(1)} %pad_maximum_fusion.4), channel_id=1, source_target_pairs={{0,1},{1,2},{2,3},{3,4},{4,5},{5,6},{6,7},{7,8},{8,9},{9,10},{10,1... | collective-permute-start | bytes 12296 | tf_op jit(solution)/shard_map/ppermute | solution.py:91
  15.3 1.3 collective-permute-start.1
  16.6 0.8 dynamic-slice_convert_fusion
  17.4 0.9 all-to-all-done
  18.3 0.7 broadcast_in_dim.118
  19.0 9.7 %all-to-all-start.1 = ((bf16[16,64,128]{2,1,0:T(8,128)(2,1)}), bf16[16,64,128]{2,1,0:T(8,128)(2,1)S(1)}, u32[]{:S(2)}, u32[]{:S(2)}) async-start(bf16[16,64,128]{2,1,0:T(8,128)(2,1)} %broadcast_in_dim.118), calls=%async_computation.1 | async-start | bytes 524288 | tf_op jit(solution)/shard_map/all_to_all | solution.py:24
  28.8 0.8 fusion.92
  29.5 6.9 %all-to-all-done.1 = bf16[16,64,128]{2,1,0:T(8,128)(2,1)S(1)} async-done(((bf16[16,64,128]{2,1,0:T(8,128)(2,1)}), bf16[16,64,128]{2,1,0:T(8,128)(2,1)S(1)}, u32[]{:S(2)}, u32[]{:S(2)}) %all-to-all-start.1) | async-done | bytes 262176 | tf_op jit(solution)/shard_map/all_to_all | solution.py:24
  36.4 2.7 %collective-permute-start.3 = (bf16[16,64,128]{2,1,0:T(8,128)(2,1)S(1)}, bf16[16,64,128]{2,1,0:T(8,128)(2,1)S(1)}, u32[]{:S(2)}, u32[]{:S(2)}) collective-permute-start(bf16[16,64,128]{2,1,0:T(8,128)(2,1)S(1)} %all-to-all-done.1), channel_id=1, source_target_pairs={{0,7},{1,0},{2,1},{3,2},{4,3},{5,4},{6,5},{7,6},{8,15},{9,8},{10,9... | collective-permute-start | bytes 786440 | tf_op jit(solution)/shard_map/ppermute | solution.py:38
  39.1 1.7 broadcast_in_dim.128
  40.9 3.7 %all-to-all-start.2 = ((bf16[16,512,128]{2,1,0:T(8,128)(2,1)}), bf16[16,512,128]{2,1,0:T(8,128)(2,1)S(1)}, u32[]{:S(2)}, u32[]{:S(2)}) async-start(bf16[16,512,128]{2,1,0:T(8,128)(2,1)} %broadcast_in_dim.128), calls=%async_computation.2 | async-start | bytes 4194304 | tf_op jit(solution)/shard_map/all_to_all | solution.py:24
  44.6 1.8 broadcast_in_dim.116
  46.4 0.8 bitcast_dynamic-update-slice_fusion.6
  47.2 2.7 %collective-permute-start.5 = (bf16[16,64,128]{2,1,0:T(8,128)(2,1)S(1)}, bf16[16,64,128]{2,1,0:T(8,128)(2,1)S(1)}, u32[]{:S(2)}, u32[]{:S(2)}) collective-permute-start(bf16[16,64,128]{2,1,0:T(8,128)(2,1)S(1)} %collective-permute-done.3), channel_id=1, source_target_pairs={{0,7},{1,0},{2,1},{3,2},{4,3},{5,4},{6,5},{7,6},{8,15},{9,8},{10,9... | collective-permute-start | bytes 786440 | tf_op jit(solution)/shard_map/ppermute | solution.py:38
  49.9 0.8 bitcast_dynamic-update-slice_fusion.5
  50.6 0.8 bitcast_dynamic-update-slice_fusion.4
  51.4 2.5 collective-permute-done.4
  53.9 2.7 %collective-permute-start.7 = (bf16[16,64,128]{2,1,0:T(8,128)(2,1)S(1)}, bf16[16,64,128]{2,1,0:T(8,128)(2,1)S(1)}, u32[]{:S(2)}, u32[]{:S(2)}) collective-permute-start(bf16[16,64,128]{2,1,0:T(8,128)(2,1)S(1)} %collective-permute-done.5), channel_id=1, source_target_pairs={{0,7},{1,0},{2,1},{3,2},{4,3},{5,4},{6,5},{7,6},{8,15},{9,8},{10,9... | collective-permute-start | bytes 786440 | tf_op jit(solution)/shard_map/ppermute | solution.py:38
  56.6 0.8 bitcast_dynamic-update-slice_fusion.3
  57.3 0.8 bitcast_dynamic-update-slice_fusion.2
  58.1 2.5 collective-permute-done.6
  60.8 2.8 %collective-permute-start.9 = (bf16[8,64,128]{2,1,0:T(8,128)(2,1)S(1)}, bf16[8,64,128]{2,1,0:T(8,128)(2,1)S(1)}, u32[]{:S(2)}, u32[]{:S(2)}) collective-permute-start(bf16[8,64,128]{2,1,0:T(8,128)(2,1)S(1)} %slice.127), channel_id=1, source_target_pairs={{0,7},{1,0},{2,1},{3,2},{4,3},{5,4},{6,5},{7,6},{8,15},{9,8},{10,9... | collective-permute-start | bytes 393224 | tf_op jit(solution)/shard_map/ppermute | solution.py:38
  63.6 0.8 bitcast_dynamic-update-slice_fusion.1
  64.4 0.8 bitcast_dynamic-update-slice_fusion
  65.2 1.6 collective-permute-done.8
  66.7 0.7 bitcast_dynamic-update-slice_fusion.7
  67.4 0.7 bitcast_dynamic-update-slice_fusion.8
  68.1 5.9 %collective-permute-start.10 = (bf16[2,4096,128]{2,1,0:T(8,128)(2,1)}, bf16[2,4096,128]{2,1,0:T(8,128)(2,1)}, u32[]{:S(2)}, u32[]{:S(2)}) collective-permute-start(bf16[2,4096,128]{2,1,0:T(8,128)(2,1)} %bitcast.34), channel_id=1, source_target_pairs={{0,64},{64,0},{1,65},{65,1},{2,66},{66,2},{3,67},{67,3},{4,68},{68... | collective-permute-start | bytes 6291464 | tf_op jit(solution)/shard_map/ppermute | solution.py:20
  74.5 2.0 fusion.89
  76.4 0.9 copy-done.3
  77.3 1.3 fusion.36
  79.1 1.7 copy-done.4
  80.8 1.3 fusion.46
  82.1 1.7 slice_bitcast_fusion.5
  83.8 1.3 fusion.41
  85.2 1.3 fusion.51
  87.6 1.3 convolution_convert_fusion.1
  89.0 4.1 %collective-permute-done.12 = bf16[256,4096]{1,0:T(8,128)(2,1)S(1)} collective-permute-done((bf16[256,4096]{1,0:T(8,128)(2,1)S(1)}, bf16[256,4096]{1,0:T(8,128)(2,1)S(1)}, u32[]{:S(2)}, u32[]{:S(2)}) %collective-permute-start.12) | collective-permute-done | bytes 2097184 | tf_op jit(solution)/shard_map/ppermute | solution.py:20
  93.1 1.3 add_convert_fusion.1
  94.4 0.9 copy.65
  95.3 0.7 copy.60
  96.0 35.0 %all_to_all.50 = bf16[16,128,512]{2,1,0:T(8,128)(2,1)} all-to-all(bf16[16,128,512]{2,1,0:T(8,128)(2,1)S(1)} %bitcast.151), channel_id=1, replica_groups=mesh['ylo'=2,'core'=2,'yhi'=2,'x'=4,'z'=8] {'ylo','yhi','x'}, dimensions={0} | all-to-all | bytes 4194304 | tf_op jit(solution)/shard_map/all_to_all | solution.py:24
  131.0 1.9 reduce_sum.120
  133.1 13.9 %all_to_all.51 = bf16[8,64,128]{2,1,0:T(8,128)(2,1)S(1)} all-to-all(bf16[8,64,128]{2,1,0:T(8,128)(2,1)S(1)} %bitcast.164), channel_id=1, replica_groups=mesh['ylo'=2,'core'=2,'yhi'=2,'x'=4,'z'=8] {'z'}, dimensions={0} | all-to-all | bytes 262144 | tf_op jit(solution)/shard_map/all_to_all | solution.py:24
  147.1 10.4 %all_to_all.52 = bf16[8,64,128]{2,1,0:T(8,128)(2,1)S(1)} all-to-all(bf16[8,64,128]{2,1,0:T(8,128)(2,1)S(1)} %broadcast_in_dim.129), channel_id=1, replica_groups=mesh['ylo'=2,'core'=2,'yhi'=2,'x'=4,'z'=8] {'z'}, dimensions={0} | all-to-all | bytes 262144 | tf_op jit(solution)/shard_map/all_to_all | solution.py:24
  157.8 27.0 %all_to_all.53 = bf16[16,512,128]{2,1,0:T(8,128)(2,1)S(1)} all-to-all(bf16[16,512,128]{2,1,0:T(8,128)(2,1)S(1)} %broadcast_in_dim.131), channel_id=1, replica_groups=mesh['ylo'=2,'core'=2,'yhi'=2,'x'=4,'z'=8] {'ylo','yhi','x'}, dimensions={0} | all-to-all | bytes 4194304 | tf_op jit(solution)/shard_map/all_to_all | solution.py:24
  184.9 5.0 %collective-permute-start.13 = (bf16[2,4096,128]{2,1,0:T(8,128)(2,1)S(1)}, bf16[2,4096,128]{2,1,0:T(8,128)(2,1)S(1)}, u32[]{:S(2)}, u32[]{:S(2)}) collective-permute-start(bf16[2,4096,128]{2,1,0:T(8,128)(2,1)S(1)} %bitcast.149), channel_id=1, source_target_pairs={{0,64},{64,0},{1,65},{65,1},{2,66},{66,2},{3,67},{67,3},{4,68},{68... | collective-permute-start | bytes 6291464 | tf_op jit(solution)/shard_map/ppermute | solution.py:20
  190.1 1.3 fusion.56
  191.4 2.3 collective-permute-done.13
  193.8 1.3 fusion.61
  196.1 1.3 convolution_convert_fusion
  197.8 3.8 %collective-permute-done.14 = bf16[256,4096]{1,0:T(8,128)(2,1)S(1)} collective-permute-done((bf16[256,4096]{1,0:T(8,128)(2,1)S(1)}, bf16[256,4096]{1,0:T(8,128)(2,1)S(1)}, u32[]{:S(2)}, u32[]{:S(2)}) %collective-permute-start.14) | collective-permute-done | bytes 2097184 | tf_op jit(solution)/shard_map/ppermute | solution.py:20
  201.6 1.3 add_convert_fusion
  202.9 0.9 copy.66
  203.8 0.7 copy.62
  204.5 30.7 %all_to_all.54 = bf16[16,128,512]{2,1,0:T(8,128)(2,1)S(1)} all-to-all(bf16[16,128,512]{2,1,0:T(8,128)(2,1)S(1)} %bitcast.153), channel_id=1, replica_groups=mesh['ylo'=2,'core'=2,'yhi'=2,'x'=4,'z'=8] {'ylo','yhi','x'}, dimensions={0} | all-to-all | bytes 4194304 | tf_op jit(solution)/shard_map/all_to_all | solution.py:24
  235.6 10.3 %all_to_all.55 = bf16[8,64,128]{2,1,0:T(8,128)(2,1)S(1)} all-to-all(bf16[8,64,128]{2,1,0:T(8,128)(2,1)S(1)} %bitcast.165), channel_id=1, replica_groups=mesh['ylo'=2,'core'=2,'yhi'=2,'x'=4,'z'=8] {'z'}, dimensions={0} | all-to-all | bytes 262144 | tf_op jit(solution)/shard_map/all_to_all | solution.py:24
  246.0 8.6 %all_to_all.56 = f32[4,64,128]{2,1,0:T(8,128)S(1)} all-to-all(f32[4,64,128]{2,1,0:T(8,128)S(1)} %broadcast_in_dim.132), channel_id=1, replica_groups=mesh['ylo'=2,'core'=2,'yhi'=2,'x'=4,'z'=8] {'ylo','core'}, dimensions={0} | all-to-all | bytes 262144 | tf_op jit(solution)/shard_map/all_to_all | solution.py:24
  254.7 0.7 pad_maximum_fusion.3
  (62 shorter events, 5.2 us)
Async XLA Ops:
  0.0 0.8 copy-start
  1.5 16.8 %all-to-all-start = ((bf16[8,64,128]{2,1,0:T(8,128)(2,1)}), bf16[8,64,128]{2,1,0:T(8,128)(2,1)S(1)}, u32[]{:S(2)}, u32[]{:S(2)}) async-start(bf16[8,64,128]{2,1,0:T(8,128)(2,1)} %broadcast_in_dim.117), calls=%async_computation | async-start | bytes 262144 | tf_op jit(solution)/shard_map/all_to_all | solution.py:24
  11.9 62.1 %collective-permute-start = (f32[2,512]{1,0:T(2,128)S(1)}, f32[2,512]{1,0:T(2,128)S(1)}, u32[]{:S(2)}, u32[]{:S(2)}) collective-permute-start(f32[2,512]{1,0:T(2,128)S(1)} %pad_maximum_fusion.4), channel_id=1, source_target_pairs={{0,1},{1,2},{2,3},{3,4},{4,5},{5,6},{6,7},{7,8},{8,9},{9,10},{10,1... | collective-permute-start | bytes 12296 | tf_op jit(solution)/shard_map/ppermute | solution.py:91
  15.3 58.7 %collective-permute-start.1 = (f32[2,512]{1,0:T(2,128)S(1)}, f32[2,512]{1,0:T(2,128)S(1)}, u32[]{:S(2)}, u32[]{:S(2)}) collective-permute-start(f32[2,512]{1,0:T(2,128)S(1)} %pad_maximum_fusion.4), channel_id=1, source_target_pairs={{1,0},{2,1},{3,2},{4,3},{5,4},{6,5},{7,6},{8,7},{9,8},{10,9},{11,1... | collective-permute-start | bytes 12296 | tf_op jit(solution)/shard_map/ppermute | solution.py:92
  19.0 17.4 %all-to-all-start.1 = ((bf16[16,64,128]{2,1,0:T(8,128)(2,1)}), bf16[16,64,128]{2,1,0:T(8,128)(2,1)S(1)}, u32[]{:S(2)}, u32[]{:S(2)}) async-start(bf16[16,64,128]{2,1,0:T(8,128)(2,1)} %broadcast_in_dim.118), calls=%async_computation.1 | async-start | bytes 524288 | tf_op jit(solution)/shard_map/all_to_all | solution.py:24
  36.4 10.8 %collective-permute-start.2 = (bf16[16,64,128]{2,1,0:T(8,128)(2,1)S(1)}, bf16[16,64,128]{2,1,0:T(8,128)(2,1)S(1)}, u32[]{:S(2)}, u32[]{:S(2)}) collective-permute-start(bf16[16,64,128]{2,1,0:T(8,128)(2,1)S(1)} %all-to-all-done.1), channel_id=1, source_target_pairs={{0,1},{1,2},{2,3},{3,4},{4,5},{5,6},{6,7},{7,0},{8,9},{9,10},{10,1... | collective-permute-start | bytes 786440 | tf_op jit(solution)/shard_map/ppermute | solution.py:38
  36.4 10.8 %collective-permute-start.3 = (bf16[16,64,128]{2,1,0:T(8,128)(2,1)S(1)}, bf16[16,64,128]{2,1,0:T(8,128)(2,1)S(1)}, u32[]{:S(2)}, u32[]{:S(2)}) collective-permute-start(bf16[16,64,128]{2,1,0:T(8,128)(2,1)S(1)} %all-to-all-done.1), channel_id=1, source_target_pairs={{0,7},{1,0},{2,1},{3,2},{4,3},{5,4},{6,5},{7,6},{8,15},{9,8},{10,9... | collective-permute-start | bytes 786440 | tf_op jit(solution)/shard_map/ppermute | solution.py:38
  40.9 37.7 %all-to-all-start.2 = ((bf16[16,512,128]{2,1,0:T(8,128)(2,1)}), bf16[16,512,128]{2,1,0:T(8,128)(2,1)S(1)}, u32[]{:S(2)}, u32[]{:S(2)}) async-start(bf16[16,512,128]{2,1,0:T(8,128)(2,1)} %broadcast_in_dim.128), calls=%async_computation.2 | async-start | bytes 4194304 | tf_op jit(solution)/shard_map/all_to_all | solution.py:24
  47.2 6.7 %collective-permute-start.4 = (bf16[16,64,128]{2,1,0:T(8,128)(2,1)S(1)}, bf16[16,64,128]{2,1,0:T(8,128)(2,1)S(1)}, u32[]{:S(2)}, u32[]{:S(2)}) collective-permute-start(bf16[16,64,128]{2,1,0:T(8,128)(2,1)S(1)} %collective-permute-done.2), channel_id=1, source_target_pairs={{0,1},{1,2},{2,3},{3,4},{4,5},{5,6},{6,7},{7,0},{8,9},{9,10},{10,1... | collective-permute-start | bytes 786440 | tf_op jit(solution)/shard_map/ppermute | solution.py:38
  47.2 6.7 %collective-permute-start.5 = (bf16[16,64,128]{2,1,0:T(8,128)(2,1)S(1)}, bf16[16,64,128]{2,1,0:T(8,128)(2,1)S(1)}, u32[]{:S(2)}, u32[]{:S(2)}) collective-permute-start(bf16[16,64,128]{2,1,0:T(8,128)(2,1)S(1)} %collective-permute-done.3), channel_id=1, source_target_pairs={{0,7},{1,0},{2,1},{3,2},{4,3},{5,4},{6,5},{7,6},{8,15},{9,8},{10,9... | collective-permute-start | bytes 786440 | tf_op jit(solution)/shard_map/ppermute | solution.py:38
  53.9 6.7 %collective-permute-start.6 = (bf16[16,64,128]{2,1,0:T(8,128)(2,1)S(1)}, bf16[16,64,128]{2,1,0:T(8,128)(2,1)S(1)}, u32[]{:S(2)}, u32[]{:S(2)}) collective-permute-start(bf16[16,64,128]{2,1,0:T(8,128)(2,1)S(1)} %collective-permute-done.4), channel_id=1, source_target_pairs={{0,1},{1,2},{2,3},{3,4},{4,5},{5,6},{6,7},{7,0},{8,9},{9,10},{10,1... | collective-permute-start | bytes 786440 | tf_op jit(solution)/shard_map/ppermute | solution.py:38
  53.9 6.8 %collective-permute-start.7 = (bf16[16,64,128]{2,1,0:T(8,128)(2,1)S(1)}, bf16[16,64,128]{2,1,0:T(8,128)(2,1)S(1)}, u32[]{:S(2)}, u32[]{:S(2)}) collective-permute-start(bf16[16,64,128]{2,1,0:T(8,128)(2,1)S(1)} %collective-permute-done.5), channel_id=1, source_target_pairs={{0,7},{1,0},{2,1},{3,2},{4,3},{5,4},{6,5},{7,6},{8,15},{9,8},{10,9... | collective-permute-start | bytes 786440 | tf_op jit(solution)/shard_map/ppermute | solution.py:38
  60.6 6.1 %collective-permute-start.8 = (bf16[8,64,128]{2,1,0:T(8,128)(2,1)S(1)}, bf16[8,64,128]{2,1,0:T(8,128)(2,1)S(1)}, u32[]{:S(2)}, u32[]{:S(2)}) collective-permute-start(bf16[8,64,128]{2,1,0:T(8,128)(2,1)S(1)} %slice.126), channel_id=1, source_target_pairs={{0,1},{1,2},{2,3},{3,4},{4,5},{5,6},{6,7},{7,0},{8,9},{9,10},{10,1... | collective-permute-start | bytes 393224 | tf_op jit(solution)/shard_map/ppermute | solution.py:38
  60.8 6.6 %collective-permute-start.9 = (bf16[8,64,128]{2,1,0:T(8,128)(2,1)S(1)}, bf16[8,64,128]{2,1,0:T(8,128)(2,1)S(1)}, u32[]{:S(2)}, u32[]{:S(2)}) collective-permute-start(bf16[8,64,128]{2,1,0:T(8,128)(2,1)S(1)} %slice.127), channel_id=1, source_target_pairs={{0,7},{1,0},{2,1},{3,2},{4,3},{5,4},{6,5},{7,6},{8,15},{9,8},{10,9... | collective-permute-start | bytes 393224 | tf_op jit(solution)/shard_map/ppermute | solution.py:38
  68.1 14.0 %collective-permute-start.10 = (bf16[2,4096,128]{2,1,0:T(8,128)(2,1)}, bf16[2,4096,128]{2,1,0:T(8,128)(2,1)}, u32[]{:S(2)}, u32[]{:S(2)}) collective-permute-start(bf16[2,4096,128]{2,1,0:T(8,128)(2,1)} %bitcast.34), channel_id=1, source_target_pairs={{0,64},{64,0},{1,65},{65,1},{2,66},{66,2},{3,67},{67,3},{4,68},{68... | collective-permute-start | bytes 6291464 | tf_op jit(solution)/shard_map/ppermute | solution.py:20
  74.5 2.8 %copy-start.3 = (bf16[1,512,4096]{2,1,0:T(8,128)(2,1)S(1)}, bf16[1,512,4096]{2,1,0:T(8,128)(2,1)}, u32[]{:S(2)}) copy-start(bf16[1,512,4096]{2,1,0:T(8,128)(2,1)} %param.6) | copy-start | bytes 12582916
  78.6 2.2 copy-start.4
  78.6 6.5 %collective-permute-start.11 = (bf16[2,4096,128]{2,1,0:T(8,128)(2,1)S(1)}, bf16[2,4096,128]{2,1,0:T(8,128)(2,1)S(1)}, u32[]{:S(2)}, u32[]{:S(2)}) collective-permute-start(bf16[2,4096,128]{2,1,0:T(8,128)(2,1)S(1)} %bitcast.148), channel_id=1, source_target_pairs={{0,64},{64,0},{1,65},{65,1},{2,66},{66,2},{3,67},{67,3},{4,68},{68... | collective-permute-start | bytes 6291464 | tf_op jit(solution)/shard_map/ppermute | solution.py:20
  88.9 4.2 %collective-permute-start.12 = (bf16[256,4096]{1,0:T(8,128)(2,1)S(1)}, bf16[256,4096]{1,0:T(8,128)(2,1)S(1)}, u32[]{:S(2)}, u32[]{:S(2)}) collective-permute-start(bf16[256,4096]{1,0:T(8,128)(2,1)S(1)} %convolution_convert_fusion.1), channel_id=1, source_target_pairs={{0,64},{64,0},{1,65},{65,1},{2,66},{66,2},{3,67},{67,3},{4,68},{68... | collective-permute-start | bytes 6291464 | tf_op jit(solution)/shard_map/ppermute | solution.py:20
  131.0 16.0 %copy-start.2 = (f32[64,512]{1,0:T(8,128)S(1)}, f32[64,512]{1,0:T(8,128)}, u32[]{:S(2)}) copy-start(f32[64,512]{1,0:T(8,128)} %param.11) | copy-start | bytes 393220
  184.9 5.2 %copy-start.5 = (bf16[1,512,4096]{2,1,0:T(8,128)(2,1)S(1)}, bf16[1,512,4096]{2,1,0:T(8,128)(2,1)}, u32[]{:S(2)}) copy-start(bf16[1,512,4096]{2,1,0:T(8,128)(2,1)} %param.6) | copy-start | bytes 12582916
  184.9 8.8 %collective-permute-start.13 = (bf16[2,4096,128]{2,1,0:T(8,128)(2,1)S(1)}, bf16[2,4096,128]{2,1,0:T(8,128)(2,1)S(1)}, u32[]{:S(2)}, u32[]{:S(2)}) collective-permute-start(bf16[2,4096,128]{2,1,0:T(8,128)(2,1)S(1)} %bitcast.149), channel_id=1, source_target_pairs={{0,64},{64,0},{1,65},{65,1},{2,66},{66,2},{3,67},{67,3},{4,68},{68... | collective-permute-start | bytes 6291464 | tf_op jit(solution)/shard_map/ppermute | solution.py:20
  197.3 4.2 %collective-permute-start.14 = (bf16[256,4096]{1,0:T(8,128)(2,1)S(1)}, bf16[256,4096]{1,0:T(8,128)(2,1)S(1)}, u32[]{:S(2)}, u32[]{:S(2)}) collective-permute-start(bf16[256,4096]{1,0:T(8,128)(2,1)S(1)} %convolution_convert_fusion), channel_id=1, source_target_pairs={{0,64},{64,0},{1,65},{65,1},{2,66},{66,2},{3,67},{67,3},{4,68},{68... | collective-permute-start | bytes 6291464 | tf_op jit(solution)/shard_map/ppermute | solution.py:20
  204.5 50.9 %copy-start.1 = (bf16[64,512]{1,0:T(8,128)(2,1)S(1)}, bf16[64,512]{1,0:T(8,128)(2,1)}, u32[]{:S(2)}) copy-start(bf16[64,512]{1,0:T(8,128)(2,1)} %param.9) | copy-start | bytes 196612

commit v6 on v5

--- a/solution.py
+++ b/solution.py
@@ -32,23 +32,33 @@
 def ring_gather(block):
     n = lax.axis_size("z")
     me = lax.axis_index("z")
-    whole = jnp.zeros((block.shape[0], n) + block.shape[1:], block.dtype)
+    wholes = [jnp.zeros((block.shape[1], n) + block.shape[2:], block.dtype) for _ in range(2)]
 
     def shift(value, step):
         return lax.ppermute(value, "z", [(i, (i + step) % n) for i in range(n)])
 
-    def put(whole, piece, owner, start=0):
-        return lax.dynamic_update_slice(whole, piece[:, None], (start, owner % n, 0, 0))
+    def put(index, piece, owner):
+        wholes[index] = lax.dynamic_update_slice(
+            wholes[index], piece[:, None], (0, owner % n, 0, 0)
+        )
 
-    whole = put(whole, block, me)
     before = after = block
+    for index in range(2):
+        put(index, block[index], me)
     for step in range(1, n // 2):
         before, after = shift(before, 1), shift(after, -1)
-        whole = put(whole, before, me + n - step)
-        whole = put(whole, after, me + step)
-    half = block.shape[0] // 2
-    whole = put(whole, shift(before[:half], 1), me + n // 2)
-    return put(whole, shift(after[half:], -1), me + n // 2, half)
+        for index in range(2):
+            put(index, before[index], me + n - step)
+            put(index, after[index], me + step)
+    put(0, shift(before[0], 1), me + n // 2)
+    put(1, shift(after[1], -1), me + n // 2)
+    return [whole.reshape(-1, block.shape[3]) for whole in wholes]
+
+
+def double_line(block, bit):
+    other = lax.ppermute(block, "z", [(i, i ^ bit) for i in range(lax.axis_size("z"))])
+    low = (lax.axis_index("z") & bit) == 0
+    return jnp.concatenate([jnp.where(low, block, other), jnp.where(low, other, block)], axis=0)
 
 
 def gather_plane(block):
@@ -110,11 +120,16 @@
     def own(array):
         return lax.dynamic_slice(array, (0, me * cols), (array.shape[0], cols))
 
-    def project(mine):
-        halves = [jnp.concatenate([pair[0], pair[1]], axis=1) for pair in (mine, core_swap(mine))]
+    def project(mine, others):
+        halves = [jnp.concatenate(pair, axis=1) for pair in (mine, others)]
         return jnp.concatenate(
             [jnp.dot(inputs, half, preferred_element_type=jnp.float32) for half in halves], axis=1
         )
+
+    def project_plane(block):
+        mine = gather_plane(block)
+        other = core_swap(mine)
+        return project([mine[0], mine[1]], [other[0], other[1]])
 
     gain = norm_gain.reshape(2, 2, cols)
     gain = jnp.concatenate(
@@ -123,12 +138,14 @@
     gain_square = gain * gain
     query = own(query_grad)
 
-    line = gather_line(own(value_weight))
-    block, line = lax.optimization_barrier((query.astype(jnp.bfloat16), line))
-    plane = spread(block, PLANE)
+    line = double_line(own(value_weight), 1)
+    line, ids, text_mask = lax.optimization_barrier((line, ids, text_mask))
+    line = double_line(double_line(line, 2), 4)
+    plane = spread(query.astype(jnp.bfloat16), PLANE)
     plane, line = lax.optimization_barrier((plane, line))
-    tangent = project(ring_gather(plane).reshape(lax.axis_size("ylo"), -1, cols))
-    values = project(gather_plane(line))
+    rows = ring_gather(plane.reshape((2, plane.shape[0] // 2) + plane.shape[1:]))
+    tangent = project(rows, [core_swap(half) for half in rows])
+    values = project_plane(line)
     own_count = turn_counts(text_mask, ids)
     turn_weight = text_mask / (jnp.maximum(own_count, 1.0) * jnp.float32(turn_total))
     root_mean = jnp.sqrt(jnp.mean(values * values, axis=-1, keepdims=True) + 1e-06)
@@ -136,7 +153,7 @@
     estimate = query
     for step in range(ITERS):
         if step:
-            tangent = project(gather_plane(gather_line(estimate.astype(jnp.bfloat16))))
+            tangent = project_plane(gather_line(estimate.astype(jnp.bfloat16)))
         inner = gain_square * norm_jacobian(tangent, unit_values, root_mean)
         adjoint = (turn_weight[:, None] * norm_jacobian(inner, unit_values, root_mean)).astype(
             jnp.bfloat16

time: 256 us -> 263 us (1.027)
  starting transfers between devices: 49.8 us -> 64.1 us
  waiting for transfers between devices: 24.7 us -> 20.6 us
  local copies, waits for them, and re-layouts: 24 us -> 20.4 us
  blocking collectives: 136 us -> 133 us
  matrix products: 12.8 us -> 15.7 us
    ppermute x0 -> x3, starting transfers between devices: none -> 11.3 us  [double_line(): lax.ppermute(block, 'z', [(i, i ^ bit) for i in range(lax.axis_size('z'))])]
    all_to_all x3 -> x2, waiting for transfers between devices: 7.84 us -> 1.38 us  [exchange(): return lax.all_to_all(blocks, axes, split_axis=0, concat_axis=0, tiled=True)]
    all_to_all x3 -> x2, starting transfers between devices: 22.4 us -> 16.6 us  [exchange(): return lax.all_to_all(blocks, axes, split_axis=0, concat_axis=0, tiled=True)]
    ppermute x5 -> x6, starting transfers between devices: 11.7 us -> 17.5 us  [core_swap(): return lax.ppermute(value, 'core', [(0, 1), (1, 0)])]
    all_to_all x7, blocking collectives: 136 us -> 133 us  [exchange(): return lax.all_to_all(blocks, axes, split_axis=0, concat_axis=0, tiled=True)]
    dot_general x6, matrix products: 7.75 us -> 10.6 us  [project(): jnp.dot(inputs, half, preferred_element_type=jnp.float32)]
    dynamic_update_slice x9 -> x10, local copies, waits for them, and re-layouts: 6.7 us -> 7.41 us  [put(): lax.dynamic_update_slice(wholes[index], piece[:, None], (0, owner % n, 0,...]
    ppermute x5 -> x6, waiting for transfers between devices: 10.2 us -> 9.88 us  [core_swap(): return lax.ppermute(value, 'core', [(0, 1), (1, 0)])]
  transfers between devices with their start and end apart: 18 -> 21, of which waited for: 8 -> 10; matrix products, arithmetic and copies ran while one was open for 9% -> 9% of each run, Pallas kernels for 0% -> 0%
where the time goes in v6:
time: 263 us
  blocking collectives  133 us (51%)
  starting transfers between devices  64.1 us (24%)
  waiting for transfers between devices  20.6 us (8%)
  local copies, waits for them, and re-layouts  20.4 us (8%)
  matrix products  15.7 us (6%)
  other arithmetic  8.4 us (3%)
    all_to_all x7, blocking collectives, exchange(): return lax.all_to_all(blocks, axes, split_axis=0, concat_axis=0, tiled=True)  133 us
    ppermute x6, starting transfers between devices, core_swap(): return lax.ppermute(value, 'core', [(0, 1), (1, 0)])  17.5 us
    all_to_all x2, starting transfers between devices, exchange(): return lax.all_to_all(blocks, axes, split_axis=0, concat_axis=0, tiled=True)  16.6 us
    ppermute x8, starting transfers between devices, shift(): return lax.ppermute(value, 'z', [(i, (i + step) % n) for i in range(n)])  13.4 us
    ppermute x3, starting transfers between devices, double_line(): lax.ppermute(block, 'z', [(i, i ^ bit) for i in range(lax.axis_size('z'))])  11.3 us
    dot_general x6, matrix products, project(): jnp.dot(inputs, half, preferred_element_type=jnp.float32)  10.6 us
    ppermute x6, waiting for transfers between devices, core_swap(): return lax.ppermute(value, 'core', [(0, 1), (1, 0)])  9.88 us
    dynamic_update_slice x10, local copies, waits for them, and re-layouts, put(): lax.dynamic_update_slice(wholes[index], piece[:, None], (0, owner % n, 0,...  7.41 us
  transfers between devices with their start and end apart: 21, of which 10 were waited for; matrix products, arithmetic and copies ran while one was open for 9% of the time, Pallas kernels for 0%

profile of v6, /device:TPU:1, one launch (start us, length us, event | category | flops | bytes accessed | tf_op | source)
XLA Modules:
  0.0 262.6 jit_solution(1361191631516157129)
XLA Ops:
  0.0 0.7 constant_dynamic-slice_fusion
  0.7 2.5 collective-permute-start
  3.2 0.8 dynamic-slice_convert_fusion
  3.9 0.7 broadcast_in_dim.83
  4.7 6.8 %all-to-all-start = ((bf16[16,64,128]{2,1,0:T(8,128)(2,1)}), bf16[16,64,128]{2,1,0:T(8,128)(2,1)S(1)}, u32[]{:S(2)}, u32[]{:S(2)}) async-start(bf16[16,64,128]{2,1,0:T(8,128)(2,1)} %broadcast_in_dim.83), calls=%async_computation | async-start | bytes 524288 | tf_op jit(solution)/shard_map/all_to_all | solution.py:24
  11.5 0.7 compare_convert_fusion
  12.2 0.8 fusion.101
  13.0 0.7 broadcast_select_fusion.5
  13.7 0.7 convert_element_type.51
  14.4 1.3 collective-permute-start.2
  15.8 4.0 %collective-permute-start.1 = (f32[2,512]{1,0:T(2,128)S(1)}, f32[2,512]{1,0:T(2,128)S(1)}, u32[]{:S(2)}, u32[]{:S(2)}) collective-permute-start(f32[2,512]{1,0:T(2,128)S(1)} %pad_maximum_fusion.7), channel_id=1, source_target_pairs={{0,1},{1,2},{2,3},{3,4},{4,5},{5,6},{6,7},{7,8},{8,9},{9,10},{10,1... | collective-permute-start | bytes 12296 | tf_op jit(solution)/shard_map/ppermute | solution.py:101
  19.8 3.1 %collective-permute-start.3 = (bf16[128,128]{1,0:T(8,128)(2,1)S(1)}, bf16[128,128]{1,0:T(8,128)(2,1)S(1)}, u32[]{:S(2)}, u32[]{:S(2)}) collective-permute-start(bf16[128,128]{1,0:T(8,128)(2,1)S(1)} %pad_maximum_fusion.6), channel_id=1, source_target_pairs={{0,2},{1,3},{2,0},{3,1},{4,6},{5,7},{6,4},{7,5},{8,10},{9,11},{10,... | collective-permute-start | bytes 98312 | tf_op jit(solution)/shard_map/ppermute | solution.py:59
  23.4 0.8 collective-permute-done.3
  24.2 5.8 %collective-permute-start.4 = (bf16[256,128]{1,0:T(8,128)(2,1)S(1)}, bf16[256,128]{1,0:T(8,128)(2,1)S(1)}, u32[]{:S(2)}, u32[]{:S(2)}) collective-permute-start(bf16[256,128]{1,0:T(8,128)(2,1)S(1)} %pad_maximum_fusion.5), channel_id=1, source_target_pairs={{0,4},{1,5},{2,6},{3,7},{4,0},{5,1},{6,2},{7,3},{8,12},{9,13},{10,... | collective-permute-start | bytes 196616 | tf_op jit(solution)/shard_map/ppermute | solution.py:59
  30.0 1.7 collective-permute-done.4
  31.8 5.9 %collective-permute-start.6 = (bf16[2,8,64,128]{3,2,1,0:T(8,128)(2,1)S(1)}, bf16[2,8,64,128]{3,2,1,0:T(8,128)(2,1)S(1)}, u32[]{:S(2)}, u32[]{:S(2)}) collective-permute-start(bf16[2,8,64,128]{3,2,1,0:T(8,128)(2,1)S(1)} %bitcast.203), channel_id=1, source_target_pairs={{0,7},{1,0},{2,1},{3,2},{4,3},{5,4},{6,5},{7,6},{8,15},{9,8},{10,9... | collective-permute-start | bytes 786440 | tf_op jit(solution)/shard_map/ppermute | solution.py:38
  37.7 1.7 broadcast_in_dim.86
  39.4 9.8 %all-to-all-start.1 = ((bf16[16,512,128]{2,1,0:T(8,128)(2,1)}), bf16[16,512,128]{2,1,0:T(8,128)(2,1)S(1)}, u32[]{:S(2)}, u32[]{:S(2)}) async-start(bf16[16,512,128]{2,1,0:T(8,128)(2,1)} %broadcast_in_dim.86), calls=%async_computation.1 | async-start | bytes 4194304 | tf_op jit(solution)/shard_map/all_to_all | solution.py:24
  49.2 1.2 broadcast.67.clone
  50.5 0.7 bitcast_dynamic-update-slice_fusion.3
  51.1 1.2 broadcast.67.clone.1
  52.4 0.7 bitcast_dynamic-update-slice_fusion.5
  53.1 1.3 collective-permute-start.8
  54.6 0.8 fusion.88
  55.3 0.8 fusion.87
  56.1 2.2 collective-permute-done.8
  58.3 2.5 collective-permute-start.10
  61.1 0.8 fusion.86
  61.9 0.8 fusion.85
  62.7 4.0 %collective-permute-done.10 = bf16[2,8,64,128]{3,2,1,0:T(8,128)(2,1)S(1)} collective-permute-done((bf16[2,8,64,128]{3,2,1,0:T(8,128)(2,1)S(1)}, bf16[2,8,64,128]{3,2,1,0:T(8,128)(2,1)S(1)}, u32[]{:S(2)}, u32[]{:S(2)}) %collective-permute-start.10) | collective-permute-done | bytes 262176 | tf_op jit(solution)/shard_map/ppermute | solution.py:38
  66.7 3.5 %collective-permute-start.12 = (bf16[8,64,128]{2,1,0:T(8,128)(2,1)S(1)}, bf16[8,64,128]{2,1,0:T(8,128)(2,1)S(1)}, u32[]{:S(2)}, u32[]{:S(2)}) collective-permute-start(bf16[8,64,128]{2,1,0:T(8,128)(2,1)S(1)} %slice_bitcast_fusion.14), channel_id=1, source_target_pairs={{0,7},{1,0},{2,1},{3,2},{4,3},{5,4},{6,5},{7,6},{8,15},{9,8},{10,9... | collective-permute-start | bytes 393224 | tf_op jit(solution)/shard_map/ppermute | solution.py:38
  70.5 0.8 bitcast_dynamic-update-slice_fusion.2
  71.3 0.8 fusion.84
  72.1 1.4 all-to-all-done.1
  73.4 7.5 %collective-permute-start.15 = (bf16[2,4096,128]{2,1,0:T(8,128)(2,1)S(1)}, bf16[2,4096,128]{2,1,0:T(8,128)(2,1)S(1)}, u32[]{:S(2)}, u32[]{:S(2)}) collective-permute-start(bf16[2,4096,128]{2,1,0:T(8,128)(2,1)S(1)} %bitcast.195), channel_id=1, source_target_pairs={{0,64},{64,0},{1,65},{65,1},{2,66},{66,2},{3,67},{67,3},{4,68},{68... | collective-permute-start | bytes 6291464 | tf_op jit(solution)/shard_map/ppermute | solution.py:20
  81.7 4.4 %collective-permute-start.13 = (bf16[4096,128]{1,0:T(8,128)(2,1)}, bf16[4096,128]{1,0:T(8,128)(2,1)S(1)}, u32[]{:S(2)}, u32[]{:S(2)}) collective-permute-start(bf16[4096,128]{1,0:T(8,128)(2,1)} %bitcast.32), channel_id=1, source_target_pairs={{0,64},{64,0},{1,65},{65,1},{2,66},{66,2},{3,67},{67,3},{4,68},{68... | collective-permute-start | bytes 3145736 | tf_op jit(solution)/shard_map/ppermute | solution.py:20
  86.0 0.7 bitcast_dynamic-update-slice_fusion.4
  86.8 4.1 %fusion.36 = f32[512,256]{0,1:T(8,128)S(1)} fusion(bf16[1,512,4096]{2,1,0:T(8,128)(2,1)} %param.6, bf16[4096,128]{1,0:T(8,128)(2,1)} %bitcast.48, bf16[4096,128]{1,0:T(8,128)(2,1)} %bitcast.32), kind=kOutput, calls=%fused_computation.40 | convolution fusion | flops 1077936128 | bytes 6815744 | tf_op jit(solution)/shard_map/dot_general | solution.py:126
  91.0 2.0 copy-done.1
  93.1 1.3 fusion.46
  94.4 1.3 fusion.41
  95.9 1.3 fusion.51
  98.3 1.3 convolution_convert_fusion.1
  100.2 3.8 %collective-permute-done.16 = bf16[256,4096]{1,0:T(8,128)(2,1)S(1)} collective-permute-done((bf16[256,4096]{1,0:T(8,128)(2,1)S(1)}, bf16[256,4096]{1,0:T(8,128)(2,1)S(1)}, u32[]{:S(2)}, u32[]{:S(2)}) %collective-permute-start.16) | collective-permute-done | bytes 2097184 | tf_op jit(solution)/shard_map/ppermute | solution.py:20
  103.9 1.3 add_convert_fusion.1
  105.2 0.9 copy.89
  106.1 0.7 copy.84
  106.9 34.9 %all_to_all.50 = bf16[16,128,512]{2,1,0:T(8,128)(2,1)} all-to-all(bf16[16,128,512]{2,1,0:T(8,128)(2,1)S(1)} %bitcast.198), channel_id=1, replica_groups=mesh['ylo'=2,'core'=2,'yhi'=2,'x'=4,'z'=8] {'ylo','yhi','x'}, dimensions={0} | all-to-all | bytes 4194304 | tf_op jit(solution)/shard_map/all_to_all | solution.py:24
  141.7 1.9 reduce_sum.120
  143.8 10.4 %all_to_all.45 = bf16[8,64,128]{2,1,0:T(8,128)(2,1)S(1)} all-to-all(bf16[8,64,128]{2,1,0:T(8,128)(2,1)S(1)} %bitcast.210), channel_id=1, replica_groups=mesh['ylo'=2,'core'=2,'yhi'=2,'x'=4,'z'=8] {'z'}, dimensions={0} | all-to-all | bytes 262144 | tf_op jit(solution)/shard_map/all_to_all | solution.py:24
  154.3 10.3 %all_to_all.46 = bf16[8,64,128]{2,1,0:T(8,128)(2,1)S(1)} all-to-all(bf16[8,64,128]{2,1,0:T(8,128)(2,1)S(1)} %broadcast_in_dim.87), channel_id=1, replica_groups=mesh['ylo'=2,'core'=2,'yhi'=2,'x'=4,'z'=8] {'z'}, dimensions={0} | all-to-all | bytes 262144 | tf_op jit(solution)/shard_map/all_to_all | solution.py:24
  165.0 27.8 %all_to_all.47 = bf16[16,512,128]{2,1,0:T(8,128)(2,1)S(1)} all-to-all(bf16[16,512,128]{2,1,0:T(8,128)(2,1)S(1)} %broadcast_in_dim.89), channel_id=1, replica_groups=mesh['ylo'=2,'core'=2,'yhi'=2,'x'=4,'z'=8] {'ylo','yhi','x'}, dimensions={0} | all-to-all | bytes 4194304 | tf_op jit(solution)/shard_map/all_to_all | solution.py:24
  192.7 4.5 %collective-permute-start.17 = (bf16[2,4096,128]{2,1,0:T(8,128)(2,1)S(1)}, bf16[2,4096,128]{2,1,0:T(8,128)(2,1)S(1)}, u32[]{:S(2)}, u32[]{:S(2)}) collective-permute-start(bf16[2,4096,128]{2,1,0:T(8,128)(2,1)S(1)} %bitcast.196), channel_id=1, source_target_pairs={{0,64},{64,0},{1,65},{65,1},{2,66},{66,2},{3,67},{67,3},{4,68},{68... | collective-permute-start | bytes 6291464 | tf_op jit(solution)/shard_map/ppermute | solution.py:20
  197.4 1.3 fusion.56
  198.8 2.3 collective-permute-done.17
  201.2 1.3 fusion.61
  203.4 1.3 convolution_convert_fusion
  205.2 3.8 %collective-permute-done.18 = bf16[256,4096]{1,0:T(8,128)(2,1)S(1)} collective-permute-done((bf16[256,4096]{1,0:T(8,128)(2,1)S(1)}, bf16[256,4096]{1,0:T(8,128)(2,1)S(1)}, u32[]{:S(2)}, u32[]{:S(2)}) %collective-permute-start.18) | collective-permute-done | bytes 2097184 | tf_op jit(solution)/shard_map/ppermute | solution.py:20
  209.0 1.3 add_convert_fusion
  210.2 0.9 copy.90
  211.1 0.7 copy.86
  211.9 30.7 %all_to_all.51 = bf16[16,128,512]{2,1,0:T(8,128)(2,1)S(1)} all-to-all(bf16[16,128,512]{2,1,0:T(8,128)(2,1)S(1)} %bitcast.200), channel_id=1, replica_groups=mesh['ylo'=2,'core'=2,'yhi'=2,'x'=4,'z'=8] {'ylo','yhi','x'}, dimensions={0} | all-to-all | bytes 4194304 | tf_op jit(solution)/shard_map/all_to_all | solution.py:24
  242.9 10.4 %all_to_all.48 = bf16[8,64,128]{2,1,0:T(8,128)(2,1)S(1)} all-to-all(bf16[8,64,128]{2,1,0:T(8,128)(2,1)S(1)} %bitcast.211), channel_id=1, replica_groups=mesh['ylo'=2,'core'=2,'yhi'=2,'x'=4,'z'=8] {'z'}, dimensions={0} | all-to-all | bytes 262144 | tf_op jit(solution)/shard_map/all_to_all | solution.py:24
  253.4 8.5 %all_to_all.49 = f32[4,64,128]{2,1,0:T(8,128)S(1)} all-to-all(f32[4,64,128]{2,1,0:T(8,128)S(1)} %broadcast_in_dim.90), channel_id=1, replica_groups=mesh['ylo'=2,'core'=2,'yhi'=2,'x'=4,'z'=8] {'ylo','core'}, dimensions={0} | all-to-all | bytes 262144 | tf_op jit(solution)/shard_map/all_to_all | solution.py:24
  (68 shorter events, 7.4 us)
Async XLA Ops:
  0.7 12.2 %collective-permute-start = (bf16[64,128]{1,0:T(8,128)(2,1)S(1)}, bf16[64,128]{1,0:T(8,128)(2,1)S(1)}, u32[]{:S(2)}, u32[]{:S(2)}) collective-permute-start(bf16[64,128]{1,0:T(8,128)(2,1)S(1)} %constant_dynamic-slice_fusion), channel_id=1, source_target_pairs={{0,1},{1,0},{2,3},{3,2},{4,5},{5,4},{6,7},{7,6},{8,9},{9,8},{10,11... | collective-permute-start | bytes 49160 | tf_op jit(solution)/shard_map/ppermute | solution.py:59
  4.7 27.1 %all-to-all-start = ((bf16[16,64,128]{2,1,0:T(8,128)(2,1)}), bf16[16,64,128]{2,1,0:T(8,128)(2,1)S(1)}, u32[]{:S(2)}, u32[]{:S(2)}) async-start(bf16[16,64,128]{2,1,0:T(8,128)(2,1)} %broadcast_in_dim.83), calls=%async_computation | async-start | bytes 524288 | tf_op jit(solution)/shard_map/all_to_all | solution.py:24
  14.4 8.5 %collective-permute-start.2 = (f32[2,512]{1,0:T(2,128)S(1)}, f32[2,512]{1,0:T(2,128)S(1)}, u32[]{:S(2)}, u32[]{:S(2)}) collective-permute-start(f32[2,512]{1,0:T(2,128)S(1)} %pad_maximum_fusion.7), channel_id=1, source_target_pairs={{1,0},{2,1},{3,2},{4,3},{5,4},{6,5},{7,6},{8,7},{9,8},{10,9},{11,1... | collective-permute-start | bytes 12296 | tf_op jit(solution)/shard_map/ppermute | solution.py:102
  15.8 7.1 %collective-permute-start.1 = (f32[2,512]{1,0:T(2,128)S(1)}, f32[2,512]{1,0:T(2,128)S(1)}, u32[]{:S(2)}, u32[]{:S(2)}) collective-permute-start(f32[2,512]{1,0:T(2,128)S(1)} %pad_maximum_fusion.7), channel_id=1, source_target_pairs={{0,1},{1,2},{2,3},{3,4},{4,5},{5,6},{6,7},{7,8},{8,9},{9,10},{10,1... | collective-permute-start | bytes 12296 | tf_op jit(solution)/shard_map/ppermute | solution.py:101
  19.8 4.4 %collective-permute-start.3 = (bf16[128,128]{1,0:T(8,128)(2,1)S(1)}, bf16[128,128]{1,0:T(8,128)(2,1)S(1)}, u32[]{:S(2)}, u32[]{:S(2)}) collective-permute-start(bf16[128,128]{1,0:T(8,128)(2,1)S(1)} %pad_maximum_fusion.6), channel_id=1, source_target_pairs={{0,2},{1,3},{2,0},{3,1},{4,6},{5,7},{6,4},{7,5},{8,10},{9,11},{10,... | collective-permute-start | bytes 98312 | tf_op jit(solution)/shard_map/ppermute | solution.py:59
  24.2 7.5 %collective-permute-start.4 = (bf16[256,128]{1,0:T(8,128)(2,1)S(1)}, bf16[256,128]{1,0:T(8,128)(2,1)S(1)}, u32[]{:S(2)}, u32[]{:S(2)}) collective-permute-start(bf16[256,128]{1,0:T(8,128)(2,1)S(1)} %pad_maximum_fusion.5), channel_id=1, source_target_pairs={{0,4},{1,5},{2,6},{3,7},{4,0},{5,1},{6,2},{7,3},{8,12},{9,13},{10,... | collective-permute-start | bytes 196616 | tf_op jit(solution)/shard_map/ppermute | solution.py:59
  31.8 21.3 %collective-permute-start.6 = (bf16[2,8,64,128]{3,2,1,0:T(8,128)(2,1)S(1)}, bf16[2,8,64,128]{3,2,1,0:T(8,128)(2,1)S(1)}, u32[]{:S(2)}, u32[]{:S(2)}) collective-permute-start(bf16[2,8,64,128]{3,2,1,0:T(8,128)(2,1)S(1)} %bitcast.203), channel_id=1, source_target_pairs={{0,7},{1,0},{2,1},{3,2},{4,3},{5,4},{6,5},{7,6},{8,15},{9,8},{10,9... | collective-permute-start | bytes 786440 | tf_op jit(solution)/shard_map/ppermute | solution.py:38
  37.7 16.7 %collective-permute-start.5 = (bf16[2,8,64,128]{3,2,1,0:T(8,128)(2,1)S(1)}, bf16[2,8,64,128]{3,2,1,0:T(8,128)(2,1)S(1)}, u32[]{:S(2)}, u32[]{:S(2)}) collective-permute-start(bf16[2,8,64,128]{3,2,1,0:T(8,128)(2,1)S(1)} %bitcast.204), channel_id=1, source_target_pairs={{0,1},{1,2},{2,3},{3,4},{4,5},{5,6},{6,7},{7,0},{8,9},{9,10},{10,1... | collective-permute-start | bytes 786440 | tf_op jit(solution)/shard_map/ppermute | solution.py:38
  39.4 34.0 %all-to-all-start.1 = ((bf16[16,512,128]{2,1,0:T(8,128)(2,1)}), bf16[16,512,128]{2,1,0:T(8,128)(2,1)S(1)}, u32[]{:S(2)}, u32[]{:S(2)}) async-start(bf16[16,512,128]{2,1,0:T(8,128)(2,1)} %broadcast_in_dim.86), calls=%async_computation.1 | async-start | bytes 4194304 | tf_op jit(solution)/shard_map/all_to_all | solution.py:24
  53.1 5.2 %collective-permute-start.8 = (bf16[2,8,64,128]{3,2,1,0:T(8,128)(2,1)S(1)}, bf16[2,8,64,128]{3,2,1,0:T(8,128)(2,1)S(1)}, u32[]{:S(2)}, u32[]{:S(2)}) collective-permute-start(bf16[2,8,64,128]{3,2,1,0:T(8,128)(2,1)S(1)} %collective-permute-done.6), channel_id=1, source_target_pairs={{0,7},{1,0},{2,1},{3,2},{4,3},{5,4},{6,5},{7,6},{8,15},{9,8},{10,9... | collective-permute-start | bytes 786440 | tf_op jit(solution)/shard_map/ppermute | solution.py:38
  54.4 6.7 %collective-permute-start.7 = (bf16[2,8,64,128]{3,2,1,0:T(8,128)(2,1)S(1)}, bf16[2,8,64,128]{3,2,1,0:T(8,128)(2,1)S(1)}, u32[]{:S(2)}, u32[]{:S(2)}) collective-permute-start(bf16[2,8,64,128]{3,2,1,0:T(8,128)(2,1)S(1)} %collective-permute-done.5), channel_id=1, source_target_pairs={{0,1},{1,2},{2,3},{3,4},{4,5},{5,6},{6,7},{7,0},{8,9},{9,10},{10,1... | collective-permute-start | bytes 786440 | tf_op jit(solution)/shard_map/ppermute | solution.py:38
  58.3 8.4 %collective-permute-start.10 = (bf16[2,8,64,128]{3,2,1,0:T(8,128)(2,1)S(1)}, bf16[2,8,64,128]{3,2,1,0:T(8,128)(2,1)S(1)}, u32[]{:S(2)}, u32[]{:S(2)}) collective-permute-start(bf16[2,8,64,128]{3,2,1,0:T(8,128)(2,1)S(1)} %collective-permute-done.8), channel_id=1, source_target_pairs={{0,7},{1,0},{2,1},{3,2},{4,3},{5,4},{6,5},{7,6},{8,15},{9,8},{10,9... | collective-permute-start | bytes 786440 | tf_op jit(solution)/shard_map/ppermute | solution.py:38
  61.1 9.3 %collective-permute-start.9 = (bf16[2,8,64,128]{3,2,1,0:T(8,128)(2,1)S(1)}, bf16[2,8,64,128]{3,2,1,0:T(8,128)(2,1)S(1)}, u32[]{:S(2)}, u32[]{:S(2)}) collective-permute-start(bf16[2,8,64,128]{3,2,1,0:T(8,128)(2,1)S(1)} %collective-permute-done.7), channel_id=1, source_target_pairs={{0,1},{1,2},{2,3},{3,4},{4,5},{5,6},{6,7},{7,0},{8,9},{9,10},{10,1... | collective-permute-start | bytes 786440 | tf_op jit(solution)/shard_map/ppermute | solution.py:38
  66.7 19.3 %collective-permute-start.12 = (bf16[8,64,128]{2,1,0:T(8,128)(2,1)S(1)}, bf16[8,64,128]{2,1,0:T(8,128)(2,1)S(1)}, u32[]{:S(2)}, u32[]{:S(2)}) collective-permute-start(bf16[8,64,128]{2,1,0:T(8,128)(2,1)S(1)} %slice_bitcast_fusion.14), channel_id=1, source_target_pairs={{0,7},{1,0},{2,1},{3,2},{4,3},{5,4},{6,5},{7,6},{8,15},{9,8},{10,9... | collective-permute-start | bytes 393224 | tf_op jit(solution)/shard_map/ppermute | solution.py:38
  70.4 10.6 %collective-permute-start.11 = (bf16[8,64,128]{2,1,0:T(8,128)(2,1)S(1)}, bf16[8,64,128]{2,1,0:T(8,128)(2,1)S(1)}, u32[]{:S(2)}, u32[]{:S(2)}) collective-permute-start(bf16[8,64,128]{2,1,0:T(8,128)(2,1)S(1)} %slice_bitcast_fusion.15), channel_id=1, source_target_pairs={{0,1},{1,2},{2,3},{3,4},{4,5},{5,6},{6,7},{7,0},{8,9},{9,10},{10,1... | collective-permute-start | bytes 393224 | tf_op jit(solution)/shard_map/ppermute | solution.py:38
  73.4 22.3 %collective-permute-start.15 = (bf16[2,4096,128]{2,1,0:T(8,128)(2,1)S(1)}, bf16[2,4096,128]{2,1,0:T(8,128)(2,1)S(1)}, u32[]{:S(2)}, u32[]{:S(2)}) collective-permute-start(bf16[2,4096,128]{2,1,0:T(8,128)(2,1)S(1)} %bitcast.195), channel_id=1, source_target_pairs={{0,64},{64,0},{1,65},{65,1},{2,66},{66,2},{3,67},{67,3},{4,68},{68... | collective-permute-start | bytes 6291464 | tf_op jit(solution)/shard_map/ppermute | solution.py:20
  81.7 12.7 %collective-permute-start.13 = (bf16[4096,128]{1,0:T(8,128)(2,1)}, bf16[4096,128]{1,0:T(8,128)(2,1)S(1)}, u32[]{:S(2)}, u32[]{:S(2)}) collective-permute-start(bf16[4096,128]{1,0:T(8,128)(2,1)} %bitcast.32), channel_id=1, source_target_pairs={{0,64},{64,0},{1,65},{65,1},{2,66},{66,2},{3,67},{67,3},{4,68},{68... | collective-permute-start | bytes 3145736 | tf_op jit(solution)/shard_map/ppermute | solution.py:20
  86.7 7.6 %collective-permute-start.14 = (bf16[4096,128]{1,0:T(8,128)(2,1)}, bf16[4096,128]{1,0:T(8,128)(2,1)S(1)}, u32[]{:S(2)}, u32[]{:S(2)}) collective-permute-start(bf16[4096,128]{1,0:T(8,128)(2,1)} %bitcast.48), channel_id=1, source_target_pairs={{0,64},{64,0},{1,65},{65,1},{2,66},{66,2},{3,67},{67,3},{4,68},{68... | collective-permute-start | bytes 3145736 | tf_op jit(solution)/shard_map/ppermute | solution.py:20
  90.9 2.2 copy-start.1
  99.6 4.4 %collective-permute-start.16 = (bf16[256,4096]{1,0:T(8,128)(2,1)S(1)}, bf16[256,4096]{1,0:T(8,128)(2,1)S(1)}, u32[]{:S(2)}, u32[]{:S(2)}) collective-permute-start(bf16[256,4096]{1,0:T(8,128)(2,1)S(1)} %convolution_convert_fusion.1), channel_id=1, source_target_pairs={{0,64},{64,0},{1,65},{65,1},{2,66},{66,2},{3,67},{67,3},{4,68},{68... | collective-permute-start | bytes 6291464 | tf_op jit(solution)/shard_map/ppermute | solution.py:20
  106.9 47.3 %copy-start = (f32[64,512]{1,0:T(8,128)S(1)}, f32[64,512]{1,0:T(8,128)}, u32[]{:S(2)}) copy-start(f32[64,512]{1,0:T(8,128)} %param.11) | copy-start | bytes 393220
  165.0 32.4 %copy-start.2 = (bf16[1,512,4096]{2,1,0:T(8,128)(2,1)S(1)}, bf16[1,512,4096]{2,1,0:T(8,128)(2,1)}, u32[]{:S(2)}) copy-start(bf16[1,512,4096]{2,1,0:T(8,128)(2,1)} %param.6) | copy-start | bytes 12582916
  192.7 8.3 %collective-permute-start.17 = (bf16[2,4096,128]{2,1,0:T(8,128)(2,1)S(1)}, bf16[2,4096,128]{2,1,0:T(8,128)(2,1)S(1)}, u32[]{:S(2)}, u32[]{:S(2)}) collective-permute-start(bf16[2,4096,128]{2,1,0:T(8,128)(2,1)S(1)} %bitcast.196), channel_id=1, source_target_pairs={{0,64},{64,0},{1,65},{65,1},{2,66},{66,2},{3,67},{67,3},{4,68},{68... | collective-permute-start | bytes 6291464 | tf_op jit(solution)/shard_map/ppermute | solution.py:20
  204.7 4.2 %collective-permute-start.18 = (bf16[256,4096]{1,0:T(8,128)(2,1)S(1)}, bf16[256,4096]{1,0:T(8,128)(2,1)S(1)}, u32[]{:S(2)}, u32[]{:S(2)}) collective-permute-start(bf16[256,4096]{1,0:T(8,128)(2,1)S(1)} %convolution_convert_fusion), channel_id=1, source_target_pairs={{0,64},{64,0},{1,65},{65,1},{2,66},{66,2},{3,67},{67,3},{4,68},{68... | collective-permute-start | bytes 6291464 | tf_op jit(solution)/shard_map/ppermute | solution.py:20

commit v7 on v6

--- a/solution.py
+++ b/solution.py
@@ -53,12 +53,6 @@
     put(0, shift(before[0], 1), me + n // 2)
     put(1, shift(after[1], -1), me + n // 2)
     return [whole.reshape(-1, block.shape[3]) for whole in wholes]
-
-
-def double_line(block, bit):
-    other = lax.ppermute(block, "z", [(i, i ^ bit) for i in range(lax.axis_size("z"))])
-    low = (lax.axis_index("z") & bit) == 0
-    return jnp.concatenate([jnp.where(low, block, other), jnp.where(low, other, block)], axis=0)
 
 
 def gather_plane(block):
@@ -138,10 +132,9 @@
     gain_square = gain * gain
     query = own(query_grad)
 
-    line = double_line(own(value_weight), 1)
-    line, ids, text_mask = lax.optimization_barrier((line, ids, text_mask))
-    line = double_line(double_line(line, 2), 4)
-    plane = spread(query.astype(jnp.bfloat16), PLANE)
+    line = gather_line(own(value_weight))
+    block, line = lax.optimization_barrier((query.astype(jnp.bfloat16), line))
+    plane = spread(block, PLANE)
     plane, line = lax.optimization_barrier((plane, line))
     rows = ring_gather(plane.reshape((2, plane.shape[0] // 2) + plane.shape[1:]))
     tangent = project(rows, [core_swap(half) for half in rows])

time: 263 us -> 261 us (level)
  starting transfers between devices: 64.1 us -> 51 us
  waiting for transfers between devices: 20.6 us -> 33 us
    all_to_all x2 -> x3, waiting for transfers between devices: 1.38 us -> 16.5 us  [exchange(): return lax.all_to_all(blocks, axes, split_axis=0, concat_axis=0, tiled=True)]
    ppermute x3 -> x0, starting transfers between devices: 11.3 us -> none  [double_line(): lax.ppermute(block, 'z', [(i, i ^ bit) for i in range(lax.axis_size('z'))])]
    ppermute x8, starting transfers between devices: 13.4 us -> 8.05 us  [shift(): return lax.ppermute(value, 'z', [(i, (i + step) % n) for i in range(n)])]
    all_to_all x2 -> x3, starting transfers between devices: 16.6 us -> 21 us  [exchange(): return lax.all_to_all(blocks, axes, split_axis=0, concat_axis=0, tiled=True)]
  transfers between devices with their start and end apart: 21 -> 19, of which waited for: 10 -> 9; matrix products, arithmetic and copies ran while one was open for 9% -> 9% of each run, Pallas kernels for 0% -> 0%
where the time goes in v7:
time: 261 us; the launch traced here: 260 us
  blocking collectives  134 us (51%)
  starting transfers between devices  51 us (20%)
  waiting for transfers between devices  33 us (13%)
  local copies, waits for them, and re-layouts  20.4 us (8%)
  matrix products  15.8 us (6%)
  other arithmetic  6.06 us (2%)
    all_to_all x7, blocking collectives, exchange(): return lax.all_to_all(blocks, axes, split_axis=0, concat_axis=0, tiled=True)  134 us
    all_to_all x3, starting transfers between devices, exchange(): return lax.all_to_all(blocks, axes, split_axis=0, concat_axis=0, tiled=True)  21 us
    all_to_all x3, waiting for transfers between devices, exchange(): return lax.all_to_all(blocks, axes, split_axis=0, concat_axis=0, tiled=True)  16.5 us
    ppermute x6, starting transfers between devices, core_swap(): return lax.ppermute(value, 'core', [(0, 1), (1, 0)])  15.6 us
    dot_general x6, matrix products, project(): jnp.dot(inputs, half, preferred_element_type=jnp.float32)  10.6 us
    ppermute x6, waiting for transfers between devices, core_swap(): return lax.ppermute(value, 'core', [(0, 1), (1, 0)])  9.86 us
    ppermute x8, starting transfers between devices, shift(): return lax.ppermute(value, 'z', [(i, (i + step) % n) for i in range(n)])  8.05 us
    dynamic_update_slice x10, local copies, waits for them, and re-layouts, put(): lax.dynamic_update_slice(wholes[index], piece[:, None], (0, owner % n, 0,...  7.39 us
  transfers between devices with their start and end apart: 19, of which 9 were waited for; matrix products, arithmetic and copies ran while one was open for 9% of the time, Pallas kernels for 0%

profile of v7, /device:TPU:1, one launch (start us, length us, event | category | flops | bytes accessed | tf_op | source)
XLA Modules:
  0.0 260.3 jit_solution(16032426132297171174)
XLA Ops:
  0.0 0.7 compare_convert_fusion
  0.7 0.7 convert_element_type.66
  1.4 1.3 collective-permute-start.1
  2.7 5.0 %collective-permute-start = (f32[2,512]{1,0:T(2,128)S(1)}, f32[2,512]{1,0:T(2,128)S(1)}, u32[]{:S(2)}, u32[]{:S(2)}) collective-permute-start(f32[2,512]{1,0:T(2,128)S(1)} %pad_maximum_fusion.4), channel_id=1, source_target_pairs={{0,1},{1,2},{2,3},{3,4},{4,5},{5,6},{6,7},{7,8},{8,9},{9,10},{10,1... | collective-permute-start | bytes 12296 | tf_op jit(solution)/shard_map/ppermute | solution.py:95
  7.8 0.7 broadcast_in_dim.92
  8.4 8.8 %all-to-all-start = ((bf16[8,64,128]{2,1,0:T(8,128)(2,1)}), bf16[8,64,128]{2,1,0:T(8,128)(2,1)S(1)}, u32[]{:S(2)}, u32[]{:S(2)}) async-start(bf16[8,64,128]{2,1,0:T(8,128)(2,1)} %broadcast_in_dim.92), calls=%async_computation | async-start | bytes 262144 | tf_op jit(solution)/shard_map/all_to_all | solution.py:24
  17.2 0.8 dynamic-slice_convert_fusion
  18.0 0.8 fusion.101
  18.9 6.3 %all-to-all-done = bf16[8,64,128]{2,1,0:T(8,128)(2,1)S(1)} async-done(((bf16[8,64,128]{2,1,0:T(8,128)(2,1)}), bf16[8,64,128]{2,1,0:T(8,128)(2,1)S(1)}, u32[]{:S(2)}, u32[]{:S(2)}) %all-to-all-start) | async-done | bytes 131104 | tf_op jit(solution)/shard_map/all_to_all | solution.py:24
  25.2 0.8 broadcast_in_dim.93
  25.9 8.5 %all-to-all-start.1 = ((bf16[16,64,128]{2,1,0:T(8,128)(2,1)}), bf16[16,64,128]{2,1,0:T(8,128)(2,1)S(1)}, u32[]{:S(2)}, u32[]{:S(2)}) async-start(bf16[16,64,128]{2,1,0:T(8,128)(2,1)} %broadcast_in_dim.93), calls=%async_computation.1 | async-start | bytes 524288 | tf_op jit(solution)/shard_map/all_to_all | solution.py:24
  34.9 7.1 %all-to-all-done.1 = bf16[16,64,128]{2,1,0:T(8,128)(2,1)S(1)} async-done(((bf16[16,64,128]{2,1,0:T(8,128)(2,1)}), bf16[16,64,128]{2,1,0:T(8,128)(2,1)S(1)}, u32[]{:S(2)}, u32[]{:S(2)}) %all-to-all-start.1) | async-done | bytes 262176 | tf_op jit(solution)/shard_map/all_to_all | solution.py:24
  42.0 1.5 collective-permute-start.2
  43.4 1.8 broadcast_in_dim.96
  45.2 3.7 %all-to-all-start.2 = ((bf16[16,512,128]{2,1,0:T(8,128)(2,1)}), bf16[16,512,128]{2,1,0:T(8,128)(2,1)S(1)}, u32[]{:S(2)}, u32[]{:S(2)}) async-start(bf16[16,512,128]{2,1,0:T(8,128)(2,1)} %broadcast_in_dim.96), calls=%async_computation.2 | async-start | bytes 4194304 | tf_op jit(solution)/shard_map/all_to_all | solution.py:24
  48.9 1.3 broadcast.77.clone
  50.2 0.7 bitcast_dynamic-update-slice_fusion.3
  50.9 1.2 broadcast.77.clone.1
  52.1 0.7 bitcast_dynamic-update-slice_fusion.5
  52.8 1.2 collective-permute-start.5
  54.3 0.8 fusion.88
  55.0 0.8 fusion.87
  55.8 2.5 collective-permute-done.5
  58.3 2.4 collective-permute-start.7
  60.7 0.8 fusion.86
  61.5 0.8 fusion.85
  62.3 3.9 %collective-permute-done.7 = bf16[2,8,64,128]{3,2,1,0:T(8,128)(2,1)S(1)} collective-permute-done((bf16[2,8,64,128]{3,2,1,0:T(8,128)(2,1)S(1)}, bf16[2,8,64,128]{3,2,1,0:T(8,128)(2,1)S(1)}, u32[]{:S(2)}, u32[]{:S(2)}) %collective-permute-start.7) | collective-permute-done | bytes 262176 | tf_op jit(solution)/shard_map/ppermute | solution.py:38
  66.2 2.6 %collective-permute-start.9 = (bf16[8,64,128]{2,1,0:T(8,128)(2,1)S(1)}, bf16[8,64,128]{2,1,0:T(8,128)(2,1)S(1)}, u32[]{:S(2)}, u32[]{:S(2)}) collective-permute-start(bf16[8,64,128]{2,1,0:T(8,128)(2,1)S(1)} %slice_bitcast_fusion.14), channel_id=1, source_target_pairs={{0,7},{1,0},{2,1},{3,2},{4,3},{5,4},{6,5},{7,6},{8,15},{9,8},{10,9... | collective-permute-start | bytes 393224 | tf_op jit(solution)/shard_map/ppermute | solution.py:38
  69.1 0.8 bitcast_dynamic-update-slice_fusion.2
  69.9 0.8 fusion.84
  70.7 3.2 %all-to-all-done.2 = bf16[16,512,128]{2,1,0:T(8,128)(2,1)S(1)} async-done(((bf16[16,512,128]{2,1,0:T(8,128)(2,1)}), bf16[16,512,128]{2,1,0:T(8,128)(2,1)S(1)}, u32[]{:S(2)}, u32[]{:S(2)}) %all-to-all-start.2) | async-done | bytes 2097184 | tf_op jit(solution)/shard_map/all_to_all | solution.py:24
  73.8 6.8 %collective-permute-start.12 = (bf16[2,4096,128]{2,1,0:T(8,128)(2,1)S(1)}, bf16[2,4096,128]{2,1,0:T(8,128)(2,1)S(1)}, u32[]{:S(2)}, u32[]{:S(2)}) collective-permute-start(bf16[2,4096,128]{2,1,0:T(8,128)(2,1)S(1)} %bitcast.194), channel_id=1, source_target_pairs={{0,64},{64,0},{1,65},{65,1},{2,66},{66,2},{3,67},{67,3},{4,68},{68... | collective-permute-start | bytes 6291464 | tf_op jit(solution)/shard_map/ppermute | solution.py:20
  80.6 0.7 bitcast_dynamic-update-slice_fusion.1
  81.3 2.7 %collective-permute-start.10 = (bf16[4096,128]{1,0:T(8,128)(2,1)}, bf16[4096,128]{1,0:T(8,128)(2,1)S(1)}, u32[]{:S(2)}, u32[]{:S(2)}) collective-permute-start(bf16[4096,128]{1,0:T(8,128)(2,1)} %bitcast.31), channel_id=1, source_target_pairs={{0,64},{64,0},{1,65},{65,1},{2,66},{66,2},{3,67},{67,3},{4,68},{68... | collective-permute-start | bytes 3145736 | tf_op jit(solution)/shard_map/ppermute | solution.py:20
  84.1 0.7 bitcast_dynamic-update-slice_fusion.4
  84.8 4.1 %fusion.36 = f32[512,256]{0,1:T(8,128)S(1)} fusion(bf16[1,512,4096]{2,1,0:T(8,128)(2,1)} %param.6, bf16[4096,128]{1,0:T(8,128)(2,1)} %bitcast.47, bf16[4096,128]{1,0:T(8,128)(2,1)} %bitcast.31), kind=kOutput, calls=%fused_computation.40 | convolution fusion | flops 1077936128 | bytes 6815744 | tf_op jit(solution)/shard_map/dot_general | solution.py:120
  89.1 2.0 copy-done.2
  91.1 1.3 fusion.46
  92.4 1.3 fusion.41
  93.9 1.3 fusion.51
  96.3 1.3 convolution_convert_fusion.1
  97.5 0.6 collective-permute-start.13
  98.1 3.8 %collective-permute-done.13 = bf16[256,4096]{1,0:T(8,128)(2,1)S(1)} collective-permute-done((bf16[256,4096]{1,0:T(8,128)(2,1)S(1)}, bf16[256,4096]{1,0:T(8,128)(2,1)S(1)}, u32[]{:S(2)}, u32[]{:S(2)}) %collective-permute-start.13) | collective-permute-done | bytes 2097184 | tf_op jit(solution)/shard_map/ppermute | solution.py:20
  101.9 1.3 add_convert_fusion.1
  103.2 0.9 copy.89
  104.1 0.7 copy.84
  104.8 35.0 %all_to_all.55 = bf16[16,128,512]{2,1,0:T(8,128)(2,1)S(1)} all-to-all(bf16[16,128,512]{2,1,0:T(8,128)(2,1)S(1)} %bitcast.197), channel_id=1, replica_groups=mesh['ylo'=2,'core'=2,'yhi'=2,'x'=4,'z'=8] {'ylo','yhi','x'}, dimensions={0} | all-to-all | bytes 4194304 | tf_op jit(solution)/shard_map/all_to_all | solution.py:24
  140.2 11.5 %all_to_all.50 = bf16[8,64,128]{2,1,0:T(8,128)(2,1)S(1)} all-to-all(bf16[8,64,128]{2,1,0:T(8,128)(2,1)S(1)} %bitcast.210), channel_id=1, replica_groups=mesh['ylo'=2,'core'=2,'yhi'=2,'x'=4,'z'=8] {'z'}, dimensions={0} | all-to-all | bytes 262144 | tf_op jit(solution)/shard_map/all_to_all | solution.py:24
  151.8 10.3 %all_to_all.51 = bf16[8,64,128]{2,1,0:T(8,128)(2,1)S(1)} all-to-all(bf16[8,64,128]{2,1,0:T(8,128)(2,1)S(1)} %broadcast_in_dim.97), channel_id=1, replica_groups=mesh['ylo'=2,'core'=2,'yhi'=2,'x'=4,'z'=8] {'z'}, dimensions={0} | all-to-all | bytes 262144 | tf_op jit(solution)/shard_map/all_to_all | solution.py:24
  162.5 27.3 %all_to_all.52 = bf16[16,512,128]{2,1,0:T(8,128)(2,1)S(1)} all-to-all(bf16[16,512,128]{2,1,0:T(8,128)(2,1)S(1)} %broadcast_in_dim.99), channel_id=1, replica_groups=mesh['ylo'=2,'core'=2,'yhi'=2,'x'=4,'z'=8] {'ylo','yhi','x'}, dimensions={0} | all-to-all | bytes 4194304 | tf_op jit(solution)/shard_map/all_to_all | solution.py:24
  189.8 5.0 %collective-permute-start.14 = (bf16[2,4096,128]{2,1,0:T(8,128)(2,1)S(1)}, bf16[2,4096,128]{2,1,0:T(8,128)(2,1)S(1)}, u32[]{:S(2)}, u32[]{:S(2)}) collective-permute-start(bf16[2,4096,128]{2,1,0:T(8,128)(2,1)S(1)} %bitcast.195), channel_id=1, source_target_pairs={{0,64},{64,0},{1,65},{65,1},{2,66},{66,2},{3,67},{67,3},{4,68},{68... | collective-permute-start | bytes 6291464 | tf_op jit(solution)/shard_map/ppermute | solution.py:20
  195.0 1.3 fusion.56
  196.3 2.3 collective-permute-done.14
  198.7 1.3 fusion.61
  201.0 1.3 convolution_convert_fusion
  202.3 0.5 collective-permute-start.15
  202.8 3.8 %collective-permute-done.15 = bf16[256,4096]{1,0:T(8,128)(2,1)S(1)} collective-permute-done((bf16[256,4096]{1,0:T(8,128)(2,1)S(1)}, bf16[256,4096]{1,0:T(8,128)(2,1)S(1)}, u32[]{:S(2)}, u32[]{:S(2)}) %collective-permute-start.15) | collective-permute-done | bytes 2097184 | tf_op jit(solution)/shard_map/ppermute | solution.py:20
  206.6 1.4 add_convert_fusion
  208.0 0.9 copy.90
  208.9 0.7 copy.86
  209.6 30.6 %all_to_all.56 = bf16[16,128,512]{2,1,0:T(8,128)(2,1)S(1)} all-to-all(bf16[16,128,512]{2,1,0:T(8,128)(2,1)S(1)} %bitcast.199), channel_id=1, replica_groups=mesh['ylo'=2,'core'=2,'yhi'=2,'x'=4,'z'=8] {'ylo','yhi','x'}, dimensions={0} | all-to-all | bytes 4194304 | tf_op jit(solution)/shard_map/all_to_all | solution.py:24
  240.6 10.3 %all_to_all.53 = bf16[8,64,128]{2,1,0:T(8,128)(2,1)S(1)} all-to-all(bf16[8,64,128]{2,1,0:T(8,128)(2,1)S(1)} %bitcast.211), channel_id=1, replica_groups=mesh['ylo'=2,'core'=2,'yhi'=2,'x'=4,'z'=8] {'z'}, dimensions={0} | all-to-all | bytes 262144 | tf_op jit(solution)/shard_map/all_to_all | solution.py:24
  251.0 8.6 %all_to_all.54 = f32[4,64,128]{2,1,0:T(8,128)S(1)} all-to-all(f32[4,64,128]{2,1,0:T(8,128)S(1)} %broadcast_in_dim.100), channel_id=1, replica_groups=mesh['ylo'=2,'core'=2,'yhi'=2,'x'=4,'z'=8] {'ylo','core'}, dimensions={0} | all-to-all | bytes 262144 | tf_op jit(solution)/shard_map/all_to_all | solution.py:24
  259.6 0.7 pad_maximum_fusion.3
  (60 shorter events, 5.1 us)
Async XLA Ops:
  0.0 7.7 %copy-start = (bf16[64,512]{1,0:T(8,128)(2,1)S(1)}, bf16[64,512]{1,0:T(8,128)(2,1)}, u32[]{:S(2)}) copy-start(bf16[64,512]{1,0:T(8,128)(2,1)} %param.9) | copy-start | bytes 196612
  1.4 17.4 %collective-permute-start.1 = (f32[2,512]{1,0:T(2,128)S(1)}, f32[2,512]{1,0:T(2,128)S(1)}, u32[]{:S(2)}, u32[]{:S(2)}) collective-permute-start(f32[2,512]{1,0:T(2,128)S(1)} %pad_maximum_fusion.4), channel_id=1, source_target_pairs={{1,0},{2,1},{3,2},{4,3},{5,4},{6,5},{7,6},{8,7},{9,8},{10,9},{11,1... | collective-permute-start | bytes 12296 | tf_op jit(solution)/shard_map/ppermute | solution.py:96
  2.7 31.7 %collective-permute-start = (f32[2,512]{1,0:T(2,128)S(1)}, f32[2,512]{1,0:T(2,128)S(1)}, u32[]{:S(2)}, u32[]{:S(2)}) collective-permute-start(f32[2,512]{1,0:T(2,128)S(1)} %pad_maximum_fusion.4), channel_id=1, source_target_pairs={{0,1},{1,2},{2,3},{3,4},{4,5},{5,6},{6,7},{7,8},{8,9},{9,10},{10,1... | collective-permute-start | bytes 12296 | tf_op jit(solution)/shard_map/ppermute | solution.py:95
  8.4 16.7 %all-to-all-start = ((bf16[8,64,128]{2,1,0:T(8,128)(2,1)}), bf16[8,64,128]{2,1,0:T(8,128)(2,1)S(1)}, u32[]{:S(2)}, u32[]{:S(2)}) async-start(bf16[8,64,128]{2,1,0:T(8,128)(2,1)} %broadcast_in_dim.92), calls=%async_computation | async-start | bytes 262144 | tf_op jit(solution)/shard_map/all_to_all | solution.py:24
  25.9 16.0 %all-to-all-start.1 = ((bf16[16,64,128]{2,1,0:T(8,128)(2,1)}), bf16[16,64,128]{2,1,0:T(8,128)(2,1)S(1)}, u32[]{:S(2)}, u32[]{:S(2)}) async-start(bf16[16,64,128]{2,1,0:T(8,128)(2,1)} %broadcast_in_dim.93), calls=%async_computation.1 | async-start | bytes 524288 | tf_op jit(solution)/shard_map/all_to_all | solution.py:24
  42.0 10.8 %collective-permute-start.3 = (bf16[2,8,64,128]{3,2,1,0:T(8,128)(2,1)S(1)}, bf16[2,8,64,128]{3,2,1,0:T(8,128)(2,1)S(1)}, u32[]{:S(2)}, u32[]{:S(2)}) collective-permute-start(bf16[2,8,64,128]{3,2,1,0:T(8,128)(2,1)S(1)} %bitcast.202), channel_id=1, source_target_pairs={{0,7},{1,0},{2,1},{3,2},{4,3},{5,4},{6,5},{7,6},{8,15},{9,8},{10,9... | collective-permute-start | bytes 786440 | tf_op jit(solution)/shard_map/ppermute | solution.py:38
  42.0 12.0 %collective-permute-start.2 = (bf16[2,8,64,128]{3,2,1,0:T(8,128)(2,1)S(1)}, bf16[2,8,64,128]{3,2,1,0:T(8,128)(2,1)S(1)}, u32[]{:S(2)}, u32[]{:S(2)}) collective-permute-start(bf16[2,8,64,128]{3,2,1,0:T(8,128)(2,1)S(1)} %bitcast.203), channel_id=1, source_target_pairs={{0,1},{1,2},{2,3},{3,4},{4,5},{5,6},{6,7},{7,0},{8,9},{9,10},{10,1... | collective-permute-start | bytes 786440 | tf_op jit(solution)/shard_map/ppermute | solution.py:38
  45.2 28.6 %all-to-all-start.2 = ((bf16[16,512,128]{2,1,0:T(8,128)(2,1)}), bf16[16,512,128]{2,1,0:T(8,128)(2,1)S(1)}, u32[]{:S(2)}, u32[]{:S(2)}) async-start(bf16[16,512,128]{2,1,0:T(8,128)(2,1)} %broadcast_in_dim.96), calls=%async_computation.2 | async-start | bytes 4194304 | tf_op jit(solution)/shard_map/all_to_all | solution.py:24
  52.8 5.5 %collective-permute-start.5 = (bf16[2,8,64,128]{3,2,1,0:T(8,128)(2,1)S(1)}, bf16[2,8,64,128]{3,2,1,0:T(8,128)(2,1)S(1)}, u32[]{:S(2)}, u32[]{:S(2)}) collective-permute-start(bf16[2,8,64,128]{3,2,1,0:T(8,128)(2,1)S(1)} %collective-permute-done.3), channel_id=1, source_target_pairs={{0,7},{1,0},{2,1},{3,2},{4,3},{5,4},{6,5},{7,6},{8,15},{9,8},{10,9... | collective-permute-start | bytes 786440 | tf_op jit(solution)/shard_map/ppermute | solution.py:38
  54.0 6.7 %collective-permute-start.4 = (bf16[2,8,64,128]{3,2,1,0:T(8,128)(2,1)S(1)}, bf16[2,8,64,128]{3,2,1,0:T(8,128)(2,1)S(1)}, u32[]{:S(2)}, u32[]{:S(2)}) collective-permute-start(bf16[2,8,64,128]{3,2,1,0:T(8,128)(2,1)S(1)} %collective-permute-done.2), channel_id=1, source_target_pairs={{0,1},{1,2},{2,3},{3,4},{4,5},{5,6},{6,7},{7,0},{8,9},{9,10},{10,1... | collective-permute-start | bytes 786440 | tf_op jit(solution)/shard_map/ppermute | solution.py:38
  58.3 7.9 %collective-permute-start.7 = (bf16[2,8,64,128]{3,2,1,0:T(8,128)(2,1)S(1)}, bf16[2,8,64,128]{3,2,1,0:T(8,128)(2,1)S(1)}, u32[]{:S(2)}, u32[]{:S(2)}) collective-permute-start(bf16[2,8,64,128]{3,2,1,0:T(8,128)(2,1)S(1)} %collective-permute-done.5), channel_id=1, source_target_pairs={{0,7},{1,0},{2,1},{3,2},{4,3},{5,4},{6,5},{7,6},{8,15},{9,8},{10,9... | collective-permute-start | bytes 786440 | tf_op jit(solution)/shard_map/ppermute | solution.py:38
  60.7 8.3 %collective-permute-start.6 = (bf16[2,8,64,128]{3,2,1,0:T(8,128)(2,1)S(1)}, bf16[2,8,64,128]{3,2,1,0:T(8,128)(2,1)S(1)}, u32[]{:S(2)}, u32[]{:S(2)}) collective-permute-start(bf16[2,8,64,128]{3,2,1,0:T(8,128)(2,1)S(1)} %collective-permute-done.4), channel_id=1, source_target_pairs={{0,1},{1,2},{2,3},{3,4},{4,5},{5,6},{6,7},{7,0},{8,9},{9,10},{10,1... | collective-permute-start | bytes 786440 | tf_op jit(solution)/shard_map/ppermute | solution.py:38
  66.2 17.9 %collective-permute-start.9 = (bf16[8,64,128]{2,1,0:T(8,128)(2,1)S(1)}, bf16[8,64,128]{2,1,0:T(8,128)(2,1)S(1)}, u32[]{:S(2)}, u32[]{:S(2)}) collective-permute-start(bf16[8,64,128]{2,1,0:T(8,128)(2,1)S(1)} %slice_bitcast_fusion.14), channel_id=1, source_target_pairs={{0,7},{1,0},{2,1},{3,2},{4,3},{5,4},{6,5},{7,6},{8,15},{9,8},{10,9... | collective-permute-start | bytes 393224 | tf_op jit(solution)/shard_map/ppermute | solution.py:38
  69.0 11.6 %collective-permute-start.8 = (bf16[8,64,128]{2,1,0:T(8,128)(2,1)S(1)}, bf16[8,64,128]{2,1,0:T(8,128)(2,1)S(1)}, u32[]{:S(2)}, u32[]{:S(2)}) collective-permute-start(bf16[8,64,128]{2,1,0:T(8,128)(2,1)S(1)} %slice_bitcast_fusion.15), channel_id=1, source_target_pairs={{0,1},{1,2},{2,3},{3,4},{4,5},{5,6},{6,7},{7,0},{8,9},{9,10},{10,1... | collective-permute-start | bytes 393224 | tf_op jit(solution)/shard_map/ppermute | solution.py:38
  73.8 19.9 %collective-permute-start.12 = (bf16[2,4096,128]{2,1,0:T(8,128)(2,1)S(1)}, bf16[2,4096,128]{2,1,0:T(8,128)(2,1)S(1)}, u32[]{:S(2)}, u32[]{:S(2)}) collective-permute-start(bf16[2,4096,128]{2,1,0:T(8,128)(2,1)S(1)} %bitcast.194), channel_id=1, source_target_pairs={{0,64},{64,0},{1,65},{65,1},{2,66},{66,2},{3,67},{67,3},{4,68},{68... | collective-permute-start | bytes 6291464 | tf_op jit(solution)/shard_map/ppermute | solution.py:20
  81.3 11.1 %collective-permute-start.10 = (bf16[4096,128]{1,0:T(8,128)(2,1)}, bf16[4096,128]{1,0:T(8,128)(2,1)S(1)}, u32[]{:S(2)}, u32[]{:S(2)}) collective-permute-start(bf16[4096,128]{1,0:T(8,128)(2,1)} %bitcast.31), channel_id=1, source_target_pairs={{0,64},{64,0},{1,65},{65,1},{2,66},{66,2},{3,67},{67,3},{4,68},{68... | collective-permute-start | bytes 3145736 | tf_op jit(solution)/shard_map/ppermute | solution.py:20
  84.8 7.6 %collective-permute-start.11 = (bf16[4096,128]{1,0:T(8,128)(2,1)}, bf16[4096,128]{1,0:T(8,128)(2,1)S(1)}, u32[]{:S(2)}, u32[]{:S(2)}) collective-permute-start(bf16[4096,128]{1,0:T(8,128)(2,1)} %bitcast.47), channel_id=1, source_target_pairs={{0,64},{64,0},{1,65},{65,1},{2,66},{66,2},{3,67},{67,3},{4,68},{68... | collective-permute-start | bytes 3145736 | tf_op jit(solution)/shard_map/ppermute | solution.py:20
  88.9 2.2 copy-start.2
  97.5 4.4 %collective-permute-start.13 = (bf16[256,4096]{1,0:T(8,128)(2,1)S(1)}, bf16[256,4096]{1,0:T(8,128)(2,1)S(1)}, u32[]{:S(2)}, u32[]{:S(2)}) collective-permute-start(bf16[256,4096]{1,0:T(8,128)(2,1)S(1)} %convolution_convert_fusion.1), channel_id=1, source_target_pairs={{0,64},{64,0},{1,65},{65,1},{2,66},{66,2},{3,67},{67,3},{4,68},{68... | collective-permute-start | bytes 6291464 | tf_op jit(solution)/shard_map/ppermute | solution.py:20
  104.8 46.9 %copy-start.1 = (f32[64,512]{1,0:T(8,128)S(1)}, f32[64,512]{1,0:T(8,128)}, u32[]{:S(2)}) copy-start(f32[64,512]{1,0:T(8,128)} %param.11) | copy-start | bytes 393220
  162.5 32.5 %copy-start.3 = (bf16[1,512,4096]{2,1,0:T(8,128)(2,1)S(1)}, bf16[1,512,4096]{2,1,0:T(8,128)(2,1)}, u32[]{:S(2)}) copy-start(bf16[1,512,4096]{2,1,0:T(8,128)(2,1)} %param.6) | copy-start | bytes 12582916
  189.8 8.8 %collective-permute-start.14 = (bf16[2,4096,128]{2,1,0:T(8,128)(2,1)S(1)}, bf16[2,4096,128]{2,1,0:T(8,128)(2,1)S(1)}, u32[]{:S(2)}, u32[]{:S(2)}) collective-permute-start(bf16[2,4096,128]{2,1,0:T(8,128)(2,1)S(1)} %bitcast.195), channel_id=1, source_target_pairs={{0,64},{64,0},{1,65},{65,1},{2,66},{66,2},{3,67},{67,3},{4,68},{68... | collective-permute-start | bytes 6291464 | tf_op jit(solution)/shard_map/ppermute | solution.py:20
  202.3 4.2 %collective-permute-start.15 = (bf16[256,4096]{1,0:T(8,128)(2,1)S(1)}, bf16[256,4096]{1,0:T(8,128)(2,1)S(1)}, u32[]{:S(2)}, u32[]{:S(2)}) collective-permute-start(bf16[256,4096]{1,0:T(8,128)(2,1)S(1)} %convolution_convert_fusion), channel_id=1, source_target_pairs={{0,64},{64,0},{1,65},{65,1},{2,66},{66,2},{3,67},{67,3},{4,68},{68... | collective-permute-start | bytes 6291464 | tf_op jit(solution)/shard_map/ppermute | solution.py:20

commit v8 on v7

--- a/solution.py
+++ b/solution.py
@@ -29,7 +29,7 @@
     return exchange(jnp.broadcast_to(block[None], (n,) + block.shape), axes)
 
 
-def ring_gather(block):
+def ring_gather(block, later):
     n = lax.axis_size("z")
     me = lax.axis_index("z")
     wholes = [jnp.zeros((block.shape[1], n) + block.shape[2:], block.dtype) for _ in range(2)]
@@ -47,12 +47,14 @@
         put(index, block[index], me)
     for step in range(1, n // 2):
         before, after = shift(before, 1), shift(after, -1)
+        if step == 1:
+            before, *later = lax.optimization_barrier((before, *later))
         for index in range(2):
             put(index, before[index], me + n - step)
             put(index, after[index], me + step)
     put(0, shift(before[0], 1), me + n // 2)
     put(1, shift(after[1], -1), me + n // 2)
-    return [whole.reshape(-1, block.shape[3]) for whole in wholes]
+    return [whole.reshape(-1, block.shape[3]) for whole in wholes], later
 
 
 def gather_plane(block):
@@ -136,7 +138,8 @@
     block, line = lax.optimization_barrier((query.astype(jnp.bfloat16), line))
     plane = spread(block, PLANE)
     plane, line = lax.optimization_barrier((plane, line))
-    rows = ring_gather(plane.reshape((2, plane.shape[0] // 2) + plane.shape[1:]))
+    blocks = plane.reshape((2, plane.shape[0] // 2) + plane.shape[1:])
+    rows, (ids, text_mask) = ring_gather(blocks, (ids, text_mask))
     tangent = project(rows, [core_swap(half) for half in rows])
     values = project_plane(line)
     own_count = turn_counts(text_mask, ids)

time: 261 us -> 263 us (level)
  waiting for transfers between devices: 33 us -> 27.7 us
  starting transfers between devices: 51 us -> 54.6 us
    ppermute x8, starting transfers between devices: 8.05 us -> 11.9 us  [shift(): return lax.ppermute(value, 'z', [(i, (i + step) % n) for i in range(n)])]
    all_to_all x3, waiting for transfers between devices: 16.5 us -> 13.1 us  [exchange(): return lax.all_to_all(blocks, axes, split_axis=0, concat_axis=0, tiled=True)]
  transfers between devices with their start and end apart: 19 -> 19, of which waited for: 9 -> 7; matrix products, arithmetic and copies ran while one was open for 9% -> 9% of each run, Pallas kernels for 0% -> 0%
where the time goes in v8:
time: 263 us; the launch traced here: 262 us
  blocking collectives  135 us (51%)
  starting transfers between devices  54.6 us (21%)
  waiting for transfers between devices  27.7 us (11%)
  local copies, waits for them, and re-layouts  21.3 us (8%)
  matrix products  15.7 us (6%)
  other arithmetic  6.95 us (3%)
    all_to_all x7, blocking collectives, exchange(): return lax.all_to_all(blocks, axes, split_axis=0, concat_axis=0, tiled=True)  135 us
    all_to_all x3, starting transfers between devices, exchange(): return lax.all_to_all(blocks, axes, split_axis=0, concat_axis=0, tiled=True)  19.5 us
    ppermute x6, starting transfers between devices, core_swap(): return lax.ppermute(value, 'core', [(0, 1), (1, 0)])  17.9 us
    all_to_all x3, waiting for transfers between devices, exchange(): return lax.all_to_all(blocks, axes, split_axis=0, concat_axis=0, tiled=True)  13.1 us
    ppermute x8, starting transfers between devices, shift(): return lax.ppermute(value, 'z', [(i, (i + step) % n) for i in range(n)])  11.9 us
    dot_general x6, matrix products, project(): jnp.dot(inputs, half, preferred_element_type=jnp.float32)  10.6 us
    ppermute x6, waiting for transfers between devices, core_swap(): return lax.ppermute(value, 'core', [(0, 1), (1, 0)])  9.88 us
    dynamic_update_slice x10, local copies, waits for them, and re-layouts, put(): lax.dynamic_update_slice(wholes[index], piece[:, None], (0, owner % n, 0,...  7.39 us
  transfers between devices with their start and end apart: 19, of which 7 were waited for; matrix products, arithmetic and copies ran while one was open for 9% of the time, Pallas kernels for 0%

profile of v8, /device:TPU:1, one launch (start us, length us, event | category | flops | bytes accessed | tf_op | source)
XLA Modules:
  0.0 261.9 jit_solution(17796061486641854078)
XLA Ops:
  0.0 0.8 copy-done
  0.8 0.7 broadcast_in_dim.83
  1.5 9.0 %all-to-all-start = ((bf16[8,64,128]{2,1,0:T(8,128)(2,1)}), bf16[8,64,128]{2,1,0:T(8,128)(2,1)S(1)}, u32[]{:S(2)}, u32[]{:S(2)}) async-start(bf16[8,64,128]{2,1,0:T(8,128)(2,1)} %broadcast_in_dim.83), calls=%async_computation | async-start | bytes 262144 | tf_op jit(solution)/shard_map/all_to_all | solution.py:24
  10.5 0.8 fusion.99
  11.3 0.8 dynamic-slice_convert_fusion
  12.1 6.2 %all-to-all-done = bf16[8,64,128]{2,1,0:T(8,128)(2,1)S(1)} async-done(((bf16[8,64,128]{2,1,0:T(8,128)(2,1)}), bf16[8,64,128]{2,1,0:T(8,128)(2,1)S(1)}, u32[]{:S(2)}, u32[]{:S(2)}) %all-to-all-start) | async-done | bytes 131104 | tf_op jit(solution)/shard_map/all_to_all | solution.py:24
  18.3 0.8 broadcast_in_dim.84
  19.1 6.8 %all-to-all-start.1 = ((bf16[16,64,128]{2,1,0:T(8,128)(2,1)}), bf16[16,64,128]{2,1,0:T(8,128)(2,1)S(1)}, u32[]{:S(2)}, u32[]{:S(2)}) async-start(bf16[16,64,128]{2,1,0:T(8,128)(2,1)} %broadcast_in_dim.84), calls=%async_computation.1 | async-start | bytes 524288 | tf_op jit(solution)/shard_map/all_to_all | solution.py:24
  25.9 0.7 compare_convert_fusion
  26.6 6.9 %all-to-all-done.1 = bf16[16,64,128]{2,1,0:T(8,128)(2,1)S(1)} async-done(((bf16[16,64,128]{2,1,0:T(8,128)(2,1)}), bf16[16,64,128]{2,1,0:T(8,128)(2,1)S(1)}, u32[]{:S(2)}, u32[]{:S(2)}) %all-to-all-start.1) | async-done | bytes 262176 | tf_op jit(solution)/shard_map/all_to_all | solution.py:24
  33.5 1.5 collective-permute-start
  35.0 1.8 broadcast_in_dim.93
  36.8 3.7 %all-to-all-start.2 = ((bf16[16,512,128]{2,1,0:T(8,128)(2,1)}), bf16[16,512,128]{2,1,0:T(8,128)(2,1)S(1)}, u32[]{:S(2)}, u32[]{:S(2)}) async-start(bf16[16,512,128]{2,1,0:T(8,128)(2,1)} %broadcast_in_dim.93), calls=%async_computation.2 | async-start | bytes 4194304 | tf_op jit(solution)/shard_map/all_to_all | solution.py:24
  40.5 1.3 broadcast.68.clone
  41.7 0.7 bitcast_dynamic-update-slice_fusion.7
  42.4 1.2 broadcast.68.clone.1
  43.7 0.7 bitcast_dynamic-update-slice_fusion.3
  44.4 1.3 collective-permute-start.2
  45.7 4.0 %collective-permute-start.1 = (f32[2,512]{1,0:T(2,128)S(1)}, f32[2,512]{1,0:T(2,128)S(1)}, u32[]{:S(2)}, u32[]{:S(2)}) collective-permute-start(f32[2,512]{1,0:T(2,128)S(1)} %pad_maximum_fusion.4), channel_id=1, source_target_pairs={{0,1},{1,2},{2,3},{3,4},{4,5},{5,6},{6,7},{7,8},{8,9},{9,10},{10,1... | collective-permute-start | bytes 12296 | tf_op jit(solution)/shard_map/ppermute | solution.py:97
  50.1 0.8 bitcast_dynamic-update-slice_fusion.5
  50.8 3.1 %collective-permute-start.5 = (bf16[2,8,64,128]{3,2,1,0:T(8,128)(2,1)S(1)}, bf16[2,8,64,128]{3,2,1,0:T(8,128)(2,1)S(1)}, u32[]{:S(2)}, u32[]{:S(2)}) collective-permute-start(bf16[2,8,64,128]{3,2,1,0:T(8,128)(2,1)S(1)} %collective-permute-done.3), channel_id=1, source_target_pairs={{0,7},{1,0},{2,1},{3,2},{4,3},{5,4},{6,5},{7,6},{8,15},{9,8},{10,9... | collective-permute-start | bytes 786440 | tf_op jit(solution)/shard_map/ppermute | solution.py:38
  53.9 0.8 fusion.86
  55.2 2.0 collective-permute-done.5
  57.2 3.4 %collective-permute-start.7 = (bf16[2,8,64,128]{3,2,1,0:T(8,128)(2,1)S(1)}, bf16[2,8,64,128]{3,2,1,0:T(8,128)(2,1)S(1)}, u32[]{:S(2)}, u32[]{:S(2)}) collective-permute-start(bf16[2,8,64,128]{3,2,1,0:T(8,128)(2,1)S(1)} %collective-permute-done.5), channel_id=1, source_target_pairs={{0,7},{1,0},{2,1},{3,2},{4,3},{5,4},{6,5},{7,6},{8,15},{9,8},{10,9... | collective-permute-start | bytes 786440 | tf_op jit(solution)/shard_map/ppermute | solution.py:38
  60.6 0.8 fusion.85
  61.4 0.8 fusion.84
  62.2 2.7 %collective-permute-done.7 = bf16[2,8,64,128]{3,2,1,0:T(8,128)(2,1)S(1)} collective-permute-done((bf16[2,8,64,128]{3,2,1,0:T(8,128)(2,1)S(1)}, bf16[2,8,64,128]{3,2,1,0:T(8,128)(2,1)S(1)}, u32[]{:S(2)}, u32[]{:S(2)}) %collective-permute-start.7) | collective-permute-done | bytes 262176 | tf_op jit(solution)/shard_map/ppermute | solution.py:38
  64.9 3.5 %collective-permute-start.9 = (bf16[8,64,128]{2,1,0:T(8,128)(2,1)S(1)}, bf16[8,64,128]{2,1,0:T(8,128)(2,1)S(1)}, u32[]{:S(2)}, u32[]{:S(2)}) collective-permute-start(bf16[8,64,128]{2,1,0:T(8,128)(2,1)S(1)} %slice_bitcast_fusion.12), channel_id=1, source_target_pairs={{0,7},{1,0},{2,1},{3,2},{4,3},{5,4},{6,5},{7,6},{8,15},{9,8},{10,9... | collective-permute-start | bytes 393224 | tf_op jit(solution)/shard_map/ppermute | solution.py:38
  68.5 0.8 bitcast_dynamic-update-slice_fusion.4
  69.3 0.8 fusion.83
  70.0 7.7 %collective-permute-start.12 = (bf16[2,4096,128]{2,1,0:T(8,128)(2,1)S(1)}, bf16[2,4096,128]{2,1,0:T(8,128)(2,1)S(1)}, u32[]{:S(2)}, u32[]{:S(2)}) collective-permute-start(bf16[2,4096,128]{2,1,0:T(8,128)(2,1)S(1)} %bitcast.192), channel_id=1, source_target_pairs={{0,64},{64,0},{1,65},{65,1},{2,66},{66,2},{3,67},{67,3},{4,68},{68... | collective-permute-start | bytes 6291464 | tf_op jit(solution)/shard_map/ppermute | solution.py:20
  77.7 0.7 bitcast_dynamic-update-slice_fusion.6
  78.4 4.6 %collective-permute-start.10 = (bf16[4096,128]{1,0:T(8,128)(2,1)}, bf16[4096,128]{1,0:T(8,128)(2,1)S(1)}, u32[]{:S(2)}, u32[]{:S(2)}) collective-permute-start(bf16[4096,128]{1,0:T(8,128)(2,1)} %bitcast.31), channel_id=1, source_target_pairs={{0,64},{64,0},{1,65},{65,1},{2,66},{66,2},{3,67},{67,3},{4,68},{68... | collective-permute-start | bytes 3145736 | tf_op jit(solution)/shard_map/ppermute | solution.py:20
  83.0 0.7 bitcast_dynamic-update-slice_fusion
  83.7 4.1 %fusion.36 = f32[512,256]{0,1:T(8,128)S(1)} fusion(bf16[1,512,4096]{2,1,0:T(8,128)(2,1)} %param.6, bf16[4096,128]{1,0:T(8,128)(2,1)} %bitcast.49, bf16[4096,128]{1,0:T(8,128)(2,1)} %bitcast.31), kind=kOutput, calls=%fused_computation.40 | convolution fusion | flops 1077936128 | bytes 6815744 | tf_op jit(solution)/shard_map/dot_general | solution.py:122
  88.1 2.0 copy-done.3
  90.1 1.3 fusion.46
  91.4 1.3 fusion.41
  92.8 1.3 fusion.51
  95.3 1.3 convolution_convert_fusion.1
  96.5 0.6 collective-permute-start.13
  97.1 3.8 %collective-permute-done.13 = bf16[256,4096]{1,0:T(8,128)(2,1)S(1)} collective-permute-done((bf16[256,4096]{1,0:T(8,128)(2,1)S(1)}, bf16[256,4096]{1,0:T(8,128)(2,1)S(1)}, u32[]{:S(2)}, u32[]{:S(2)}) %collective-permute-start.13) | collective-permute-done | bytes 2097184 | tf_op jit(solution)/shard_map/ppermute | solution.py:20
  100.9 1.3 add_convert_fusion.1
  102.2 0.9 copy.75
  103.1 0.7 copy.70
  103.8 37.2 %all_to_all.55 = bf16[16,128,512]{2,1,0:T(8,128)(2,1)} all-to-all(bf16[16,128,512]{2,1,0:T(8,128)(2,1)S(1)} %bitcast.195), channel_id=1, replica_groups=mesh['ylo'=2,'core'=2,'yhi'=2,'x'=4,'z'=8] {'ylo','yhi','x'}, dimensions={0} | all-to-all | bytes 4194304 | tf_op jit(solution)/shard_map/all_to_all | solution.py:24
  141.0 1.9 reduce_sum.120
  143.1 10.4 %all_to_all.50 = bf16[8,64,128]{2,1,0:T(8,128)(2,1)S(1)} all-to-all(bf16[8,64,128]{2,1,0:T(8,128)(2,1)S(1)} %bitcast.208), channel_id=1, replica_groups=mesh['ylo'=2,'core'=2,'yhi'=2,'x'=4,'z'=8] {'z'}, dimensions={0} | all-to-all | bytes 262144 | tf_op jit(solution)/shard_map/all_to_all | solution.py:24
  153.6 10.3 %all_to_all.51 = bf16[8,64,128]{2,1,0:T(8,128)(2,1)S(1)} all-to-all(bf16[8,64,128]{2,1,0:T(8,128)(2,1)S(1)} %broadcast_in_dim.94), channel_id=1, replica_groups=mesh['ylo'=2,'core'=2,'yhi'=2,'x'=4,'z'=8] {'z'}, dimensions={0} | all-to-all | bytes 262144 | tf_op jit(solution)/shard_map/all_to_all | solution.py:24
  164.3 27.8 %all_to_all.52 = bf16[16,512,128]{2,1,0:T(8,128)(2,1)S(1)} all-to-all(bf16[16,512,128]{2,1,0:T(8,128)(2,1)S(1)} %broadcast_in_dim.96), channel_id=1, replica_groups=mesh['ylo'=2,'core'=2,'yhi'=2,'x'=4,'z'=8] {'ylo','yhi','x'}, dimensions={0} | all-to-all | bytes 4194304 | tf_op jit(solution)/shard_map/all_to_all | solution.py:24
  192.1 4.5 %collective-permute-start.14 = (bf16[2,4096,128]{2,1,0:T(8,128)(2,1)S(1)}, bf16[2,4096,128]{2,1,0:T(8,128)(2,1)S(1)}, u32[]{:S(2)}, u32[]{:S(2)}) collective-permute-start(bf16[2,4096,128]{2,1,0:T(8,128)(2,1)S(1)} %bitcast.193), channel_id=1, source_target_pairs={{0,64},{64,0},{1,65},{65,1},{2,66},{66,2},{3,67},{67,3},{4,68},{68... | collective-permute-start | bytes 6291464 | tf_op jit(solution)/shard_map/ppermute | solution.py:20
  196.7 1.3 fusion.56
  198.1 2.3 collective-permute-done.14
  200.5 1.3 fusion.61
  202.8 1.3 convolution_convert_fusion
  204.0 0.5 collective-permute-start.15
  204.5 3.8 %collective-permute-done.15 = bf16[256,4096]{1,0:T(8,128)(2,1)S(1)} collective-permute-done((bf16[256,4096]{1,0:T(8,128)(2,1)S(1)}, bf16[256,4096]{1,0:T(8,128)(2,1)S(1)}, u32[]{:S(2)}, u32[]{:S(2)}) %collective-permute-start.15) | collective-permute-done | bytes 2097184 | tf_op jit(solution)/shard_map/ppermute | solution.py:20
  208.3 1.3 add_convert_fusion
  209.6 0.9 copy.76
  210.5 0.7 copy.72
  211.2 30.7 %all_to_all.56 = bf16[16,128,512]{2,1,0:T(8,128)(2,1)S(1)} all-to-all(bf16[16,128,512]{2,1,0:T(8,128)(2,1)S(1)} %bitcast.197), channel_id=1, replica_groups=mesh['ylo'=2,'core'=2,'yhi'=2,'x'=4,'z'=8] {'ylo','yhi','x'}, dimensions={0} | all-to-all | bytes 4194304 | tf_op jit(solution)/shard_map/all_to_all | solution.py:24
  242.3 10.4 %all_to_all.53 = bf16[8,64,128]{2,1,0:T(8,128)(2,1)S(1)} all-to-all(bf16[8,64,128]{2,1,0:T(8,128)(2,1)S(1)} %bitcast.209), channel_id=1, replica_groups=mesh['ylo'=2,'core'=2,'yhi'=2,'x'=4,'z'=8] {'z'}, dimensions={0} | all-to-all | bytes 262144 | tf_op jit(solution)/shard_map/all_to_all | solution.py:24
  252.8 8.5 %all_to_all.54 = f32[4,64,128]{2,1,0:T(8,128)S(1)} all-to-all(f32[4,64,128]{2,1,0:T(8,128)S(1)} %broadcast_in_dim.97), channel_id=1, replica_groups=mesh['ylo'=2,'core'=2,'yhi'=2,'x'=4,'z'=8] {'ylo','core'}, dimensions={0} | all-to-all | bytes 262144 | tf_op jit(solution)/shard_map/all_to_all | solution.py:24
  261.3 0.7 pad_maximum_fusion.3
  (63 shorter events, 4.8 us)
Async XLA Ops:
  0.0 0.8 copy-start
  1.5 16.8 %all-to-all-start = ((bf16[8,64,128]{2,1,0:T(8,128)(2,1)}), bf16[8,64,128]{2,1,0:T(8,128)(2,1)S(1)}, u32[]{:S(2)}, u32[]{:S(2)}) async-start(bf16[8,64,128]{2,1,0:T(8,128)(2,1)} %broadcast_in_dim.83), calls=%async_computation | async-start | bytes 262144 | tf_op jit(solution)/shard_map/all_to_all | solution.py:24
  19.1 14.5 %all-to-all-start.1 = ((bf16[16,64,128]{2,1,0:T(8,128)(2,1)}), bf16[16,64,128]{2,1,0:T(8,128)(2,1)S(1)}, u32[]{:S(2)}, u32[]{:S(2)}) async-start(bf16[16,64,128]{2,1,0:T(8,128)(2,1)} %broadcast_in_dim.84), calls=%async_computation.1 | async-start | bytes 524288 | tf_op jit(solution)/shard_map/all_to_all | solution.py:24
  33.5 10.8 %copy-start.2 = (s32[1,512]{1,0:T(1,128)S(1)}, s32[1,512]{1,0:T(1,128)}, u32[]{:S(2)}) copy-start(s32[1,512]{1,0:T(1,128)} %param.8) | copy-start | bytes 6148
  33.5 17.3 %collective-permute-start.3 = (bf16[2,8,64,128]{3,2,1,0:T(8,128)(2,1)S(1)}, bf16[2,8,64,128]{3,2,1,0:T(8,128)(2,1)S(1)}, u32[]{:S(2)}, u32[]{:S(2)}) collective-permute-start(bf16[2,8,64,128]{3,2,1,0:T(8,128)(2,1)S(1)} %bitcast.200), channel_id=1, source_target_pairs={{0,7},{1,0},{2,1},{3,2},{4,3},{5,4},{6,5},{7,6},{8,15},{9,8},{10,9... | collective-permute-start | bytes 786440 | tf_op jit(solution)/shard_map/ppermute | solution.py:38
  33.5 10.8 %collective-permute-start = (bf16[2,8,64,128]{3,2,1,0:T(8,128)(2,1)S(1)}, bf16[2,8,64,128]{3,2,1,0:T(8,128)(2,1)S(1)}, u32[]{:S(2)}, u32[]{:S(2)}) collective-permute-start(bf16[2,8,64,128]{3,2,1,0:T(8,128)(2,1)S(1)} %bitcast.201), channel_id=1, source_target_pairs={{0,1},{1,2},{2,3},{3,4},{4,5},{5,6},{6,7},{7,0},{8,9},{9,10},{10,1... | collective-permute-start | bytes 786440 | tf_op jit(solution)/shard_map/ppermute | solution.py:38
  36.8 33.3 %all-to-all-start.2 = ((bf16[16,512,128]{2,1,0:T(8,128)(2,1)}), bf16[16,512,128]{2,1,0:T(8,128)(2,1)S(1)}, u32[]{:S(2)}, u32[]{:S(2)}) async-start(bf16[16,512,128]{2,1,0:T(8,128)(2,1)} %broadcast_in_dim.93), calls=%async_computation.2 | async-start | bytes 4194304 | tf_op jit(solution)/shard_map/all_to_all | solution.py:24
  44.4 10.3 %collective-permute-start.2 = (f32[2,512]{1,0:T(2,128)S(1)}, f32[2,512]{1,0:T(2,128)S(1)}, u32[]{:S(2)}, u32[]{:S(2)}) collective-permute-start(f32[2,512]{1,0:T(2,128)S(1)} %pad_maximum_fusion.4), channel_id=1, source_target_pairs={{1,0},{2,1},{3,2},{4,3},{5,4},{6,5},{7,6},{8,7},{9,8},{10,9},{11,1... | collective-permute-start | bytes 12296 | tf_op jit(solution)/shard_map/ppermute | solution.py:98
  45.7 9.0 %collective-permute-start.1 = (f32[2,512]{1,0:T(2,128)S(1)}, f32[2,512]{1,0:T(2,128)S(1)}, u32[]{:S(2)}, u32[]{:S(2)}) collective-permute-start(f32[2,512]{1,0:T(2,128)S(1)} %pad_maximum_fusion.4), channel_id=1, source_target_pairs={{0,1},{1,2},{2,3},{3,4},{4,5},{5,6},{6,7},{7,8},{8,9},{9,10},{10,1... | collective-permute-start | bytes 12296 | tf_op jit(solution)/shard_map/ppermute | solution.py:97
  49.7 10.9 %collective-permute-start.4 = (bf16[2,8,64,128]{3,2,1,0:T(8,128)(2,1)S(1)}, bf16[2,8,64,128]{3,2,1,0:T(8,128)(2,1)S(1)}, u32[]{:S(2)}, u32[]{:S(2)}) collective-permute-start(bf16[2,8,64,128]{3,2,1,0:T(8,128)(2,1)S(1)} %collective-permute-done), channel_id=1, source_target_pairs={{0,1},{1,2},{2,3},{3,4},{4,5},{5,6},{6,7},{7,0},{8,9},{9,10},{10,1... | collective-permute-start | bytes 786440 | tf_op jit(solution)/shard_map/ppermute | solution.py:38
  50.8 6.4 %collective-permute-start.5 = (bf16[2,8,64,128]{3,2,1,0:T(8,128)(2,1)S(1)}, bf16[2,8,64,128]{3,2,1,0:T(8,128)(2,1)S(1)}, u32[]{:S(2)}, u32[]{:S(2)}) collective-permute-start(bf16[2,8,64,128]{3,2,1,0:T(8,128)(2,1)S(1)} %collective-permute-done.3), channel_id=1, source_target_pairs={{0,7},{1,0},{2,1},{3,2},{4,3},{5,4},{6,5},{7,6},{8,15},{9,8},{10,9... | collective-permute-start | bytes 786440 | tf_op jit(solution)/shard_map/ppermute | solution.py:38
  57.2 7.7 %collective-permute-start.7 = (bf16[2,8,64,128]{3,2,1,0:T(8,128)(2,1)S(1)}, bf16[2,8,64,128]{3,2,1,0:T(8,128)(2,1)S(1)}, u32[]{:S(2)}, u32[]{:S(2)}) collective-permute-start(bf16[2,8,64,128]{3,2,1,0:T(8,128)(2,1)S(1)} %collective-permute-done.5), channel_id=1, source_target_pairs={{0,7},{1,0},{2,1},{3,2},{4,3},{5,4},{6,5},{7,6},{8,15},{9,8},{10,9... | collective-permute-start | bytes 786440 | tf_op jit(solution)/shard_map/ppermute | solution.py:38
  60.6 7.7 %collective-permute-start.6 = (bf16[2,8,64,128]{3,2,1,0:T(8,128)(2,1)S(1)}, bf16[2,8,64,128]{3,2,1,0:T(8,128)(2,1)S(1)}, u32[]{:S(2)}, u32[]{:S(2)}) collective-permute-start(bf16[2,8,64,128]{3,2,1,0:T(8,128)(2,1)S(1)} %collective-permute-done.4), channel_id=1, source_target_pairs={{0,1},{1,2},{2,3},{3,4},{4,5},{5,6},{6,7},{7,0},{8,9},{9,10},{10,1... | collective-permute-start | bytes 786440 | tf_op jit(solution)/shard_map/ppermute | solution.py:38
  64.9 18.2 %collective-permute-start.9 = (bf16[8,64,128]{2,1,0:T(8,128)(2,1)S(1)}, bf16[8,64,128]{2,1,0:T(8,128)(2,1)S(1)}, u32[]{:S(2)}, u32[]{:S(2)}) collective-permute-start(bf16[8,64,128]{2,1,0:T(8,128)(2,1)S(1)} %slice_bitcast_fusion.12), channel_id=1, source_target_pairs={{0,7},{1,0},{2,1},{3,2},{4,3},{5,4},{6,5},{7,6},{8,15},{9,8},{10,9... | collective-permute-start | bytes 393224 | tf_op jit(solution)/shard_map/ppermute | solution.py:38
  68.4 9.3 %collective-permute-start.8 = (bf16[8,64,128]{2,1,0:T(8,128)(2,1)S(1)}, bf16[8,64,128]{2,1,0:T(8,128)(2,1)S(1)}, u32[]{:S(2)}, u32[]{:S(2)}) collective-permute-start(bf16[8,64,128]{2,1,0:T(8,128)(2,1)S(1)} %slice_bitcast_fusion.13), channel_id=1, source_target_pairs={{0,1},{1,2},{2,3},{3,4},{4,5},{5,6},{6,7},{7,0},{8,9},{9,10},{10,1... | collective-permute-start | bytes 393224 | tf_op jit(solution)/shard_map/ppermute | solution.py:38
  70.0 22.7 %collective-permute-start.12 = (bf16[2,4096,128]{2,1,0:T(8,128)(2,1)S(1)}, bf16[2,4096,128]{2,1,0:T(8,128)(2,1)S(1)}, u32[]{:S(2)}, u32[]{:S(2)}) collective-permute-start(bf16[2,4096,128]{2,1,0:T(8,128)(2,1)S(1)} %bitcast.192), channel_id=1, source_target_pairs={{0,64},{64,0},{1,65},{65,1},{2,66},{66,2},{3,67},{67,3},{4,68},{68... | collective-permute-start | bytes 6291464 | tf_op jit(solution)/shard_map/ppermute | solution.py:20
  78.4 12.9 %collective-permute-start.10 = (bf16[4096,128]{1,0:T(8,128)(2,1)}, bf16[4096,128]{1,0:T(8,128)(2,1)S(1)}, u32[]{:S(2)}, u32[]{:S(2)}) collective-permute-start(bf16[4096,128]{1,0:T(8,128)(2,1)} %bitcast.31), channel_id=1, source_target_pairs={{0,64},{64,0},{1,65},{65,1},{2,66},{66,2},{3,67},{67,3},{4,68},{68... | collective-permute-start | bytes 3145736 | tf_op jit(solution)/shard_map/ppermute | solution.py:20
  83.7 7.6 %collective-permute-start.11 = (bf16[4096,128]{1,0:T(8,128)(2,1)}, bf16[4096,128]{1,0:T(8,128)(2,1)S(1)}, u32[]{:S(2)}, u32[]{:S(2)}) collective-permute-start(bf16[4096,128]{1,0:T(8,128)(2,1)} %bitcast.49), channel_id=1, source_target_pairs={{0,64},{64,0},{1,65},{65,1},{2,66},{66,2},{3,67},{67,3},{4,68},{68... | collective-permute-start | bytes 3145736 | tf_op jit(solution)/shard_map/ppermute | solution.py:20
  87.9 2.2 copy-start.3
  96.5 4.4 %collective-permute-start.13 = (bf16[256,4096]{1,0:T(8,128)(2,1)S(1)}, bf16[256,4096]{1,0:T(8,128)(2,1)S(1)}, u32[]{:S(2)}, u32[]{:S(2)}) collective-permute-start(bf16[256,4096]{1,0:T(8,128)(2,1)S(1)} %convolution_convert_fusion.1), channel_id=1, source_target_pairs={{0,64},{64,0},{1,65},{65,1},{2,66},{66,2},{3,67},{67,3},{4,68},{68... | collective-permute-start | bytes 6291464 | tf_op jit(solution)/shard_map/ppermute | solution.py:20
  103.8 49.7 %copy-start.1 = (f32[64,512]{1,0:T(8,128)S(1)}, f32[64,512]{1,0:T(8,128)}, u32[]{:S(2)}) copy-start(f32[64,512]{1,0:T(8,128)} %param.11) | copy-start | bytes 393220
  164.3 32.4 %copy-start.4 = (bf16[1,512,4096]{2,1,0:T(8,128)(2,1)S(1)}, bf16[1,512,4096]{2,1,0:T(8,128)(2,1)}, u32[]{:S(2)}) copy-start(bf16[1,512,4096]{2,1,0:T(8,128)(2,1)} %param.6) | copy-start | bytes 12582916
  192.1 8.3 %collective-permute-start.14 = (bf16[2,4096,128]{2,1,0:T(8,128)(2,1)S(1)}, bf16[2,4096,128]{2,1,0:T(8,128)(2,1)S(1)}, u32[]{:S(2)}, u32[]{:S(2)}) collective-permute-start(bf16[2,4096,128]{2,1,0:T(8,128)(2,1)S(1)} %bitcast.193), channel_id=1, source_target_pairs={{0,64},{64,0},{1,65},{65,1},{2,66},{66,2},{3,67},{67,3},{4,68},{68... | collective-permute-start | bytes 6291464 | tf_op jit(solution)/shard_map/ppermute | solution.py:20
  204.0 4.2 %collective-permute-start.15 = (bf16[256,4096]{1,0:T(8,128)(2,1)S(1)}, bf16[256,4096]{1,0:T(8,128)(2,1)S(1)}, u32[]{:S(2)}, u32[]{:S(2)}) collective-permute-start(bf16[256,4096]{1,0:T(8,128)(2,1)S(1)} %convolution_convert_fusion), channel_id=1, source_target_pairs={{0,64},{64,0},{1,65},{65,1},{2,66},{66,2},{3,67},{67,3},{4,68},{68... | collective-permute-start | bytes 6291464 | tf_op jit(solution)/shard_map/ppermute | solution.py:20

commit v9 on v5

--- a/solution.py
+++ b/solution.py
@@ -60,16 +60,17 @@
     return line.reshape(line.shape[0] * line.shape[1], line.shape[2])
 
 
-def reduce_blocks(inputs, adjoint):
+def reduce_blocks(inputs, other_inputs, adjoint):
     half = adjoint.shape[1] // 2
 
-    def outer(part):
+    def outer(part, rows):
         return lax.dot_general(
-            part, inputs, (((0,), (0,)), ((), ())), preferred_element_type=jnp.float32
+            part, rows, (((0,), (0,)), ((), ())), preferred_element_type=jnp.float32
         )
 
-    other = core_swap(outer(adjoint[:, half:]).astype(jnp.bfloat16))
-    chip = (outer(adjoint[:, :half]) + other.astype(jnp.float32)).astype(jnp.bfloat16)
+    swapped = core_swap(adjoint[:, half:])
+    chip = outer(adjoint[:, :half], inputs) + outer(swapped, other_inputs)
+    chip = chip.astype(jnp.bfloat16)
     n_low, n_plane, n_line = lax.axis_size("ylo"), lax.axis_size(PLANE), lax.axis_size("z")
     cols = half // n_low
     blocks = chip.reshape(n_low, cols, n_plane // n_low, -1).transpose(0, 2, 1, 3)
@@ -110,11 +111,13 @@
     def own(array):
         return lax.dynamic_slice(array, (0, me * cols), (array.shape[0], cols))
 
+    other_inputs = core_swap(inputs)
+
     def project(mine):
-        halves = [jnp.concatenate([pair[0], pair[1]], axis=1) for pair in (mine, core_swap(mine))]
-        return jnp.concatenate(
-            [jnp.dot(inputs, half, preferred_element_type=jnp.float32) for half in halves], axis=1
-        )
+        half = jnp.concatenate([mine[0], mine[1]], axis=1)
+        swapped = core_swap(jnp.dot(other_inputs, half, preferred_element_type=jnp.float32))
+        own_part = jnp.dot(inputs, half, preferred_element_type=jnp.float32)
+        return jnp.concatenate([own_part, swapped], axis=1)
 
     gain = norm_gain.reshape(2, 2, cols)
     gain = jnp.concatenate(
@@ -141,7 +144,7 @@
         adjoint = (turn_weight[:, None] * norm_jacobian(inner, unit_values, root_mean)).astype(
             jnp.bfloat16
         )
-        curvature = reduce_blocks(inputs, adjoint)
+        curvature = reduce_blocks(inputs, other_inputs, adjoint)
         estimate = query + estimate - (curvature + damping * estimate) / lissa_scale
     whole = spread(estimate, GROUP)
     return jnp.concatenate([whole[i] for i in range(n_group)], axis=1)

time: 256 us -> 256 us (level)
  local copies, waits for them, and re-layouts: 24 us -> 11.9 us
  matrix products: 12.8 us -> 24 us
  waiting for transfers between devices: 24.7 us -> 28.7 us
  blocking collectives: 136 us -> 133 us
    dot_general x10, matrix products: 12.8 us -> 24 us  [the longest x3 10.7 us: project(): jnp.dot(other_inputs, half, preferred_element_type=jnp.float32)]
    ppermute x5 -> x6, waiting for transfers between devices: 10.2 us -> 0.63 us  [core_swap(): return lax.ppermute(value, 'core', [(0, 1), (1, 0)])]
    ppermute x8, waiting for transfers between devices: 6.65 us -> 16.2 us  [shift(): return lax.ppermute(value, 'z', [(i, (i + step) % n) for i in range(n)])]
    dynamic_update_slice x9, local copies, waits for them, and re-layouts: 6.7 us -> 0.32 us  [put(): lax.dynamic_update_slice(whole, piece[:, None], (start, owner % n, 0, 0))]
    ppermute x5 -> x6, starting transfers between devices: 11.7 us -> 16 us  [core_swap(): return lax.ppermute(value, 'core', [(0, 1), (1, 0)])]
    all_to_all x3, waiting for transfers between devices: 7.84 us -> 11.9 us  [exchange(): return lax.all_to_all(blocks, axes, split_axis=0, concat_axis=0, tiled=True)]
    all_to_all x7, blocking collectives: 136 us -> 133 us  [exchange(): return lax.all_to_all(blocks, axes, split_axis=0, concat_axis=0, tiled=True)]
    ppermute x8, starting transfers between devices: 10.9 us -> 8.13 us  [shift(): return lax.ppermute(value, 'z', [(i, (i + step) % n) for i in range(n)])]
  transfers between devices with their start and end apart: 18 -> 19, of which waited for: 8 -> 9; matrix products, arithmetic and copies ran while one was open for 9% -> 6% of each run, Pallas kernels for 0% -> 0%
where the time goes in v9:
time: 256 us
  blocking collectives  133 us (52%)
  starting transfers between devices  51.4 us (20%)
  waiting for transfers between devices  28.7 us (11%)
  matrix products  24 us (9%)
  local copies, waits for them, and re-layouts  11.9 us (5%)
  other arithmetic  5.99 us (2%)
    all_to_all x7, blocking collectives, exchange(): return lax.all_to_all(blocks, axes, split_axis=0, concat_axis=0, tiled=True)  133 us
    all_to_all x3, starting transfers between devices, exchange(): return lax.all_to_all(blocks, axes, split_axis=0, concat_axis=0, tiled=True)  21 us
    ppermute x8, waiting for transfers between devices, shift(): return lax.ppermute(value, 'z', [(i, (i + step) % n) for i in range(n)])  16.2 us
    ppermute x6, starting transfers between devices, core_swap(): return lax.ppermute(value, 'core', [(0, 1), (1, 0)])  16 us
    all_to_all x3, waiting for transfers between devices, exchange(): return lax.all_to_all(blocks, axes, split_axis=0, concat_axis=0, tiled=True)  11.9 us
    dot_general x3, matrix products, project(): jnp.dot(other_inputs, half, preferred_element_type=jnp.float32)  10.7 us
    dot_general x4, matrix products, outer(): lax.dot_general(part, rows, (((0,), (0,)), ((), ())), preferred_element_t...  9.4 us
    ppermute x8, starting transfers between devices, shift(): return lax.ppermute(value, 'z', [(i, (i + step) % n) for i in range(n)])  8.13 us
  transfers between devices with their start and end apart: 19, of which 9 were waited for; matrix products, arithmetic and copies ran while one was open for 6% of the time, Pallas kernels for 0%

profile of v9, /device:TPU:1, one launch (start us, length us, event | category | flops | bytes accessed | tf_op | source)
XLA Modules:
  0.0 255.5 jit_solution(12848947211014589193)
XLA Ops:
  0.0 0.7 compare_convert_fusion
  0.7 0.7 convert_element_type.54
  1.4 1.3 collective-permute-start.1
  2.7 5.0 %collective-permute-start = (f32[2,512]{1,0:T(2,128)S(1)}, f32[2,512]{1,0:T(2,128)S(1)}, u32[]{:S(2)}, u32[]{:S(2)}) collective-permute-start(f32[2,512]{1,0:T(2,128)S(1)} %pad_maximum_fusion.25), channel_id=1, source_target_pairs={{0,1},{1,2},{2,3},{3,4},{4,5},{5,6},{6,7},{7,8},{8,9},{9,10},{10,1... | collective-permute-start | bytes 12296 | tf_op jit(solution)/shard_map/ppermute | solution.py:92
  7.8 0.7 broadcast_in_dim.117
  8.4 8.8 %all-to-all-start = ((bf16[8,64,128]{2,1,0:T(8,128)(2,1)}), bf16[8,64,128]{2,1,0:T(8,128)(2,1)S(1)}, u32[]{:S(2)}, u32[]{:S(2)}) async-start(bf16[8,64,128]{2,1,0:T(8,128)(2,1)} %broadcast_in_dim.117), calls=%async_computation | async-start | bytes 262144 | tf_op jit(solution)/shard_map/all_to_all | solution.py:24
  17.2 1.5 collective-permute-start.10
  18.7 0.8 fusion.37
  19.5 0.8 dynamic-slice_convert_fusion
  20.3 4.9 %all-to-all-done = bf16[8,64,128]{2,1,0:T(8,128)(2,1)S(1)} async-done(((bf16[8,64,128]{2,1,0:T(8,128)(2,1)}), bf16[8,64,128]{2,1,0:T(8,128)(2,1)S(1)}, u32[]{:S(2)}, u32[]{:S(2)}) %all-to-all-start) | async-done | bytes 131104 | tf_op jit(solution)/shard_map/all_to_all | solution.py:24
  25.2 0.7 broadcast_in_dim.118
  25.9 8.5 %all-to-all-start.1 = ((bf16[16,64,128]{2,1,0:T(8,128)(2,1)}), bf16[16,64,128]{2,1,0:T(8,128)(2,1)S(1)}, u32[]{:S(2)}, u32[]{:S(2)}) async-start(bf16[16,64,128]{2,1,0:T(8,128)(2,1)} %broadcast_in_dim.118), calls=%async_computation.1 | async-start | bytes 524288 | tf_op jit(solution)/shard_map/all_to_all | solution.py:24
  34.4 0.5 select_reduce_fusion.1
  34.9 7.1 %all-to-all-done.1 = bf16[16,64,128]{2,1,0:T(8,128)(2,1)S(1)} async-done(((bf16[16,64,128]{2,1,0:T(8,128)(2,1)}), bf16[16,64,128]{2,1,0:T(8,128)(2,1)S(1)}, u32[]{:S(2)}, u32[]{:S(2)}) %all-to-all-start.1) | async-done | bytes 262176 | tf_op jit(solution)/shard_map/all_to_all | solution.py:24
  42.0 1.5 collective-permute-start.2
  43.4 1.7 broadcast_in_dim.128
  45.2 3.7 %all-to-all-start.2 = ((bf16[16,512,128]{2,1,0:T(8,128)(2,1)}), bf16[16,512,128]{2,1,0:T(8,128)(2,1)S(1)}, u32[]{:S(2)}, u32[]{:S(2)}) async-start(bf16[16,512,128]{2,1,0:T(8,128)(2,1)} %broadcast_in_dim.128), calls=%async_computation.2 | async-start | bytes 4194304 | tf_op jit(solution)/shard_map/all_to_all | solution.py:24
  48.9 0.5 broadcast_in_dim.116
  49.5 1.3 collective-permute-start.5
  51.1 3.7 %collective-permute-done.5 = bf16[16,64,128]{2,1,0:T(8,128)(2,1)S(1)} collective-permute-done((bf16[16,64,128]{2,1,0:T(8,128)(2,1)S(1)}, bf16[16,64,128]{2,1,0:T(8,128)(2,1)S(1)}, u32[]{:S(2)}, u32[]{:S(2)}) %collective-permute-start.5) | collective-permute-done | bytes 262176 | tf_op jit(solution)/shard_map/ppermute | solution.py:38
  54.8 2.4 collective-permute-start.7
  57.3 5.7 %collective-permute-done.7 = bf16[16,64,128]{2,1,0:T(8,128)(2,1)S(1)} collective-permute-done((bf16[16,64,128]{2,1,0:T(8,128)(2,1)S(1)}, bf16[16,64,128]{2,1,0:T(8,128)(2,1)S(1)}, u32[]{:S(2)}, u32[]{:S(2)}) %collective-permute-start.7) | collective-permute-done | bytes 262176 | tf_op jit(solution)/shard_map/ppermute | solution.py:38
  63.0 2.6 %collective-permute-start.9 = (bf16[8,64,128]{2,1,0:T(8,128)(2,1)S(1)}, bf16[8,64,128]{2,1,0:T(8,128)(2,1)S(1)}, u32[]{:S(2)}, u32[]{:S(2)}) collective-permute-start(bf16[8,64,128]{2,1,0:T(8,128)(2,1)S(1)} %slice.103), channel_id=1, source_target_pairs={{0,7},{1,0},{2,1},{3,2},{4,3},{5,4},{6,5},{7,6},{8,15},{9,8},{10,9... | collective-permute-start | bytes 393224 | tf_op jit(solution)/shard_map/ppermute | solution.py:38
  66.0 6.6 %collective-permute-done.8 = bf16[8,64,128]{2,1,0:T(8,128)(2,1)S(1)} collective-permute-done((bf16[8,64,128]{2,1,0:T(8,128)(2,1)S(1)}, bf16[8,64,128]{2,1,0:T(8,128)(2,1)S(1)}, u32[]{:S(2)}, u32[]{:S(2)}) %collective-permute-start.8) | collective-permute-done | bytes 131104 | tf_op jit(solution)/shard_map/ppermute | solution.py:38
  72.9 1.0 copy-done.4
  73.8 0.3 copy-done.6
  74.2 1.4 copy-done.1
  75.6 1.3 fusion.8
  77.1 3.6 %fusion.11 = f32[512,256]{0,1:T(8,128)S(1)} fusion(bf16[512,4096]{1,0:T(8,128)(2,1)} %collective-permute-done.10, bf16[4096,128]{1,0:T(8,128)(2,1)S(1)} %bitcast.127, bf16[4096,128]{1,0:T(8,128)(2,1)S(1)} %bitcast.125), kind=kOutput, calls=%fused_computation.16 | convolution fusion | flops 1077936128 | bytes 6815744 | tf_op jit(solution)/shard_map/dot_general | solution.py:118
  80.8 8.1 %collective-permute-start.12 = (f32[512,256]{0,1:T(8,128)S(1)}, f32[512,256]{0,1:T(8,128)S(1)}, u32[]{:S(2)}, u32[]{:S(2)}) collective-permute-start(f32[512,256]{0,1:T(8,128)S(1)} %fusion.11), channel_id=1, source_target_pairs={{0,64},{64,0},{1,65},{65,1},{2,66},{66,2},{3,67},{67,3},{4,68},{68... | collective-permute-start | bytes 1572872 | tf_op jit(solution)/shard_map/ppermute | solution.py:20
  88.9 3.5 %fusion.9 = f32[512,256]{0,1:T(8,128)S(1)} fusion(bf16[512,4096]{1,0:T(8,128)(2,1)} %collective-permute-done.10, bf16[4096,128]{1,0:T(8,128)(2,1)S(1)} %bitcast.124, bf16[4096,128]{1,0:T(8,128)(2,1)S(1)} %bitcast.122), kind=kOutput, calls=%fused_computation.14 | convolution fusion | flops 1077936128 | bytes 6815744 | tf_op jit(solution)/shard_map/dot_general | solution.py:118
  92.4 0.3 collective-permute-start.11
  92.7 1.3 fusion.10
  94.1 0.3 collective-permute-done.11
  94.4 0.3 multiply_reduce_fusion.3
  94.7 0.3 multiply_reduce_fusion.2
  95.0 0.4 multiply_convert_fusion.1
  95.4 0.3 collective-permute-start.13
  95.6 1.3 fusion.17
  97.0 3.4 %fusion = bf16[256,4096]{1,0:T(8,128)(2,1)S(1)} fusion(f32[256,4096]{1,0:T(8,128)S(1)} %fusion.17, bf16[512,256]{0,1:T(8,128)(2,1)S(1)} %collective-permute-done.13, bf16[512,4096]{1,0:T(8,128)(2,1)} %collective-permute-done.10), kind=kOutput, calls=%fused_computation.2 | convolution fusion | flops 1075838976 | bytes 10747904 | tf_op jit(solution)/shard_map/dot_general | solution.py:67
  100.5 0.9 copy.65
  101.4 0.7 copy.60
  102.0 34.6 %all_to_all.50 = bf16[16,128,512]{2,1,0:T(8,128)(2,1)S(1)} all-to-all(bf16[16,128,512]{2,1,0:T(8,128)(2,1)S(1)} %bitcast.116), channel_id=1, replica_groups=mesh['ylo'=2,'core'=2,'yhi'=2,'x'=4,'z'=8] {'ylo','yhi','x'}, dimensions={0} | all-to-all | bytes 4194304 | tf_op jit(solution)/shard_map/all_to_all | solution.py:24
  136.7 0.3 reduce_sum.120
  137.1 11.5 %all_to_all.51 = bf16[8,64,128]{2,1,0:T(8,128)(2,1)S(1)} all-to-all(bf16[8,64,128]{2,1,0:T(8,128)(2,1)S(1)} %bitcast.135), channel_id=1, replica_groups=mesh['ylo'=2,'core'=2,'yhi'=2,'x'=4,'z'=8] {'z'}, dimensions={0} | all-to-all | bytes 262144 | tf_op jit(solution)/shard_map/all_to_all | solution.py:24
  148.6 10.3 %all_to_all.52 = bf16[8,64,128]{2,1,0:T(8,128)(2,1)S(1)} all-to-all(bf16[8,64,128]{2,1,0:T(8,128)(2,1)S(1)} %broadcast_in_dim.129), channel_id=1, replica_groups=mesh['ylo'=2,'core'=2,'yhi'=2,'x'=4,'z'=8] {'z'}, dimensions={0} | all-to-all | bytes 262144 | tf_op jit(solution)/shard_map/all_to_all | solution.py:24
  158.9 0.4 broadcast_in_dim.131
  159.3 27.1 %all_to_all.53 = bf16[16,512,128]{2,1,0:T(8,128)(2,1)S(1)} all-to-all(bf16[16,512,128]{2,1,0:T(8,128)(2,1)S(1)} %broadcast_in_dim.131), channel_id=1, replica_groups=mesh['ylo'=2,'core'=2,'yhi'=2,'x'=4,'z'=8] {'ylo','yhi','x'}, dimensions={0} | all-to-all | bytes 4194304 | tf_op jit(solution)/shard_map/all_to_all | solution.py:24
  186.6 3.6 %fusion.13 = f32[512,256]{0,1:T(8,128)S(1)} fusion(bf16[512,4096]{1,0:T(8,128)(2,1)} %collective-permute-done.10, bf16[4096,128]{1,0:T(8,128)(2,1)S(1)} %bitcast.131, bf16[4096,128]{1,0:T(8,128)(2,1)S(1)} %bitcast.129), kind=kOutput, calls=%fused_computation.18 | convolution fusion | flops 1077936128 | bytes 6815744 | tf_op jit(solution)/shard_map/dot_general | solution.py:118
  190.2 5.3 %collective-permute-start.14 = (f32[512,256]{0,1:T(8,128)S(1)}, f32[512,256]{0,1:T(8,128)S(1)}, u32[]{:S(2)}, u32[]{:S(2)}) collective-permute-start(f32[512,256]{0,1:T(8,128)S(1)} %fusion.13), channel_id=1, source_target_pairs={{0,64},{64,0},{1,65},{65,1},{2,66},{66,2},{3,67},{67,3},{4,68},{68... | collective-permute-start | bytes 1572872 | tf_op jit(solution)/shard_map/ppermute | solution.py:20
  195.5 1.3 fusion.12
  197.0 0.3 multiply_reduce_fusion.1
  197.3 0.3 multiply_reduce_fusion
  197.6 0.4 multiply_convert_fusion
  198.0 0.5 collective-permute-start.15
  198.5 1.3 fusion.15
  199.7 3.4 %fusion.1 = bf16[256,4096]{1,0:T(8,128)(2,1)S(1)} fusion(f32[256,4096]{1,0:T(8,128)S(1)} %fusion.15, bf16[512,256]{0,1:T(8,128)(2,1)S(1)} %collective-permute-done.15, bf16[512,4096]{1,0:T(8,128)(2,1)} %collective-permute-done.10), kind=kOutput, calls=%fused_computation.3 | convolution fusion | flops 1075838976 | bytes 10747904 | tf_op jit(solution)/shard_map/dot_general | solution.py:67
  203.2 0.9 copy.66
  204.1 0.7 copy.62
  204.8 30.7 %all_to_all.54 = bf16[16,128,512]{2,1,0:T(8,128)(2,1)S(1)} all-to-all(bf16[16,128,512]{2,1,0:T(8,128)(2,1)S(1)} %bitcast.118), channel_id=1, replica_groups=mesh['ylo'=2,'core'=2,'yhi'=2,'x'=4,'z'=8] {'ylo','yhi','x'}, dimensions={0} | all-to-all | bytes 4194304 | tf_op jit(solution)/shard_map/all_to_all | solution.py:24
  235.5 0.3 reduce_sum.124
  235.9 10.4 %all_to_all.55 = bf16[8,64,128]{2,1,0:T(8,128)(2,1)S(1)} all-to-all(bf16[8,64,128]{2,1,0:T(8,128)(2,1)S(1)} %bitcast.136), channel_id=1, replica_groups=mesh['ylo'=2,'core'=2,'yhi'=2,'x'=4,'z'=8] {'z'}, dimensions={0} | all-to-all | bytes 262144 | tf_op jit(solution)/shard_map/all_to_all | solution.py:24
  246.4 8.4 %all_to_all.56 = f32[4,64,128]{2,1,0:T(8,128)S(1)} all-to-all(f32[4,64,128]{2,1,0:T(8,128)S(1)} %broadcast_in_dim.132), channel_id=1, replica_groups=mesh['ylo'=2,'core'=2,'yhi'=2,'x'=4,'z'=8] {'ylo','core'}, dimensions={0} | all-to-all | bytes 262144 | tf_op jit(solution)/shard_map/all_to_all | solution.py:24
  254.8 0.7 pad_maximum_fusion.24
  (70 shorter events, 2.4 us)
Async XLA Ops:
  0.0 7.7 %copy-start = (bf16[64,512]{1,0:T(8,128)(2,1)S(1)}, bf16[64,512]{1,0:T(8,128)(2,1)}, u32[]{:S(2)}) copy-start(bf16[64,512]{1,0:T(8,128)(2,1)} %param.9) | copy-start | bytes 196612
  1.4 18.9 %collective-permute-start.1 = (f32[2,512]{1,0:T(2,128)S(1)}, f32[2,512]{1,0:T(2,128)S(1)}, u32[]{:S(2)}, u32[]{:S(2)}) collective-permute-start(f32[2,512]{1,0:T(2,128)S(1)} %pad_maximum_fusion.25), channel_id=1, source_target_pairs={{1,0},{2,1},{3,2},{4,3},{5,4},{6,5},{7,6},{8,7},{9,8},{10,9},{11,1... | collective-permute-start | bytes 12296 | tf_op jit(solution)/shard_map/ppermute | solution.py:93
  2.7 31.7 %collective-permute-start = (f32[2,512]{1,0:T(2,128)S(1)}, f32[2,512]{1,0:T(2,128)S(1)}, u32[]{:S(2)}, u32[]{:S(2)}) collective-permute-start(f32[2,512]{1,0:T(2,128)S(1)} %pad_maximum_fusion.25), channel_id=1, source_target_pairs={{0,1},{1,2},{2,3},{3,4},{4,5},{5,6},{6,7},{7,8},{8,9},{9,10},{10,1... | collective-permute-start | bytes 12296 | tf_op jit(solution)/shard_map/ppermute | solution.py:92
  8.4 16.7 %all-to-all-start = ((bf16[8,64,128]{2,1,0:T(8,128)(2,1)}), bf16[8,64,128]{2,1,0:T(8,128)(2,1)S(1)}, u32[]{:S(2)}, u32[]{:S(2)}) async-start(bf16[8,64,128]{2,1,0:T(8,128)(2,1)} %broadcast_in_dim.117), calls=%async_computation | async-start | bytes 262144 | tf_op jit(solution)/shard_map/all_to_all | solution.py:24
  17.2 59.9 %collective-permute-start.10 = (bf16[512,4096]{1,0:T(8,128)(2,1)}, bf16[512,4096]{1,0:T(8,128)(2,1)}, u32[]{:S(2)}, u32[]{:S(2)}) collective-permute-start(bf16[512,4096]{1,0:T(8,128)(2,1)} %bitcast.114), channel_id=1, source_target_pairs={{0,64},{64,0},{1,65},{65,1},{2,66},{66,2},{3,67},{67,3},{4,68},{68... | collective-permute-start | bytes 12582920 | tf_op jit(solution)/shard_map/ppermute | solution.py:20
  25.9 16.0 %all-to-all-start.1 = ((bf16[16,64,128]{2,1,0:T(8,128)(2,1)}), bf16[16,64,128]{2,1,0:T(8,128)(2,1)S(1)}, u32[]{:S(2)}, u32[]{:S(2)}) async-start(bf16[16,64,128]{2,1,0:T(8,128)(2,1)} %broadcast_in_dim.118), calls=%async_computation.1 | async-start | bytes 524288 | tf_op jit(solution)/shard_map/all_to_all | solution.py:24
  42.0 7.5 %collective-permute-start.3 = (bf16[16,64,128]{2,1,0:T(8,128)(2,1)S(1)}, bf16[16,64,128]{2,1,0:T(8,128)(2,1)S(1)}, u32[]{:S(2)}, u32[]{:S(2)}) collective-permute-start(bf16[16,64,128]{2,1,0:T(8,128)(2,1)S(1)} %all-to-all-done.1), channel_id=1, source_target_pairs={{0,7},{1,0},{2,1},{3,2},{4,3},{5,4},{6,5},{7,6},{8,15},{9,8},{10,9... | collective-permute-start | bytes 786440 | tf_op jit(solution)/shard_map/ppermute | solution.py:38
  42.0 8.8 %collective-permute-start.2 = (bf16[16,64,128]{2,1,0:T(8,128)(2,1)S(1)}, bf16[16,64,128]{2,1,0:T(8,128)(2,1)S(1)}, u32[]{:S(2)}, u32[]{:S(2)}) collective-permute-start(bf16[16,64,128]{2,1,0:T(8,128)(2,1)S(1)} %all-to-all-done.1), channel_id=1, source_target_pairs={{0,1},{1,2},{2,3},{3,4},{4,5},{5,6},{6,7},{7,0},{8,9},{9,10},{10,1... | collective-permute-start | bytes 786440 | tf_op jit(solution)/shard_map/ppermute | solution.py:38
  45.2 31.7 %all-to-all-start.2 = ((bf16[16,512,128]{2,1,0:T(8,128)(2,1)}), bf16[16,512,128]{2,1,0:T(8,128)(2,1)S(1)}, u32[]{:S(2)}, u32[]{:S(2)}) async-start(bf16[16,512,128]{2,1,0:T(8,128)(2,1)} %broadcast_in_dim.128), calls=%async_computation.2 | async-start | bytes 4194304 | tf_op jit(solution)/shard_map/all_to_all | solution.py:24
  49.5 5.3 %collective-permute-start.5 = (bf16[16,64,128]{2,1,0:T(8,128)(2,1)S(1)}, bf16[16,64,128]{2,1,0:T(8,128)(2,1)S(1)}, u32[]{:S(2)}, u32[]{:S(2)}) collective-permute-start(bf16[16,64,128]{2,1,0:T(8,128)(2,1)S(1)} %collective-permute-done.3), channel_id=1, source_target_pairs={{0,7},{1,0},{2,1},{3,2},{4,3},{5,4},{6,5},{7,6},{8,15},{9,8},{10,9... | collective-permute-start | bytes 786440 | tf_op jit(solution)/shard_map/ppermute | solution.py:38
  50.8 6.4 %collective-permute-start.4 = (bf16[16,64,128]{2,1,0:T(8,128)(2,1)S(1)}, bf16[16,64,128]{2,1,0:T(8,128)(2,1)S(1)}, u32[]{:S(2)}, u32[]{:S(2)}) collective-permute-start(bf16[16,64,128]{2,1,0:T(8,128)(2,1)S(1)} %collective-permute-done.2), channel_id=1, source_target_pairs={{0,1},{1,2},{2,3},{3,4},{4,5},{5,6},{6,7},{7,0},{8,9},{9,10},{10,1... | collective-permute-start | bytes 786440 | tf_op jit(solution)/shard_map/ppermute | solution.py:38
  54.8 8.2 %collective-permute-start.7 = (bf16[16,64,128]{2,1,0:T(8,128)(2,1)S(1)}, bf16[16,64,128]{2,1,0:T(8,128)(2,1)S(1)}, u32[]{:S(2)}, u32[]{:S(2)}) collective-permute-start(bf16[16,64,128]{2,1,0:T(8,128)(2,1)S(1)} %collective-permute-done.5), channel_id=1, source_target_pairs={{0,7},{1,0},{2,1},{3,2},{4,3},{5,4},{6,5},{7,6},{8,15},{9,8},{10,9... | collective-permute-start | bytes 786440 | tf_op jit(solution)/shard_map/ppermute | solution.py:38
  57.2 8.6 %collective-permute-start.6 = (bf16[16,64,128]{2,1,0:T(8,128)(2,1)S(1)}, bf16[16,64,128]{2,1,0:T(8,128)(2,1)S(1)}, u32[]{:S(2)}, u32[]{:S(2)}) collective-permute-start(bf16[16,64,128]{2,1,0:T(8,128)(2,1)S(1)} %collective-permute-done.4), channel_id=1, source_target_pairs={{0,1},{1,2},{2,3},{3,4},{4,5},{5,6},{6,7},{7,0},{8,9},{9,10},{10,1... | collective-permute-start | bytes 786440 | tf_op jit(solution)/shard_map/ppermute | solution.py:38
  63.0 9.6 %collective-permute-start.9 = (bf16[8,64,128]{2,1,0:T(8,128)(2,1)S(1)}, bf16[8,64,128]{2,1,0:T(8,128)(2,1)S(1)}, u32[]{:S(2)}, u32[]{:S(2)}) collective-permute-start(bf16[8,64,128]{2,1,0:T(8,128)(2,1)S(1)} %slice.103), channel_id=1, source_target_pairs={{0,7},{1,0},{2,1},{3,2},{4,3},{5,4},{6,5},{7,6},{8,15},{9,8},{10,9... | collective-permute-start | bytes 393224 | tf_op jit(solution)/shard_map/ppermute | solution.py:38
  65.8 6.8 %collective-permute-start.8 = (bf16[8,64,128]{2,1,0:T(8,128)(2,1)S(1)}, bf16[8,64,128]{2,1,0:T(8,128)(2,1)S(1)}, u32[]{:S(2)}, u32[]{:S(2)}) collective-permute-start(bf16[8,64,128]{2,1,0:T(8,128)(2,1)S(1)} %slice.102), channel_id=1, source_target_pairs={{0,1},{1,2},{2,3},{3,4},{4,5},{5,6},{6,7},{7,0},{8,9},{9,10},{10,1... | collective-permute-start | bytes 393224 | tf_op jit(solution)/shard_map/ppermute | solution.py:38
  72.6 2.9 %copy-start.1 = (bf16[1,512,4096]{2,1,0:T(8,128)(2,1)S(1)}, bf16[1,512,4096]{2,1,0:T(8,128)(2,1)}, u32[]{:S(2)}) copy-start(bf16[1,512,4096]{2,1,0:T(8,128)(2,1)} %param.6) | copy-start | bytes 12582916
  72.8 1.0 copy-start.4
  72.8 1.3 copy-start.6
  77.1 11.8 %copy-start.5 = (bf16[8,8,64,128]{3,2,1,0:T(8,128)(2,1)S(1)}, bf16[8,8,64,128]{3,2,1,0:T(8,128)(2,1)}, u32[]{:S(2)}) copy-start(bf16[8,8,64,128]{3,2,1,0:T(8,128)(2,1)} %copy-done.4) | copy-start | bytes 3145732
  77.1 11.8 %copy-start.7 = (bf16[8,8,64,128]{3,2,1,0:T(8,128)(2,1)S(1)}, bf16[8,8,64,128]{3,2,1,0:T(8,128)(2,1)}, u32[]{:S(2)}) copy-start(bf16[8,8,64,128]{3,2,1,0:T(8,128)(2,1)} %copy-done.6) | copy-start | bytes 3145732
  80.8 11.9 %copy-start.2 = (bf16[1,512,4096]{2,1,0:T(8,128)(2,1)S(1)}, bf16[1,512,4096]{2,1,0:T(8,128)(2,1)}, u32[]{:S(2)}) copy-start(bf16[1,512,4096]{2,1,0:T(8,128)(2,1)} %param.6) | copy-start | bytes 12582916
  80.8 13.2 %collective-permute-start.12 = (f32[512,256]{0,1:T(8,128)S(1)}, f32[512,256]{0,1:T(8,128)S(1)}, u32[]{:S(2)}, u32[]{:S(2)}) collective-permute-start(f32[512,256]{0,1:T(8,128)S(1)} %fusion.11), channel_id=1, source_target_pairs={{0,64},{64,0},{1,65},{65,1},{2,66},{66,2},{3,67},{67,3},{4,68},{68... | collective-permute-start | bytes 1572872 | tf_op jit(solution)/shard_map/ppermute | solution.py:20
  92.4 2.0 collective-permute-start.11
  95.4 1.6 collective-permute-start.13
  136.7 11.9 %copy-start.8 = (f32[64,512]{1,0:T(8,128)S(1)}, f32[64,512]{1,0:T(8,128)}, u32[]{:S(2)}) copy-start(f32[64,512]{1,0:T(8,128)} %param.11) | copy-start | bytes 393220
  186.5 9.0 %copy-start.3 = (bf16[1,512,4096]{2,1,0:T(8,128)(2,1)S(1)}, bf16[1,512,4096]{2,1,0:T(8,128)(2,1)}, u32[]{:S(2)}) copy-start(bf16[1,512,4096]{2,1,0:T(8,128)(2,1)} %param.6) | copy-start | bytes 12582916
  190.2 6.9 %collective-permute-start.14 = (f32[512,256]{0,1:T(8,128)S(1)}, f32[512,256]{0,1:T(8,128)S(1)}, u32[]{:S(2)}, u32[]{:S(2)}) collective-permute-start(f32[512,256]{0,1:T(8,128)S(1)} %fusion.13), channel_id=1, source_target_pairs={{0,64},{64,0},{1,65},{65,1},{2,66},{66,2},{3,67},{67,3},{4,68},{68... | collective-permute-start | bytes 1572872 | tf_op jit(solution)/shard_map/ppermute | solution.py:20
  198.0 1.7 collective-permute-start.15

commit v10 on v9

--- a/solution.py
+++ b/solution.py
@@ -85,16 +85,20 @@
     return (vector - unit_values * inner) / root_mean
 
 
-def turn_counts(text_mask, turn_ids):
-    n = lax.axis_size(SHARD)
+def turn_rows(text_mask, turn_ids, cols):
+    flat = jnp.concatenate([turn_ids.astype(jnp.float32), text_mask]).astype(jnp.bfloat16)
+    return jnp.pad(flat, (0, -flat.shape[0] % (16 * cols))).reshape(-1, cols)
+
+
+def turn_counts(text_mask, turn_ids, before, after):
+    n = turn_ids.shape[0]
     turns = turn_ids.astype(jnp.float32)
-    here = jnp.stack([turns, text_mask])
-    left = lax.ppermute(here, SHARD, [(i, i + 1) for i in range(n - 1)])
-    right = lax.ppermute(here, SHARD, [(i + 1, i) for i in range(n - 1)])
-    return sum(
-        jnp.sum(jnp.where(turns[:, None] == other[0][None, :], other[1][None, :], 0.0), axis=1)
-        for other in (here, left, right)
-    )
+    counts = jnp.sum(jnp.where(turns[:, None] == turns[None, :], text_mask[None, :], 0.0), axis=1)
+    for rows, there in (before, after):
+        flat = rows.astype(jnp.float32).reshape(-1)
+        same = (turns[:, None] == flat[None, :n]) & there
+        counts = counts + jnp.sum(jnp.where(same, flat[None, n : 2 * n], 0.0), axis=1)
+    return counts
 
 
 def local(acts, token_ids, turn_ids, value_weight, norm_gain, query_grad):
@@ -126,13 +130,39 @@
     gain_square = gain * gain
     query = own(query_grad)
 
-    line = gather_line(own(value_weight))
-    block, line = lax.optimization_barrier((query.astype(jnp.bfloat16), line))
+    n_z = lax.axis_size("z")
+    tokens = turn_rows(text_mask, ids, cols)
+    count = tokens.shape[0]
+    rows = value_weight.shape[0]
+    line = spread(jnp.concatenate([own(value_weight), tokens]), "z")
+    line, tokens = line[:, :rows].reshape(-1, cols), line[:, rows:]
+    block = jnp.concatenate([query.astype(jnp.bfloat16), tokens[0], tokens[n_z - 1]])
+    block, line = lax.optimization_barrier((block, line))
     plane = spread(block, PLANE)
     plane, line = lax.optimization_barrier((plane, line))
+    plane, ends = plane[:, :rows], plane[:, rows:]
+    place, chain = lax.axis_index("z"), lax.axis_index(("yhi", "x"))
+    n_chain = lax.axis_size(("yhi", "x"))
+    base = lax.axis_index("ylo") * n_chain
+
+    def pick(array, index):
+        return lax.dynamic_index_in_dim(array, index, keepdims=False)
+
+    before = jnp.where(
+        place > 0,
+        pick(tokens, jnp.maximum(place - 1, 0)),
+        pick(ends, base + jnp.maximum(chain - 1, 0))[count:],
+    )
+    after = jnp.where(
+        place < n_z - 1,
+        pick(tokens, jnp.minimum(place + 1, n_z - 1)),
+        pick(ends, base + jnp.minimum(chain + 1, n_chain - 1))[:count],
+    )
+    before = (before, (place > 0) | (chain > 0))
+    after = (after, (place < n_z - 1) | (chain < n_chain - 1))
     tangent = project(ring_gather(plane).reshape(lax.axis_size("ylo"), -1, cols))
     values = project(gather_plane(line))
-    own_count = turn_counts(text_mask, ids)
+    own_count = turn_counts(text_mask, ids, before, after)
     turn_weight = text_mask / (jnp.maximum(own_count, 1.0) * jnp.float32(turn_total))
     root_mean = jnp.sqrt(jnp.mean(values * values, axis=-1, keepdims=True) + 1e-06)
     unit_values = values / root_mean

time: 256 us -> 250 us (0.977)
  starting transfers between devices: 51.4 us -> 45.8 us
    ppermute x2 -> x0, starting transfers between devices: 6.29 us -> none  [the longest x1 5 us: turn_counts(): left = lax.ppermute(here, SHARD, [(i, i + 1) for i in range(n - 1)])]
    ppermute x8, waiting for transfers between devices: 16.2 us -> 12 us  [shift(): return lax.ppermute(value, 'z', [(i, (i + step) % n) for i in range(n)])]
    ppermute x8, starting transfers between devices: 8.13 us -> 11.6 us  [shift(): return lax.ppermute(value, 'z', [(i, (i + step) % n) for i in range(n)])]
    all_to_all x3, waiting for transfers between devices: 11.9 us -> 14.7 us  [exchange(): return lax.all_to_all(blocks, axes, split_axis=0, concat_axis=0, tiled=True)]
  transfers between devices with their start and end apart: 19 -> 17, of which waited for: 9 -> 8; matrix products, arithmetic and copies ran while one was open for 6% -> 6% of each run, Pallas kernels for 0% -> 0%
where the time goes in v10:
time: 250 us; the launch traced here: 249 us
  blocking collectives  134 us (54%)
  starting transfers between devices  45.8 us (18%)
  waiting for transfers between devices  27.3 us (11%)
  matrix products  24 us (10%)
  local copies, waits for them, and re-layouts  12 us (5%)
  other arithmetic  5.49 us (2%)
    all_to_all x7, blocking collectives, exchange(): return lax.all_to_all(blocks, axes, split_axis=0, concat_axis=0, tiled=True)  134 us
    all_to_all x3, starting transfers between devices, exchange(): return lax.all_to_all(blocks, axes, split_axis=0, concat_axis=0, tiled=True)  19.5 us
    all_to_all x3, waiting for transfers between devices, exchange(): return lax.all_to_all(blocks, axes, split_axis=0, concat_axis=0, tiled=True)  14.7 us
    ppermute x6, starting transfers between devices, core_swap(): return lax.ppermute(value, 'core', [(0, 1), (1, 0)])  14.7 us
    ppermute x8, waiting for transfers between devices, shift(): return lax.ppermute(value, 'z', [(i, (i + step) % n) for i in range(n)])  12 us
    ppermute x8, starting transfers between devices, shift(): return lax.ppermute(value, 'z', [(i, (i + step) % n) for i in range(n)])  11.6 us
    dot_general x3, matrix products, project(): jnp.dot(other_inputs, half, preferred_element_type=jnp.float32)  10.7 us
    dot_general x4, matrix products, outer(): lax.dot_general(part, rows, (((0,), (0,)), ((), ())), preferred_element_t...  9.4 us
  transfers between devices with their start and end apart: 17, of which 8 were waited for; matrix products, arithmetic and copies ran while one was open for 6% of the time, Pallas kernels for 0%

profile of v10, /device:TPU:1, one launch (start us, length us, event | category | flops | bytes accessed | tf_op | source)
XLA Modules:
  0.0 249.3 jit_solution(18308465361257117042)
XLA Ops:
  0.0 0.7 compare_convert_fusion
  0.7 0.7 convert_element_type.64
  1.5 0.7 broadcast_in_dim.116
  2.1 9.0 %all-to-all-start = ((bf16[8,80,128]{2,1,0:T(8,128)(2,1)}), bf16[8,80,128]{2,1,0:T(8,128)(2,1)S(1)}, u32[]{:S(2)}, u32[]{:S(2)}) async-start(bf16[8,80,128]{2,1,0:T(8,128)(2,1)} %broadcast_in_dim.116), calls=%async_computation | async-start | bytes 327680 | tf_op jit(solution)/shard_map/all_to_all | solution.py:24
  11.2 1.0 collective-permute-start.8
  12.1 0.8 dynamic-slice_convert_fusion
  12.9 6.4 %all-to-all-done = bf16[8,80,128]{2,1,0:T(8,128)(2,1)S(1)} async-done(((bf16[8,80,128]{2,1,0:T(8,128)(2,1)}), bf16[8,80,128]{2,1,0:T(8,128)(2,1)S(1)}, u32[]{:S(2)}, u32[]{:S(2)}) %all-to-all-start) | async-done | bytes 163872 | tf_op jit(solution)/shard_map/all_to_all | solution.py:24
  19.3 0.8 broadcast_in_dim.117
  20.1 6.8 %all-to-all-start.1 = ((bf16[16,96,128]{2,1,0:T(8,128)(2,1)}), bf16[16,96,128]{2,1,0:T(8,128)(2,1)S(1)}, u32[]{:S(2)}, u32[]{:S(2)}) async-start(bf16[16,96,128]{2,1,0:T(8,128)(2,1)} %broadcast_in_dim.117), calls=%async_computation.1 | async-start | bytes 786432 | tf_op jit(solution)/shard_map/all_to_all | solution.py:24
  27.1 8.3 %all-to-all-done.1 = bf16[16,96,128]{2,1,0:T(8,128)(2,1)S(1)} async-done(((bf16[16,96,128]{2,1,0:T(8,128)(2,1)}), bf16[16,96,128]{2,1,0:T(8,128)(2,1)S(1)}, u32[]{:S(2)}, u32[]{:S(2)}) %all-to-all-start.1) | async-done | bytes 393248 | tf_op jit(solution)/shard_map/all_to_all | solution.py:24
  35.4 0.5 collective-permute-start
  35.9 2.3 collective-permute-start.1
  38.2 1.7 broadcast_in_dim.132
  39.9 3.7 %all-to-all-start.2 = ((bf16[16,512,128]{2,1,0:T(8,128)(2,1)}), bf16[16,512,128]{2,1,0:T(8,128)(2,1)S(1)}, u32[]{:S(2)}, u32[]{:S(2)}) async-start(bf16[16,512,128]{2,1,0:T(8,128)(2,1)} %broadcast_in_dim.132), calls=%async_computation.2 | async-start | bytes 4194304 | tf_op jit(solution)/shard_map/all_to_all | solution.py:24
  43.7 0.7 select_reduce_fusion.1
  44.4 0.5 broadcast_in_dim.122
  45.1 2.7 %collective-permute-start.3 = (bf16[16,64,128]{2,1,0:T(8,128)(2,1)S(1)}, bf16[16,64,128]{2,1,0:T(8,128)(2,1)S(1)}, u32[]{:S(2)}, u32[]{:S(2)}) collective-permute-start(bf16[16,64,128]{2,1,0:T(8,128)(2,1)S(1)} %collective-permute-done.1), channel_id=1, source_target_pairs={{0,7},{1,0},{2,1},{3,2},{4,3},{5,4},{6,5},{7,6},{8,15},{9,8},{10,9... | collective-permute-start | bytes 786440 | tf_op jit(solution)/shard_map/ppermute | solution.py:38
  47.8 3.7 %collective-permute-done.2 = bf16[16,64,128]{2,1,0:T(8,128)(2,1)S(1)} collective-permute-done((bf16[16,64,128]{2,1,0:T(8,128)(2,1)S(1)}, bf16[16,64,128]{2,1,0:T(8,128)(2,1)S(1)}, u32[]{:S(2)}, u32[]{:S(2)}) %collective-permute-start.2) | collective-permute-done | bytes 262176 | tf_op jit(solution)/shard_map/ppermute | solution.py:38
  51.5 3.0 %collective-permute-start.5 = (bf16[16,64,128]{2,1,0:T(8,128)(2,1)S(1)}, bf16[16,64,128]{2,1,0:T(8,128)(2,1)S(1)}, u32[]{:S(2)}, u32[]{:S(2)}) collective-permute-start(bf16[16,64,128]{2,1,0:T(8,128)(2,1)S(1)} %collective-permute-done.3), channel_id=1, source_target_pairs={{0,7},{1,0},{2,1},{3,2},{4,3},{5,4},{6,5},{7,6},{8,15},{9,8},{10,9... | collective-permute-start | bytes 786440 | tf_op jit(solution)/shard_map/ppermute | solution.py:38
  54.5 4.8 %collective-permute-done.4 = bf16[16,64,128]{2,1,0:T(8,128)(2,1)S(1)} collective-permute-done((bf16[16,64,128]{2,1,0:T(8,128)(2,1)S(1)}, bf16[16,64,128]{2,1,0:T(8,128)(2,1)S(1)}, u32[]{:S(2)}, u32[]{:S(2)}) %collective-permute-start.4) | collective-permute-done | bytes 262176 | tf_op jit(solution)/shard_map/ppermute | solution.py:38
  59.5 3.1 %collective-permute-start.7 = (bf16[8,64,128]{2,1,0:T(8,128)(2,1)S(1)}, bf16[8,64,128]{2,1,0:T(8,128)(2,1)S(1)}, u32[]{:S(2)}, u32[]{:S(2)}) collective-permute-start(bf16[8,64,128]{2,1,0:T(8,128)(2,1)S(1)} %slice.151), channel_id=1, source_target_pairs={{0,7},{1,0},{2,1},{3,2},{4,3},{5,4},{6,5},{7,6},{8,15},{9,8},{10,9... | collective-permute-start | bytes 393224 | tf_op jit(solution)/shard_map/ppermute | solution.py:38
  62.6 3.5 %collective-permute-done.6 = bf16[8,64,128]{2,1,0:T(8,128)(2,1)S(1)} collective-permute-done((bf16[8,64,128]{2,1,0:T(8,128)(2,1)S(1)}, bf16[8,64,128]{2,1,0:T(8,128)(2,1)S(1)}, u32[]{:S(2)}, u32[]{:S(2)}) %collective-permute-start.6) | collective-permute-done | bytes 131104 | tf_op jit(solution)/shard_map/ppermute | solution.py:38
  66.4 1.0 copy-done.4
  67.4 0.3 copy-done.6
  67.7 1.4 copy-done.1
  69.2 1.3 fusion.8
  70.5 0.2 fusion.39
  70.7 3.6 %fusion.11 = f32[512,256]{0,1:T(8,128)S(1)} fusion(bf16[512,4096]{1,0:T(8,128)(2,1)} %collective-permute-done.8, bf16[4096,128]{1,0:T(8,128)(2,1)S(1)} %bitcast.137, bf16[4096,128]{1,0:T(8,128)(2,1)S(1)} %bitcast.135), kind=kOutput, calls=%fused_computation.16 | convolution fusion | flops 1077936128 | bytes 6815744 | tf_op jit(solution)/shard_map/dot_general | solution.py:122
  74.3 7.2 %collective-permute-start.10 = (f32[512,256]{0,1:T(8,128)S(1)}, f32[512,256]{0,1:T(8,128)S(1)}, u32[]{:S(2)}, u32[]{:S(2)}) collective-permute-start(f32[512,256]{0,1:T(8,128)S(1)} %fusion.11), channel_id=1, source_target_pairs={{0,64},{64,0},{1,65},{65,1},{2,66},{66,2},{3,67},{67,3},{4,68},{68... | collective-permute-start | bytes 1572872 | tf_op jit(solution)/shard_map/ppermute | solution.py:20
  81.5 3.5 %fusion.9 = f32[512,256]{0,1:T(8,128)S(1)} fusion(bf16[512,4096]{1,0:T(8,128)(2,1)} %collective-permute-done.8, bf16[4096,128]{1,0:T(8,128)(2,1)S(1)} %bitcast.134, bf16[4096,128]{1,0:T(8,128)(2,1)S(1)} %bitcast.132), kind=kOutput, calls=%fused_computation.14 | convolution fusion | flops 1077936128 | bytes 6815744 | tf_op jit(solution)/shard_map/dot_general | solution.py:122
  85.0 0.3 collective-permute-start.9
  85.3 1.3 fusion.10
  86.7 0.3 collective-permute-done.9
  87.0 0.3 multiply_reduce_fusion.3
  87.3 0.3 multiply_reduce_fusion.2
  87.6 0.4 multiply_convert_fusion.1
  88.0 0.5 collective-permute-start.11
  88.5 1.3 fusion.17
  89.8 3.4 %fusion = bf16[256,4096]{1,0:T(8,128)(2,1)S(1)} fusion(f32[256,4096]{1,0:T(8,128)S(1)} %fusion.17, bf16[512,256]{0,1:T(8,128)(2,1)S(1)} %collective-permute-done.11, bf16[512,4096]{1,0:T(8,128)(2,1)} %collective-permute-done.8), kind=kOutput, calls=%fused_computation.2 | convolution fusion | flops 1075838976 | bytes 10747904 | tf_op jit(solution)/shard_map/dot_general | solution.py:67
  93.3 0.9 copy.57
  94.2 0.7 copy.52
  94.9 34.6 %all_to_all.50 = bf16[16,128,512]{2,1,0:T(8,128)(2,1)S(1)} all-to-all(bf16[16,128,512]{2,1,0:T(8,128)(2,1)S(1)} %bitcast.126), channel_id=1, replica_groups=mesh['ylo'=2,'core'=2,'yhi'=2,'x'=4,'z'=8] {'ylo','yhi','x'}, dimensions={0} | all-to-all | bytes 4194304 | tf_op jit(solution)/shard_map/all_to_all | solution.py:24
  129.5 0.3 reduce_sum.120
  129.9 12.4 %all_to_all.51 = bf16[8,64,128]{2,1,0:T(8,128)(2,1)S(1)} all-to-all(bf16[8,64,128]{2,1,0:T(8,128)(2,1)S(1)} %bitcast.145), channel_id=1, replica_groups=mesh['ylo'=2,'core'=2,'yhi'=2,'x'=4,'z'=8] {'z'}, dimensions={0} | all-to-all | bytes 262144 | tf_op jit(solution)/shard_map/all_to_all | solution.py:24
  142.4 10.3 %all_to_all.52 = bf16[8,64,128]{2,1,0:T(8,128)(2,1)S(1)} all-to-all(bf16[8,64,128]{2,1,0:T(8,128)(2,1)S(1)} %broadcast_in_dim.133), channel_id=1, replica_groups=mesh['ylo'=2,'core'=2,'yhi'=2,'x'=4,'z'=8] {'z'}, dimensions={0} | all-to-all | bytes 262144 | tf_op jit(solution)/shard_map/all_to_all | solution.py:24
  152.7 0.4 broadcast_in_dim.135
  153.1 27.1 %all_to_all.53 = bf16[16,512,128]{2,1,0:T(8,128)(2,1)S(1)} all-to-all(bf16[16,512,128]{2,1,0:T(8,128)(2,1)S(1)} %broadcast_in_dim.135), channel_id=1, replica_groups=mesh['ylo'=2,'core'=2,'yhi'=2,'x'=4,'z'=8] {'ylo','yhi','x'}, dimensions={0} | all-to-all | bytes 4194304 | tf_op jit(solution)/shard_map/all_to_all | solution.py:24
  180.3 3.6 %fusion.13 = f32[512,256]{0,1:T(8,128)S(1)} fusion(bf16[512,4096]{1,0:T(8,128)(2,1)} %collective-permute-done.8, bf16[4096,128]{1,0:T(8,128)(2,1)S(1)} %bitcast.141, bf16[4096,128]{1,0:T(8,128)(2,1)S(1)} %bitcast.139), kind=kOutput, calls=%fused_computation.18 | convolution fusion | flops 1077936128 | bytes 6815744 | tf_op jit(solution)/shard_map/dot_general | solution.py:122
  184.0 5.1 %collective-permute-start.12 = (f32[512,256]{0,1:T(8,128)S(1)}, f32[512,256]{0,1:T(8,128)S(1)}, u32[]{:S(2)}, u32[]{:S(2)}) collective-permute-start(f32[512,256]{0,1:T(8,128)S(1)} %fusion.13), channel_id=1, source_target_pairs={{0,64},{64,0},{1,65},{65,1},{2,66},{66,2},{3,67},{67,3},{4,68},{68... | collective-permute-start | bytes 1572872 | tf_op jit(solution)/shard_map/ppermute | solution.py:20
  189.1 1.3 fusion.12
  190.4 0.2 collective-permute-done.12
  190.6 0.3 multiply_reduce_fusion.1
  190.9 0.3 multiply_reduce_fusion
  191.2 0.4 multiply_convert_fusion
  191.6 0.7 collective-permute-start.13
  192.3 1.3 fusion.15
  193.6 3.4 %fusion.1 = bf16[256,4096]{1,0:T(8,128)(2,1)S(1)} fusion(f32[256,4096]{1,0:T(8,128)S(1)} %fusion.15, bf16[512,256]{0,1:T(8,128)(2,1)S(1)} %collective-permute-done.13, bf16[512,4096]{1,0:T(8,128)(2,1)} %collective-permute-done.8), kind=kOutput, calls=%fused_computation.3 | convolution fusion | flops 1075838976 | bytes 10747904 | tf_op jit(solution)/shard_map/dot_general | solution.py:67
  197.0 0.9 copy.58
  197.9 0.7 copy.54
  198.6 30.7 %all_to_all.54 = bf16[16,128,512]{2,1,0:T(8,128)(2,1)S(1)} all-to-all(bf16[16,128,512]{2,1,0:T(8,128)(2,1)S(1)} %bitcast.128), channel_id=1, replica_groups=mesh['ylo'=2,'core'=2,'yhi'=2,'x'=4,'z'=8] {'ylo','yhi','x'}, dimensions={0} | all-to-all | bytes 4194304 | tf_op jit(solution)/shard_map/all_to_all | solution.py:24
  229.3 0.3 reduce_sum.124
  229.7 10.4 %all_to_all.55 = bf16[8,64,128]{2,1,0:T(8,128)(2,1)S(1)} all-to-all(bf16[8,64,128]{2,1,0:T(8,128)(2,1)S(1)} %bitcast.146), channel_id=1, replica_groups=mesh['ylo'=2,'core'=2,'yhi'=2,'x'=4,'z'=8] {'z'}, dimensions={0} | all-to-all | bytes 262144 | tf_op jit(solution)/shard_map/all_to_all | solution.py:24
  240.2 8.4 %all_to_all.56 = f32[4,64,128]{2,1,0:T(8,128)S(1)} all-to-all(f32[4,64,128]{2,1,0:T(8,128)S(1)} %broadcast_in_dim.136), channel_id=1, replica_groups=mesh['ylo'=2,'core'=2,'yhi'=2,'x'=4,'z'=8] {'ylo','core'}, dimensions={0} | all-to-all | bytes 262144 | tf_op jit(solution)/shard_map/all_to_all | solution.py:24
  248.6 0.7 pad_maximum_fusion.24
  (77 shorter events, 1.7 us)
Async XLA Ops:
  0.0 1.4 copy-start
  0.0 26.9 %copy-start.9 = (f32[512]{0:T(512)S(1)}, f32[512]{0:T(512)}, u32[]{:S(2)}) copy-start(f32[512]{0:T(512)} %param.10) | copy-start | bytes 6148
  2.1 17.2 %all-to-all-start = ((bf16[8,80,128]{2,1,0:T(8,128)(2,1)}), bf16[8,80,128]{2,1,0:T(8,128)(2,1)S(1)}, u32[]{:S(2)}, u32[]{:S(2)}) async-start(bf16[8,80,128]{2,1,0:T(8,128)(2,1)} %broadcast_in_dim.116), calls=%async_computation | async-start | bytes 327680 | tf_op jit(solution)/shard_map/all_to_all | solution.py:24
  11.2 59.5 %collective-permute-start.8 = (bf16[512,4096]{1,0:T(8,128)(2,1)}, bf16[512,4096]{1,0:T(8,128)(2,1)}, u32[]{:S(2)}, u32[]{:S(2)}) collective-permute-start(bf16[512,4096]{1,0:T(8,128)(2,1)} %bitcast.124), channel_id=1, source_target_pairs={{0,64},{64,0},{1,65},{65,1},{2,66},{66,2},{3,67},{67,3},{4,68},{68... | collective-permute-start | bytes 12582920 | tf_op jit(solution)/shard_map/ppermute | solution.py:20
  20.1 15.3 %all-to-all-start.1 = ((bf16[16,96,128]{2,1,0:T(8,128)(2,1)}), bf16[16,96,128]{2,1,0:T(8,128)(2,1)S(1)}, u32[]{:S(2)}, u32[]{:S(2)}) async-start(bf16[16,96,128]{2,1,0:T(8,128)(2,1)} %broadcast_in_dim.117), calls=%async_computation.1 | async-start | bytes 786432 | tf_op jit(solution)/shard_map/all_to_all | solution.py:24
  35.4 9.5 %collective-permute-start = (bf16[16,64,128]{2,1,0:T(8,128)(2,1)S(1)}, bf16[16,64,128]{2,1,0:T(8,128)(2,1)S(1)}, u32[]{:S(2)}, u32[]{:S(2)}) collective-permute-start(bf16[16,64,128]{2,1,0:T(8,128)(2,1)S(1)} %slice.123), channel_id=1, source_target_pairs={{0,1},{1,2},{2,3},{3,4},{4,5},{5,6},{6,7},{7,0},{8,9},{9,10},{10,1... | collective-permute-start | bytes 786440 | tf_op jit(solution)/shard_map/ppermute | solution.py:38
  35.9 9.1 %collective-permute-start.1 = (bf16[16,64,128]{2,1,0:T(8,128)(2,1)S(1)}, bf16[16,64,128]{2,1,0:T(8,128)(2,1)S(1)}, u32[]{:S(2)}, u32[]{:S(2)}) collective-permute-start(bf16[16,64,128]{2,1,0:T(8,128)(2,1)S(1)} %slice.123), channel_id=1, source_target_pairs={{0,7},{1,0},{2,1},{3,2},{4,3},{5,4},{6,5},{7,6},{8,15},{9,8},{10,9... | collective-permute-start | bytes 786440 | tf_op jit(solution)/shard_map/ppermute | solution.py:38
  39.9 30.5 %all-to-all-start.2 = ((bf16[16,512,128]{2,1,0:T(8,128)(2,1)}), bf16[16,512,128]{2,1,0:T(8,128)(2,1)S(1)}, u32[]{:S(2)}, u32[]{:S(2)}) async-start(bf16[16,512,128]{2,1,0:T(8,128)(2,1)} %broadcast_in_dim.132), calls=%async_computation.2 | async-start | bytes 4194304 | tf_op jit(solution)/shard_map/all_to_all | solution.py:24
  45.0 6.5 %collective-permute-start.2 = (bf16[16,64,128]{2,1,0:T(8,128)(2,1)S(1)}, bf16[16,64,128]{2,1,0:T(8,128)(2,1)S(1)}, u32[]{:S(2)}, u32[]{:S(2)}) collective-permute-start(bf16[16,64,128]{2,1,0:T(8,128)(2,1)S(1)} %collective-permute-done), channel_id=1, source_target_pairs={{0,1},{1,2},{2,3},{3,4},{4,5},{5,6},{6,7},{7,0},{8,9},{9,10},{10,1... | collective-permute-start | bytes 786440 | tf_op jit(solution)/shard_map/ppermute | solution.py:38
  45.1 6.4 %collective-permute-start.3 = (bf16[16,64,128]{2,1,0:T(8,128)(2,1)S(1)}, bf16[16,64,128]{2,1,0:T(8,128)(2,1)S(1)}, u32[]{:S(2)}, u32[]{:S(2)}) collective-permute-start(bf16[16,64,128]{2,1,0:T(8,128)(2,1)S(1)} %collective-permute-done.1), channel_id=1, source_target_pairs={{0,7},{1,0},{2,1},{3,2},{4,3},{5,4},{6,5},{7,6},{8,15},{9,8},{10,9... | collective-permute-start | bytes 786440 | tf_op jit(solution)/shard_map/ppermute | solution.py:38
  51.5 7.9 %collective-permute-start.4 = (bf16[16,64,128]{2,1,0:T(8,128)(2,1)S(1)}, bf16[16,64,128]{2,1,0:T(8,128)(2,1)S(1)}, u32[]{:S(2)}, u32[]{:S(2)}) collective-permute-start(bf16[16,64,128]{2,1,0:T(8,128)(2,1)S(1)} %collective-permute-done.2), channel_id=1, source_target_pairs={{0,1},{1,2},{2,3},{3,4},{4,5},{5,6},{6,7},{7,0},{8,9},{9,10},{10,1... | collective-permute-start | bytes 786440 | tf_op jit(solution)/shard_map/ppermute | solution.py:38
  51.5 8.0 %collective-permute-start.5 = (bf16[16,64,128]{2,1,0:T(8,128)(2,1)S(1)}, bf16[16,64,128]{2,1,0:T(8,128)(2,1)S(1)}, u32[]{:S(2)}, u32[]{:S(2)}) collective-permute-start(bf16[16,64,128]{2,1,0:T(8,128)(2,1)S(1)} %collective-permute-done.3), channel_id=1, source_target_pairs={{0,7},{1,0},{2,1},{3,2},{4,3},{5,4},{6,5},{7,6},{8,15},{9,8},{10,9... | collective-permute-start | bytes 786440 | tf_op jit(solution)/shard_map/ppermute | solution.py:38
  59.3 6.8 %collective-permute-start.6 = (bf16[8,64,128]{2,1,0:T(8,128)(2,1)S(1)}, bf16[8,64,128]{2,1,0:T(8,128)(2,1)S(1)}, u32[]{:S(2)}, u32[]{:S(2)}) collective-permute-start(bf16[8,64,128]{2,1,0:T(8,128)(2,1)S(1)} %slice.150), channel_id=1, source_target_pairs={{0,1},{1,2},{2,3},{3,4},{4,5},{5,6},{6,7},{7,0},{8,9},{9,10},{10,1... | collective-permute-start | bytes 393224 | tf_op jit(solution)/shard_map/ppermute | solution.py:38
  59.5 6.7 %collective-permute-start.7 = (bf16[8,64,128]{2,1,0:T(8,128)(2,1)S(1)}, bf16[8,64,128]{2,1,0:T(8,128)(2,1)S(1)}, u32[]{:S(2)}, u32[]{:S(2)}) collective-permute-start(bf16[8,64,128]{2,1,0:T(8,128)(2,1)S(1)} %slice.151), channel_id=1, source_target_pairs={{0,7},{1,0},{2,1},{3,2},{4,3},{5,4},{6,5},{7,6},{8,15},{9,8},{10,9... | collective-permute-start | bytes 393224 | tf_op jit(solution)/shard_map/ppermute | solution.py:38
  66.2 2.9 %copy-start.1 = (bf16[1,512,4096]{2,1,0:T(8,128)(2,1)S(1)}, bf16[1,512,4096]{2,1,0:T(8,128)(2,1)}, u32[]{:S(2)}) copy-start(bf16[1,512,4096]{2,1,0:T(8,128)(2,1)} %param.6) | copy-start | bytes 12582916
  66.4 1.0 copy-start.4
  66.4 1.3 copy-start.6
  70.7 10.9 %copy-start.5 = (bf16[8,8,64,128]{3,2,1,0:T(8,128)(2,1)S(1)}, bf16[8,8,64,128]{3,2,1,0:T(8,128)(2,1)}, u32[]{:S(2)}) copy-start(bf16[8,8,64,128]{3,2,1,0:T(8,128)(2,1)} %copy-done.4) | copy-start | bytes 3145732
  70.7 10.8 %copy-start.7 = (bf16[8,8,64,128]{3,2,1,0:T(8,128)(2,1)S(1)}, bf16[8,8,64,128]{3,2,1,0:T(8,128)(2,1)}, u32[]{:S(2)}) copy-start(bf16[8,8,64,128]{3,2,1,0:T(8,128)(2,1)} %copy-done.6) | copy-start | bytes 3145732
  74.3 11.0 %copy-start.2 = (bf16[1,512,4096]{2,1,0:T(8,128)(2,1)S(1)}, bf16[1,512,4096]{2,1,0:T(8,128)(2,1)}, u32[]{:S(2)}) copy-start(bf16[1,512,4096]{2,1,0:T(8,128)(2,1)} %param.6) | copy-start | bytes 12582916
  74.3 12.2 %collective-permute-start.10 = (f32[512,256]{0,1:T(8,128)S(1)}, f32[512,256]{0,1:T(8,128)S(1)}, u32[]{:S(2)}, u32[]{:S(2)}) collective-permute-start(f32[512,256]{0,1:T(8,128)S(1)} %fusion.11), channel_id=1, source_target_pairs={{0,64},{64,0},{1,65},{65,1},{2,66},{66,2},{3,67},{67,3},{4,68},{68... | collective-permute-start | bytes 1572872 | tf_op jit(solution)/shard_map/ppermute | solution.py:20
  85.0 2.0 collective-permute-start.9
  88.0 1.8 collective-permute-start.11
  129.5 12.8 %copy-start.8 = (f32[64,512]{1,0:T(8,128)S(1)}, f32[64,512]{1,0:T(8,128)}, u32[]{:S(2)}) copy-start(f32[64,512]{1,0:T(8,128)} %param.11) | copy-start | bytes 393220
  180.3 8.7 %copy-start.3 = (bf16[1,512,4096]{2,1,0:T(8,128)(2,1)S(1)}, bf16[1,512,4096]{2,1,0:T(8,128)(2,1)}, u32[]{:S(2)}) copy-start(bf16[1,512,4096]{2,1,0:T(8,128)(2,1)} %param.6) | copy-start | bytes 12582916
  184.0 6.6 %collective-permute-start.12 = (f32[512,256]{0,1:T(8,128)S(1)}, f32[512,256]{0,1:T(8,128)S(1)}, u32[]{:S(2)}, u32[]{:S(2)}) collective-permute-start(f32[512,256]{0,1:T(8,128)S(1)} %fusion.13), channel_id=1, source_target_pairs={{0,64},{64,0},{1,65},{65,1},{2,66},{66,2},{3,67},{67,3},{4,68},{68... | collective-permute-start | bytes 1572872 | tf_op jit(solution)/shard_map/ppermute | solution.py:20
  191.6 2.0 collective-permute-start.13

commit v11 on v10

--- a/solution.py
+++ b/solution.py
@@ -117,7 +117,7 @@
 
     other_inputs = core_swap(inputs)
 
-    def project(mine):
+    def project(mine, other_inputs=other_inputs):
         half = jnp.concatenate([mine[0], mine[1]], axis=1)
         swapped = core_swap(jnp.dot(other_inputs, half, preferred_element_type=jnp.float32))
         own_part = jnp.dot(inputs, half, preferred_element_type=jnp.float32)
@@ -169,7 +169,10 @@
     estimate = query
     for step in range(ITERS):
         if step:
-            tangent = project(gather_plane(gather_line(estimate.astype(jnp.bfloat16))))
+            line = gather_line(estimate.astype(jnp.bfloat16))
+            line, acts_now = lax.optimization_barrier((line, inputs))
+            other_inputs = core_swap(acts_now)
+            tangent = project(gather_plane(line), other_inputs)
         inner = gain_square * norm_jacobian(tangent, unit_values, root_mean)
         adjoint = (turn_weight[:, None] * norm_jacobian(inner, unit_values, root_mean)).astype(
             jnp.bfloat16

time: 250 us -> 250 us (level)
  matrix products: 24 us -> 19.6 us
  blocking collectives: 134 us -> 138 us
    all_to_all x7, blocking collectives: 134 us -> 138 us  [exchange(): return lax.all_to_all(blocks, axes, split_axis=0, concat_axis=0, tiled=True)]
    ppermute x6 -> x7, starting transfers between devices: 14.7 us -> 14.9 us  [core_swap(): return lax.ppermute(value, 'core', [(0, 1), (1, 0)])]
  transfers between devices with their start and end apart: 17 -> 18, of which waited for: 8 -> 8; matrix products, arithmetic and copies ran while one was open for 6% -> 6% of each run, Pallas kernels for 0% -> 0%
where the time goes in v11:
time: 250 us; the launch traced here: 249 us
  blocking collectives  138 us (55%)
  starting transfers between devices  46 us (18%)
  waiting for transfers between devices  27.3 us (11%)
  matrix products  19.6 us (8%)
  local copies, waits for them, and re-layouts  12 us (5%)
  other arithmetic  5.49 us (2%)
    all_to_all x7, blocking collectives, exchange(): return lax.all_to_all(blocks, axes, split_axis=0, concat_axis=0, tiled=True)  138 us
    all_to_all x3, starting transfers between devices, exchange(): return lax.all_to_all(blocks, axes, split_axis=0, concat_axis=0, tiled=True)  19.5 us
    ppermute x7, starting transfers between devices, core_swap(): return lax.ppermute(value, 'core', [(0, 1), (1, 0)])  14.9 us
    all_to_all x3, waiting for transfers between devices, exchange(): return lax.all_to_all(blocks, axes, split_axis=0, concat_axis=0, tiled=True)  14.7 us
    ppermute x8, waiting for transfers between devices, shift(): return lax.ppermute(value, 'z', [(i, (i + step) % n) for i in range(n)])  12 us
    ppermute x8, starting transfers between devices, shift(): return lax.ppermute(value, 'z', [(i, (i + step) % n) for i in range(n)])  11.6 us
    dot_general x3, matrix products, project(): jnp.dot(other_inputs, half, preferred_element_type=jnp.float32)  8.39 us
    dot_general x4, matrix products, outer(): lax.dot_general(part, rows, (((0,), (0,)), ((), ())), preferred_element_t...  7.37 us
  transfers between devices with their start and end apart: 18, of which 8 were waited for; matrix products, arithmetic and copies ran while one was open for 6% of the time, Pallas kernels for 0%

profile of v11, /device:TPU:1, one launch (start us, length us, event | category | flops | bytes accessed | tf_op | source)
XLA Modules:
  0.0 249.3 jit_solution(9575486829732714456)
XLA Ops:
  0.0 0.7 compare_convert_fusion
  0.7 0.7 convert_element_type.64
  1.5 0.7 broadcast_in_dim.115
  2.1 9.0 %all-to-all-start = ((bf16[8,80,128]{2,1,0:T(8,128)(2,1)}), bf16[8,80,128]{2,1,0:T(8,128)(2,1)S(1)}, u32[]{:S(2)}, u32[]{:S(2)}) async-start(bf16[8,80,128]{2,1,0:T(8,128)(2,1)} %broadcast_in_dim.115), calls=%async_computation | async-start | bytes 327680 | tf_op jit(solution)/shard_map/all_to_all | solution.py:24
  11.2 1.0 collective-permute-start.8
  12.1 0.8 dynamic-slice_convert_fusion
  12.9 6.4 %all-to-all-done = bf16[8,80,128]{2,1,0:T(8,128)(2,1)S(1)} async-done(((bf16[8,80,128]{2,1,0:T(8,128)(2,1)}), bf16[8,80,128]{2,1,0:T(8,128)(2,1)S(1)}, u32[]{:S(2)}, u32[]{:S(2)}) %all-to-all-start) | async-done | bytes 163872 | tf_op jit(solution)/shard_map/all_to_all | solution.py:24
  19.3 0.8 broadcast_in_dim.116
  20.1 6.8 %all-to-all-start.1 = ((bf16[16,96,128]{2,1,0:T(8,128)(2,1)}), bf16[16,96,128]{2,1,0:T(8,128)(2,1)S(1)}, u32[]{:S(2)}, u32[]{:S(2)}) async-start(bf16[16,96,128]{2,1,0:T(8,128)(2,1)} %broadcast_in_dim.116), calls=%async_computation.1 | async-start | bytes 786432 | tf_op jit(solution)/shard_map/all_to_all | solution.py:24
  27.1 8.3 %all-to-all-done.1 = bf16[16,96,128]{2,1,0:T(8,128)(2,1)S(1)} async-done(((bf16[16,96,128]{2,1,0:T(8,128)(2,1)}), bf16[16,96,128]{2,1,0:T(8,128)(2,1)S(1)}, u32[]{:S(2)}, u32[]{:S(2)}) %all-to-all-start.1) | async-done | bytes 393248 | tf_op jit(solution)/shard_map/all_to_all | solution.py:24
  35.4 0.5 collective-permute-start
  35.9 2.3 collective-permute-start.1
  38.2 1.7 broadcast_in_dim.131
  39.9 3.7 %all-to-all-start.2 = ((bf16[16,512,128]{2,1,0:T(8,128)(2,1)}), bf16[16,512,128]{2,1,0:T(8,128)(2,1)S(1)}, u32[]{:S(2)}, u32[]{:S(2)}) async-start(bf16[16,512,128]{2,1,0:T(8,128)(2,1)} %broadcast_in_dim.131), calls=%async_computation.2 | async-start | bytes 4194304 | tf_op jit(solution)/shard_map/all_to_all | solution.py:24
  43.7 0.7 select_reduce_fusion.1
  44.4 0.5 broadcast_in_dim.121
  45.1 2.7 %collective-permute-start.3 = (bf16[16,64,128]{2,1,0:T(8,128)(2,1)S(1)}, bf16[16,64,128]{2,1,0:T(8,128)(2,1)S(1)}, u32[]{:S(2)}, u32[]{:S(2)}) collective-permute-start(bf16[16,64,128]{2,1,0:T(8,128)(2,1)S(1)} %collective-permute-done.1), channel_id=1, source_target_pairs={{0,7},{1,0},{2,1},{3,2},{4,3},{5,4},{6,5},{7,6},{8,15},{9,8},{10,9... | collective-permute-start | bytes 786440 | tf_op jit(solution)/shard_map/ppermute | solution.py:38
  47.8 3.7 %collective-permute-done.2 = bf16[16,64,128]{2,1,0:T(8,128)(2,1)S(1)} collective-permute-done((bf16[16,64,128]{2,1,0:T(8,128)(2,1)S(1)}, bf16[16,64,128]{2,1,0:T(8,128)(2,1)S(1)}, u32[]{:S(2)}, u32[]{:S(2)}) %collective-permute-start.2) | collective-permute-done | bytes 262176 | tf_op jit(solution)/shard_map/ppermute | solution.py:38
  51.5 3.0 %collective-permute-start.5 = (bf16[16,64,128]{2,1,0:T(8,128)(2,1)S(1)}, bf16[16,64,128]{2,1,0:T(8,128)(2,1)S(1)}, u32[]{:S(2)}, u32[]{:S(2)}) collective-permute-start(bf16[16,64,128]{2,1,0:T(8,128)(2,1)S(1)} %collective-permute-done.3), channel_id=1, source_target_pairs={{0,7},{1,0},{2,1},{3,2},{4,3},{5,4},{6,5},{7,6},{8,15},{9,8},{10,9... | collective-permute-start | bytes 786440 | tf_op jit(solution)/shard_map/ppermute | solution.py:38
  54.5 4.8 %collective-permute-done.4 = bf16[16,64,128]{2,1,0:T(8,128)(2,1)S(1)} collective-permute-done((bf16[16,64,128]{2,1,0:T(8,128)(2,1)S(1)}, bf16[16,64,128]{2,1,0:T(8,128)(2,1)S(1)}, u32[]{:S(2)}, u32[]{:S(2)}) %collective-permute-start.4) | collective-permute-done | bytes 262176 | tf_op jit(solution)/shard_map/ppermute | solution.py:38
  59.5 3.1 %collective-permute-start.7 = (bf16[8,64,128]{2,1,0:T(8,128)(2,1)S(1)}, bf16[8,64,128]{2,1,0:T(8,128)(2,1)S(1)}, u32[]{:S(2)}, u32[]{:S(2)}) collective-permute-start(bf16[8,64,128]{2,1,0:T(8,128)(2,1)S(1)} %slice.151), channel_id=1, source_target_pairs={{0,7},{1,0},{2,1},{3,2},{4,3},{5,4},{6,5},{7,6},{8,15},{9,8},{10,9... | collective-permute-start | bytes 393224 | tf_op jit(solution)/shard_map/ppermute | solution.py:38
  62.7 3.5 %collective-permute-done.6 = bf16[8,64,128]{2,1,0:T(8,128)(2,1)S(1)} collective-permute-done((bf16[8,64,128]{2,1,0:T(8,128)(2,1)S(1)}, bf16[8,64,128]{2,1,0:T(8,128)(2,1)S(1)}, u32[]{:S(2)}, u32[]{:S(2)}) %collective-permute-start.6) | collective-permute-done | bytes 131104 | tf_op jit(solution)/shard_map/ppermute | solution.py:38
  66.4 1.0 copy-done.5
  67.4 0.3 copy-done.7
  67.7 1.4 copy-done.2
  69.2 1.3 fusion.8
  70.7 3.6 %fusion.11 = f32[512,256]{0,1:T(8,128)S(1)} fusion(bf16[512,4096]{1,0:T(8,128)(2,1)} %collective-permute-done.8, bf16[4096,128]{1,0:T(8,128)(2,1)S(1)} %bitcast.136, bf16[4096,128]{1,0:T(8,128)(2,1)S(1)} %bitcast.134), kind=kOutput, calls=%fused_computation.16 | convolution fusion | flops 1077936128 | bytes 6815744 | tf_op jit(solution)/shard_map/dot_general | solution.py:122
  74.3 7.2 %collective-permute-start.10 = (f32[512,256]{0,1:T(8,128)S(1)}, f32[512,256]{0,1:T(8,128)S(1)}, u32[]{:S(2)}, u32[]{:S(2)}) collective-permute-start(f32[512,256]{0,1:T(8,128)S(1)} %fusion.11), channel_id=1, source_target_pairs={{0,64},{64,0},{1,65},{65,1},{2,66},{66,2},{3,67},{67,3},{4,68},{68... | collective-permute-start | bytes 1572872 | tf_op jit(solution)/shard_map/ppermute | solution.py:20
  81.5 3.5 %fusion.9 = f32[512,256]{0,1:T(8,128)S(1)} fusion(bf16[512,4096]{1,0:T(8,128)(2,1)} %collective-permute-done.8, bf16[4096,128]{1,0:T(8,128)(2,1)S(1)} %bitcast.133, bf16[4096,128]{1,0:T(8,128)(2,1)S(1)} %bitcast.131), kind=kOutput, calls=%fused_computation.14 | convolution fusion | flops 1077936128 | bytes 6815744 | tf_op jit(solution)/shard_map/dot_general | solution.py:122
  85.0 0.3 collective-permute-start.9
  85.3 1.3 fusion.10
  86.7 0.3 collective-permute-done.9
  87.0 0.3 multiply_reduce_fusion.3
  87.3 0.3 multiply_reduce_fusion.2
  87.6 0.4 multiply_convert_fusion.1
  88.0 0.5 collective-permute-start.11
  88.5 1.3 fusion.16
  89.8 3.4 %fusion = bf16[256,4096]{1,0:T(8,128)(2,1)S(1)} fusion(f32[256,4096]{1,0:T(8,128)S(1)} %fusion.16, bf16[512,256]{0,1:T(8,128)(2,1)S(1)} %collective-permute-done.11, bf16[512,4096]{1,0:T(8,128)(2,1)} %collective-permute-done.8), kind=kOutput, calls=%fused_computation.2 | convolution fusion | flops 1075838976 | bytes 10747904 | tf_op jit(solution)/shard_map/dot_general | solution.py:67
  93.3 0.9 copy.62
  94.2 0.7 copy.55
  94.9 34.6 %all_to_all.50 = bf16[16,128,512]{2,1,0:T(8,128)(2,1)S(1)} all-to-all(bf16[16,128,512]{2,1,0:T(8,128)(2,1)S(1)} %bitcast.125), channel_id=1, replica_groups=mesh['ylo'=2,'core'=2,'yhi'=2,'x'=4,'z'=8] {'ylo','yhi','x'}, dimensions={0} | all-to-all | bytes 4194304 | tf_op jit(solution)/shard_map/all_to_all | solution.py:24
  129.5 0.3 reduce_sum.120
  129.9 12.4 %all_to_all.51 = bf16[8,64,128]{2,1,0:T(8,128)(2,1)S(1)} all-to-all(bf16[8,64,128]{2,1,0:T(8,128)(2,1)S(1)} %bitcast.144), channel_id=1, replica_groups=mesh['ylo'=2,'core'=2,'yhi'=2,'x'=4,'z'=8] {'z'}, dimensions={0} | all-to-all | bytes 262144 | tf_op jit(solution)/shard_map/all_to_all | solution.py:24
  142.4 10.3 %all_to_all.52 = bf16[8,64,128]{2,1,0:T(8,128)(2,1)S(1)} all-to-all(bf16[8,64,128]{2,1,0:T(8,128)(2,1)S(1)} %broadcast_in_dim.132), channel_id=1, replica_groups=mesh['ylo'=2,'core'=2,'yhi'=2,'x'=4,'z'=8] {'z'}, dimensions={0} | all-to-all | bytes 262144 | tf_op jit(solution)/shard_map/all_to_all | solution.py:24
  152.7 3.9 %collective-permute-start.12 = (bf16[512,4096]{1,0:T(8,128)(2,1)}, bf16[512,4096]{1,0:T(8,128)(2,1)S(1)}, u32[]{:S(2)}, u32[]{:S(2)}) collective-permute-start(bf16[512,4096]{1,0:T(8,128)(2,1)} %bitcast.123), channel_id=1, source_target_pairs={{0,64},{64,0},{1,65},{65,1},{2,66},{66,2},{3,67},{67,3},{4,68},{68... | collective-permute-start | bytes 12582920 | tf_op jit(solution)/shard_map/ppermute | solution.py:20
  156.6 0.4 broadcast_in_dim.133
  157.0 31.0 %all_to_all.53 = bf16[16,512,128]{2,1,0:T(8,128)(2,1)S(1)} all-to-all(bf16[16,512,128]{2,1,0:T(8,128)(2,1)S(1)} %broadcast_in_dim.133), channel_id=1, replica_groups=mesh['ylo'=2,'core'=2,'yhi'=2,'x'=4,'z'=8] {'ylo','yhi','x'}, dimensions={0} | all-to-all | bytes 4194304 | tf_op jit(solution)/shard_map/all_to_all | solution.py:24
  188.2 1.3 fusion.2
  189.5 1.2 collective-permute-start.13
  190.7 1.3 fusion.12
  192.0 0.2 collective-permute-done.13
  192.2 0.3 multiply_reduce_fusion.1
  192.5 0.3 multiply_reduce_fusion
  192.8 0.4 multiply_convert_fusion
  193.2 0.9 collective-permute-start.14
  194.1 1.3 fusion.14
  195.4 1.4 fusion.1
  196.8 0.9 copy.63
  197.7 0.7 copy.58
  198.4 30.9 %all_to_all.54 = bf16[16,128,512]{2,1,0:T(8,128)(2,1)S(1)} all-to-all(bf16[16,128,512]{2,1,0:T(8,128)(2,1)S(1)} %bitcast.127), channel_id=1, replica_groups=mesh['ylo'=2,'core'=2,'yhi'=2,'x'=4,'z'=8] {'ylo','yhi','x'}, dimensions={0} | all-to-all | bytes 4194304 | tf_op jit(solution)/shard_map/all_to_all | solution.py:24
  229.3 0.3 reduce_sum.124
  229.8 10.4 %all_to_all.55 = bf16[8,64,128]{2,1,0:T(8,128)(2,1)S(1)} all-to-all(bf16[8,64,128]{2,1,0:T(8,128)(2,1)S(1)} %bitcast.145), channel_id=1, replica_groups=mesh['ylo'=2,'core'=2,'yhi'=2,'x'=4,'z'=8] {'z'}, dimensions={0} | all-to-all | bytes 262144 | tf_op jit(solution)/shard_map/all_to_all | solution.py:24
  240.2 8.3 %all_to_all.56 = f32[4,64,128]{2,1,0:T(8,128)S(1)} all-to-all(f32[4,64,128]{2,1,0:T(8,128)S(1)} %broadcast_in_dim.134), channel_id=1, replica_groups=mesh['ylo'=2,'core'=2,'yhi'=2,'x'=4,'z'=8] {'ylo','core'}, dimensions={0} | all-to-all | bytes 262144 | tf_op jit(solution)/shard_map/all_to_all | solution.py:24
  248.6 0.7 pad_maximum_fusion.22
  (81 shorter events, 1.9 us)
Async XLA Ops:
  0.0 1.4 copy-start
  0.0 26.9 %copy-start.10 = (f32[512]{0:T(512)S(1)}, f32[512]{0:T(512)}, u32[]{:S(2)}) copy-start(f32[512]{0:T(512)} %param.10) | copy-start | bytes 6148
  2.1 17.2 %all-to-all-start = ((bf16[8,80,128]{2,1,0:T(8,128)(2,1)}), bf16[8,80,128]{2,1,0:T(8,128)(2,1)S(1)}, u32[]{:S(2)}, u32[]{:S(2)}) async-start(bf16[8,80,128]{2,1,0:T(8,128)(2,1)} %broadcast_in_dim.115), calls=%async_computation | async-start | bytes 327680 | tf_op jit(solution)/shard_map/all_to_all | solution.py:24
  11.2 59.5 %collective-permute-start.8 = (bf16[512,4096]{1,0:T(8,128)(2,1)}, bf16[512,4096]{1,0:T(8,128)(2,1)}, u32[]{:S(2)}, u32[]{:S(2)}) collective-permute-start(bf16[512,4096]{1,0:T(8,128)(2,1)} %bitcast.122), channel_id=1, source_target_pairs={{0,64},{64,0},{1,65},{65,1},{2,66},{66,2},{3,67},{67,3},{4,68},{68... | collective-permute-start | bytes 12582920 | tf_op jit(solution)/shard_map/ppermute | solution.py:20
  20.1 15.3 %all-to-all-start.1 = ((bf16[16,96,128]{2,1,0:T(8,128)(2,1)}), bf16[16,96,128]{2,1,0:T(8,128)(2,1)S(1)}, u32[]{:S(2)}, u32[]{:S(2)}) async-start(bf16[16,96,128]{2,1,0:T(8,128)(2,1)} %broadcast_in_dim.116), calls=%async_computation.1 | async-start | bytes 786432 | tf_op jit(solution)/shard_map/all_to_all | solution.py:24
  35.4 9.5 %collective-permute-start = (bf16[16,64,128]{2,1,0:T(8,128)(2,1)S(1)}, bf16[16,64,128]{2,1,0:T(8,128)(2,1)S(1)}, u32[]{:S(2)}, u32[]{:S(2)}) collective-permute-start(bf16[16,64,128]{2,1,0:T(8,128)(2,1)S(1)} %slice.123), channel_id=1, source_target_pairs={{0,1},{1,2},{2,3},{3,4},{4,5},{5,6},{6,7},{7,0},{8,9},{9,10},{10,1... | collective-permute-start | bytes 786440 | tf_op jit(solution)/shard_map/ppermute | solution.py:38
  35.9 9.1 %collective-permute-start.1 = (bf16[16,64,128]{2,1,0:T(8,128)(2,1)S(1)}, bf16[16,64,128]{2,1,0:T(8,128)(2,1)S(1)}, u32[]{:S(2)}, u32[]{:S(2)}) collective-permute-start(bf16[16,64,128]{2,1,0:T(8,128)(2,1)S(1)} %slice.123), channel_id=1, source_target_pairs={{0,7},{1,0},{2,1},{3,2},{4,3},{5,4},{6,5},{7,6},{8,15},{9,8},{10,9... | collective-permute-start | bytes 786440 | tf_op jit(solution)/shard_map/ppermute | solution.py:38
  39.9 30.5 %all-to-all-start.2 = ((bf16[16,512,128]{2,1,0:T(8,128)(2,1)}), bf16[16,512,128]{2,1,0:T(8,128)(2,1)S(1)}, u32[]{:S(2)}, u32[]{:S(2)}) async-start(bf16[16,512,128]{2,1,0:T(8,128)(2,1)} %broadcast_in_dim.131), calls=%async_computation.2 | async-start | bytes 4194304 | tf_op jit(solution)/shard_map/all_to_all | solution.py:24
  45.0 6.5 %collective-permute-start.2 = (bf16[16,64,128]{2,1,0:T(8,128)(2,1)S(1)}, bf16[16,64,128]{2,1,0:T(8,128)(2,1)S(1)}, u32[]{:S(2)}, u32[]{:S(2)}) collective-permute-start(bf16[16,64,128]{2,1,0:T(8,128)(2,1)S(1)} %collective-permute-done), channel_id=1, source_target_pairs={{0,1},{1,2},{2,3},{3,4},{4,5},{5,6},{6,7},{7,0},{8,9},{9,10},{10,1... | collective-permute-start | bytes 786440 | tf_op jit(solution)/shard_map/ppermute | solution.py:38
  45.1 6.4 %collective-permute-start.3 = (bf16[16,64,128]{2,1,0:T(8,128)(2,1)S(1)}, bf16[16,64,128]{2,1,0:T(8,128)(2,1)S(1)}, u32[]{:S(2)}, u32[]{:S(2)}) collective-permute-start(bf16[16,64,128]{2,1,0:T(8,128)(2,1)S(1)} %collective-permute-done.1), channel_id=1, source_target_pairs={{0,7},{1,0},{2,1},{3,2},{4,3},{5,4},{6,5},{7,6},{8,15},{9,8},{10,9... | collective-permute-start | bytes 786440 | tf_op jit(solution)/shard_map/ppermute | solution.py:38
  51.5 7.9 %collective-permute-start.4 = (bf16[16,64,128]{2,1,0:T(8,128)(2,1)S(1)}, bf16[16,64,128]{2,1,0:T(8,128)(2,1)S(1)}, u32[]{:S(2)}, u32[]{:S(2)}) collective-permute-start(bf16[16,64,128]{2,1,0:T(8,128)(2,1)S(1)} %collective-permute-done.2), channel_id=1, source_target_pairs={{0,1},{1,2},{2,3},{3,4},{4,5},{5,6},{6,7},{7,0},{8,9},{9,10},{10,1... | collective-permute-start | bytes 786440 | tf_op jit(solution)/shard_map/ppermute | solution.py:38
  51.5 8.0 %collective-permute-start.5 = (bf16[16,64,128]{2,1,0:T(8,128)(2,1)S(1)}, bf16[16,64,128]{2,1,0:T(8,128)(2,1)S(1)}, u32[]{:S(2)}, u32[]{:S(2)}) collective-permute-start(bf16[16,64,128]{2,1,0:T(8,128)(2,1)S(1)} %collective-permute-done.3), channel_id=1, source_target_pairs={{0,7},{1,0},{2,1},{3,2},{4,3},{5,4},{6,5},{7,6},{8,15},{9,8},{10,9... | collective-permute-start | bytes 786440 | tf_op jit(solution)/shard_map/ppermute | solution.py:38
  59.3 6.8 %collective-permute-start.6 = (bf16[8,64,128]{2,1,0:T(8,128)(2,1)S(1)}, bf16[8,64,128]{2,1,0:T(8,128)(2,1)S(1)}, u32[]{:S(2)}, u32[]{:S(2)}) collective-permute-start(bf16[8,64,128]{2,1,0:T(8,128)(2,1)S(1)} %slice.150), channel_id=1, source_target_pairs={{0,1},{1,2},{2,3},{3,4},{4,5},{5,6},{6,7},{7,0},{8,9},{9,10},{10,1... | collective-permute-start | bytes 393224 | tf_op jit(solution)/shard_map/ppermute | solution.py:38
  59.5 6.7 %collective-permute-start.7 = (bf16[8,64,128]{2,1,0:T(8,128)(2,1)S(1)}, bf16[8,64,128]{2,1,0:T(8,128)(2,1)S(1)}, u32[]{:S(2)}, u32[]{:S(2)}) collective-permute-start(bf16[8,64,128]{2,1,0:T(8,128)(2,1)S(1)} %slice.151), channel_id=1, source_target_pairs={{0,7},{1,0},{2,1},{3,2},{4,3},{5,4},{6,5},{7,6},{8,15},{9,8},{10,9... | collective-permute-start | bytes 393224 | tf_op jit(solution)/shard_map/ppermute | solution.py:38
  66.2 2.9 %copy-start.2 = (bf16[1,512,4096]{2,1,0:T(8,128)(2,1)S(1)}, bf16[1,512,4096]{2,1,0:T(8,128)(2,1)}, u32[]{:S(2)}) copy-start(bf16[1,512,4096]{2,1,0:T(8,128)(2,1)} %param.6) | copy-start | bytes 12582916
  66.4 1.0 copy-start.5
  66.4 1.3 copy-start.7
  70.7 10.9 %copy-start.6 = (bf16[8,8,64,128]{3,2,1,0:T(8,128)(2,1)S(1)}, bf16[8,8,64,128]{3,2,1,0:T(8,128)(2,1)}, u32[]{:S(2)}) copy-start(bf16[8,8,64,128]{3,2,1,0:T(8,128)(2,1)} %copy-done.5) | copy-start | bytes 3145732
  70.7 10.9 %copy-start.8 = (bf16[8,8,64,128]{3,2,1,0:T(8,128)(2,1)S(1)}, bf16[8,8,64,128]{3,2,1,0:T(8,128)(2,1)}, u32[]{:S(2)}) copy-start(bf16[8,8,64,128]{3,2,1,0:T(8,128)(2,1)} %copy-done.7) | copy-start | bytes 3145732
  74.3 11.0 %copy-start.3 = (bf16[1,512,4096]{2,1,0:T(8,128)(2,1)S(1)}, bf16[1,512,4096]{2,1,0:T(8,128)(2,1)}, u32[]{:S(2)}) copy-start(bf16[1,512,4096]{2,1,0:T(8,128)(2,1)} %param.6) | copy-start | bytes 12582916
  74.3 12.3 %collective-permute-start.10 = (f32[512,256]{0,1:T(8,128)S(1)}, f32[512,256]{0,1:T(8,128)S(1)}, u32[]{:S(2)}, u32[]{:S(2)}) collective-permute-start(f32[512,256]{0,1:T(8,128)S(1)} %fusion.11), channel_id=1, source_target_pairs={{0,64},{64,0},{1,65},{65,1},{2,66},{66,2},{3,67},{67,3},{4,68},{68... | collective-permute-start | bytes 1572872 | tf_op jit(solution)/shard_map/ppermute | solution.py:20
  85.0 2.0 collective-permute-start.9
  88.0 1.8 collective-permute-start.11
  129.5 12.8 %copy-start.9 = (f32[64,512]{1,0:T(8,128)S(1)}, f32[64,512]{1,0:T(8,128)}, u32[]{:S(2)}) copy-start(f32[64,512]{1,0:T(8,128)} %param.11) | copy-start | bytes 393220
  152.7 35.5 %collective-permute-start.12 = (bf16[512,4096]{1,0:T(8,128)(2,1)}, bf16[512,4096]{1,0:T(8,128)(2,1)S(1)}, u32[]{:S(2)}, u32[]{:S(2)}) collective-permute-start(bf16[512,4096]{1,0:T(8,128)(2,1)} %bitcast.123), channel_id=1, source_target_pairs={{0,64},{64,0},{1,65},{65,1},{2,66},{66,2},{3,67},{67,3},{4,68},{68... | collective-permute-start | bytes 12582920 | tf_op jit(solution)/shard_map/ppermute | solution.py:20
  188.2 2.5 copy-start.4
  189.5 2.7 %collective-permute-start.13 = (f32[512,256]{0,1:T(8,128)S(1)}, f32[512,256]{0,1:T(8,128)S(1)}, u32[]{:S(2)}, u32[]{:S(2)}) collective-permute-start(f32[512,256]{0,1:T(8,128)S(1)} %fusion.2), channel_id=1, source_target_pairs={{0,64},{64,0},{1,65},{65,1},{2,66},{66,2},{3,67},{67,3},{4,68},{68... | collective-permute-start | bytes 1572872 | tf_op jit(solution)/shard_map/ppermute | solution.py:20
  193.2 2.2 collective-permute-start.14
  198.4 50.9 %copy-start.1 = (bf16[64,512]{1,0:T(8,128)(2,1)S(1)}, bf16[64,512]{1,0:T(8,128)(2,1)}, u32[]{:S(2)}) copy-start(bf16[64,512]{1,0:T(8,128)(2,1)} %param.9) | copy-start | bytes 196612

commit v12 on v11

--- a/solution.py
+++ b/solution.py
@@ -169,9 +169,10 @@
     estimate = query
     for step in range(ITERS):
         if step:
-            line = gather_line(estimate.astype(jnp.bfloat16))
-            line, acts_now = lax.optimization_barrier((line, inputs))
-            other_inputs = core_swap(acts_now)
+            block, acts_now = lax.optimization_barrier((estimate.astype(jnp.bfloat16), inputs))
+            line, other_inputs = lax.optimization_barrier(
+                (gather_line(block), core_swap(acts_now))
+            )
             tangent = project(gather_plane(line), other_inputs)
         inner = gain_square * norm_jacobian(tangent, unit_values, root_mean)
         adjoint = (turn_weight[:, None] * norm_jacobian(inner, unit_values, root_mean)).astype(

time: 250 us -> 250 us (level)
  no operation moved by 1% of the time
where the time goes in v12:
time: 250 us
  blocking collectives  139 us (56%)
  starting transfers between devices  45.3 us (18%)
  waiting for transfers between devices  27.3 us (11%)
  matrix products  19.6 us (8%)
  local copies, waits for them, and re-layouts  12 us (5%)
  other arithmetic  5.49 us (2%)
    all_to_all x7, blocking collectives, exchange(): return lax.all_to_all(blocks, axes, split_axis=0, concat_axis=0, tiled=True)  139 us
    all_to_all x3, starting transfers between devices, exchange(): return lax.all_to_all(blocks, axes, split_axis=0, concat_axis=0, tiled=True)  19.5 us
    all_to_all x3, waiting for transfers between devices, exchange(): return lax.all_to_all(blocks, axes, split_axis=0, concat_axis=0, tiled=True)  14.7 us
    ppermute x7, starting transfers between devices, core_swap(): return lax.ppermute(value, 'core', [(0, 1), (1, 0)])  14.1 us
    ppermute x8, waiting for transfers between devices, shift(): return lax.ppermute(value, 'z', [(i, (i + step) % n) for i in range(n)])  12 us
    ppermute x8, starting transfers between devices, shift(): return lax.ppermute(value, 'z', [(i, (i + step) % n) for i in range(n)])  11.6 us
    dot_general x3, matrix products, project(): jnp.dot(other_inputs, half, preferred_element_type=jnp.float32)  8.39 us
    dot_general x4, matrix products, outer(): lax.dot_general(part, rows, (((0,), (0,)), ((), ())), preferred_element_t...  7.37 us
  transfers between devices with their start and end apart: 18, of which 8 were waited for; matrix products, arithmetic and copies ran while one was open for 6% of the time, Pallas kernels for 0%

profile of v12, /device:TPU:1, one launch (start us, length us, event | category | flops | bytes accessed | tf_op | source)
XLA Modules:
  0.0 249.6 jit_solution(69516897950712275)
XLA Ops:
  0.0 0.7 compare_convert_fusion
  0.7 0.7 convert_element_type.64
  1.5 0.7 broadcast_in_dim.115
  2.1 9.0 %all-to-all-start = ((bf16[8,80,128]{2,1,0:T(8,128)(2,1)}), bf16[8,80,128]{2,1,0:T(8,128)(2,1)S(1)}, u32[]{:S(2)}, u32[]{:S(2)}) async-start(bf16[8,80,128]{2,1,0:T(8,128)(2,1)} %broadcast_in_dim.115), calls=%async_computation | async-start | bytes 327680 | tf_op jit(solution)/shard_map/all_to_all | solution.py:24
  11.2 1.0 collective-permute-start.8
  12.1 0.8 dynamic-slice_convert_fusion
  12.9 6.4 %all-to-all-done = bf16[8,80,128]{2,1,0:T(8,128)(2,1)S(1)} async-done(((bf16[8,80,128]{2,1,0:T(8,128)(2,1)}), bf16[8,80,128]{2,1,0:T(8,128)(2,1)S(1)}, u32[]{:S(2)}, u32[]{:S(2)}) %all-to-all-start) | async-done | bytes 163872 | tf_op jit(solution)/shard_map/all_to_all | solution.py:24
  19.3 0.8 broadcast_in_dim.116
  20.1 6.8 %all-to-all-start.1 = ((bf16[16,96,128]{2,1,0:T(8,128)(2,1)}), bf16[16,96,128]{2,1,0:T(8,128)(2,1)S(1)}, u32[]{:S(2)}, u32[]{:S(2)}) async-start(bf16[16,96,128]{2,1,0:T(8,128)(2,1)} %broadcast_in_dim.116), calls=%async_computation.1 | async-start | bytes 786432 | tf_op jit(solution)/shard_map/all_to_all | solution.py:24
  27.1 8.3 %all-to-all-done.1 = bf16[16,96,128]{2,1,0:T(8,128)(2,1)S(1)} async-done(((bf16[16,96,128]{2,1,0:T(8,128)(2,1)}), bf16[16,96,128]{2,1,0:T(8,128)(2,1)S(1)}, u32[]{:S(2)}, u32[]{:S(2)}) %all-to-all-start.1) | async-done | bytes 393248 | tf_op jit(solution)/shard_map/all_to_all | solution.py:24
  35.4 0.5 collective-permute-start
  35.9 2.3 collective-permute-start.1
  38.2 1.7 broadcast_in_dim.131
  39.9 3.7 %all-to-all-start.2 = ((bf16[16,512,128]{2,1,0:T(8,128)(2,1)}), bf16[16,512,128]{2,1,0:T(8,128)(2,1)S(1)}, u32[]{:S(2)}, u32[]{:S(2)}) async-start(bf16[16,512,128]{2,1,0:T(8,128)(2,1)} %broadcast_in_dim.131), calls=%async_computation.2 | async-start | bytes 4194304 | tf_op jit(solution)/shard_map/all_to_all | solution.py:24
  43.7 0.7 select_reduce_fusion.1
  44.4 0.5 broadcast_in_dim.121
  45.1 2.7 %collective-permute-start.3 = (bf16[16,64,128]{2,1,0:T(8,128)(2,1)S(1)}, bf16[16,64,128]{2,1,0:T(8,128)(2,1)S(1)}, u32[]{:S(2)}, u32[]{:S(2)}) collective-permute-start(bf16[16,64,128]{2,1,0:T(8,128)(2,1)S(1)} %collective-permute-done.1), channel_id=1, source_target_pairs={{0,7},{1,0},{2,1},{3,2},{4,3},{5,4},{6,5},{7,6},{8,15},{9,8},{10,9... | collective-permute-start | bytes 786440 | tf_op jit(solution)/shard_map/ppermute | solution.py:38
  47.8 3.7 %collective-permute-done.2 = bf16[16,64,128]{2,1,0:T(8,128)(2,1)S(1)} collective-permute-done((bf16[16,64,128]{2,1,0:T(8,128)(2,1)S(1)}, bf16[16,64,128]{2,1,0:T(8,128)(2,1)S(1)}, u32[]{:S(2)}, u32[]{:S(2)}) %collective-permute-start.2) | collective-permute-done | bytes 262176 | tf_op jit(solution)/shard_map/ppermute | solution.py:38
  51.5 3.0 %collective-permute-start.5 = (bf16[16,64,128]{2,1,0:T(8,128)(2,1)S(1)}, bf16[16,64,128]{2,1,0:T(8,128)(2,1)S(1)}, u32[]{:S(2)}, u32[]{:S(2)}) collective-permute-start(bf16[16,64,128]{2,1,0:T(8,128)(2,1)S(1)} %collective-permute-done.3), channel_id=1, source_target_pairs={{0,7},{1,0},{2,1},{3,2},{4,3},{5,4},{6,5},{7,6},{8,15},{9,8},{10,9... | collective-permute-start | bytes 786440 | tf_op jit(solution)/shard_map/ppermute | solution.py:38
  54.5 4.8 %collective-permute-done.4 = bf16[16,64,128]{2,1,0:T(8,128)(2,1)S(1)} collective-permute-done((bf16[16,64,128]{2,1,0:T(8,128)(2,1)S(1)}, bf16[16,64,128]{2,1,0:T(8,128)(2,1)S(1)}, u32[]{:S(2)}, u32[]{:S(2)}) %collective-permute-start.4) | collective-permute-done | bytes 262176 | tf_op jit(solution)/shard_map/ppermute | solution.py:38
  59.5 3.1 %collective-permute-start.7 = (bf16[8,64,128]{2,1,0:T(8,128)(2,1)S(1)}, bf16[8,64,128]{2,1,0:T(8,128)(2,1)S(1)}, u32[]{:S(2)}, u32[]{:S(2)}) collective-permute-start(bf16[8,64,128]{2,1,0:T(8,128)(2,1)S(1)} %slice.151), channel_id=1, source_target_pairs={{0,7},{1,0},{2,1},{3,2},{4,3},{5,4},{6,5},{7,6},{8,15},{9,8},{10,9... | collective-permute-start | bytes 393224 | tf_op jit(solution)/shard_map/ppermute | solution.py:38
  62.7 3.5 %collective-permute-done.6 = bf16[8,64,128]{2,1,0:T(8,128)(2,1)S(1)} collective-permute-done((bf16[8,64,128]{2,1,0:T(8,128)(2,1)S(1)}, bf16[8,64,128]{2,1,0:T(8,128)(2,1)S(1)}, u32[]{:S(2)}, u32[]{:S(2)}) %collective-permute-start.6) | collective-permute-done | bytes 131104 | tf_op jit(solution)/shard_map/ppermute | solution.py:38
  66.4 1.0 copy-done.5
  67.4 0.3 copy-done.7
  67.7 1.4 copy-done.2
  69.2 1.3 fusion.8
  70.7 3.6 %fusion.11 = f32[512,256]{0,1:T(8,128)S(1)} fusion(bf16[512,4096]{1,0:T(8,128)(2,1)} %collective-permute-done.8, bf16[4096,128]{1,0:T(8,128)(2,1)S(1)} %bitcast.136, bf16[4096,128]{1,0:T(8,128)(2,1)S(1)} %bitcast.134), kind=kOutput, calls=%fused_computation.16 | convolution fusion | flops 1077936128 | bytes 6815744 | tf_op jit(solution)/shard_map/dot_general | solution.py:122
  74.3 7.2 %collective-permute-start.10 = (f32[512,256]{0,1:T(8,128)S(1)}, f32[512,256]{0,1:T(8,128)S(1)}, u32[]{:S(2)}, u32[]{:S(2)}) collective-permute-start(f32[512,256]{0,1:T(8,128)S(1)} %fusion.11), channel_id=1, source_target_pairs={{0,64},{64,0},{1,65},{65,1},{2,66},{66,2},{3,67},{67,3},{4,68},{68... | collective-permute-start | bytes 1572872 | tf_op jit(solution)/shard_map/ppermute | solution.py:20
  81.5 3.5 %fusion.9 = f32[512,256]{0,1:T(8,128)S(1)} fusion(bf16[512,4096]{1,0:T(8,128)(2,1)} %collective-permute-done.8, bf16[4096,128]{1,0:T(8,128)(2,1)S(1)} %bitcast.133, bf16[4096,128]{1,0:T(8,128)(2,1)S(1)} %bitcast.131), kind=kOutput, calls=%fused_computation.14 | convolution fusion | flops 1077936128 | bytes 6815744 | tf_op jit(solution)/shard_map/dot_general | solution.py:122
  85.0 0.3 collective-permute-start.9
  85.3 1.3 fusion.10
  86.7 0.3 collective-permute-done.9
  87.0 0.3 multiply_reduce_fusion.3
  87.3 0.3 multiply_reduce_fusion.2
  87.6 0.4 multiply_convert_fusion.1
  88.0 0.5 collective-permute-start.11
  88.5 1.3 fusion.16
  89.8 3.4 %fusion = bf16[256,4096]{1,0:T(8,128)(2,1)S(1)} fusion(f32[256,4096]{1,0:T(8,128)S(1)} %fusion.16, bf16[512,256]{0,1:T(8,128)(2,1)S(1)} %collective-permute-done.11, bf16[512,4096]{1,0:T(8,128)(2,1)} %collective-permute-done.8), kind=kOutput, calls=%fused_computation.2 | convolution fusion | flops 1075838976 | bytes 10747904 | tf_op jit(solution)/shard_map/dot_general | solution.py:67
  93.3 0.9 copy.62
  94.2 0.7 copy.55
  94.9 34.6 %all_to_all.50 = bf16[16,128,512]{2,1,0:T(8,128)(2,1)S(1)} all-to-all(bf16[16,128,512]{2,1,0:T(8,128)(2,1)S(1)} %bitcast.125), channel_id=1, replica_groups=mesh['ylo'=2,'core'=2,'yhi'=2,'x'=4,'z'=8] {'ylo','yhi','x'}, dimensions={0} | all-to-all | bytes 4194304 | tf_op jit(solution)/shard_map/all_to_all | solution.py:24
  129.5 0.3 reduce_sum.120
  129.9 12.4 %all_to_all.51 = bf16[8,64,128]{2,1,0:T(8,128)(2,1)S(1)} all-to-all(bf16[8,64,128]{2,1,0:T(8,128)(2,1)S(1)} %bitcast.144), channel_id=1, replica_groups=mesh['ylo'=2,'core'=2,'yhi'=2,'x'=4,'z'=8] {'z'}, dimensions={0} | all-to-all | bytes 262144 | tf_op jit(solution)/shard_map/all_to_all | solution.py:24
  142.4 2.9 %collective-permute-start.12 = (bf16[512,4096]{1,0:T(8,128)(2,1)}, bf16[512,4096]{1,0:T(8,128)(2,1)S(1)}, u32[]{:S(2)}, u32[]{:S(2)}) collective-permute-start(bf16[512,4096]{1,0:T(8,128)(2,1)} %bitcast.123), channel_id=1, source_target_pairs={{0,64},{64,0},{1,65},{65,1},{2,66},{66,2},{3,67},{67,3},{4,68},{68... | collective-permute-start | bytes 12582920 | tf_op jit(solution)/shard_map/ppermute | solution.py:20
  145.2 11.8 %all_to_all.52 = bf16[8,64,128]{2,1,0:T(8,128)(2,1)S(1)} all-to-all(bf16[8,64,128]{2,1,0:T(8,128)(2,1)S(1)} %broadcast_in_dim.132), channel_id=1, replica_groups=mesh['ylo'=2,'core'=2,'yhi'=2,'x'=4,'z'=8] {'z'}, dimensions={0} | all-to-all | bytes 262144 | tf_op jit(solution)/shard_map/all_to_all | solution.py:24
  157.1 0.4 broadcast_in_dim.133
  157.5 30.6 %all_to_all.53 = bf16[16,512,128]{2,1,0:T(8,128)(2,1)S(1)} all-to-all(bf16[16,512,128]{2,1,0:T(8,128)(2,1)S(1)} %broadcast_in_dim.133), channel_id=1, replica_groups=mesh['ylo'=2,'core'=2,'yhi'=2,'x'=4,'z'=8] {'ylo','yhi','x'}, dimensions={0} | all-to-all | bytes 4194304 | tf_op jit(solution)/shard_map/all_to_all | solution.py:24
  188.3 1.3 fusion.2
  189.6 1.5 collective-permute-start.13
  191.0 1.3 fusion.12
  192.3 0.2 collective-permute-done.13
  192.6 0.3 multiply_reduce_fusion.1
  192.8 0.3 multiply_reduce_fusion
  193.1 0.4 multiply_convert_fusion
  193.5 0.9 collective-permute-start.14
  194.4 1.3 fusion.14
  195.8 1.4 fusion.1
  197.1 0.9 copy.63
  198.0 0.7 copy.58
  198.7 30.9 %all_to_all.54 = bf16[16,128,512]{2,1,0:T(8,128)(2,1)S(1)} all-to-all(bf16[16,128,512]{2,1,0:T(8,128)(2,1)S(1)} %bitcast.127), channel_id=1, replica_groups=mesh['ylo'=2,'core'=2,'yhi'=2,'x'=4,'z'=8] {'ylo','yhi','x'}, dimensions={0} | all-to-all | bytes 4194304 | tf_op jit(solution)/shard_map/all_to_all | solution.py:24
  229.7 0.3 reduce_sum.124
  230.1 10.4 %all_to_all.55 = bf16[8,64,128]{2,1,0:T(8,128)(2,1)S(1)} all-to-all(bf16[8,64,128]{2,1,0:T(8,128)(2,1)S(1)} %bitcast.145), channel_id=1, replica_groups=mesh['ylo'=2,'core'=2,'yhi'=2,'x'=4,'z'=8] {'z'}, dimensions={0} | all-to-all | bytes 262144 | tf_op jit(solution)/shard_map/all_to_all | solution.py:24
  240.6 8.3 %all_to_all.56 = f32[4,64,128]{2,1,0:T(8,128)S(1)} all-to-all(f32[4,64,128]{2,1,0:T(8,128)S(1)} %broadcast_in_dim.134), channel_id=1, replica_groups=mesh['ylo'=2,'core'=2,'yhi'=2,'x'=4,'z'=8] {'ylo','core'}, dimensions={0} | all-to-all | bytes 262144 | tf_op jit(solution)/shard_map/all_to_all | solution.py:24
  248.9 0.7 pad_maximum_fusion.22
  (81 shorter events, 1.9 us)
Async XLA Ops:
  0.0 1.4 copy-start
  0.0 26.9 %copy-start.10 = (f32[512]{0:T(512)S(1)}, f32[512]{0:T(512)}, u32[]{:S(2)}) copy-start(f32[512]{0:T(512)} %param.10) | copy-start | bytes 6148
  2.1 17.2 %all-to-all-start = ((bf16[8,80,128]{2,1,0:T(8,128)(2,1)}), bf16[8,80,128]{2,1,0:T(8,128)(2,1)S(1)}, u32[]{:S(2)}, u32[]{:S(2)}) async-start(bf16[8,80,128]{2,1,0:T(8,128)(2,1)} %broadcast_in_dim.115), calls=%async_computation | async-start | bytes 327680 | tf_op jit(solution)/shard_map/all_to_all | solution.py:24
  11.2 59.5 %collective-permute-start.8 = (bf16[512,4096]{1,0:T(8,128)(2,1)}, bf16[512,4096]{1,0:T(8,128)(2,1)}, u32[]{:S(2)}, u32[]{:S(2)}) collective-permute-start(bf16[512,4096]{1,0:T(8,128)(2,1)} %bitcast.122), channel_id=1, source_target_pairs={{0,64},{64,0},{1,65},{65,1},{2,66},{66,2},{3,67},{67,3},{4,68},{68... | collective-permute-start | bytes 12582920 | tf_op jit(solution)/shard_map/ppermute | solution.py:20
  20.1 15.3 %all-to-all-start.1 = ((bf16[16,96,128]{2,1,0:T(8,128)(2,1)}), bf16[16,96,128]{2,1,0:T(8,128)(2,1)S(1)}, u32[]{:S(2)}, u32[]{:S(2)}) async-start(bf16[16,96,128]{2,1,0:T(8,128)(2,1)} %broadcast_in_dim.116), calls=%async_computation.1 | async-start | bytes 786432 | tf_op jit(solution)/shard_map/all_to_all | solution.py:24
  35.4 9.5 %collective-permute-start = (bf16[16,64,128]{2,1,0:T(8,128)(2,1)S(1)}, bf16[16,64,128]{2,1,0:T(8,128)(2,1)S(1)}, u32[]{:S(2)}, u32[]{:S(2)}) collective-permute-start(bf16[16,64,128]{2,1,0:T(8,128)(2,1)S(1)} %slice.123), channel_id=1, source_target_pairs={{0,1},{1,2},{2,3},{3,4},{4,5},{5,6},{6,7},{7,0},{8,9},{9,10},{10,1... | collective-permute-start | bytes 786440 | tf_op jit(solution)/shard_map/ppermute | solution.py:38
  35.9 9.1 %collective-permute-start.1 = (bf16[16,64,128]{2,1,0:T(8,128)(2,1)S(1)}, bf16[16,64,128]{2,1,0:T(8,128)(2,1)S(1)}, u32[]{:S(2)}, u32[]{:S(2)}) collective-permute-start(bf16[16,64,128]{2,1,0:T(8,128)(2,1)S(1)} %slice.123), channel_id=1, source_target_pairs={{0,7},{1,0},{2,1},{3,2},{4,3},{5,4},{6,5},{7,6},{8,15},{9,8},{10,9... | collective-permute-start | bytes 786440 | tf_op jit(solution)/shard_map/ppermute | solution.py:38
  39.9 30.5 %all-to-all-start.2 = ((bf16[16,512,128]{2,1,0:T(8,128)(2,1)}), bf16[16,512,128]{2,1,0:T(8,128)(2,1)S(1)}, u32[]{:S(2)}, u32[]{:S(2)}) async-start(bf16[16,512,128]{2,1,0:T(8,128)(2,1)} %broadcast_in_dim.131), calls=%async_computation.2 | async-start | bytes 4194304 | tf_op jit(solution)/shard_map/all_to_all | solution.py:24
  45.0 6.5 %collective-permute-start.2 = (bf16[16,64,128]{2,1,0:T(8,128)(2,1)S(1)}, bf16[16,64,128]{2,1,0:T(8,128)(2,1)S(1)}, u32[]{:S(2)}, u32[]{:S(2)}) collective-permute-start(bf16[16,64,128]{2,1,0:T(8,128)(2,1)S(1)} %collective-permute-done), channel_id=1, source_target_pairs={{0,1},{1,2},{2,3},{3,4},{4,5},{5,6},{6,7},{7,0},{8,9},{9,10},{10,1... | collective-permute-start | bytes 786440 | tf_op jit(solution)/shard_map/ppermute | solution.py:38
  45.1 6.4 %collective-permute-start.3 = (bf16[16,64,128]{2,1,0:T(8,128)(2,1)S(1)}, bf16[16,64,128]{2,1,0:T(8,128)(2,1)S(1)}, u32[]{:S(2)}, u32[]{:S(2)}) collective-permute-start(bf16[16,64,128]{2,1,0:T(8,128)(2,1)S(1)} %collective-permute-done.1), channel_id=1, source_target_pairs={{0,7},{1,0},{2,1},{3,2},{4,3},{5,4},{6,5},{7,6},{8,15},{9,8},{10,9... | collective-permute-start | bytes 786440 | tf_op jit(solution)/shard_map/ppermute | solution.py:38
  51.5 7.9 %collective-permute-start.4 = (bf16[16,64,128]{2,1,0:T(8,128)(2,1)S(1)}, bf16[16,64,128]{2,1,0:T(8,128)(2,1)S(1)}, u32[]{:S(2)}, u32[]{:S(2)}) collective-permute-start(bf16[16,64,128]{2,1,0:T(8,128)(2,1)S(1)} %collective-permute-done.2), channel_id=1, source_target_pairs={{0,1},{1,2},{2,3},{3,4},{4,5},{5,6},{6,7},{7,0},{8,9},{9,10},{10,1... | collective-permute-start | bytes 786440 | tf_op jit(solution)/shard_map/ppermute | solution.py:38
  51.5 8.0 %collective-permute-start.5 = (bf16[16,64,128]{2,1,0:T(8,128)(2,1)S(1)}, bf16[16,64,128]{2,1,0:T(8,128)(2,1)S(1)}, u32[]{:S(2)}, u32[]{:S(2)}) collective-permute-start(bf16[16,64,128]{2,1,0:T(8,128)(2,1)S(1)} %collective-permute-done.3), channel_id=1, source_target_pairs={{0,7},{1,0},{2,1},{3,2},{4,3},{5,4},{6,5},{7,6},{8,15},{9,8},{10,9... | collective-permute-start | bytes 786440 | tf_op jit(solution)/shard_map/ppermute | solution.py:38
  59.3 6.8 %collective-permute-start.6 = (bf16[8,64,128]{2,1,0:T(8,128)(2,1)S(1)}, bf16[8,64,128]{2,1,0:T(8,128)(2,1)S(1)}, u32[]{:S(2)}, u32[]{:S(2)}) collective-permute-start(bf16[8,64,128]{2,1,0:T(8,128)(2,1)S(1)} %slice.150), channel_id=1, source_target_pairs={{0,1},{1,2},{2,3},{3,4},{4,5},{5,6},{6,7},{7,0},{8,9},{9,10},{10,1... | collective-permute-start | bytes 393224 | tf_op jit(solution)/shard_map/ppermute | solution.py:38
  59.5 6.7 %collective-permute-start.7 = (bf16[8,64,128]{2,1,0:T(8,128)(2,1)S(1)}, bf16[8,64,128]{2,1,0:T(8,128)(2,1)S(1)}, u32[]{:S(2)}, u32[]{:S(2)}) collective-permute-start(bf16[8,64,128]{2,1,0:T(8,128)(2,1)S(1)} %slice.151), channel_id=1, source_target_pairs={{0,7},{1,0},{2,1},{3,2},{4,3},{5,4},{6,5},{7,6},{8,15},{9,8},{10,9... | collective-permute-start | bytes 393224 | tf_op jit(solution)/shard_map/ppermute | solution.py:38
  66.2 2.9 %copy-start.2 = (bf16[1,512,4096]{2,1,0:T(8,128)(2,1)S(1)}, bf16[1,512,4096]{2,1,0:T(8,128)(2,1)}, u32[]{:S(2)}) copy-start(bf16[1,512,4096]{2,1,0:T(8,128)(2,1)} %param.6) | copy-start | bytes 12582916
  66.4 1.0 copy-start.5
  66.4 1.3 copy-start.7
  70.7 10.9 %copy-start.6 = (bf16[8,8,64,128]{3,2,1,0:T(8,128)(2,1)S(1)}, bf16[8,8,64,128]{3,2,1,0:T(8,128)(2,1)}, u32[]{:S(2)}) copy-start(bf16[8,8,64,128]{3,2,1,0:T(8,128)(2,1)} %copy-done.5) | copy-start | bytes 3145732
  70.7 10.9 %copy-start.8 = (bf16[8,8,64,128]{3,2,1,0:T(8,128)(2,1)S(1)}, bf16[8,8,64,128]{3,2,1,0:T(8,128)(2,1)}, u32[]{:S(2)}) copy-start(bf16[8,8,64,128]{3,2,1,0:T(8,128)(2,1)} %copy-done.7) | copy-start | bytes 3145732
  74.3 11.0 %copy-start.3 = (bf16[1,512,4096]{2,1,0:T(8,128)(2,1)S(1)}, bf16[1,512,4096]{2,1,0:T(8,128)(2,1)}, u32[]{:S(2)}) copy-start(bf16[1,512,4096]{2,1,0:T(8,128)(2,1)} %param.6) | copy-start | bytes 12582916
  74.3 12.3 %collective-permute-start.10 = (f32[512,256]{0,1:T(8,128)S(1)}, f32[512,256]{0,1:T(8,128)S(1)}, u32[]{:S(2)}, u32[]{:S(2)}) collective-permute-start(f32[512,256]{0,1:T(8,128)S(1)} %fusion.11), channel_id=1, source_target_pairs={{0,64},{64,0},{1,65},{65,1},{2,66},{66,2},{3,67},{67,3},{4,68},{68... | collective-permute-start | bytes 1572872 | tf_op jit(solution)/shard_map/ppermute | solution.py:20
  85.0 2.0 collective-permute-start.9
  88.0 1.8 collective-permute-start.11
  129.5 12.8 %copy-start.9 = (f32[64,512]{1,0:T(8,128)S(1)}, f32[64,512]{1,0:T(8,128)}, u32[]{:S(2)}) copy-start(f32[64,512]{1,0:T(8,128)} %param.11) | copy-start | bytes 393220
  142.4 14.7 %collective-permute-start.12 = (bf16[512,4096]{1,0:T(8,128)(2,1)}, bf16[512,4096]{1,0:T(8,128)(2,1)S(1)}, u32[]{:S(2)}, u32[]{:S(2)}) collective-permute-start(bf16[512,4096]{1,0:T(8,128)(2,1)} %bitcast.123), channel_id=1, source_target_pairs={{0,64},{64,0},{1,65},{65,1},{2,66},{66,2},{3,67},{67,3},{4,68},{68... | collective-permute-start | bytes 12582920 | tf_op jit(solution)/shard_map/ppermute | solution.py:20
  188.3 2.8 %copy-start.4 = (bf16[1,512,4096]{2,1,0:T(8,128)(2,1)S(1)}, bf16[1,512,4096]{2,1,0:T(8,128)(2,1)}, u32[]{:S(2)}) copy-start(bf16[1,512,4096]{2,1,0:T(8,128)(2,1)} %param.6) | copy-start | bytes 12582916
  189.6 3.0 %collective-permute-start.13 = (f32[512,256]{0,1:T(8,128)S(1)}, f32[512,256]{0,1:T(8,128)S(1)}, u32[]{:S(2)}, u32[]{:S(2)}) collective-permute-start(f32[512,256]{0,1:T(8,128)S(1)} %fusion.2), channel_id=1, source_target_pairs={{0,64},{64,0},{1,65},{65,1},{2,66},{66,2},{3,67},{67,3},{4,68},{68... | collective-permute-start | bytes 1572872 | tf_op jit(solution)/shard_map/ppermute | solution.py:20
  193.5 2.2 collective-permute-start.14
  198.7 50.9 %copy-start.1 = (bf16[64,512]{1,0:T(8,128)(2,1)S(1)}, bf16[64,512]{1,0:T(8,128)(2,1)}, u32[]{:S(2)}) copy-start(bf16[64,512]{1,0:T(8,128)(2,1)} %param.9) | copy-start | bytes 196612
